TPU v7x, 512 devices: a whole 4x8x8 slice. The times are simulated.
512 devices in a mesh: dp: 16 (over z_lo, x, core), vocab: 32 (over z_hi, y).
Axes of the slice: x: 4, y: 8, z: 8 (z_hi: 4, z_lo: 2; z = z_hi * 2 + z_lo), core: 2. Of those that a mesh axis runs over, the one named last changes fastest.
Arguments:
- hidden: bfloat16 [4096, 1024], P(('dp', 'vocab')), may hold values from -8 to 8
- embed_grad: bfloat16 [4096, 1024], P(('dp', 'vocab')), may hold values from -6 to 6
- token_ids: int32 [4096], P(('dp', 'vocab')), may hold values from 0 to 126975
- lengths: int32 [32], P('dp'), may hold values from 32 to 128, as said below
- pool_index: int32 [32, 126976], P('dp', 'vocab'), may hold values from 0 to 127, as said below
- embedding: bfloat16 [1024, 126976], P('dp', 'vocab'), may hold values from -0.1875 to 0.1875
- head_bias: float32 [126976], P('vocab'), may hold values from -5 to 5
- pooled_grad: float32 [32, 126976], P('dp', 'vocab'), may hold values from -6 to 6
Outputs:
- hidden_grad: bfloat16 [4096, 1024], P(('dp', 'vocab'))
- embedding_grad: float32 [1024, 126976], P('dp', 'vocab')
- bias_grad: float32 [126976], P('vocab')
Inputs may be any that keep to these rules, and one draw needn't show every extreme that they name: `lengths`: passage 0 has all 128 tokens live. pool_index[p, v] is below lengths[p]; pool_index[0, 0] = 127.
All inputs are finite; a program needn't handle non-finite values.
Results may differ from a plain program's by a relative error of at most 0.011.
Values may be sent and summed in bfloat16 or wider, within the bound.
No kernel may reach another device: no remote copies, remote signals or barrier semaphores. Data moves between devices by JAX's collectives and lax.ppermute only.
A program may use at most 64 MiB of HBM per device.

v0:
```python
import math

import jax
import jax.numpy as jnp
from jax import lax
from jax.sharding import PartitionSpec as P


def block_count(passages, seq_len):
    return math.gcd(passages, max(1, 512 // seq_len))


def spread_grads(all_index, all_grad, column_hidden, embedding, seq_len):
    passages, voc_dev = all_index.shape
    block = block_count(passages, seq_len)
    steps = passages // block
    col_dev = embedding.shape[0]
    spots = jnp.arange(seq_len, dtype=jnp.int32)

    def one_block(total, pieces):
        index_block, grad_block, hidden_block = pieces
        hit = index_block[:, :, None] == spots[None, None, :]
        weights = jnp.where(hit, grad_block[:, :, None], jnp.zeros((), jnp.bfloat16))
        total = total + jnp.einsum(
            "bvs,bsc->cv", weights, hidden_block, preferred_element_type=jnp.float32
        )
        part = jnp.zeros((1,), jnp.float32)
        return (total, part)

    total, parts = lax.scan(
        one_block,
        jnp.zeros((col_dev, voc_dev), jnp.float32),
        (
            all_index.reshape(steps, block, voc_dev),
            all_grad.reshape(steps, block, voc_dev),
            column_hidden.reshape(steps, block, seq_len, col_dev),
        ),
    )
    return (total, parts)


def on_device(
    hidden, embed_grad, token_ids, lengths, pool_index, embedding, head_bias, pooled_grad
):
    n_dp = lax.axis_size("dp")
    n_vocab = lax.axis_size("vocab")
    rows, width = hidden.shape
    col_dev, voc_dev = embedding.shape
    p_dev = lengths.shape[0]
    tok_dev = rows * n_vocab
    seq_len = tok_dev // p_dev
    passages = p_dev * n_dp
    vocab_place = lax.axis_index("vocab")
    own_token = vocab_place * rows + jnp.arange(rows, dtype=jnp.int32)
    own_passage = own_token // seq_len
    live = own_token % seq_len < jnp.take(lengths, own_passage)
    masked = jnp.where(live[:, None], embed_grad, jnp.zeros((), jnp.bfloat16))
    group_hidden, group_grad = (
        lax.all_gather(hidden, "vocab", axis=0, tiled=True),
        lax.all_gather(masked, "vocab", axis=0, tiled=True),
    )
    column_hidden, column_grad = (
        lax.all_to_all(group_hidden, "dp", split_axis=1, concat_axis=0, tiled=True),
        lax.all_to_all(group_grad, "dp", split_axis=1, concat_axis=0, tiled=True),
    )
    all_ids = lax.all_gather(token_ids, ("dp", "vocab"), axis=0, tiled=True)
    all_index = lax.all_gather(pool_index, "dp", axis=0, tiled=True)
    spots = jnp.arange(seq_len, dtype=jnp.int32)
    full_embed = lax.all_gather(embedding, "dp", axis=0, tiled=True)
    dense = jnp.dot(group_hidden, full_embed, preferred_element_type=jnp.float32)
    dense = dense.reshape(p_dev, seq_len, voc_dev)
    hit = pool_index[:, None, :] == spots[None, :, None]
    logits = jnp.sum(jnp.where(hit, dense, 0.0), axis=1) + head_bias[None, :]
    softened = jax.nn.softplus(logits)
    pooled = jnp.log1p(softened)
    slope = jax.nn.sigmoid(logits) / (1.0 + softened)
    mean_pooled = lax.psum(jnp.sum(pooled, axis=0), "dp") / passages
    logit_grad = ((pooled_grad + mean_pooled[None, :]) * slope).astype(jnp.bfloat16)
    all_grad = lax.all_gather(logit_grad, "dp", axis=0, tiled=True)
    bias_grad = jnp.sum(all_grad.astype(jnp.float32), axis=0)
    decoder_grad, unused = spread_grads(all_index, all_grad, column_hidden, embedding, seq_len)
    token = jnp.arange(rows * lax.axis_size("vocab"), dtype=jnp.int32)
    owner = token // seq_len
    spot = token % seq_len
    index_rows = jnp.take(pool_index, owner, axis=0)
    grad_rows = jnp.take(logit_grad, owner, axis=0)
    weights = jnp.where(index_rows == spot[:, None], grad_rows, jnp.zeros((), jnp.bfloat16))
    hidden_grad = lax.psum_scatter(
        lax.dot_general(
            weights, full_embed, (((1,), (1,)), ((), ())), preferred_element_type=jnp.float32
        ),
        "vocab",
        scatter_dimension=0,
        tiled=True,
    ).astype(jnp.bfloat16)
    local_ids = all_ids - vocab_place * voc_dev
    inside = (local_ids >= 0) & (local_ids < voc_dev)
    target = jnp.where(inside, local_ids, voc_dev)
    input_grad = (
        jnp.zeros((col_dev, voc_dev), jnp.float32)
        .at[:, target]
        .add(jnp.transpose(column_grad.astype(jnp.float32)), mode="drop")
    )
    embedding_grad = decoder_grad + input_grad
    return (hidden_grad, embedding_grad, bias_grad)


def solution(mesh):
    return jax.shard_map(
        on_device,
        mesh=mesh,
        in_specs=(
            P(("dp", "vocab"), None),
            P(("dp", "vocab"), None),
            P(("dp", "vocab")),
            P("dp"),
            P("dp", "vocab"),
            P("dp", "vocab"),
            P("vocab"),
            P("dp", "vocab"),
        ),
        out_specs=(P(("dp", "vocab"), None), P("dp", "vocab"), P("vocab")),
        check_vma=False,
    )
```

profile of v0, /device:TPU:1, one launch (start us, length us, event | category | flops | bytes accessed | tf_op | source)
XLA Modules:
  0.0 612.0 jit_solution(16660612881928461334)
XLA Ops:
  7.9 78.5 %all_gather.18 = bf16[256,1024]{1,0:T(8,128)(2,1)S(1)} all-gather(bf16[8,1024]{1,0:T(8,128)(2,1)} %param.10), channel_id=1, replica_groups=mesh['dp'=16,'vocab'=32] {'vocab'}, dimensions={0}, use_global_device_ids=true | all-gather | bytes 540672 | tf_op jit(solution)/shard_map/all_gather | solution.py:59
  87.4 20.0 %all-to-all-start = ((bf16[256,16,64]{0,2,1:T(8,128)(2,1)}), bf16[256,16,64]{0,2,1:T(8,128)(2,1)S(1)}, u32[]{:S(2)}, u32[]{:S(2)}) async-start(bf16[256,16,64]{0,2,1:T(8,128)(2,1)} %bitcast.2), calls=%async_computation.1 | async-start | bytes 1048576 | tf_op jit(solution)/shard_map/all_to_all | solution.py:63
  108.9 65.7 %all_gather.23 = bf16[256,1024]{1,0:T(8,128)(2,1)S(1)} all-gather(bf16[8,1024]{1,0:T(8,128)(2,1)S(1)} %broadcast_select_fusion), channel_id=1, replica_groups=mesh['dp'=16,'vocab'=32] {'vocab'}, dimensions={0}, use_global_device_ids=true | all-gather | bytes 540672 | tf_op jit(solution)/shard_map/all_gather | solution.py:60
  175.6 19.0 %all-to-all-start.1 = ((bf16[256,16,64]{0,2,1:T(8,128)(2,1)}), bf16[256,16,64]{0,2,1:T(8,128)(2,1)S(1)}, u32[]{:S(2)}, u32[]{:S(2)}) async-start(bf16[256,16,64]{0,2,1:T(8,128)(2,1)} %bitcast.7), calls=%async_computation.2 | async-start | bytes 1048576 | tf_op jit(solution)/shard_map/all_to_all | solution.py:64
  194.7 3.4 gather_fusion
  198.1 21.3 %all-gather = s32[16,2,3968]{2,1,0:T(2,128)S(1)} all-gather(s32[1,2,3968]{2,1,0:T(2,128)S(1)} %bitcast.37), channel_id=1, replica_groups=mesh['dp'=16,'vocab'=32] {'dp'}, dimensions={0}, use_global_device_ids=true | all-gather | bytes 539648 | tf_op jit(solution)/shard_map/all_gather | solution.py:67
  220.1 93.9 %all-reduce = s32[4096]{0:T(1024)S(1)} all-reduce(s32[4096]{0:T(1024)S(1)} %dynamic-update-slice), channel_id=1, replica_groups=mesh['dp'=16,'vocab'=32] {'dp','vocab'}, use_global_device_ids=true, to_apply=%add | all-reduce | flops 4096 | bytes 32768
  314.7 2.0 copy.36
  316.6 5.7 select_reduce_fusion
  322.6 50.3 %psum.7 = f32[3968]{0:T(1024)S(1)} all-reduce(f32[3968]{0:T(1024)S(1)} %log-plus-one_reduce_fusion), channel_id=1, replica_groups=mesh['dp'=16,'vocab'=32] {'dp'}, use_global_device_ids=true, to_apply=%region_2.3 | all-reduce | flops 3968 | bytes 31744 | tf_op jit(solution)/shard_map/psum | solution.py:77
  373.0 1.8 gather_fusion.1
  374.8 8.1 %fusion.10 = f32[256,1024]{1,0:T(8,128)} fusion(bf16[1024,3968]{1,0:T(8,128)(2,1)} %all-gather.4.cloned.1.call-done, s32[256,3968]{1,0:T(8,128)} %gather_fusion, bf16[256,3968]{1,0:T(8,128)(2,1)S(1)} %gather_fusion.1, s32[256]{0:T(256)S(1)} %and_select_fusion.5, pred[256]{0:T(512)(128)(4,1)S(1)} %compare_and_fusion), kind=kOutput, calls=%fused_computation.21 | convolution fusion | flops 2084438016 | bytes 15271168 | tf_op jit(solution)/shard_map/dot_general | solution.py:89
  383.0 21.1 %all-gather.1 = bf16[16,2,3968]{2,1,0:T(2,128)(2,1)S(1)} all-gather(bf16[1,2,3968]{2,1,0:T(2,128)(2,1)S(1)} %bitcast.38), channel_id=1, replica_groups=mesh['dp'=16,'vocab'=32] {'dp'}, dimensions={0}, use_global_device_ids=true | all-gather | bytes 269824 | tf_op jit(solution)/shard_map/all_gather | solution.py:79
  404.2 52.9 %while.11 = (s32[]{:T(128)}, f32[64,3968]{1,0:T(8,128)}, bf16[8,4,128,64]{2,1,0,3:T(4,128)(2,1)S(1)}, s32[8,4,3968]{2,1,0:T(4,128)S(1)}, bf16[8,4,3968]{2,1,0:T(4,128)(2,1)S(1)}, /*index=5*/s32[]{:T(128)}, s32[]{:T(128)}) while((s32[]{:T(128)}, f32[64,3968]{1,0:T(8,128)}, bf16[8,4,128,64]{2,1,0,3:T(4,128)(2,1)S(1)}, ...), condition=%wide.region_5.6_spmd.clone, body=%wide.region_4.5_spmd.clone.sunk | while | flops 264617984 | bytes 2514027 | solution.py:30
  404.3 5.5 fusion.32
  409.8 6.7 %fusion.32 = f32[64,3968]{1,0:T(8,128)} fusion(s32[4,3968]{1,0:T(4,128)S(1)} %dynamic-slice_bitcast_fusion.4, bf16[4,3968]{1,0:T(4,128)(2,1)S(1)} %dynamic-slice_bitcast_fusion.5, f32[64,3968]{1,0:T(8,128)} %get-tuple-element.132, pred[]{:T(512)S(6)} %compare.34, bf16[1,4,128,64]{2,1,0,3:T(4,128)(2,1)S(1)} %constant_dynamic-slice_fusion.2), kind=kOutput, calls=%fused_computation.8.clone.1 | convolution fusion | flops 264617984 | bytes 2192385 | tf_op jit(solution)/shard_map/while/body/eval_jaxpr/bvs,bsc->cv/dot_general | solution.py:24
  416.6 6.7 %fusion.32 = f32[64,3968]{1,0:T(8,128)} fusion(s32[4,3968]{1,0:T(4,128)S(1)} %dynamic-slice_bitcast_fusion.4, bf16[4,3968]{1,0:T(4,128)(2,1)S(1)} %dynamic-slice_bitcast_fusion.5, f32[64,3968]{1,0:T(8,128)} %get-tuple-element.132, pred[]{:T(512)S(6)} %compare.34, bf16[1,4,128,64]{2,1,0,3:T(4,128)(2,1)S(1)} %constant_dynamic-slice_fusion.2), kind=kOutput, calls=%fused_computation.8.clone.1 | convolution fusion | flops 264617984 | bytes 2192385 | tf_op jit(solution)/shard_map/while/body/eval_jaxpr/bvs,bsc->cv/dot_general | solution.py:24
  423.3 6.7 %fusion.32 = f32[64,3968]{1,0:T(8,128)} fusion(s32[4,3968]{1,0:T(4,128)S(1)} %dynamic-slice_bitcast_fusion.4, bf16[4,3968]{1,0:T(4,128)(2,1)S(1)} %dynamic-slice_bitcast_fusion.5, f32[64,3968]{1,0:T(8,128)} %get-tuple-element.132, pred[]{:T(512)S(6)} %compare.34, bf16[1,4,128,64]{2,1,0,3:T(4,128)(2,1)S(1)} %constant_dynamic-slice_fusion.2), kind=kOutput, calls=%fused_computation.8.clone.1 | convolution fusion | flops 264617984 | bytes 2192385 | tf_op jit(solution)/shard_map/while/body/eval_jaxpr/bvs,bsc->cv/dot_general | solution.py:24
  430.1 6.7 %fusion.32 = f32[64,3968]{1,0:T(8,128)} fusion(s32[4,3968]{1,0:T(4,128)S(1)} %dynamic-slice_bitcast_fusion.4, bf16[4,3968]{1,0:T(4,128)(2,1)S(1)} %dynamic-slice_bitcast_fusion.5, f32[64,3968]{1,0:T(8,128)} %get-tuple-element.132, pred[]{:T(512)S(6)} %compare.34, bf16[1,4,128,64]{2,1,0,3:T(4,128)(2,1)S(1)} %constant_dynamic-slice_fusion.2), kind=kOutput, calls=%fused_computation.8.clone.1 | convolution fusion | flops 264617984 | bytes 2192385 | tf_op jit(solution)/shard_map/while/body/eval_jaxpr/bvs,bsc->cv/dot_general | solution.py:24
  436.9 6.7 %fusion.32 = f32[64,3968]{1,0:T(8,128)} fusion(s32[4,3968]{1,0:T(4,128)S(1)} %dynamic-slice_bitcast_fusion.4, bf16[4,3968]{1,0:T(4,128)(2,1)S(1)} %dynamic-slice_bitcast_fusion.5, f32[64,3968]{1,0:T(8,128)} %get-tuple-element.132, pred[]{:T(512)S(6)} %compare.34, bf16[1,4,128,64]{2,1,0,3:T(4,128)(2,1)S(1)} %constant_dynamic-slice_fusion.2), kind=kOutput, calls=%fused_computation.8.clone.1 | convolution fusion | flops 264617984 | bytes 2192385 | tf_op jit(solution)/shard_map/while/body/eval_jaxpr/bvs,bsc->cv/dot_general | solution.py:24
  443.6 6.7 %fusion.32 = f32[64,3968]{1,0:T(8,128)} fusion(s32[4,3968]{1,0:T(4,128)S(1)} %dynamic-slice_bitcast_fusion.4, bf16[4,3968]{1,0:T(4,128)(2,1)S(1)} %dynamic-slice_bitcast_fusion.5, f32[64,3968]{1,0:T(8,128)} %get-tuple-element.132, pred[]{:T(512)S(6)} %compare.34, bf16[1,4,128,64]{2,1,0,3:T(4,128)(2,1)S(1)} %constant_dynamic-slice_fusion.2), kind=kOutput, calls=%fused_computation.8.clone.1 | convolution fusion | flops 264617984 | bytes 2192385 | tf_op jit(solution)/shard_map/while/body/eval_jaxpr/bvs,bsc->cv/dot_general | solution.py:24
  450.4 6.7 %fusion.32 = f32[64,3968]{1,0:T(8,128)} fusion(s32[4,3968]{1,0:T(4,128)S(1)} %dynamic-slice_bitcast_fusion.4, bf16[4,3968]{1,0:T(4,128)(2,1)S(1)} %dynamic-slice_bitcast_fusion.5, f32[64,3968]{1,0:T(8,128)} %get-tuple-element.132, pred[]{:T(512)S(6)} %compare.34, bf16[1,4,128,64]{2,1,0,3:T(4,128)(2,1)S(1)} %constant_dynamic-slice_fusion.2), kind=kOutput, calls=%fused_computation.8.clone.1 | convolution fusion | flops 264617984 | bytes 2192385 | tf_op jit(solution)/shard_map/while/body/eval_jaxpr/bvs,bsc->cv/dot_general | solution.py:24
  458.9 23.4 %scatter_fusion = f32[64,3968]{0,1:T(8,128)S(1)} fusion(f32[64,3968]{0,1:T(8,128)S(1)} %copy.33, s32[4096]{0:T(1024)S(1)} %compare_select_fusion.1, f32[4096,64]{1,0:T(8,128)} %bitcast.39), kind=kCustom, calls=%fused_computation.3 | custom fusion | flops 262144 | bytes 3162112 | tf_op jit(solution)/shard_map/scatter-add | solution.py:102
  484.7 119.1 %reduce-scatter.2.cloned.1.call-done = f32[8,1024]{1,0:T(8,128)} async-done(((f32[256,1024]{1,0:T(8,128)}), f32[8,1024]{1,0:T(8,128)}) %reduce-scatter.2.cloned.1.call-update) | async-done | bytes 32784 | tf_op jit(solution)/shard_map/reduce_scatter | solution.py:88
  (68 shorter events, 11.9 us)
Async XLA Ops:
  7.2 100.2 %copy-start = (s32[2]{0:T(128)S(1)}, s32[2]{0:T(128)}, u32[]{:S(2)}) copy-start(s32[2]{0:T(128)} %param.13) | copy-start | bytes 28
  7.2 187.5 %copy-start.1 = (s32[2,3968]{1,0:T(2,128)S(1)}, s32[2,3968]{1,0:T(2,128)}, u32[]{:S(2)}) copy-start(s32[2,3968]{1,0:T(2,128)} %param.14) | copy-start | bytes 95236
  7.2 309.5 %all-gather.4.cloned.1.call-start = ((), (), s32[]{:S(2)}) async-start(), calls=%async_computation.3 | async-start | bytes 8634368 | tf_op jit(solution)/shard_map/all_gather | solution.py:69
  87.4 88.2 %all-to-all-start = ((bf16[256,16,64]{0,2,1:T(8,128)(2,1)}), bf16[256,16,64]{0,2,1:T(8,128)(2,1)S(1)}, u32[]{:S(2)}, u32[]{:S(2)}) async-start(bf16[256,16,64]{0,2,1:T(8,128)(2,1)} %bitcast.2), calls=%async_computation.1 | async-start | bytes 1048576 | tf_op jit(solution)/shard_map/all_to_all | solution.py:63
  175.6 139.0 %all-to-all-start.1 = ((bf16[256,16,64]{0,2,1:T(8,128)(2,1)}), bf16[256,16,64]{0,2,1:T(8,128)(2,1)S(1)}, u32[]{:S(2)}, u32[]{:S(2)}) async-start(bf16[256,16,64]{0,2,1:T(8,128)(2,1)} %bitcast.7), calls=%async_computation.2 | async-start | bytes 1048576 | tf_op jit(solution)/shard_map/all_to_all | solution.py:64
  194.6 409.2 %reduce-scatter.2.cloned.1.call-start = ((), (), s32[]{:S(2)}) async-start(), calls=%async_computation.4 | async-start | bytes 1081344 | tf_op jit(solution)/shard_map/reduce_scatter | solution.py:88
  194.7 25.2 %copy-start.4 = (s32[8]{0:T(128)S(1)}, s32[8]{0:T(128)}, u32[]{:S(2)}) copy-start(s32[8]{0:T(128)} %param.12) | copy-start | bytes 100
  316.6 5.8 copy-start.2
  316.6 56.2 %copy-start.3 = (f32[2,3968]{1,0:T(2,128)S(1)}, f32[2,3968]{1,0:T(2,128)}, u32[]{:S(2)}) copy-start(f32[2,3968]{1,0:T(2,128)} %param.17) | copy-start | bytes 95236
Sparse Core Ops, SparseCore 0:
  10.2 65.6 all-gather.3
  383.1 220.6 reduce-scatter.1
where the time goes:
time: 617 us; the launch traced here: 612 us
  blocking collectives  331 us (54%)
  waiting for transfers between devices  120 us (19%)
  matrix products  66.1 us (11%)
  starting transfers between devices  39.1 us (6%)
  other arithmetic  26.9 us (4%)
  local copies, waits for them, and re-layouts  14.9 us (2%)
  between operations  14.2 us (2%)
    reduce_scatter x1, waiting for transfers between devices, on_device(): lax.psum_scatter(lax.dot_general(weights, full_embed, (((1,), (1,)), ((),...  119 us
    unnamed x1, blocking collectives  93.9 us
    all_gather x1, blocking collectives, on_device(): lax.all_gather(hidden, 'vocab', axis=0, tiled=True)  78.5 us
    all_gather x1, blocking collectives, on_device(): lax.all_gather(masked, 'vocab', axis=0, tiled=True)  65.7 us
    dot_general x8, matrix products, one_block(): jnp.einsum('bvs,bsc->cv', weights, hidden_block, preferred_element_type=j...  52.3 us
    psum x1, blocking collectives, on_device(): mean_pooled = lax.psum(jnp.sum(pooled, axis=0), 'dp') / passages  50.3 us
    scatter-add x1, other arithmetic, on_device(): input_grad = jnp.zeros((col_dev, voc_dev), jnp.float32).at[:, target].add...  23.4 us
    all_gather x1, blocking collectives, on_device(): all_index = lax.all_gather(pool_index, 'dp', axis=0, tiled=True)  21.3 us
  transfers between devices with their start and end apart: 4, of which 1 were waited for; matrix products, arithmetic and copies ran while one was open for 15% of the time, Pallas kernels for 0%

commit v1 on v0

v1 whole, which is shorter than its diff:
```python
import functools

import jax
import jax.numpy as jnp
from jax import lax
from jax.experimental import pallas as pl
from jax.experimental.pallas import tpu as pltpu
from jax.sharding import PartitionSpec as P

F32 = jnp.float32
BF16 = jnp.bfloat16
I16 = jnp.int16
I32 = jnp.int32
LANES = 128
PARAMS = pltpu.CompilerParams(vmem_limit_bytes=48 * 1024 * 1024)
SMEM = pl.BlockSpec(memory_space=pltpu.SMEM)
VMEM = pl.BlockSpec(memory_space=pltpu.VMEM)

GROUPS = 16
SHARDS = 32
SEQ = 128
PASSAGES = 32
COLS = 64
ROWS = 8
TILES = 31
VOC = TILES * LANES
CHUNK = 256


def lane_gather(table, index):
    numbers = lax.GatherDimensionNumbers(
        offset_dims=(),
        collapsed_slice_dims=(1,),
        start_index_map=(1,),
        operand_batching_dims=(0,),
        start_indices_batching_dims=(0,),
    )
    return lax.gather(
        table,
        index[..., None],
        numbers,
        (1, 1),
        mode=lax.GatherScatterMode.PROMISE_IN_BOUNDS,
    )


def pack_body(place_ref, lengths_ref, ids_ref, hidden_ref, grad_ref, index_ref, out_ref, rows):
    place = place_ref[0]
    limit = lengths_ref[place // (SEQ // ROWS)]
    spot = (place % (SEQ // ROWS)) * ROWS + lax.broadcasted_iota(I32, (ROWS, 1), 0)
    hidden = hidden_ref[...].astype(F32)
    masked = jnp.where(spot < limit, grad_ref[...].astype(F32), 0.0)
    row = lax.broadcasted_iota(I32, (ROWS, LANES), 0)
    lane = lax.broadcasted_iota(I32, (ROWS, LANES), 1)
    ids = jnp.zeros((ROWS, LANES), I32)
    for r in range(ROWS):
        ids = jnp.where(row == r, ids_ref[r], ids)
    digits = jnp.where(lane == 0, ids & 127, jnp.where(lane == 1, (ids >> 7) & 127, ids >> 14))
    digits = jnp.where(lane < 3, digits, 0).astype(F32)
    rows[...] = jnp.zeros_like(rows)
    for tile in range(TILES):
        rows[2 * tile : 2 * tile + 2, :] = index_ref[:, tile * LANES : (tile + 1) * LANES].astype(F32)
    spots = rows[...].astype(BF16)
    for g in range(GROUPS):
        own = jnp.concatenate(
            [hidden[:, g * COLS : (g + 1) * COLS], masked[:, g * COLS : (g + 1) * COLS]], axis=1
        )
        out_ref[g, 0:16, :] = jnp.concatenate([own, digits], axis=0).astype(BF16)
        out_ref[g, 16:80, :] = spots


def spread_body(got_ref, hidden_out, grad_out):
    hidden = []
    grads = []
    digits = []
    for g in range(GROUPS):
        block = got_ref[g, 0:16, :].astype(F32)
        hidden.append(block[0:8, 0:COLS])
        grads.append(block[0:8, COLS:])
        digits.append(block[8:16, :])
    hidden = jnp.concatenate(
        [jnp.concatenate([hidden[g], hidden[g + 1]], axis=1) for g in range(0, GROUPS, 2)], axis=0
    ).astype(BF16)
    grads = jnp.concatenate(
        [jnp.concatenate([grads[g], grads[g + 1]], axis=1) for g in range(0, GROUPS, 2)], axis=0
    ).astype(BF16)
    digits = jnp.concatenate(digits[0::2] + digits[1::2], axis=0).T[0:16, :].astype(BF16)
    for s in range(SHARDS):
        hidden_out[s] = hidden
        grad_out[s, 0:64, :] = grads
        grad_out[s, 64:80, :] = digits


def logits_body(hidden_ref, got_ref, embed_ref, pooled_ref, out_ref, table_ref, spots):
    for pair in range(4):
        for half in range(2):
            block = hidden_ref[half * 16 : half * 16 + 16, pair * 16 : pair * 16 + 16, :].astype(F32)
            for s in range(2):
                turned = block[:, s * 8 : s * 8 + 8, :].reshape(SEQ, LANES).T.astype(BF16)
                first = 4 * (2 * pair + s) + half
                table_ref[first] = turned[0:COLS]
                table_ref[first + 2] = turned[COLS:]
    for g in range(GROUPS):
        spots[g] = got_ref[g, 16:80, :].astype(I32)

    def one_tile(tile, carry):
        at = pl.multiple_of(tile * LANES, LANES)
        embed = embed_ref[:, pl.ds(at, LANES)].astype(F32)
        lane_at = pl.multiple_of((tile % 2) * LANES, LANES)
        for p in range(PASSAGES):
            index = spots[p // 2, pl.ds(2 * tile + p % 2, 1), :]
            index = jnp.broadcast_to(index, (16, LANES)).astype(I16)
            total = jnp.zeros((8, LANES), F32)
            for d in range(0, COLS, 16):
                picked = lane_gather(table_ref[p, d : d + 16, :], index).astype(F32)
                product = picked * embed[d : d + 16]
                total = total + product[0:8] + product[8:16]
            out_ref[tile // 2, p : p + 1, pl.ds(lane_at, LANES)] = jnp.sum(total, axis=0, keepdims=True)
        out_ref[tile // 2, 32:34, pl.ds(lane_at, LANES)] = pooled_ref[:, pl.ds(at, LANES)]
        return carry

    lax.fori_loop(0, TILES, one_tile, 0)
    out_ref[GROUPS - 1, :, LANES:] = jnp.zeros((40, LANES), F32)


def slope_body(part_ref, bias_ref, out_ref):
    total = part_ref[0, 0:32, :]
    for g in range(1, GROUPS):
        total = total + part_ref[g, 0:32, :]
    logits = total + bias_ref[...]
    softened = jnp.maximum(logits, 0.0) + jnp.log1p(jnp.exp(-jnp.abs(logits)))
    pooled = jnp.log1p(softened)
    sigmoid = 1.0 / (1.0 + jnp.exp(-logits))
    slope = sigmoid / (1.0 + softened)
    mean_pooled = jnp.sum(pooled, axis=0, keepdims=True) / PASSAGES
    upstream = jnp.concatenate([part_ref[g, 32:34, :] for g in range(GROUPS)], axis=0)
    grad = ((upstream + mean_pooled) * slope).astype(BF16)
    for g in range(GROUPS):
        out_ref[g] = grad


def hidden_body(grad_ref, got_ref, embed_ref, out_ref, spots, grads, total):
    for g in range(GROUPS):
        spots[g] = got_ref[g, 16:80, :].astype(I32)
    total[...] = jnp.zeros_like(total)
    here = lax.broadcasted_iota(I32, (SEQ, LANES), 0).astype(I16)
    zero = jnp.zeros((), BF16)

    def one_chunk(chunk, width):
        at = pl.multiple_of(chunk * CHUNK, CHUNK)
        embed = embed_ref[:, pl.ds(at, width)]
        blank = jnp.zeros((COLS, width), BF16)
        right = jnp.concatenate(
            [jnp.concatenate([embed, blank], axis=1), jnp.concatenate([blank, embed], axis=1)], axis=0
        )
        grads[...] = grad_ref[chunk].astype(F32)

        def weights(p):
            parts = []
            for tile in range(width // LANES):
                index = spots[p // 2, pl.ds(4 * chunk + 2 * tile + p % 2, 1), :]
                index = jnp.broadcast_to(index, (16, LANES)).astype(I16)
                value = grads[p : p + 1, tile * LANES : (tile + 1) * LANES]
                value = jnp.broadcast_to(value, (16, LANES)).astype(BF16)
                index = jnp.concatenate([index] * 8, axis=0)
                value = jnp.concatenate([value] * 8, axis=0)
                parts.append(jnp.where(index == here, value, zero))
            return parts

        for pair in range(8):
            for half in range(2):
                first = 4 * pair + half
                left = jnp.concatenate(weights(first) + weights(first + 2), axis=1)
                product = lax.dot_general(
                    left, right, (((1,), (1,)), ((), ())), preferred_element_type=F32
                )
                rows = (slice(half * 16, half * 16 + 16), slice(pair * 8, pair * 8 + 8))
                total[rows] += product.reshape(16, 8, LANES)

    def loop(chunk, carry):
        one_chunk(chunk, CHUNK)
        return carry

    lax.fori_loop(0, GROUPS - 1, loop, 0)
    one_chunk(GROUPS - 1, LANES)
    out_ref[...] = total[...].astype(BF16)


def token_body(place_ref, got_ref, out_ref, left, right):
    base = place_ref[0] * VOC
    low_row = lax.broadcasted_iota(I32, (512, LANES), 0)
    out_ref[...] = jnp.zeros_like(out_ref)

    def one_block(block, carry):
        for s in range(8):
            shard = block * 8 + s
            rows = got_ref[shard].astype(F32)
            digits = rows[64:72].astype(I32)
            local = (digits[2:3] << 14) + (digits[1:2] << 7) + digits[0:1] - base
            high = local >> 9
            low = local & 511
            turned = rows[0:64].T
            grads = jnp.concatenate([turned[0:COLS], turned[COLS:]], axis=1)
            lanes = slice(s * LANES, (s + 1) * LANES)
            for h in range(8):
                left[h * COLS : (h + 1) * COLS, lanes] = jnp.where(high == h, grads, 0.0).astype(BF16)
            right[:, lanes] = jnp.where(low_row == low, 1.0, 0.0).astype(BF16)
        for h in range(8):
            out_ref[:, h * 512 : (h + 1) * 512] += lax.dot_general(
                left[h * COLS : (h + 1) * COLS, :],
                right[...],
                (((1,), (1,)), ((), ())),
                preferred_element_type=F32,
            )
        return carry

    lax.fori_loop(0, 4, one_block, 0)


def embed_body(grad_ref, got_ref, table_ref, token_ref, out_ref, bias_ref, spots, grads):
    for g in range(GROUPS):
        spots[g] = got_ref[g, 16:80, :].astype(I32)
        grads[g] = grad_ref[g].astype(F32)

    def one_tile(tile, carry):
        at = pl.multiple_of(tile * LANES, LANES)
        lane_at = pl.multiple_of((tile % 2) * LANES, LANES)
        totals = [token_ref[d : d + 16, pl.ds(at, LANES)] for d in range(0, COLS, 16)]
        for p in range(PASSAGES):
            index = spots[p // 2, pl.ds(2 * tile + p % 2, 1), :]
            index = jnp.broadcast_to(index, (16, LANES)).astype(I16)
            value = grads[tile // 2, p : p + 1, pl.ds(lane_at, LANES)]
            for n in range(COLS // 16):
                picked = lane_gather(table_ref[p, n * 16 : n * 16 + 16, :], index).astype(F32)
                totals[n] = totals[n] + picked * value
        for n in range(COLS // 16):
            out_ref[n * 16 : n * 16 + 16, pl.ds(at, LANES)] = totals[n]
        bias_ref[:, pl.ds(at, LANES)] = jnp.sum(
            grads[tile // 2, :, pl.ds(lane_at, LANES)], axis=0, keepdims=True
        )
        return carry

    lax.fori_loop(0, TILES, one_tile, 0)


def sum_body(part_ref, out_ref):
    total = part_ref[0].astype(F32)
    for s in range(1, SHARDS):
        total = total + part_ref[s].astype(F32)
    for g in range(GROUPS):
        rows = total[(g // 2) * 8 : (g // 2) * 8 + 8, :]
        if g % 2:
            rows = jnp.concatenate([rows[:, COLS:], rows[:, :COLS]], axis=1)
        out_ref[g] = rows


def call(body, name, out, scratch=(), specs=None, flops=0, reads=0):
    return pl.pallas_call(
        body,
        out_shape=out,
        in_specs=specs,
        scratch_shapes=scratch,
        compiler_params=PARAMS,
        cost_estimate=pl.CostEstimate(flops=flops, bytes_accessed=reads, transcendentals=0),
        name=name,
    )


def shape(dims, dtype):
    return jax.ShapeDtypeStruct(dims, dtype)


def exchange(x, axis):
    return lax.all_to_all(x, axis, split_axis=0, concat_axis=0, tiled=True)


def on_device(
    hidden, embed_grad, token_ids, lengths, pool_index, embedding, head_bias, pooled_grad
):
    place = lax.axis_index("vocab").astype(I32).reshape(1)
    packed = call(
        pack_body,
        "pack",
        shape((GROUPS, 80, LANES), BF16),
        [pltpu.VMEM((64, LANES), F32)],
        [SMEM, SMEM, SMEM, VMEM, VMEM, VMEM],
    )(place, lengths, token_ids, hidden, embed_grad, pool_index)
    got = exchange(packed, "dp")
    hidden_rows, grad_rows = call(
        spread_body,
        "spread",
        (shape((SHARDS, 64, LANES), BF16), shape((SHARDS, 80, LANES), BF16)),
        specs=[VMEM],
    )(got)
    all_hidden = exchange(hidden_rows, "vocab")
    all_grads = exchange(grad_rows, "vocab")
    partial, table = call(
        logits_body,
        "logits",
        (shape((GROUPS, 40, CHUNK), F32), shape((PASSAGES, COLS, LANES), BF16)),
        [pltpu.VMEM((GROUPS, 64, LANES), I32)],
        [VMEM, VMEM, VMEM, VMEM],
    )(all_hidden, got, embedding, pooled_grad)
    parts = exchange(partial, "dp")
    bias = jnp.pad(head_bias, (0, GROUPS * CHUNK - VOC)).reshape(GROUPS, 1, CHUNK)
    bias = lax.dynamic_index_in_dim(bias, lax.axis_index("dp"), 0, keepdims=False)
    grad_block = call(
        slope_body, "slope", shape((GROUPS, PASSAGES, CHUNK), BF16), specs=[VMEM, VMEM]
    )(parts, bias)
    all_grad = exchange(grad_block, "dp")
    hidden_parts = call(
        hidden_body,
        "hidden_grad",
        shape((SHARDS, 64, LANES), BF16),
        [
            pltpu.VMEM((GROUPS, 64, LANES), I32),
            pltpu.VMEM((PASSAGES, CHUNK), F32),
            pltpu.VMEM((SHARDS, 64, LANES), F32),
        ],
        [VMEM, VMEM, VMEM],
    )(all_grad, got, embedding)
    hidden_got = exchange(hidden_parts, "vocab")
    token_grad = call(
        token_body,
        "token_grad",
        shape((COLS, 4096), F32),
        [pltpu.VMEM((512, 1024), BF16), pltpu.VMEM((512, 1024), BF16)],
        [SMEM, VMEM],
    )(place, all_grads)
    embedding_grad, bias_grad = call(
        embed_body,
        "embedding_grad",
        (shape((COLS, VOC), F32), shape((1, VOC), F32)),
        [pltpu.VMEM((GROUPS, 64, LANES), I32), pltpu.VMEM((GROUPS, PASSAGES, CHUNK), F32)],
        [VMEM, VMEM, VMEM, VMEM],
    )(all_grad, got, table, token_grad)
    hidden_sum = call(sum_body, "sum_shards", shape((GROUPS, ROWS, LANES), F32), specs=[VMEM])(
        hidden_got
    )
    blocks = exchange(hidden_sum, "dp")
    hidden_grad = blocks[:, :, :COLS].transpose(1, 0, 2).reshape(ROWS, GROUPS * COLS).astype(BF16)
    return hidden_grad, embedding_grad, bias_grad.reshape(VOC)


def solution(mesh):
    return jax.shard_map(
        on_device,
        mesh=mesh,
        in_specs=(
            P(("dp", "vocab"), None),
            P(("dp", "vocab"), None),
            P(("dp", "vocab")),
            P("dp"),
            P("dp", "vocab"),
            P("dp", "vocab"),
            P("vocab"),
            P("dp", "vocab"),
        ),
        out_specs=(P(("dp", "vocab"), None), P("dp", "vocab"), P("vocab")),
        check_vma=False,
    )
```

time: 617 us -> 185 us (0.30)
  blocking collectives: 331 us -> 77.8 us
  waiting for transfers between devices: 120 us -> 28.2 us
  matrix products: 66.1 us -> 0 us
  Pallas kernels: 0 us -> 47.9 us
  other arithmetic: 26.9 us -> 1.26 us
  starting transfers between devices: 39.1 us -> 24.6 us
  between operations: 14.2 us -> 0.71 us
  local copies, waits for them, and re-layouts: 14.9 us -> 3.59 us
    all_gather x4 -> x0, blocking collectives: 187 us -> none  [the longest x1 78.5 us: on_device(): lax.all_gather(hidden, 'vocab', axis=0, tiled=True)]
    reduce_scatter x1 -> x0, waiting for transfers between devices: 119 us -> none  [on_device(): lax.psum_scatter(lax.dot_general(weights, full_embed, (((1,), (1,)), ((),...]
    unnamed x1 -> x0, blocking collectives: 93.9 us -> none
    all_to_all x0 -> x4, blocking collectives: none -> 77.8 us  [exchange(): return lax.all_to_all(x, axis, split_axis=0, concat_axis=0, tiled=True)]
    dot_general x10 -> x0, matrix products: 66.1 us -> none  [the longest x8 52.3 us: one_block(): jnp.einsum('bvs,bsc->cv', weights, hidden_block, preferred_element_type=j...]
    psum x1 -> x0, blocking collectives: 50.3 us -> none  [on_device(): mean_pooled = lax.psum(jnp.sum(pooled, axis=0), 'dp') / passages]
    pallas_call x0 -> x8, Pallas kernels: none -> 47.9 us  [the longest x1 12.8 us: on_device(): call(token_body, 'token_grad', shape((COLS, 4096), F32), [pltpu.VMEM((512...]
    all_to_all x2 -> x3, waiting for transfers between devices: 0.01 us -> 28.2 us  [exchange(): return lax.all_to_all(x, axis, split_axis=0, concat_axis=0, tiled=True)]
  transfers between devices with their start and end apart: 4 -> 3, of which waited for: 1 -> 2; matrix products, arithmetic and copies ran while one was open for 15% -> 1% of each run, Pallas kernels for 0% -> 13%
where the time goes in v1:
time: 185 us; the launch traced here: 184 us
  blocking collectives  77.8 us (42%)
  Pallas kernels  47.9 us (26%)
  waiting for transfers between devices  28.2 us (15%)
  starting transfers between devices  24.6 us (13%)
  local copies, waits for them, and re-layouts  3.59 us (2%)
    all_to_all x4, blocking collectives, exchange(): return lax.all_to_all(x, axis, split_axis=0, concat_axis=0, tiled=True)  77.8 us
    all_to_all x3, waiting for transfers between devices, exchange(): return lax.all_to_all(x, axis, split_axis=0, concat_axis=0, tiled=True)  28.2 us
    all_to_all x3, starting transfers between devices, exchange(): return lax.all_to_all(x, axis, split_axis=0, concat_axis=0, tiled=True)  24.6 us
    pallas_call x1, Pallas kernels, on_device(): call(token_body, 'token_grad', shape((COLS, 4096), F32), [pltpu.VMEM((512...  12.8 us
    pallas_call x1, Pallas kernels, on_device(): call(logits_body, 'logits', (shape((GROUPS, 40, CHUNK), F32), shape((PASS...  11.6 us
    pallas_call x1, Pallas kernels, on_device(): call(hidden_body, 'hidden_grad', shape((SHARDS, 64, LANES), BF16), [pltpu...  11 us
    pallas_call x1, Pallas kernels, on_device(): call(embed_body, 'embedding_grad', (shape((COLS, VOC), F32), shape((1, VO...  10.6 us
  transfers between devices with their start and end apart: 3, of which 2 were waited for; matrix products, arithmetic and copies ran while one was open for 1% of the time, Pallas kernels for 13%

profile of v1, /device:TPU:1, one launch (start us, length us, event | category | flops | bytes accessed | tf_op | source)
XLA Modules:
  0.0 184.1 jit_solution(3711852558439735809)
XLA Ops:
  0.7 0.6 copy-done.5
  1.3 0.8 copy-done.2
  2.1 0.7 copy-done.3
  2.8 0.7 copy-done.4
  3.5 0.6 pack.1
  4.1 17.1 %all_to_all.35.got_ref = bf16[16,80,128]{2,1,0:T(8,128)(2,1)S(1)} all-to-all(bf16[16,80,128]{2,1,0:T(8,128)(2,1)S(1)} %pack.1), channel_id=1, replica_groups=mesh['dp'=16,'vocab'=32] {'dp'}, dimensions={0} | all-to-all | bytes 655360 | tf_op jit(solution)/shard_map/all_to_all | solution.py:274
  21.2 1.0 spread.1
  22.2 28.7 %all_to_all.36.hidden_ref = bf16[32,64,128]{2,1,0:T(8,128)(2,1)S(1)} all-to-all(bf16[32,64,128]{2,1,0:T(8,128)(2,1)S(1)} %get-tuple-element.9), channel_id=1, replica_groups=mesh['dp'=16,'vocab'=32] {'vocab'}, dimensions={0} | all-to-all | bytes 1048576 | tf_op jit(solution)/shard_map/all_to_all | solution.py:274
  50.9 11.6 %logits.1 = (f32[16,40,256]{2,1,0:T(8,128)}, bf16[32,64,128]{2,1,0:T(8,128)(2,1)S(1)}) custom-call(bf16[32,64,128]{2,1,0:T(8,128)(2,1)S(1)} %all_to_all.36.hidden_ref, bf16[16,80,128]{2,1,0:T(8,128)(2,1)S(1)} %all_to_all.35.got_ref, bf16[64,3968]{1,0:T(8,128)(2,1)S(1)} %copy-done, f32[2,3968]{1,0:T(2,128)S(1)} %copy-done.1), custom_call_target="tpu_custom_call" | custom-call | tf_op jit(solution)/shard_map/logits/pallas_call | solution.py:297
  62.5 7.8 %all-to-all-start.2 = ((f32[16,40,256]{2,1,0:T(8,128)}), f32[16,40,256]{2,1,0:T(8,128)S(1)}, u32[]{:S(2)}, u32[]{:S(2)}) async-start(f32[16,40,256]{2,1,0:T(8,128)} %get-tuple-element.10), calls=%async_computation.2 | async-start | bytes 1310720 | tf_op jit(solution)/shard_map/all_to_all | solution.py:274
  70.4 11.2 %all-to-all-done.2.part_ref = f32[16,40,256]{2,1,0:T(8,128)S(1)} async-done(((f32[16,40,256]{2,1,0:T(8,128)}), f32[16,40,256]{2,1,0:T(8,128)S(1)}, u32[]{:S(2)}, u32[]{:S(2)}) %all-to-all-start.2) | async-done | bytes 655392 | tf_op jit(solution)/shard_map/all_to_all | solution.py:274
  81.6 0.1 slope.1
  81.7 10.8 %all_to_all.37.grad_ref = bf16[16,32,256]{2,1,0:T(8,128)(2,1)S(1)} all-to-all(bf16[16,32,256]{2,1,0:T(8,128)(2,1)S(1)} %slope.1), channel_id=1, replica_groups=mesh['dp'=16,'vocab'=32] {'dp'}, dimensions={0} | all-to-all | bytes 524288 | tf_op jit(solution)/shard_map/all_to_all | solution.py:274
  92.5 11.0 %hidden_grad.1 = bf16[32,64,128]{2,1,0:T(8,128)(2,1)S(1)} custom-call(bf16[16,32,256]{2,1,0:T(8,128)(2,1)S(1)} %all_to_all.37.grad_ref, bf16[16,80,128]{2,1,0:T(8,128)(2,1)S(1)} %all_to_all.35.got_ref, bf16[64,3968]{1,0:T(8,128)(2,1)S(1)} %copy-done), custom_call_target="tpu_custom_call" | custom-call | tf_op jit(solution)/shard_map/hidden_grad/pallas_call | solution.py:311
  103.5 21.2 %all_to_all.38.part_ref = bf16[32,64,128]{2,1,0:T(8,128)(2,1)S(1)} all-to-all(bf16[32,64,128]{2,1,0:T(8,128)(2,1)S(1)} %hidden_grad.1), channel_id=1, replica_groups=mesh['dp'=16,'vocab'=32] {'vocab'}, dimensions={0} | all-to-all | bytes 1048576 | tf_op jit(solution)/shard_map/all_to_all | solution.py:274
  124.8 8.1 %all-to-all-start.6 = ((bf16[32,80,128]{2,1,0:T(8,128)(2,1)}), bf16[32,80,128]{2,1,0:T(8,128)(2,1)S(1)}, u32[]{:S(2)}, u32[]{:S(2)}) async-start(bf16[32,80,128]{2,1,0:T(8,128)(2,1)} %get-tuple-element.12), calls=%async_computation.6 | async-start | bytes 1310720 | tf_op jit(solution)/shard_map/all_to_all | solution.py:274
  132.9 0.2 sum_shards.1
  133.1 0.6 convert.7
  133.7 17.0 %all-to-all-done.6.got_ref = bf16[32,80,128]{2,1,0:T(8,128)(2,1)S(1)} async-done(((bf16[32,80,128]{2,1,0:T(8,128)(2,1)}), bf16[32,80,128]{2,1,0:T(8,128)(2,1)S(1)}, u32[]{:S(2)}, u32[]{:S(2)}) %all-to-all-start.6) | async-done | bytes 655392 | tf_op jit(solution)/shard_map/all_to_all | solution.py:274
  150.7 8.7 %all-to-all-start.5 = ((bf16[16,8,128]{2,1,0:T(8,128)(2,1)}), bf16[16,8,128]{2,1,0:T(8,128)(2,1)S(1)}, u32[]{:S(2)}, u32[]{:S(2)}) async-start(bf16[16,8,128]{2,1,0:T(8,128)(2,1)} %convert.7), calls=%async_computation.5 | async-start | bytes 65536 | tf_op jit(solution)/shard_map/all_to_all | solution.py:274
  159.4 12.8 %token_grad.1.token_ref = f32[64,4096]{1,0:T(8,128)S(1)} custom-call(s32[1]{0:T(128)} %bitcast.place_ref, bf16[32,80,128]{2,1,0:T(8,128)(2,1)S(1)} %all-to-all-done.6.got_ref), custom_call_target="tpu_custom_call" | custom-call | tf_op jit(solution)/shard_map/token_grad/pallas_call | solution.py:323
  172.2 10.6 %embedding_grad.1 = (f32[64,3968]{1,0:T(8,128)}, f32[1,3968]{1,0:T(1,128)S(1)}) custom-call(bf16[16,32,256]{2,1,0:T(8,128)(2,1)S(1)} %all_to_all.37.grad_ref, bf16[16,80,128]{2,1,0:T(8,128)(2,1)S(1)} %all_to_all.35.got_ref, bf16[32,64,128]{2,1,0:T(8,128)(2,1)S(1)} %get-tuple-element.11.table_ref, f32[64,4096]{1,0:T(8,128)S(1)} %token_grad.1.token_ref), custom_call_target="tpu_custom_call" | custom-call | tf_op jit(solution)/shard_map/embedding_grad/pallas_call | solution.py:330
  182.8 0.6 reduce
  183.4 0.7 convert_element_type.10
  (17 shorter events, 0.1 us)
Async XLA Ops:
  0.6 0.7 copy-start.5
  0.6 0.7 copy-start.6
  1.3 0.8 copy-start.2
  2.1 0.7 copy-start.3
  2.8 0.7 copy-start.4
  22.2 28.7 %copy-start = (bf16[64,3968]{1,0:T(8,128)(2,1)S(1)}, bf16[64,3968]{1,0:T(8,128)(2,1)}, u32[]{:S(2)}) copy-start(bf16[64,3968]{1,0:T(8,128)(2,1)} %embed_ref.3) | copy-start | bytes 1523716
  22.2 28.7 %copy-start.1 = (f32[2,3968]{1,0:T(2,128)S(1)}, f32[2,3968]{1,0:T(2,128)}, u32[]{:S(2)}) copy-start(f32[2,3968]{1,0:T(2,128)} %pooled_ref.1) | copy-start | bytes 95236
  62.5 7.8 %copy-start.7 = (f32[3968]{0:T(1024)S(1)}, f32[3968]{0:T(1024)}, u32[]{:S(2)}) copy-start(f32[3968]{0:T(1024)} %param.14) | copy-start | bytes 47620
  62.5 19.0 %all-to-all-start.2 = ((f32[16,40,256]{2,1,0:T(8,128)}), f32[16,40,256]{2,1,0:T(8,128)S(1)}, u32[]{:S(2)}, u32[]{:S(2)}) async-start(f32[16,40,256]{2,1,0:T(8,128)} %get-tuple-element.10), calls=%async_computation.2 | async-start | bytes 1310720 | tf_op jit(solution)/shard_map/all_to_all | solution.py:274
  124.8 25.9 %all-to-all-start.6 = ((bf16[32,80,128]{2,1,0:T(8,128)(2,1)}), bf16[32,80,128]{2,1,0:T(8,128)(2,1)S(1)}, u32[]{:S(2)}, u32[]{:S(2)}) async-start(bf16[32,80,128]{2,1,0:T(8,128)(2,1)} %get-tuple-element.12), calls=%async_computation.6 | async-start | bytes 1310720 | tf_op jit(solution)/shard_map/all_to_all | solution.py:274
  150.7 32.7 %all-to-all-start.5 = ((bf16[16,8,128]{2,1,0:T(8,128)(2,1)}), bf16[16,8,128]{2,1,0:T(8,128)(2,1)S(1)}, u32[]{:S(2)}, u32[]{:S(2)}) async-start(bf16[16,8,128]{2,1,0:T(8,128)(2,1)} %convert.7), calls=%async_computation.5 | async-start | bytes 65536 | tf_op jit(solution)/shard_map/all_to_all | solution.py:274

commit v2 on v0

v2 whole, which is shorter than its diff:
```python
import jax
import jax.numpy as jnp
from jax import lax
from jax.experimental import pallas as pl
from jax.experimental.pallas import tpu as pltpu
from jax.sharding import Mesh, PartitionSpec as P

F32 = jnp.float32
BF16 = jnp.bfloat16
I16 = jnp.int16
I32 = jnp.int32
LANES = 128
PARAMS = pltpu.CompilerParams(vmem_limit_bytes=48 * 1024 * 1024)
SMEM = pl.BlockSpec(memory_space=pltpu.SMEM)
VMEM = pl.BlockSpec(memory_space=pltpu.VMEM)

GROUP = ("zl", "x", "core")
SHARD = ("zh", "y")
PLANE = ("zl", "zh", "y")
ROW = ("x", "core")
GROUPS = 16
SHARDS = 32
PEERS = 8
SEQ = 128
PASSAGES = 32
COLS = 64
HALF = 512
ROWS = 8
TILES = 31
VOC = TILES * LANES
PAD = 4096


def lane_gather(table, index):
    numbers = lax.GatherDimensionNumbers(
        offset_dims=(),
        collapsed_slice_dims=(1,),
        start_index_map=(1,),
        operand_batching_dims=(0,),
        start_indices_batching_dims=(0,),
    )
    return lax.gather(
        table,
        index[..., None],
        numbers,
        (1, 1),
        mode=lax.GatherScatterMode.PROMISE_IN_BOUNDS,
    )


def pack_body(
    place_ref, lengths_ref, ids_ref, hidden_ref, grad_ref, index_ref, pooled_ref, hidden_out, grad_out, side_out
):
    place = place_ref[0]
    limit = lengths_ref[place // (SEQ // ROWS)]
    spot = (place % (SEQ // ROWS)) * ROWS + lax.broadcasted_iota(I32, (ROWS, 1), 0)
    hidden = hidden_ref[...]
    masked = jnp.where(spot < limit, grad_ref[...].astype(F32), 0.0)
    row = lax.broadcasted_iota(I32, (ROWS, LANES), 0)
    lane = lax.broadcasted_iota(I32, (ROWS, LANES), 1)
    ids = jnp.zeros((ROWS, LANES), I32)
    for r in range(ROWS):
        ids = jnp.where(row == r, ids_ref[r], ids)
    digits = jnp.where(lane == 0, ids & 127, jnp.where(lane == 1, (ids >> 7) & 127, ids >> 14))
    digits = jnp.where(lane < 3, digits, 0).astype(F32)
    for half in range(2):
        cols = slice(half * HALF, (half + 1) * HALF)
        own = hidden[:, cols]
        rest = jnp.concatenate([masked[:, cols], digits], axis=1).astype(BF16)
        for s in range(SHARDS):
            hidden_out[half * SHARDS + s] = own
            grad_out[half * SHARDS + s] = rest
    side = jnp.concatenate([pooled_ref[...], index_ref[...].astype(F32)], axis=0)
    for g in range(GROUPS):
        side_out[g, :, 0:VOC] = side
        side_out[g, :, VOC:] = jnp.zeros((4, PAD - VOC), F32)


def logits_body(place_ref, hidden_ref, side_ref, embed_ref, out_ref):
    row = place_ref[1]
    here = lax.broadcasted_iota(I32, (SEQ, 1), 0).astype(F32)

    def one_chunk(at, width):
        dense = jnp.dot(
            hidden_ref[...], embed_ref[:, pl.ds(at, width)], preferred_element_type=F32
        )
        picked = []
        for n in range(4):
            index = side_ref[(n // 2) * PEERS + row, 2 + n % 2 : 3 + n % 2, pl.ds(at, width)]
            scores = dense[n * SEQ : (n + 1) * SEQ]
            picked.append(jnp.sum(jnp.where(index == here, scores, 0.0), axis=0, keepdims=True))
        picked = jnp.concatenate(picked, axis=0)
        for g in range(GROUPS):
            out_ref[g, :, pl.ds(at, width)] = picked

    def loop(chunk, carry):
        one_chunk(pl.multiple_of(chunk * 256, 256), 256)
        return carry

    lax.fori_loop(0, VOC // 256, loop, 0)
    one_chunk(VOC - 128, 128)


def hidden_body(
    place_ref, part_ref, side_ref, bias_ref, embed_ref, out_ref, grad_ref, bias_out, total, left
):
    row = place_ref[1]
    here = lax.broadcasted_iota(I32, (SEQ, LANES), 0).astype(I16)
    zero = jnp.zeros((), BF16)
    total[...] = jnp.zeros_like(total)

    def slopes(at, width):
        lanes = pl.ds(at, width)
        logits = jnp.concatenate(
            [part_ref[x, :, lanes] + part_ref[PEERS + x, :, lanes] for x in range(PEERS)], axis=0
        )
        upstream = jnp.concatenate(
            [side_ref[z * PEERS + x, 0:2, lanes] for x in range(PEERS) for z in range(2)], axis=0
        )
        logits = logits + bias_ref[:, lanes]
        softened = jnp.maximum(logits, 0.0) + jnp.log1p(jnp.exp(-jnp.abs(logits)))
        pooled = jnp.log1p(softened)
        sigmoid = 1.0 / (1.0 + jnp.exp(-logits))
        slope = sigmoid / (1.0 + softened)
        mean_pooled = jnp.sum(pooled, axis=0, keepdims=True) / PASSAGES
        grad = ((upstream + mean_pooled) * slope).astype(BF16).astype(F32)
        for x in range(PEERS):
            grad_ref[x, :, lanes] = grad[4 * x : 4 * x + 4]
        bias_out[:, lanes] = jnp.sum(grad, axis=0, keepdims=True)

    def one_chunk(at, width):
        slopes(at, width)
        for n in range(4):
            for tile in range(width // LANES):
                lanes = pl.ds(at + tile * LANES, LANES)
                index = side_ref[(n // 2) * PEERS + row, 2 + n % 2 : 3 + n % 2, lanes]
                index = jnp.broadcast_to(index, (16, LANES)).astype(I32).astype(I16)
                value = grad_ref[row, n : n + 1, lanes]
                value = jnp.broadcast_to(value, (16, LANES)).astype(BF16)
                index = jnp.concatenate([index] * 8, axis=0)
                value = jnp.concatenate([value] * 8, axis=0)
                left[n * SEQ : (n + 1) * SEQ, tile * LANES : (tile + 1) * LANES] = jnp.where(
                    index == here, value, zero
                )
        total[...] += lax.dot_general(
            left[:, 0:width],
            embed_ref[:, pl.ds(at, width)],
            (((1,), (1,)), ((), ())),
            preferred_element_type=F32,
        )

    def loop(chunk, carry):
        one_chunk(pl.multiple_of(chunk * 512, 512), 512)
        return carry

    lax.fori_loop(0, 7, loop, 0)
    one_chunk(7 * 512, VOC - 7 * 512)
    out_ref[...] = total[...].astype(BF16)


def turn_body(hidden_ref, grad_ref, out_ref):
    digits = []
    for n in range(4):
        rows = slice(n * SEQ, (n + 1) * SEQ)
        hidden = hidden_ref[rows, :].astype(F32).T.astype(BF16)
        grads = grad_ref[rows, :].astype(F32)
        digits.append(grads[:, HALF:].T[0:8])
        grads = grads[:, 0:HALF].T.astype(BF16)
        for x in range(PEERS):
            out_ref[x, n * SEQ : n * SEQ + COLS, :] = hidden[x * COLS : (x + 1) * COLS]
            out_ref[x, n * SEQ + COLS : (n + 1) * SEQ, :] = grads[x * COLS : (x + 1) * COLS]
    digits = jnp.concatenate(digits, axis=0).astype(BF16)
    for x in range(PEERS):
        out_ref[x, HALF:, :] = digits


def embed_body(place_ref, grad_ref, side_ref, got_ref, out_ref, left, right, total):
    base = place_ref[0] * VOC
    low_row = lax.broadcasted_iota(I32, (HALF, LANES), 0).astype(I16)
    zero = jnp.zeros((), BF16)
    one = jnp.ones((), BF16)
    total[...] = jnp.zeros_like(total)

    def one_block(block, carry):
        for s in range(8):
            peer = block * 2 + s // 4
            n = s % 4
            digits = got_ref[peer, HALF + (n // 2) * 16 : HALF + (n // 2) * 16 + 16, :].astype(F32).astype(I32)
            digits = digits[(n % 2) * 8 : (n % 2) * 8 + 8]
            local = (digits[2:3] << 14) + (digits[1:2] << 7) + digits[0:1] - base
            inside = (local >= 0) & (local < VOC)
            high = jnp.where(inside, local >> 9, 15)
            high = jnp.broadcast_to(high, (16, LANES)).astype(I16)
            low = jnp.broadcast_to(local & 511, (16, LANES)).astype(I16)
            high = jnp.concatenate([high] * 4, axis=0)
            low = jnp.concatenate([low] * 32, axis=0)
            grads = got_ref[peer, n * SEQ + COLS : (n + 1) * SEQ, :]
            lanes = slice(s * LANES, (s + 1) * LANES)
            for h in range(8):
                left[h * COLS : (h + 1) * COLS, lanes] = jnp.where(high == jnp.int16(h), grads, zero)
            right[:, lanes] = jnp.where(low_row == low, one, zero)
        total[...] += lax.dot_general(
            left[...], right[...], (((1,), (1,)), ((), ())), preferred_element_type=F32
        )
        return carry

    lax.fori_loop(0, 4, one_block, 0)
    for h in range(8):
        width = min(HALF, VOC - h * HALF)
        out_ref[:, h * HALF : h * HALF + width] = total[h * COLS : (h + 1) * COLS, 0:width]

    def one_tile(tile, carry):
        lanes = pl.ds(pl.multiple_of(tile * LANES, LANES), LANES)
        totals = [out_ref[d : d + 16, lanes] for d in range(0, COLS, 16)]
        for q in range(PASSAGES):
            x, z, n = q // 4, (q // 2) % 2, q % 2
            index = side_ref[z * PEERS + x, 2 + n : 3 + n, lanes]
            index = jnp.broadcast_to(index, (16, LANES)).astype(I32).astype(I16)
            value = grad_ref[x, q % 4 : q % 4 + 1, lanes]
            for d in range(COLS // 16):
                at = (q % 4) * SEQ + d * 16
                picked = lane_gather(got_ref[x, at : at + 16, :], index).astype(F32)
                totals[d] = totals[d] + picked * value
        for d in range(COLS // 16):
            out_ref[d * 16 : d * 16 + 16, lanes] = totals[d]
        return carry

    lax.fori_loop(0, TILES, one_tile, 0)


def sum_body(part_ref, out_ref):
    for half in range(2):
        total = part_ref[half * SHARDS].astype(F32)
        for s in range(1, SHARDS):
            total = total + part_ref[half * SHARDS + s].astype(F32)
        out_ref[:, half * HALF : (half + 1) * HALF] = total.astype(BF16)


def call(body, name, out, scratch=(), specs=None, us=1):
    return pl.pallas_call(
        body,
        out_shape=out,
        in_specs=specs,
        scratch_shapes=scratch,
        compiler_params=PARAMS,
        cost_estimate=pl.CostEstimate(flops=0, bytes_accessed=3_700_000 * us, transcendentals=0),
        name=name,
    )


def shape(dims, dtype):
    return jax.ShapeDtypeStruct(dims, dtype)


def exchange(x, axis):
    return lax.all_to_all(x, axis, split_axis=0, concat_axis=0, tiled=True)


def on_device(
    hidden, embed_grad, token_ids, lengths, pool_index, embedding, head_bias, pooled_grad
):
    place = jnp.stack([lax.axis_index(SHARD), lax.axis_index(ROW)]).astype(I32)
    embed = lax.all_gather(embedding, ROW, axis=0, tiled=True)
    hidden_rows, grad_rows, side = call(
        pack_body,
        "pack",
        (
            shape((2 * SHARDS, ROWS, HALF), BF16),
            shape((2 * SHARDS, ROWS, HALF + LANES), BF16),
            shape((GROUPS, 4, PAD), F32),
        ),
        specs=[SMEM, SMEM, SMEM, VMEM, VMEM, VMEM, VMEM],
    )(place, lengths, token_ids, hidden, embed_grad, pool_index, pooled_grad)
    all_hidden = exchange(hidden_rows, PLANE).reshape(4 * SEQ, HALF)
    all_side = exchange(side, GROUP)
    all_grads = exchange(grad_rows, PLANE).reshape(4 * SEQ, HALF + LANES)
    partial = call(
        logits_body,
        "logits",
        shape((GROUPS, 4, VOC), F32),
        specs=[SMEM, VMEM, VMEM, VMEM],
        us=5,
    )(place, all_hidden, all_side, embed)
    parts = exchange(partial, GROUP)
    turned = call(
        turn_body,
        "turn",
        shape((PEERS, HALF + 32, LANES), BF16),
        specs=[VMEM, VMEM],
        us=3,
    )(all_hidden, all_grads)
    got = exchange(turned, ROW)
    hidden_parts, all_grad, bias_grad = call(
        hidden_body,
        "hidden_grad",
        (shape((4 * SEQ, HALF), BF16), shape((PEERS, 4, VOC), F32), shape((1, VOC), F32)),
        [pltpu.VMEM((4 * SEQ, HALF), F32), pltpu.VMEM((4 * SEQ, HALF), BF16)],
        [SMEM, VMEM, VMEM, VMEM, VMEM],
        us=8,
    )(place, parts, all_side, head_bias.reshape(1, VOC), embed)
    hidden_got = exchange(hidden_parts.reshape(2 * SHARDS, ROWS, HALF), PLANE)
    embedding_grad = call(
        embed_body,
        "embedding_grad",
        shape((COLS, VOC), F32),
        [
            pltpu.VMEM((HALF, 1024), BF16),
            pltpu.VMEM((HALF, 1024), BF16),
            pltpu.VMEM((HALF, HALF), F32),
        ],
        [SMEM, VMEM, VMEM, VMEM],
        us=16,
    )(place, all_grad, all_side, got)
    hidden_grad = call(sum_body, "sum_shards", shape((ROWS, 2 * HALF), BF16), specs=[VMEM])(
        hidden_got
    )
    return hidden_grad, embedding_grad, bias_grad.reshape(VOC)


def solution(mesh):
    fine = Mesh(mesh.devices.reshape(2, 4, 2, 4, 8), GROUP + SHARD)
    every = P(GROUP + SHARD, None)
    split = P(GROUP, SHARD)
    return jax.shard_map(
        on_device,
        mesh=fine,
        in_specs=(every, every, P(GROUP + SHARD), P(GROUP), split, split, P(SHARD), split),
        out_specs=(every, split, P(SHARD)),
        check_vma=False,
    )
```

time: 617 us -> 175 us (0.28)
  blocking collectives: 331 us -> 58.8 us
  waiting for transfers between devices: 120 us -> 38.3 us
  matrix products: 66.1 us -> 0 us
  Pallas kernels: 0 us -> 32.1 us
  other arithmetic: 26.9 us -> 0.72 us
  starting transfers between devices: 39.1 us -> 20.8 us
  local copies, waits for them, and re-layouts: 14.9 us -> 8.73 us
    all_gather x4 -> x0, blocking collectives: 187 us -> none  [the longest x1 78.5 us: on_device(): lax.all_gather(hidden, 'vocab', axis=0, tiled=True)]
    reduce_scatter x1 -> x0, waiting for transfers between devices: 119 us -> none  [on_device(): lax.psum_scatter(lax.dot_general(weights, full_embed, (((1,), (1,)), ((),...]
    unnamed x1 -> x0, blocking collectives: 93.9 us -> none
    dot_general x10 -> x0, matrix products: 66.1 us -> none  [the longest x8 52.3 us: one_block(): jnp.einsum('bvs,bsc->cv', weights, hidden_block, preferred_element_type=j...]
    all_to_all x0 -> x2, blocking collectives: none -> 58.8 us  [exchange(): return lax.all_to_all(x, axis, split_axis=0, concat_axis=0, tiled=True)]
    psum x1 -> x0, blocking collectives: 50.3 us -> none  [on_device(): mean_pooled = lax.psum(jnp.sum(pooled, axis=0), 'dp') / passages]
    all_to_all x2 -> x4, waiting for transfers between devices: 0.01 us -> 37.6 us  [exchange(): return lax.all_to_all(x, axis, split_axis=0, concat_axis=0, tiled=True)]
    pallas_call x0 -> x6, Pallas kernels: none -> 32.1 us  [the longest x1 14.5 us: on_device(): call(embed_body, 'embedding_grad', shape((COLS, VOC), F32), [pltpu.VMEM((...]
  transfers between devices with their start and end apart: 4 -> 5, of which waited for: 1 -> 4; matrix products, arithmetic and copies ran while one was open for 15% -> 0% of each run, Pallas kernels for 0% -> 18%
where the time goes in v2:
time: 175 us; the launch traced here: 174 us
  blocking collectives  58.8 us (34%)
  waiting for transfers between devices  38.3 us (22%)
  Pallas kernels  32.1 us (18%)
  starting transfers between devices  20.8 us (12%)
  between operations  14.1 us (8%)
  local copies, waits for them, and re-layouts  8.73 us (5%)
    all_to_all x2, blocking collectives, exchange(): return lax.all_to_all(x, axis, split_axis=0, concat_axis=0, tiled=True)  58.8 us
    all_to_all x4, waiting for transfers between devices, exchange(): return lax.all_to_all(x, axis, split_axis=0, concat_axis=0, tiled=True)  37.6 us
    all_to_all x4, starting transfers between devices, exchange(): return lax.all_to_all(x, axis, split_axis=0, concat_axis=0, tiled=True)  20.7 us
    pallas_call x1, Pallas kernels, on_device(): call(embed_body, 'embedding_grad', shape((COLS, VOC), F32), [pltpu.VMEM((...  14.5 us
    unnamed x26, local copies, waits for them, and re-layouts  8.72 us
    pallas_call x1, Pallas kernels, on_device(): call(logits_body, 'logits', shape((GROUPS, 4, VOC), F32), specs=[SMEM, VM...  7.15 us
    pallas_call x1, Pallas kernels, on_device(): call(hidden_body, 'hidden_grad', (shape((4 * SEQ, HALF), BF16), shape((PE...  6.93 us
  transfers between devices with their start and end apart: 5, of which 4 were waited for; matrix products, arithmetic and copies ran while one was open for 0% of the time, Pallas kernels for 18%

profile of v2, /device:TPU:1, one launch (start us, length us, event | category | flops | bytes accessed | tf_op | source)
XLA Modules:
  0.0 173.6 jit_solution(14005444302452766427)
XLA Ops:
  8.0 0.8 copy-done.6
  8.7 0.8 copy-done.7
  9.5 0.7 copy-done.8
  10.2 0.7 copy-done.9
  12.2 1.5 pack.1
  13.8 36.1 %all_to_all.30 = bf16[64,8,512]{2,1,0:T(8,128)(2,1)S(1)} all-to-all(bf16[64,8,512]{2,1,0:T(8,128)(2,1)S(1)} %get-tuple-element.9), channel_id=1, replica_groups=mesh['zl'=2,'x'=4,'core'=2,'zh'=4,'y'=8] {'zl','zh','y'}, dimensions={0} | all-to-all | bytes 1048576 | tf_op jit(solution)/shard_map/all_to_all | solution.py:256
  49.9 22.6 %all_to_all.31.side_ref = f32[16,4,4096]{2,1,0:T(4,128)S(1)} all-to-all(f32[16,4,4096]{2,1,0:T(4,128)S(1)} %get-tuple-element.10), channel_id=1, replica_groups=mesh['zl'=2,'x'=4,'core'=2,'zh'=4,'y'=8] {'zl','x','core'}, dimensions={0} | all-to-all | bytes 2097152 | tf_op jit(solution)/shard_map/all_to_all | solution.py:256
  72.5 4.6 %all-to-all-start.4 = ((bf16[64,8,640]{2,1,0:T(8,128)(2,1)}), bf16[64,8,640]{2,1,0:T(8,128)(2,1)S(1)}, u32[]{:S(2)}, u32[]{:S(2)}) async-start(bf16[64,8,640]{2,1,0:T(8,128)(2,1)} %get-tuple-element.13), calls=%async_computation.4 | async-start | bytes 1310720 | tf_op jit(solution)/shard_map/all_to_all | solution.py:256
  77.2 7.1 %logits.1 = f32[16,4,3968]{2,1,0:T(4,128)S(1)} custom-call(s32[2]{0:T(128)S(1)} %pad_add_fusion.place_ref, bf16[512,512]{1,0:T(8,128)(2,1)S(1)} %bitcast.5, f32[16,4,4096]{2,1,0:T(4,128)S(1)} %all_to_all.31.side_ref, bf16[512,3968]{1,0:T(8,128)(2,1)} %all-gather.2.cloned.1.call-done.embed_ref), custom_call_target="tpu_custom_call" | custom-call | bytes 18500000 | tf_op jit(solution)/shard_map/logits/pallas_call | solution.py:277
  84.4 0.9 copy-done
  85.3 13.2 %all-to-all-done.4 = bf16[64,8,640]{2,1,0:T(8,128)(2,1)S(1)} async-done(((bf16[64,8,640]{2,1,0:T(8,128)(2,1)}), bf16[64,8,640]{2,1,0:T(8,128)(2,1)S(1)}, u32[]{:S(2)}, u32[]{:S(2)}) %all-to-all-start.4) | async-done | bytes 655392 | tf_op jit(solution)/shard_map/all_to_all | solution.py:256
  98.5 0.8 copy-done.1
  99.3 7.0 %all-to-all-start.2 = ((f32[16,4,3968]{2,1,0:T(4,128)}), f32[16,4,3968]{2,1,0:T(4,128)S(1)}, u32[]{:S(2)}, u32[]{:S(2)}) async-start(f32[16,4,3968]{2,1,0:T(4,128)} %copy-done), calls=%async_computation.2 | async-start | bytes 2031616 | tf_op jit(solution)/shard_map/all_to_all | solution.py:256
  106.3 1.1 copy-done.2
  107.4 1.4 turn.1
  108.8 13.1 %all-to-all-done.2.part_ref = f32[16,4,3968]{2,1,0:T(4,128)S(1)} async-done(((f32[16,4,3968]{2,1,0:T(4,128)}), f32[16,4,3968]{2,1,0:T(4,128)S(1)}, u32[]{:S(2)}, u32[]{:S(2)}) %all-to-all-start.2) | async-done | bytes 1015840 | tf_op jit(solution)/shard_map/all_to_all | solution.py:256
  121.8 4.3 %all-to-all-start.5 = ((bf16[8,544,128]{2,1,0:T(8,128)(2,1)}), bf16[8,544,128]{2,1,0:T(8,128)(2,1)S(1)}, u32[]{:S(2)}, u32[]{:S(2)}) async-start(bf16[8,544,128]{2,1,0:T(8,128)(2,1)} %turn.1), calls=%async_computation.5 | async-start | bytes 2228224 | tf_op jit(solution)/shard_map/all_to_all | solution.py:256
  126.2 6.9 %hidden_grad.1 = (bf16[512,512]{1,0:T(8,128)(2,1)S(1)}, f32[8,4,3968]{2,1,0:T(4,128)S(1)}, f32[1,3968]{1,0:T(1,128)S(1)}) custom-call(s32[2]{0:T(128)S(1)} %pad_add_fusion.place_ref, f32[16,4,3968]{2,1,0:T(4,128)S(1)} %all-to-all-done.2.part_ref, f32[16,4,4096]{2,1,0:T(4,128)S(1)} %all_to_all.31.side_ref, f32[1,3968]{1,0:T(1,128)S(1)} %reshape.22.bias_ref, ...), custom_call_target="tpu_custom_call" | custom-call | bytes 29600000 | tf_op jit(solution)/shard_map/hidden_grad/pallas_call | solution.py:293
  133.1 0.8 copy-done.3
  133.9 0.8 copy-done.4
  134.7 7.3 %all-to-all-done.5.got_ref = bf16[8,544,128]{2,1,0:T(8,128)(2,1)S(1)} async-done(((bf16[8,544,128]{2,1,0:T(8,128)(2,1)}), bf16[8,544,128]{2,1,0:T(8,128)(2,1)S(1)}, u32[]{:S(2)}, u32[]{:S(2)}) %all-to-all-start.5) | async-done | bytes 1114144 | tf_op jit(solution)/shard_map/all_to_all | solution.py:256
  142.0 4.8 %all-to-all-start.3 = ((bf16[64,8,512]{2,1,0:T(8,128)(2,1)}), bf16[64,8,512]{2,1,0:T(8,128)(2,1)S(1)}, u32[]{:S(2)}, u32[]{:S(2)}) async-start(bf16[64,8,512]{2,1,0:T(8,128)(2,1)} %bitcast.8), calls=%async_computation.3 | async-start | bytes 1048576 | tf_op jit(solution)/shard_map/all_to_all | solution.py:256
  147.4 14.5 %embedding_grad.1 = f32[64,3968]{1,0:T(8,128)} custom-call(s32[2]{0:T(128)S(1)} %pad_add_fusion.place_ref, f32[8,4,3968]{2,1,0:T(4,128)S(1)} %copy-done.5, f32[16,4,4096]{2,1,0:T(4,128)S(1)} %all_to_all.31.side_ref, bf16[8,544,128]{2,1,0:T(8,128)(2,1)S(1)} %all-to-all-done.5.got_ref), custom_call_target="tpu_custom_call" | custom-call | bytes 59200000 | tf_op jit(solution)/shard_map/embedding_grad/pallas_call | solution.py:302
  161.9 4.1 %all-to-all-done.3.part_ref = bf16[64,8,512]{2,1,0:T(8,128)(2,1)S(1)} async-done(((bf16[64,8,512]{2,1,0:T(8,128)(2,1)}), bf16[64,8,512]{2,1,0:T(8,128)(2,1)S(1)}, u32[]{:S(2)}, u32[]{:S(2)}) %all-to-all-start.3) | async-done | bytes 524320 | tf_op jit(solution)/shard_map/all_to_all | solution.py:256
  (24 shorter events, 3.5 us)
Async XLA Ops:
  7.2 70.0 %all-gather.2.cloned.1.call-start = ((), (), s32[]{:S(2)}) async-start(), calls=%async_computation.6 | async-start | bytes 4571136 | tf_op jit(solution)/shard_map/all_gather | solution.py:263
  8.0 0.8 copy-start.6
  8.7 0.8 copy-start.7
  9.5 0.7 copy-start.8
  10.2 0.7 copy-start.9
  10.9 0.7 copy-start.10
  11.6 0.7 copy-start.11
  72.5 25.9 %all-to-all-start.4 = ((bf16[64,8,640]{2,1,0:T(8,128)(2,1)}), bf16[64,8,640]{2,1,0:T(8,128)(2,1)S(1)}, u32[]{:S(2)}, u32[]{:S(2)}) async-start(bf16[64,8,640]{2,1,0:T(8,128)(2,1)} %get-tuple-element.13), calls=%async_computation.4 | async-start | bytes 1310720 | tf_op jit(solution)/shard_map/all_to_all | solution.py:256
  84.4 1.0 copy-start
  98.5 0.8 copy-start.1
  99.3 22.5 %all-to-all-start.2 = ((f32[16,4,3968]{2,1,0:T(4,128)}), f32[16,4,3968]{2,1,0:T(4,128)S(1)}, u32[]{:S(2)}, u32[]{:S(2)}) async-start(f32[16,4,3968]{2,1,0:T(4,128)} %copy-done), calls=%async_computation.2 | async-start | bytes 2031616 | tf_op jit(solution)/shard_map/all_to_all | solution.py:256
  106.3 1.1 copy-start.2
  108.8 17.4 %copy-start.12 = (f32[3968]{0:T(1024)S(1)}, f32[3968]{0:T(1024)}, u32[]{:S(2)}) copy-start(f32[3968]{0:T(1024)} %param.14) | copy-start | bytes 47620
  121.8 20.2 %all-to-all-start.5 = ((bf16[8,544,128]{2,1,0:T(8,128)(2,1)}), bf16[8,544,128]{2,1,0:T(8,128)(2,1)S(1)}, u32[]{:S(2)}, u32[]{:S(2)}) async-start(bf16[8,544,128]{2,1,0:T(8,128)(2,1)} %turn.1), calls=%async_computation.5 | async-start | bytes 2228224 | tf_op jit(solution)/shard_map/all_to_all | solution.py:256
  133.1 0.8 copy-start.3
  133.9 0.8 copy-start.4
  142.0 5.4 %copy-start.5 = (f32[8,4,3968]{2,1,0:T(4,128)S(1)}, f32[8,4,3968]{2,1,0:T(4,128)}, u32[]{:S(2)}) copy-start(f32[8,4,3968]{2,1,0:T(4,128)} %copy-done.4) | copy-start | bytes 1523716
  142.0 24.1 %all-to-all-start.3 = ((bf16[64,8,512]{2,1,0:T(8,128)(2,1)}), bf16[64,8,512]{2,1,0:T(8,128)(2,1)S(1)}, u32[]{:S(2)}, u32[]{:S(2)}) async-start(bf16[64,8,512]{2,1,0:T(8,128)(2,1)} %bitcast.8), calls=%async_computation.3 | async-start | bytes 1048576 | tf_op jit(solution)/shard_map/all_to_all | solution.py:256
Sparse Core Ops, SparseCore 0:
  10.1 42.7 all-gather.1

commit v3 on v2

v3 whole, which is shorter than its diff:
```python
import jax
import jax.numpy as jnp
from jax import lax
from jax.experimental import pallas as pl
from jax.experimental.pallas import tpu as pltpu
from jax.sharding import Mesh, PartitionSpec as P

F32 = jnp.float32
BF16 = jnp.bfloat16
I16 = jnp.int16
I32 = jnp.int32
LANES = 128
SMEM = pl.BlockSpec(memory_space=pltpu.SMEM)
VMEM = pl.BlockSpec(memory_space=pltpu.VMEM)

GROUP = ("zl", "x", "core")
SHARD = ("zh", "y")
PLANE = ("zl", "zh", "y")
ROW = ("x", "core")
GROUPS = 16
SHARDS = 32
PEERS = 8
SEQ = 128
PASSAGES = 32
COLS = 64
HALF = 512
ROWS = 8
TILES = 31
VOC = TILES * LANES
PAD = 4096
ROOM = 56
STEP = 512
STEPS = 8


def lane_gather(table, index):
    numbers = lax.GatherDimensionNumbers(
        offset_dims=(),
        collapsed_slice_dims=(1,),
        start_index_map=(1,),
        operand_batching_dims=(0,),
        start_indices_batching_dims=(0,),
    )
    return lax.gather(
        table,
        index[..., None],
        numbers,
        (1, 1),
        mode=lax.GatherScatterMode.PROMISE_IN_BOUNDS,
    )


def pack_body(place_ref, lengths, ids, hidden, grad, index, pooled, row_out, side_out, *scratch):
    held, sem = scratch[:-1], scratch[-1]
    copies = [
        pltpu.make_async_copy(source, target, sem.at[n])
        for n, (source, target) in enumerate(zip((lengths, ids, hidden, grad, index, pooled), held))
    ]
    for copy in copies:
        copy.start()
    for copy in copies:
        copy.wait()
    lengths_ref, ids_ref, hidden_ref, grad_ref, index_ref, pooled_ref = held
    place = place_ref[0]
    limit = lengths_ref[place // (SEQ // ROWS)]
    spot = (place % (SEQ // ROWS)) * ROWS + lax.broadcasted_iota(I32, (ROWS, 1), 0)
    masked = jnp.where(spot < limit, grad_ref[...].astype(F32), 0.0).astype(BF16)
    row = lax.broadcasted_iota(I32, (ROWS, LANES), 0)
    lane = lax.broadcasted_iota(I32, (ROWS, LANES), 1)
    ids = jnp.zeros((ROWS, LANES), I32)
    for r in range(ROWS):
        ids = jnp.where(row == r, ids_ref[r], ids)
    digits = jnp.where(lane == 0, ids & 127, jnp.where(lane == 1, (ids >> 7) & 127, ids >> 14))
    digits = jnp.where(lane < 3, digits, 0).astype(F32).astype(BF16)
    for half in range(2):
        cols = slice(half * HALF, (half + 1) * HALF)
        own = jnp.concatenate([hidden_ref[:, cols], masked[:, cols], digits], axis=1)
        for s in range(SHARDS):
            row_out[half * SHARDS + s] = own
    side_out[:, 0:VOC] = jnp.concatenate([pooled_ref[...], index_ref[...].astype(F32)], axis=0)
    side_out[:, VOC:] = jnp.zeros((4, PAD - VOC), F32)


def logits_body(hidden_ref, index_ref, embed_ref, out_ref):
    here = lax.broadcasted_iota(I32, (SEQ, 1), 0)
    dense = jnp.dot(hidden_ref[...], embed_ref[...], preferred_element_type=F32)
    picked = []
    for n in range(4):
        scores = dense[n * SEQ : (n + 1) * SEQ]
        hit = index_ref[n : n + 1, :] == here
        picked.append(jnp.sum(jnp.where(hit, scores, 0.0), axis=0, keepdims=True))
    picked = jnp.concatenate(picked, axis=0)
    for g in range(GROUPS):
        out_ref[g] = picked


def hidden_body(
    place_ref, part_ref, side_ref, index_ref, bias_ref, embed_ref, out_ref, grad_ref, bias_out, total, left
):
    row = place_ref[1]
    step = pl.program_id(0)
    here = lax.broadcasted_iota(I32, (SEQ, LANES), 0).astype(I16)
    zero = jnp.zeros((), BF16)

    logits = jnp.concatenate([part_ref[x] + part_ref[PEERS + x] for x in range(PEERS)], axis=0)
    upstream = jnp.concatenate(
        [side_ref[z * PEERS + x, 0:2, :] for x in range(PEERS) for z in range(2)], axis=0
    )
    logits = logits + bias_ref[...]
    softened = jnp.maximum(logits, 0.0) + jnp.log1p(jnp.exp(-jnp.abs(logits)))
    pooled = jnp.log1p(softened)
    sigmoid = 1.0 / (1.0 + jnp.exp(-logits))
    slope = sigmoid / (1.0 + softened)
    mean_pooled = jnp.sum(pooled, axis=0, keepdims=True) / PASSAGES
    grad = ((upstream + mean_pooled) * slope).astype(BF16).astype(F32)
    for x in range(PEERS):
        grad_ref[x] = grad[4 * x : 4 * x + 4]
    bias_out[...] = jnp.sum(grad, axis=0, keepdims=True)

    def scatter(width):
        for n in range(4):
            for tile in range(width // LANES):
                lanes = slice(tile * LANES, (tile + 1) * LANES)
                index = jnp.broadcast_to(index_ref[n : n + 1, lanes], (16, LANES)).astype(I16)
                value = jnp.broadcast_to(grad_ref[row, n : n + 1, lanes], (16, LANES)).astype(BF16)
                index = jnp.concatenate([index] * 8, axis=0)
                value = jnp.concatenate([value] * 8, axis=0)
                left[n * SEQ : (n + 1) * SEQ, lanes] = jnp.where(index == here, value, zero)
        return lax.dot_general(
            left[:, 0:width],
            embed_ref[:, 0:width],
            (((1,), (1,)), ((), ())),
            preferred_element_type=F32,
        )

    @pl.when(step == 0)
    def first():
        total[...] = scatter(STEP)

    @pl.when((step > 0) & (step < STEPS - 1))
    def middle():
        total[...] += scatter(STEP)

    @pl.when(step == STEPS - 1)
    def last():
        out_ref[...] = (total[...] + scatter(VOC - (STEPS - 1) * STEP)).astype(BF16)


def turn_body(rows_ref, out_ref):
    digits = []
    for n in range(4):
        rows = rows_ref[n * SEQ : (n + 1) * SEQ, :].astype(F32)
        digits.append(rows[:, 2 * HALF :].T[0:8])
        hidden = rows[:, 0:HALF].T.astype(BF16)
        grads = rows[:, HALF : 2 * HALF].T.astype(BF16)
        for x in range(PEERS):
            out_ref[x, n * SEQ : n * SEQ + COLS, :] = hidden[x * COLS : (x + 1) * COLS]
            out_ref[x, n * SEQ + COLS : (n + 1) * SEQ, :] = grads[x * COLS : (x + 1) * COLS]
    digits = jnp.concatenate(digits, axis=0).astype(BF16)
    for x in range(PEERS):
        out_ref[x, HALF:, :] = digits


def embed_body(place_ref, grad_ref, side_ref, got_ref, out_ref, left, right, total):
    base = place_ref[0] * VOC
    low_row = lax.broadcasted_iota(I32, (HALF, LANES), 0).astype(I16)
    zero = jnp.zeros((), BF16)
    one = jnp.ones((), BF16)
    total[...] = jnp.zeros_like(total)

    def one_block(block, carry):
        for s in range(8):
            peer = block * 2 + s // 4
            n = s % 4
            digits = got_ref[peer, HALF + (n // 2) * 16 : HALF + (n // 2) * 16 + 16, :].astype(F32).astype(I32)
            digits = digits[(n % 2) * 8 : (n % 2) * 8 + 8]
            local = (digits[2:3] << 14) + (digits[1:2] << 7) + digits[0:1] - base
            inside = (local >= 0) & (local < VOC)
            high = jnp.where(inside, local >> 9, 15)
            high = jnp.broadcast_to(high, (16, LANES)).astype(I16)
            low = jnp.broadcast_to(local & 511, (16, LANES)).astype(I16)
            high = jnp.concatenate([high] * 4, axis=0)
            low = jnp.concatenate([low] * 32, axis=0)
            grads = got_ref[peer, n * SEQ + COLS : (n + 1) * SEQ, :]
            lanes = slice(s * LANES, (s + 1) * LANES)
            for h in range(8):
                left[h * COLS : (h + 1) * COLS, lanes] = jnp.where(high == jnp.int16(h), grads, zero)
            right[:, lanes] = jnp.where(low_row == low, one, zero)
        total[...] += lax.dot_general(
            left[...], right[...], (((1,), (1,)), ((), ())), preferred_element_type=F32
        )
        return carry

    lax.fori_loop(0, 4, one_block, 0)
    for h in range(8):
        width = min(HALF, VOC - h * HALF)
        out_ref[:, h * HALF : h * HALF + width] = total[h * COLS : (h + 1) * COLS, 0:width]

    def one_tile(tile, carry):
        lanes = pl.ds(pl.multiple_of(tile * LANES, LANES), LANES)
        totals = [out_ref[d : d + 16, lanes] for d in range(0, COLS, 16)]
        for q in range(PASSAGES):
            x, z, n = q // 4, (q // 2) % 2, q % 2
            index = side_ref[z * PEERS + x, 2 + n : 3 + n, lanes]
            index = jnp.broadcast_to(index, (16, LANES)).astype(I32).astype(I16)
            value = grad_ref[x, q % 4 : q % 4 + 1, lanes]
            for d in range(COLS // 16):
                at = (q % 4) * SEQ + d * 16
                picked = lane_gather(got_ref[x, at : at + 16, :], index).astype(F32)
                totals[d] = totals[d] + picked * value
        for d in range(COLS // 16):
            out_ref[d * 16 : d * 16 + 16, lanes] = totals[d]
        return carry

    lax.fori_loop(0, TILES, one_tile, 0)


def sum_body(part_ref, out_ref):
    for half in range(2):
        total = part_ref[half * SHARDS].astype(F32)
        for s in range(1, SHARDS):
            total = total + part_ref[half * SHARDS + s].astype(F32)
        out_ref[:, half * HALF : (half + 1) * HALF] = total.astype(BF16)


def call(body, name, out, scratch=(), specs=None, us=1, grid=(), out_specs=None, room=ROOM):
    extra = {key: value for key, value in (("grid", grid), ("out_specs", out_specs)) if value}
    return pl.pallas_call(
        body,
        out_shape=out,
        in_specs=specs,
        scratch_shapes=scratch,
        compiler_params=pltpu.CompilerParams(vmem_limit_bytes=room * 1024 * 1024),
        cost_estimate=pl.CostEstimate(flops=0, bytes_accessed=3_700_000 * us, transcendentals=0),
        name=name,
        **extra,
    )


def shape(dims, dtype):
    return jax.ShapeDtypeStruct(dims, dtype)


def chunk(*dims):
    return pl.BlockSpec(dims + (STEP,), lambda i: (0,) * len(dims) + (i,))


def whole(*dims):
    return pl.BlockSpec(dims, lambda i: (0,) * len(dims))


def exchange(x, axis):
    return lax.all_to_all(x, axis, split_axis=0, concat_axis=0, tiled=True)


def on_device(
    hidden, embed_grad, token_ids, lengths, pool_index, embedding, head_bias, pooled_grad
):
    place = jnp.stack([lax.axis_index(SHARD), lax.axis_index(ROW)]).astype(I32)
    width = 2 * HALF + LANES
    rows, side = call(
        pack_body,
        "pack",
        (shape((2 * SHARDS, ROWS, width), BF16), shape((4, PAD), F32)),
        [
            pltpu.SMEM((2,), I32),
            pltpu.SMEM((ROWS,), I32),
            pltpu.VMEM((ROWS, 2 * HALF), BF16),
            pltpu.VMEM((ROWS, 2 * HALF), BF16),
            pltpu.VMEM((2, VOC), I32),
            pltpu.VMEM((2, VOC), F32),
            pltpu.SemaphoreType.DMA((6,)),
        ],
        [SMEM] + [pl.BlockSpec(memory_space=pl.ANY)] * 6,
        room=ROOM,
    )(place, lengths, token_ids, hidden, embed_grad, pool_index, pooled_grad)
    embedding, rows = lax.optimization_barrier((embedding, rows))
    embed = lax.all_gather(embedding, ROW, axis=0, tiled=True)
    all_rows = exchange(rows, PLANE).reshape(4 * SEQ, width)
    index = lax.all_gather(pool_index, "zl", axis=0, tiled=True)
    side, embed = lax.optimization_barrier((side, embed))
    all_side = lax.all_gather(side, GROUP, axis=0, tiled=False)
    turned = call(
        turn_body,
        "turn",
        shape((PEERS, HALF + 32, LANES), BF16),
        specs=[VMEM],
        us=2,
    )(all_rows)
    got = exchange(turned, ROW)
    partial = call(
        logits_body,
        "logits",
        shape((GROUPS, 4, VOC), F32),
        specs=[whole(4 * SEQ, HALF), chunk(4), chunk(HALF)],
        out_specs=chunk(GROUPS, 4),
        grid=(STEPS,),
        us=6,
    )(all_rows, index, embed)
    partial, got = lax.optimization_barrier((partial, got))
    parts = exchange(partial, GROUP)
    hidden_parts, all_grad, bias_grad = call(
        hidden_body,
        "hidden_grad",
        (shape((4 * SEQ, HALF), BF16), shape((PEERS, 4, VOC), F32), shape((1, VOC), F32)),
        [pltpu.VMEM((4 * SEQ, HALF), F32), pltpu.VMEM((4 * SEQ, STEP), BF16)],
        [SMEM, chunk(GROUPS, 4), chunk(GROUPS, 4), chunk(4), chunk(1), chunk(HALF)],
        out_specs=(whole(4 * SEQ, HALF), chunk(PEERS, 4), chunk(1)),
        grid=(STEPS,),
        us=7,
    )(place, parts, all_side, index, head_bias.reshape(1, VOC), embed)
    hidden_got = exchange(hidden_parts.reshape(2 * SHARDS, ROWS, HALF), PLANE)
    embedding_grad = call(
        embed_body,
        "embedding_grad",
        shape((COLS, VOC), F32),
        [
            pltpu.VMEM((HALF, 1024), BF16),
            pltpu.VMEM((HALF, 1024), BF16),
            pltpu.VMEM((HALF, HALF), F32),
        ],
        [SMEM, VMEM, VMEM, VMEM],
        us=16,
    )(place, all_grad, all_side, got)
    hidden_grad = call(sum_body, "sum_shards", shape((ROWS, 2 * HALF), BF16), specs=[VMEM])(
        hidden_got
    )
    return hidden_grad, embedding_grad, bias_grad.reshape(VOC)


def solution(mesh):
    fine = Mesh(mesh.devices.reshape(2, 4, 2, 4, 8), GROUP + SHARD)
    every = P(GROUP + SHARD, None)
    split = P(GROUP, SHARD)
    return jax.shard_map(
        on_device,
        mesh=fine,
        in_specs=(every, every, P(GROUP + SHARD), P(GROUP), split, split, P(SHARD), split),
        out_specs=(every, split, P(SHARD)),
        check_vma=False,
    )
```

time: 175 us -> 164 us (0.937)
  waiting for transfers between devices: 38.3 us -> 26.5 us
  Pallas kernels: 32.1 us -> 39.6 us
  local copies, waits for them, and re-layouts: 8.73 us -> 2.1 us
  blocking collectives: 58.8 us -> 53.9 us
  starting transfers between devices: 20.8 us -> 24.2 us
    all_to_all x4 -> x3, waiting for transfers between devices: 37.6 us -> 23.7 us  [exchange(): return lax.all_to_all(x, axis, split_axis=0, concat_axis=0, tiled=True)]
    all_to_all x2 -> x1, blocking collectives: 58.8 us -> 50.2 us  [exchange(): return lax.all_to_all(x, axis, split_axis=0, concat_axis=0, tiled=True)]
    unnamed x26 -> x11, local copies, waits for them, and re-layouts: 8.72 us -> 1.49 us
    all_gather x0 -> x1, blocking collectives: none -> 3.73 us  [on_device(): index = lax.all_gather(pool_index, 'zl', axis=0, tiled=True)]
    all_to_all x4 -> x3, starting transfers between devices: 20.7 us -> 24.1 us  [exchange(): return lax.all_to_all(x, axis, split_axis=0, concat_axis=0, tiled=True)]
    pallas_call x1, Pallas kernels: 6.93 us -> 9.1 us  [on_device(): call(hidden_body, 'hidden_grad', (shape((4 * SEQ, HALF), BF16), shape((PE...]
    all_gather x0 -> x1, waiting for transfers between devices: none -> 2.1 us  [on_device(): all_side = lax.all_gather(side, GROUP, axis=0, tiled=False)]
  transfers between devices with their start and end apart: 5 -> 5, of which waited for: 4 -> 4; matrix products, arithmetic and copies ran while one was open for 0% -> 2% of each run, Pallas kernels for 18% -> 16%
where the time goes in v3:
time: 164 us; the launch traced here: 162 us
  blocking collectives  53.9 us (33%)
  Pallas kernels  39.6 us (24%)
  waiting for transfers between devices  26.5 us (16%)
  starting transfers between devices  24.2 us (15%)
  between operations  14.1 us (9%)
  local copies, waits for them, and re-layouts  2.1 us (1%)
  other arithmetic  1.95 us (1%)
    all_to_all x1, blocking collectives, exchange(): return lax.all_to_all(x, axis, split_axis=0, concat_axis=0, tiled=True)  50.2 us
    all_to_all x3, starting transfers between devices, exchange(): return lax.all_to_all(x, axis, split_axis=0, concat_axis=0, tiled=True)  24.1 us
    all_to_all x3, waiting for transfers between devices, exchange(): return lax.all_to_all(x, axis, split_axis=0, concat_axis=0, tiled=True)  23.7 us
    pallas_call x1, Pallas kernels, on_device(): call(embed_body, 'embedding_grad', shape((COLS, VOC), F32), [pltpu.VMEM((...  15.7 us
    pallas_call x1, Pallas kernels, on_device(): call(hidden_body, 'hidden_grad', (shape((4 * SEQ, HALF), BF16), shape((PE...  9.1 us
    pallas_call x1, Pallas kernels, on_device(): call(logits_body, 'logits', shape((GROUPS, 4, VOC), F32), specs=[whole(4...  7.72 us
    all_gather x1, blocking collectives, on_device(): index = lax.all_gather(pool_index, 'zl', axis=0, tiled=True)  3.73 us
  transfers between devices with their start and end apart: 5, of which 4 were waited for; matrix products, arithmetic and copies ran while one was open for 2% of the time, Pallas kernels for 16%

profile of v3, /device:TPU:1, one launch (start us, length us, event | category | flops | bytes accessed | tf_op | source)
XLA Modules:
  0.0 162.3 jit_solution(15878583769017083880)
XLA Ops:
  7.2 0.0 all-gather.6.cloned.1.call-start
  7.2 0.6 pad_add_fusion.place_ref
  7.8 2.7 %pack.1 = (bf16[64,8,1152]{2,1,0:T(8,128)(2,1)}, f32[4,4096]{1,0:T(4,128)}) custom-call(s32[2]{0:T(128)} %pad_add_fusion.place_ref, s32[2]{0:T(128)} %lengths.1, s32[8]{0:T(128)} %ids.1, bf16[8,1024]{1,0:T(8,128)(2,1)} %hidden.1, bf16[8,1024]{1,0:T(8,128)(2,1)} %grad.1, s32[2,3968]{1,0:T(2,128)} %index.1, f32[2,3968]{1,0:T(2,128)} %pooled.1), custom_call_target="tpu_custom_call" | custom-call | bytes 3700000 | tf_op jit(solution)/shard_map/pack/pallas_call | solution.py:261
  10.5 0.0 all-gather.6.cloned.1.call-update
  10.5 50.2 %all_to_all.20 = bf16[64,8,1152]{2,1,0:T(8,128)(2,1)} all-to-all(bf16[64,8,1152]{2,1,0:T(8,128)(2,1)} %get-tuple-element.15), channel_id=1, replica_groups=mesh['zl'=2,'x'=4,'core'=2,'zh'=4,'y'=8] {'zl','zh','y'}, dimensions={0} | all-to-all | bytes 2359296 | tf_op jit(solution)/shard_map/all_to_all | solution.py:253
  60.7 2.7 %turn.1 = bf16[8,544,128]{2,1,0:T(8,128)(2,1)} custom-call(bf16[512,1152]{1,0:T(8,128)(2,1)} %bitcast.6), custom_call_target="tpu_custom_call" | custom-call | bytes 7400000 | tf_op jit(solution)/shard_map/turn/pallas_call | solution.py:283
  63.4 7.1 %all-to-all-start.1 = ((bf16[8,544,128]{2,1,0:T(8,128)(2,1)}), bf16[8,544,128]{2,1,0:T(8,128)(2,1)S(1)}, u32[]{:S(2)}, u32[]{:S(2)}) async-start(bf16[8,544,128]{2,1,0:T(8,128)(2,1)} %turn.1), calls=%async_computation.1 | async-start | bytes 2228224 | tf_op jit(solution)/shard_map/all_to_all | solution.py:253
  70.5 0.7 all-gather.8.cloned.1.call-update
  71.3 3.7 %all-gather.1 = s32[2,2,3968]{2,1,0:T(2,128)S(1)} all-gather(s32[1,2,3968]{2,1,0:T(2,128)S(1)} %bitcast.9), channel_id=1, replica_groups=mesh['zl'=2,'x'=4,'core'=2,'zh'=4,'y'=8] {'zl'}, dimensions={0}, use_global_device_ids=true | all-gather | bytes 95232 | tf_op jit(solution)/shard_map/all_gather | solution.py:280
  75.0 0.7 reshape.24.index_ref
  75.7 7.7 %logits.1 = f32[16,4,3968]{2,1,0:T(4,128)} custom-call(bf16[512,1152]{1,0:T(8,128)(2,1)} %bitcast.7, s32[4,3968]{1,0:T(4,128)} %reshape.24.index_ref, bf16[512,3968]{1,0:T(8,128)(2,1)} %all-gather.6.cloned.1.call-done.embed_ref), custom_call_target="tpu_custom_call" | custom-call | bytes 22200000 | tf_op jit(solution)/shard_map/logits/pallas_call | solution.py:291
  83.4 3.7 %all-to-all-done.1.got_ref = bf16[8,544,128]{2,1,0:T(8,128)(2,1)S(1)} async-done(((bf16[8,544,128]{2,1,0:T(8,128)(2,1)}), bf16[8,544,128]{2,1,0:T(8,128)(2,1)S(1)}, u32[]{:S(2)}, u32[]{:S(2)}) %all-to-all-start.1) | async-done | bytes 1114144 | tf_op jit(solution)/shard_map/all_to_all | solution.py:253
  87.1 4.3 %all-to-all-start.2 = ((f32[16,4,3968]{2,1,0:T(4,128)}), f32[16,4,3968]{2,1,0:T(4,128)S(1)}, u32[]{:S(2)}, u32[]{:S(2)}) async-start(f32[16,4,3968]{2,1,0:T(4,128)} %logits.1), calls=%async_computation.2 | async-start | bytes 2031616 | tf_op jit(solution)/shard_map/all_to_all | solution.py:253
  91.4 0.6 reshape.19.bias_ref
  92.0 17.2 %all-to-all-done.2.part_ref = f32[16,4,3968]{2,1,0:T(4,128)S(1)} async-done(((f32[16,4,3968]{2,1,0:T(4,128)}), f32[16,4,3968]{2,1,0:T(4,128)S(1)}, u32[]{:S(2)}, u32[]{:S(2)}) %all-to-all-start.2) | async-done | bytes 1015840 | tf_op jit(solution)/shard_map/all_to_all | solution.py:253
  109.2 2.1 %all-gather.8.cloned.1.call-done.side_ref = f32[16,4,4096]{2,1,0:T(4,128)} async-done(((f32[1,4,4096]{2,1,0:T(4,128)}), f32[16,4,4096]{2,1,0:T(4,128)}) %all-gather.8.cloned.1.call-update) | async-done | bytes 1048592 | tf_op jit(solution)/shard_map/all_gather | solution.py:282
  111.3 9.1 %hidden_grad.1 = (bf16[512,512]{1,0:T(8,128)(2,1)}, f32[8,4,3968]{2,1,0:T(4,128)}, f32[1,3968]{1,0:T(1,128)}) custom-call(s32[2]{0:T(128)} %pad_add_fusion.place_ref, f32[16,4,3968]{2,1,0:T(4,128)} %copy-done.1, f32[16,4,4096]{2,1,0:T(4,128)} %all-gather.8.cloned.1.call-done.side_ref, s32[4,3968]{1,0:T(4,128)} %reshape.24.index_ref, ...), custom_call_target="tpu_custom_call" | custom-call | bytes 25900000 | tf_op jit(solution)/shard_map/hidden_grad/pallas_call | solution.py:302
  120.4 0.0 copy-done
  120.4 12.7 %all-to-all-start.3 = ((bf16[64,8,512]{2,1,0:T(8,128)(2,1)}), bf16[64,8,512]{2,1,0:T(8,128)(2,1)S(1)}, u32[]{:S(2)}, u32[]{:S(2)}) async-start(bf16[64,8,512]{2,1,0:T(8,128)(2,1)} %bitcast.8), calls=%async_computation.3 | async-start | bytes 1048576 | tf_op jit(solution)/shard_map/all_to_all | solution.py:253
  133.1 1.4 reduce
  134.5 15.7 %embedding_grad.1 = f32[64,3968]{1,0:T(8,128)} custom-call(s32[2]{0:T(128)} %pad_add_fusion.place_ref, f32[8,4,3968]{2,1,0:T(4,128)} %get-tuple-element.22.grad_ref, f32[16,4,4096]{2,1,0:T(4,128)} %all-gather.8.cloned.1.call-done.side_ref, bf16[8,544,128]{2,1,0:T(8,128)(2,1)} %copy-done), custom_call_target="tpu_custom_call" | custom-call | bytes 59200000 | tf_op jit(solution)/shard_map/embedding_grad/pallas_call | solution.py:313
  150.2 2.8 %all-to-all-done.3.part_ref = bf16[64,8,512]{2,1,0:T(8,128)(2,1)S(1)} async-done(((bf16[64,8,512]{2,1,0:T(8,128)(2,1)}), bf16[64,8,512]{2,1,0:T(8,128)(2,1)S(1)}, u32[]{:S(2)}, u32[]{:S(2)}) %all-to-all-start.3) | async-done | bytes 524320 | tf_op jit(solution)/shard_map/all_to_all | solution.py:253
  153.0 0.8 copy-done.2
  153.8 1.7 %sum_shards.1 = bf16[8,1024]{1,0:T(8,128)(2,1)} custom-call(bf16[64,8,512]{2,1,0:T(8,128)(2,1)} %copy-done.2), custom_call_target="tpu_custom_call" | custom-call | bytes 3700000 | tf_op jit(solution)/shard_map/sum_shards/pallas_call | solution.py:325
  (10 shorter events, 0.0 us)
Async XLA Ops:
  7.2 63.4 %all-gather.6.cloned.1.call-start = ((), (), s32[]{:S(2)}) async-start(), calls=%async_computation.4 | async-start | bytes 4571136 | tf_op jit(solution)/shard_map/all_gather | solution.py:278
  63.4 7.9 %copy-start.3 = (s32[2,3968]{1,0:T(2,128)S(1)}, s32[2,3968]{1,0:T(2,128)}, u32[]{:S(2)}) copy-start(s32[2,3968]{1,0:T(2,128)} %index.1) | copy-start | bytes 95236
  63.4 23.7 %all-to-all-start.1 = ((bf16[8,544,128]{2,1,0:T(8,128)(2,1)}), bf16[8,544,128]{2,1,0:T(8,128)(2,1)S(1)}, u32[]{:S(2)}, u32[]{:S(2)}) async-start(bf16[8,544,128]{2,1,0:T(8,128)(2,1)} %turn.1), calls=%async_computation.1 | async-start | bytes 2228224 | tf_op jit(solution)/shard_map/all_to_all | solution.py:253
  70.5 40.8 %all-gather.8.cloned.1.call-start = ((), (), s32[]{:S(2)}) async-start(), calls=%async_computation.5 | async-start | bytes 1114112 | tf_op jit(solution)/shard_map/all_gather | solution.py:282
  83.4 8.0 %copy-start.4 = (f32[3968]{0:T(1024)S(1)}, f32[3968]{0:T(1024)}, u32[]{:S(2)}) copy-start(f32[3968]{0:T(1024)} %param.14) | copy-start | bytes 47620
  87.1 33.3 %copy-start = (bf16[8,544,128]{2,1,0:T(8,128)(2,1)}, bf16[8,544,128]{2,1,0:T(8,128)(2,1)S(1)}, u32[]{:S(2)}) copy-start(bf16[8,544,128]{2,1,0:T(8,128)(2,1)S(1)} %all-to-all-done.1.got_ref) | copy-start | bytes 3342340
  87.1 22.1 %all-to-all-start.2 = ((f32[16,4,3968]{2,1,0:T(4,128)}), f32[16,4,3968]{2,1,0:T(4,128)S(1)}, u32[]{:S(2)}, u32[]{:S(2)}) async-start(f32[16,4,3968]{2,1,0:T(4,128)} %logits.1), calls=%async_computation.2 | async-start | bytes 2031616 | tf_op jit(solution)/shard_map/all_to_all | solution.py:253
  109.2 2.1 %copy-start.1 = (f32[16,4,3968]{2,1,0:T(4,128)}, f32[16,4,3968]{2,1,0:T(4,128)S(1)}, u32[]{:S(2)}) copy-start(f32[16,4,3968]{2,1,0:T(4,128)S(1)} %all-to-all-done.2.part_ref) | copy-start | bytes 3047428
  120.4 32.5 %all-to-all-start.3 = ((bf16[64,8,512]{2,1,0:T(8,128)(2,1)}), bf16[64,8,512]{2,1,0:T(8,128)(2,1)S(1)}, u32[]{:S(2)}, u32[]{:S(2)}) async-start(bf16[64,8,512]{2,1,0:T(8,128)(2,1)} %bitcast.8), calls=%async_computation.3 | async-start | bytes 1048576 | tf_op jit(solution)/shard_map/all_to_all | solution.py:253
  153.0 0.8 copy-start.2
Sparse Core Ops, SparseCore 0:
  10.6 42.7 all-gather.5
  73.5 37.8 all-gather.7

commit v4 on v3

v4 whole, which is shorter than its diff:
```python
import jax
import jax.numpy as jnp
from jax import lax
from jax.experimental import pallas as pl
from jax.experimental.pallas import tpu as pltpu
from jax.sharding import Mesh, PartitionSpec as P

F32 = jnp.float32
BF16 = jnp.bfloat16
I16 = jnp.int16
I32 = jnp.int32
LANES = 128
SMEM = pl.BlockSpec(memory_space=pltpu.SMEM)
VMEM = pl.BlockSpec(memory_space=pltpu.VMEM)
ANY = pl.BlockSpec(memory_space=pl.ANY)

GROUP = ("zl", "x", "core")
SHARD = ("zh", "y")
HOME = ("zl", "x", "zh", "y")
GROUPS = 16
SHARDS = 32
CHIPS = 8
SEQ = 128
PASSAGES = 32
OWN = 16
COLS = 64
PAIR = 128
WIDTH = 8 * PAIR
ROWS = 8
TILES = 31
VOC = TILES * LANES
CHUNK = 256
STEP = 512
STEPS = 8
ROOM = 56
CARRY = 4 * 2 * PAIR + LANES


def lane_gather(table, index):
    numbers = lax.GatherDimensionNumbers(
        offset_dims=(),
        collapsed_slice_dims=(1,),
        start_index_map=(1,),
        operand_batching_dims=(0,),
        start_indices_batching_dims=(0,),
    )
    return lax.gather(
        table,
        index[..., None],
        numbers,
        (1, 1),
        mode=lax.GatherScatterMode.PROMISE_IN_BOUNDS,
    )


def slot(place_ref, m):
    return ((m // 4) ^ place_ref[2]) * 4 + ((place_ref[3] - m % 4) & 3)


def turned_spot(index):
    return ((index & 3) << 5) | (index >> 2)


def pack_body(place_ref, lengths, ids, hidden, grad, out_ref, *scratch):
    held, block, sem, out_sem = scratch[:4], scratch[4], scratch[5], scratch[6]
    copies = [
        pltpu.make_async_copy(source, target, sem.at[n])
        for n, (source, target) in enumerate(zip((lengths, ids, hidden, grad), held))
    ]
    for copy in copies:
        copy.start()
    for copy in copies:
        copy.wait()
    lengths_ref, ids_ref, hidden_ref, grad_ref = held
    place = place_ref[0]
    swap = place_ref[1] == 1
    limit = lengths_ref[place // (SEQ // ROWS)]
    spot = (place % (SEQ // ROWS)) * ROWS + lax.broadcasted_iota(I32, (ROWS, 1), 0)
    rows = [hidden_ref[...].astype(F32), jnp.where(spot < limit, grad_ref[...].astype(F32), 0.0)]
    row = lax.broadcasted_iota(I32, (2, LANES), 0)
    lane = lax.broadcasted_iota(I32, (2, LANES), 1)
    digits = jnp.zeros((2, LANES), I32)
    for r in range(ROWS):
        for d in range(3):
            here = (row == r // 4) & (lane == (r % 4) * 8 + d)
            digits = jnp.where(here, (ids_ref[r] >> (7 * d)) & 127, digits)
    digits = digits.astype(F32)
    for m in range(CHIPS):
        parts = []
        for q in range(4):
            for array in rows:
                two = jnp.concatenate(
                    [array[r : r + 1, m * PAIR : (m + 1) * PAIR] for r in (q, 4 + q)], axis=0
                )
                other = jnp.concatenate([two[:, COLS:], two[:, :COLS]], axis=1)
                parts.append(jnp.where(swap, other, two))
        block[m] = jnp.concatenate(parts + [digits], axis=1).astype(BF16)
    copies = [
        pltpu.make_async_copy(block, out_ref.at[:, s], out_sem.at[s]) for s in range(SHARDS)
    ]
    for copy in copies:
        copy.start()
    for copy in copies:
        copy.wait()


def turn_body(rows_ref, hidden_out, keep_out, send_out):
    for p in range(OWN):
        rows = rows_ref[p * 32 : (p + 1) * 32, :].astype(F32)
        tokens = jnp.concatenate([rows[:, q * CHUNK : (q + 1) * CHUNK] for q in range(4)], axis=0)
        hidden_out[p * SEQ : (p + 1) * SEQ, :] = tokens[:, 0:PAIR].astype(BF16)
        turned = tokens.T.astype(BF16)
        digits = rows[:, 4 * CHUNK :].T
        digits = jnp.concatenate([digits[q * 8 : q * 8 + 8] for q in range(4)], axis=1)
        digits = jnp.concatenate([digits, jnp.zeros((8, SEQ), F32)], axis=0).astype(BF16)
        for n, out in enumerate((keep_out, send_out)):
            out[p, 0:COLS, :] = turned[n * COLS : (n + 1) * COLS]
            out[p, COLS:PAIR, :] = turned[PAIR + n * COLS : PAIR + (n + 1) * COLS]
            out[p, PAIR:, :] = digits


def logits_body(place_ref, hidden_ref, index_ref, own_ref, other_ref, pooled_ref, out_ref):
    here = lax.broadcasted_iota(I32, (SEQ, 1), 0)
    inside = pl.program_id(0) * STEP + lax.broadcasted_iota(I32, (1, STEP), 1) < VOC
    embed = jnp.concatenate([own_ref[...], other_ref[...]], axis=0)
    picked = []
    for p in range(OWN):
        scores = jnp.dot(
            hidden_ref[p * SEQ : (p + 1) * SEQ, :], embed, preferred_element_type=F32
        )
        index = turned_spot(index_ref[slot(place_ref, p // 2), p % 2 : p % 2 + 1, :])
        picked.append(jnp.sum(jnp.where(index == here, scores, 0.0), axis=0, keepdims=True))
    picked = jnp.concatenate(picked + [pooled_ref[...], jnp.zeros((6, STEP), F32)], axis=0)
    picked = jnp.where(inside, picked, 0.0)
    for n in range(2):
        out_ref[n] = picked[:, n * CHUNK : (n + 1) * CHUNK]


def slope_body(part_ref, bias_ref, out_ref):
    logits = []
    upstream = []
    for c in range(2):
        total = part_ref[c, 0:OWN, :]
        for m in range(1, CHIPS):
            total = total + part_ref[2 * m + c, 0:OWN, :]
        logits.append(total)
        upstream += [part_ref[2 * m + c, OWN : OWN + 2, :] for m in range(CHIPS)]
    logits = jnp.concatenate(logits, axis=0) + bias_ref[...]
    upstream = jnp.concatenate(upstream, axis=0)
    softened = jnp.maximum(logits, 0.0) + jnp.log1p(jnp.exp(-jnp.abs(logits)))
    pooled = jnp.log1p(softened)
    sigmoid = 1.0 / (1.0 + jnp.exp(-logits))
    slope = sigmoid / (1.0 + softened)
    mean_pooled = jnp.sum(pooled, axis=0, keepdims=True) / PASSAGES
    grad = ((upstream + mean_pooled) * slope).astype(BF16)
    for g in range(GROUPS):
        out_ref[g] = grad


def hidden_body(place_ref, grad_ref, index_ref, own_ref, other_ref, out_ref, total, grads):
    step = pl.program_id(0)
    here = lax.broadcasted_iota(I32, (SEQ, LANES), 0).astype(I16)
    zero = jnp.zeros((), BF16)
    first_core = place_ref[1] == 0
    for n in range(2):
        both = grad_ref[n].astype(F32)
        grads[:, n * CHUNK : (n + 1) * CHUNK] = jnp.where(first_core, both[0:OWN], both[OWN:])

    def scatter(width, p):
        parts = []
        for tile in range(width // LANES):
            lanes = slice(tile * LANES, (tile + 1) * LANES)
            index = index_ref[slot(place_ref, p // 2), p % 2 : p % 2 + 1, lanes]
            index = jnp.broadcast_to(index, (16, LANES)).astype(I16)
            value = jnp.broadcast_to(grads[p : p + 1, lanes], (16, LANES)).astype(BF16)
            index = jnp.concatenate([index] * 8, axis=0)
            value = jnp.concatenate([value] * 8, axis=0)
            parts.append(jnp.where(index == here, value, zero))
        embed = jnp.concatenate([own_ref[:, 0:width], other_ref[:, 0:width]], axis=0)
        return lax.dot_general(
            jnp.concatenate(parts, axis=1),
            embed,
            (((1,), (1,)), ((), ())),
            preferred_element_type=F32,
        )

    def rows(p):
        return slice(p * SEQ, (p + 1) * SEQ)

    @pl.when(step == 0)
    def first():
        for p in range(OWN):
            total[rows(p), :] = scatter(STEP, p)

    @pl.when((step > 0) & (step < STEPS - 1))
    def middle():
        for p in range(OWN):
            total[rows(p), :] += scatter(STEP, p)

    @pl.when(step == STEPS - 1)
    def last():
        for p in range(OWN):
            out_ref[rows(p), :] = (total[rows(p), :] + scatter(VOC - (STEPS - 1) * STEP, p)).astype(BF16)


def embed_body(
    place_ref, grad_ref, own_index, other_index, keep_ref, got_ref, out_ref, bias_ref, left, right, total, grads
):
    base = place_ref[0] * VOC
    first_core = place_ref[1] == 0
    low_row = lax.broadcasted_iota(I32, (512, LANES), 0).astype(I16)
    zero = jnp.zeros((), BF16)
    one = jnp.ones((), BF16)
    total[...] = jnp.zeros_like(total)

    def token_block(table_ref, block):
        for s in range(8):
            p = block * 8 + s
            digits = table_ref[p, PAIR:, :].astype(F32).astype(I32)
            local = (digits[2:3] << 14) + (digits[1:2] << 7) + digits[0:1] - base
            inside = (local >= 0) & (local < VOC)
            high = jnp.where(inside, local >> 9, 15)
            high = jnp.broadcast_to(high, (16, LANES)).astype(I16)
            low = jnp.broadcast_to(local & 511, (16, LANES)).astype(I16)
            high = jnp.concatenate([high] * 4, axis=0)
            low = jnp.concatenate([low] * 32, axis=0)
            cotangents = table_ref[p, COLS:PAIR, :]
            lanes = slice(s * LANES, (s + 1) * LANES)
            for h in range(8):
                left[h * COLS : (h + 1) * COLS, lanes] = jnp.where(
                    high == jnp.int16(h), cotangents, zero
                )
            right[:, lanes] = jnp.where(low_row == low, one, zero)
        total[...] += lax.dot_general(
            left[...], right[...], (((1,), (1,)), ((), ())), preferred_element_type=F32
        )

    for table_ref in (keep_ref, got_ref):

        def one_block(block, carry, table_ref=table_ref):
            token_block(table_ref, block)
            return carry

        lax.fori_loop(0, 2, one_block, 0)
    for h in range(8):
        width = min(512, VOC - h * 512)
        out_ref[:, h * 512 : h * 512 + width] = total[h * COLS : (h + 1) * COLS, 0:width]
    for g in range(GROUPS):
        both = grad_ref[g].astype(F32)
        grads[g] = jnp.where(first_core, both, jnp.concatenate([both[OWN:], both[:OWN]], axis=0))

    def one_tile(tile, carry):
        lanes = pl.ds(pl.multiple_of(tile * LANES, LANES), LANES)
        half = pl.ds(pl.multiple_of((tile % 2) * LANES, LANES), LANES)
        totals = [out_ref[d : d + 16, lanes] for d in range(0, COLS, 16)]
        for n, (table_ref, index_ref) in enumerate(((keep_ref, own_index), (got_ref, other_index))):
            for p in range(OWN):
                index = turned_spot(index_ref[slot(place_ref, p // 2), p % 2 : p % 2 + 1, lanes])
                index = jnp.broadcast_to(index, (16, LANES)).astype(I16)
                value = grads[tile // 2, n * OWN + p : n * OWN + p + 1, half]
                for d in range(COLS // 16):
                    picked = lane_gather(table_ref[p, d * 16 : d * 16 + 16, :], index).astype(F32)
                    totals[d] = totals[d] + picked * value
        for d in range(COLS // 16):
            out_ref[d * 16 : d * 16 + 16, lanes] = totals[d]
        bias_ref[:, lanes] = jnp.sum(grads[tile // 2, :, half], axis=0, keepdims=True)
        return carry

    lax.fori_loop(0, TILES, one_tile, 0)


def sum_body(place_ref, part_ref, out_ref):
    swap = place_ref[1] == 1
    for m in range(CHIPS):
        total = part_ref[m * SHARDS].astype(F32)
        for s in range(1, SHARDS):
            total = total + part_ref[m * SHARDS + s].astype(F32)
        other = jnp.concatenate([total[:, COLS:], total[:, :COLS]], axis=1)
        out_ref[:, m * PAIR : (m + 1) * PAIR] = jnp.where(swap, other, total).astype(BF16)


def call(body, name, out, scratch=(), specs=None, us=1, grid=(), out_specs=None):
    extra = {key: value for key, value in (("grid", grid), ("out_specs", out_specs)) if value}
    return pl.pallas_call(
        body,
        out_shape=out,
        in_specs=specs,
        scratch_shapes=scratch,
        compiler_params=pltpu.CompilerParams(vmem_limit_bytes=ROOM * 1024 * 1024),
        cost_estimate=pl.CostEstimate(flops=0, bytes_accessed=3_700_000 * us, transcendentals=0),
        name=name,
        **extra,
    )


def shape(dims, dtype):
    return jax.ShapeDtypeStruct(dims, dtype)


def lanes_of(*dims):
    return pl.BlockSpec(dims + (STEP,), lambda i: (0,) * len(dims) + (i,))


def chunks_of(*dims):
    return pl.BlockSpec((2,) + dims, lambda i: (i,) + (0,) * len(dims))


def whole(*dims):
    return pl.BlockSpec(dims, lambda i: (0,) * len(dims))


def exchange(x, axis):
    return lax.all_to_all(x, axis, split_axis=0, concat_axis=0, tiled=True)


def swap_over(x, axis):
    return lax.ppermute(x, axis, [(0, 1), (1, 0)])


def on_device(
    hidden, embed_grad, token_ids, lengths, pool_index, embedding, head_bias, pooled_grad
):
    place = jnp.stack([lax.axis_index(name) for name in (SHARD, "core", "zl", "x")]).astype(I32)
    rows = call(
        pack_body,
        "pack",
        shape((CHIPS, SHARDS, 2, CARRY), BF16),
        [
            pltpu.SMEM((2,), I32),
            pltpu.SMEM((ROWS,), I32),
            pltpu.VMEM((ROWS, WIDTH), BF16),
            pltpu.VMEM((ROWS, WIDTH), BF16),
            pltpu.VMEM((CHIPS, 2, CARRY), BF16),
            pltpu.SemaphoreType.DMA((4,)),
            pltpu.SemaphoreType.DMA((SHARDS,)),
        ],
        [SMEM] + [ANY] * 4,
        out_specs=ANY,
    )(place, lengths, token_ids, hidden, embed_grad)
    all_rows = exchange(rows.reshape(CHIPS * SHARDS, 2, CARRY), HOME).reshape(-1, CARRY)
    other_embed = swap_over(embedding, "core")
    index = jnp.stack([pool_index, swap_over(pool_index, "zl")])
    shifts = [
        lax.ppermute(index, "x", [(k, (k + s) % 4) for k in range(4)]) for s in range(1, 4)
    ]
    own_index = jnp.stack([index] + shifts, axis=1).reshape(CHIPS, 2, VOC)
    other_index = swap_over(own_index, "core")
    hidden_rows, keep, send = call(
        turn_body,
        "turn",
        (
            shape((OWN * SEQ, PAIR), BF16),
            shape((OWN, PAIR + 16, SEQ), BF16),
            shape((OWN, PAIR + 16, SEQ), BF16),
        ),
        specs=[VMEM],
        us=2,
    )(all_rows)
    got = swap_over(send, "core")
    partial = call(
        logits_body,
        "logits",
        shape((GROUPS, 24, CHUNK), F32),
        specs=[
            SMEM,
            whole(OWN * SEQ, PAIR),
            lanes_of(CHIPS, 2),
            lanes_of(COLS),
            lanes_of(COLS),
            lanes_of(2),
        ],
        out_specs=chunks_of(24, CHUNK),
        grid=(STEPS,),
        us=6,
    )(place, hidden_rows, own_index, embedding, other_embed, pooled_grad)
    parts = exchange(partial, GROUP)
    bias = jnp.pad(head_bias, (0, GROUPS * CHUNK - VOC)).reshape(GROUPS, 1, CHUNK)
    bias = lax.dynamic_index_in_dim(bias, lax.axis_index(GROUP), 0, keepdims=False)
    grad_block = call(
        slope_body, "slope", shape((GROUPS, PASSAGES, CHUNK), BF16), specs=[VMEM, VMEM]
    )(parts, bias)
    all_grad = exchange(grad_block, GROUP)
    hidden_parts = call(
        hidden_body,
        "hidden_grad",
        shape((OWN * SEQ, PAIR), BF16),
        [pltpu.VMEM((OWN * SEQ, PAIR), F32), pltpu.VMEM((OWN, STEP), F32)],
        [SMEM, chunks_of(PASSAGES, CHUNK), lanes_of(CHIPS, 2), lanes_of(COLS), lanes_of(COLS)],
        out_specs=whole(OWN * SEQ, PAIR),
        grid=(STEPS,),
        us=7,
    )(place, all_grad, own_index, embedding, other_embed)
    hidden_got = exchange(hidden_parts.reshape(CHIPS * SHARDS, ROWS, PAIR), HOME)
    embedding_grad, bias_grad = call(
        embed_body,
        "embedding_grad",
        (shape((COLS, VOC), F32), shape((1, VOC), F32)),
        [
            pltpu.VMEM((512, 1024), BF16),
            pltpu.VMEM((512, 1024), BF16),
            pltpu.VMEM((512, 512), F32),
            pltpu.VMEM((GROUPS, PASSAGES, CHUNK), F32),
        ],
        [SMEM] + [VMEM] * 5,
        us=16,
    )(place, all_grad, own_index, other_index, keep, got)
    hidden_grad = call(
        sum_body, "sum_shards", shape((ROWS, WIDTH), BF16), specs=[SMEM, VMEM]
    )(place, hidden_got)
    return hidden_grad, embedding_grad, bias_grad.reshape(VOC)


def solution(mesh):
    fine = Mesh(mesh.devices.reshape(2, 4, 2, 4, 8), GROUP + SHARD)
    every = P(GROUP + SHARD, None)
    split = P(GROUP, SHARD)
    return jax.shard_map(
        on_device,
        mesh=fine,
        in_specs=(every, every, P(GROUP + SHARD), P(GROUP), split, split, P(SHARD), split),
        out_specs=(every, split, P(SHARD)),
        check_vma=False,
    )
```

time: 164 us -> 162 us (0.988)
  starting transfers between devices: 24.2 us -> 73.8 us
  blocking collectives: 53.9 us -> 12.4 us
  between operations: 14.1 us -> 0.83 us
  local copies, waits for them, and re-layouts: 2.1 us -> 5.9 us
  waiting for transfers between devices: 26.5 us -> 23.8 us
  Pallas kernels: 39.6 us -> 41.7 us
    all_to_all x1, blocking collectives: 50.2 us -> 12.4 us  [exchange(): return lax.all_to_all(x, axis, split_axis=0, concat_axis=0, tiled=True)]
    all_to_all x3, starting transfers between devices: 24.1 us -> 53.1 us  [exchange(): return lax.all_to_all(x, axis, split_axis=0, concat_axis=0, tiled=True)]
    ppermute x0 -> x7, starting transfers between devices: none -> 20.6 us  [the longest x4 13.4 us: swap_over(): return lax.ppermute(x, axis, [(0, 1), (1, 0)])]
    ppermute x0 -> x7, waiting for transfers between devices: none -> 13.9 us  [the longest x4 13.9 us: swap_over(): return lax.ppermute(x, axis, [(0, 1), (1, 0)])]
    all_to_all x3, waiting for transfers between devices: 23.7 us -> 9.88 us  [exchange(): return lax.all_to_all(x, axis, split_axis=0, concat_axis=0, tiled=True)]
    all_gather x1 -> x0, blocking collectives: 3.73 us -> none  [on_device(): index = lax.all_gather(pool_index, 'zl', axis=0, tiled=True)]
    pallas_call x6 -> x7, Pallas kernels: 39.6 us -> 41.7 us  [the longest x1 15.6 us: on_device(): call(embed_body, 'embedding_grad', (shape((COLS, VOC), F32), shape((1, VO...]
    all_gather x2 -> x0, waiting for transfers between devices: 2.1 us -> none  [the longest x1 2.1 us: on_device(): all_side = lax.all_gather(side, GROUP, axis=0, tiled=False)]
  transfers between devices with their start and end apart: 5 -> 10, of which waited for: 4 -> 4; matrix products, arithmetic and copies ran while one was open for 2% -> 2% of each run, Pallas kernels for 16% -> 11%
where the time goes in v4:
time: 162 us; the launch traced here: 160 us
  starting transfers between devices  73.8 us (46%)
  Pallas kernels  41.7 us (26%)
  waiting for transfers between devices  23.8 us (15%)
  blocking collectives  12.4 us (8%)
  local copies, waits for them, and re-layouts  5.9 us (4%)
  other arithmetic  2 us (1%)
    all_to_all x3, starting transfers between devices, exchange(): return lax.all_to_all(x, axis, split_axis=0, concat_axis=0, tiled=True)  53.1 us
    pallas_call x1, Pallas kernels, on_device(): call(embed_body, 'embedding_grad', (shape((COLS, VOC), F32), shape((1, VO...  15.6 us
    ppermute x4, waiting for transfers between devices, swap_over(): return lax.ppermute(x, axis, [(0, 1), (1, 0)])  13.9 us
    ppermute x4, starting transfers between devices, swap_over(): return lax.ppermute(x, axis, [(0, 1), (1, 0)])  13.4 us
    all_to_all x1, blocking collectives, exchange(): return lax.all_to_all(x, axis, split_axis=0, concat_axis=0, tiled=True)  12.4 us
    all_to_all x3, waiting for transfers between devices, exchange(): return lax.all_to_all(x, axis, split_axis=0, concat_axis=0, tiled=True)  9.88 us
    pallas_call x1, Pallas kernels, on_device(): call(logits_body, 'logits', shape((GROUPS, 24, CHUNK), F32), specs=[SMEM,...  8.5 us
    pallas_call x1, Pallas kernels, on_device(): call(hidden_body, 'hidden_grad', shape((OWN * SEQ, PAIR), BF16), [pltpu.V...  8.33 us
  transfers between devices with their start and end apart: 10, of which 4 were waited for; matrix products, arithmetic and copies ran while one was open for 2% of the time, Pallas kernels for 11%

profile of v4, /device:TPU:1, one launch (start us, length us, event | category | flops | bytes accessed | tf_op | source)
XLA Modules:
  0.0 160.5 jit_solution(6619080604860947622)
XLA Ops:
  1.2 2.9 %pack.1 = bf16[8,32,2,1152]{3,2,1,0:T(2,128)(2,1)} custom-call(s32[4]{0:T(128)} %pad_add_fusion.2.place_ref, s32[2]{0:T(128)} %lengths.1, s32[8]{0:T(128)} %ids.1, bf16[8,1024]{1,0:T(8,128)(2,1)} %hidden.1, bf16[8,1024]{1,0:T(8,128)(2,1)} %grad.1), custom_call_target="tpu_custom_call" | custom-call | bytes 3700000 | tf_op jit(solution)/shard_map/pack/pallas_call | solution.py:324
  4.1 23.3 %all-to-all-start = ((bf16[256,2,1152]{2,1,0:T(2,128)(2,1)}), bf16[256,2,1152]{2,1,0:T(2,128)(2,1)S(1)}, u32[]{:S(2)}, u32[]{:S(2)}) async-start(bf16[256,2,1152]{2,1,0:T(2,128)(2,1)} %bitcast.17), calls=%async_computation | async-start | bytes 2359296 | tf_op jit(solution)/shard_map/all_to_all | solution.py:313
  27.5 2.4 %collective-permute-start = (s32[2,3968]{1,0:T(2,128)S(1)}, s32[2,3968]{1,0:T(2,128)S(1)}, u32[]{:S(2)}, u32[]{:S(2)}) collective-permute-start(s32[2,3968]{1,0:T(2,128)S(1)} %copy-done.7), channel_id=1, source_target_pairs={{0,256},{256,0},{1,257},{257,1},{2,258},{258,2},{3,259},{259,3},{4... | collective-permute-start | bytes 95240 | tf_op jit(solution)/shard_map/ppermute | solution.py:317
  29.9 12.4 %collective-permute-done = s32[2,3968]{1,0:T(2,128)S(1)} collective-permute-done((s32[2,3968]{1,0:T(2,128)S(1)}, s32[2,3968]{1,0:T(2,128)S(1)}, u32[]{:S(2)}, u32[]{:S(2)}) %collective-permute-start) | collective-permute-done | bytes 31776 | tf_op jit(solution)/shard_map/ppermute | solution.py:317
  42.4 1.9 %collective-permute-start.3 = (s32[2,2,3968]{2,1,0:T(2,128)S(1)}, s32[2,2,3968]{2,1,0:T(2,128)S(1)}, u32[]{:S(2)}, u32[]{:S(2)}) collective-permute-start(s32[2,2,3968]{2,1,0:T(2,128)S(1)} %get-tuple-element.14), channel_id=1, source_target_pairs={{0,192},{64,0},{128,64},{192,128},{1,193},{65,1},{129,65},{193,129... | collective-permute-start | bytes 190472 | tf_op jit(solution)/shard_map/ppermute | solution.py:344
  44.3 2.4 %collective-permute-start.2 = (s32[2,2,3968]{2,1,0:T(2,128)S(1)}, s32[2,2,3968]{2,1,0:T(2,128)S(1)}, u32[]{:S(2)}, u32[]{:S(2)}) collective-permute-start(s32[2,2,3968]{2,1,0:T(2,128)S(1)} %get-tuple-element.14), channel_id=1, source_target_pairs={{0,128},{64,192},{128,0},{192,64},{1,129},{65,193},{129,1},{193,65... | collective-permute-start | bytes 190472 | tf_op jit(solution)/shard_map/ppermute | solution.py:344
  46.7 2.9 %collective-permute-start.1 = (s32[2,2,3968]{2,1,0:T(2,128)S(1)}, s32[2,2,3968]{2,1,0:T(2,128)S(1)}, u32[]{:S(2)}, u32[]{:S(2)}) collective-permute-start(s32[2,2,3968]{2,1,0:T(2,128)S(1)} %get-tuple-element.14), channel_id=1, source_target_pairs={{0,64},{64,128},{128,192},{192,0},{1,65},{65,129},{129,193},{193,1... | collective-permute-start | bytes 190472 | tf_op jit(solution)/shard_map/ppermute | solution.py:344
  49.6 6.8 %collective-permute-start.4 = (bf16[64,3968]{1,0:T(8,128)(2,1)S(1)}, bf16[64,3968]{1,0:T(8,128)(2,1)S(1)}, u32[]{:S(2)}, u32[]{:S(2)}) collective-permute-start(bf16[64,3968]{1,0:T(8,128)(2,1)S(1)} %copy-done.2), channel_id=1, source_target_pairs={{0,32},{32,0},{1,33},{33,1},{2,34},{34,2},{3,35},{35,3},{4,36},{36... | collective-permute-start | bytes 1523720 | tf_op jit(solution)/shard_map/ppermute | solution.py:317
  57.1 2.1 %all-to-all-done = bf16[256,2,1152]{2,1,0:T(2,128)(2,1)S(1)} async-done(((bf16[256,2,1152]{2,1,0:T(2,128)(2,1)}), bf16[256,2,1152]{2,1,0:T(2,128)(2,1)S(1)}, u32[]{:S(2)}, u32[]{:S(2)}) %all-to-all-start) | async-done | bytes 1179680 | tf_op jit(solution)/shard_map/all_to_all | solution.py:313
  59.2 1.3 reshape.25.rows_ref
  60.5 2.8 %turn.1 = (bf16[2048,128]{1,0:T(8,128)(2,1)}, bf16[16,144,128]{2,1,0:T(8,128)(2,1)}, bf16[16,144,128]{2,1,0:T(8,128)(2,1)}) custom-call(bf16[512,1152]{1,0:T(8,128)(2,1)} %reshape.25.rows_ref), custom_call_target="tpu_custom_call" | custom-call | bytes 7400000 | tf_op jit(solution)/shard_map/turn/pallas_call | solution.py:348
  64.1 8.5 %logits.1 = f32[16,24,256]{2,1,0:T(8,128)} custom-call(s32[4]{0:T(128)} %pad_add_fusion.2.place_ref, bf16[2048,128]{1,0:T(8,128)(2,1)} %get-tuple-element.8.hidden_ref, s32[8,2,3968]{2,1,0:T(2,128)} %bitcast.18, bf16[64,3968]{1,0:T(8,128)(2,1)} %own_ref.3, bf16[64,3968]{1,0:T(8,128)(2,1)} %copy-done.3, f32[2,3968]{1,0:T(2,128)} %pooled_ref.1), custom_call_target="tpu_custom_call" | custom-call | bytes 22200000 | tf_op jit(solution)/shard_map/logits/pallas_call | solution.py:360
  72.6 7.0 %all-to-all-start.1 = ((f32[16,24,256]{2,1,0:T(8,128)}), f32[16,24,256]{2,1,0:T(8,128)S(1)}, u32[]{:S(2)}, u32[]{:S(2)}) async-start(f32[16,24,256]{2,1,0:T(8,128)} %logits.1), calls=%async_computation.1 | async-start | bytes 786432 | tf_op jit(solution)/shard_map/all_to_all | solution.py:313
  80.2 7.8 %all-to-all-done.1.part_ref = f32[16,24,256]{2,1,0:T(8,128)S(1)} async-done(((f32[16,24,256]{2,1,0:T(8,128)}), f32[16,24,256]{2,1,0:T(8,128)S(1)}, u32[]{:S(2)}, u32[]{:S(2)}) %all-to-all-start.1) | async-done | bytes 393248 | tf_op jit(solution)/shard_map/all_to_all | solution.py:313
  88.8 1.8 %slope.1 = bf16[16,32,256]{2,1,0:T(8,128)(2,1)} custom-call(f32[16,24,256]{2,1,0:T(8,128)} %copy-done.4, f32[1,256]{1,0:T(1,128)} %dynamic-slice_bitcast_fusion.bias_ref), custom_call_target="tpu_custom_call" | custom-call | bytes 3700000 | tf_op jit(solution)/shard_map/slope/pallas_call | solution.py:379
  90.6 12.4 %all_to_all.20.grad_ref = bf16[16,32,256]{2,1,0:T(8,128)(2,1)} all-to-all(bf16[16,32,256]{2,1,0:T(8,128)(2,1)} %slope.1), channel_id=1, replica_groups=mesh['zl'=2,'x'=4,'core'=2,'zh'=4,'y'=8] {'zl','x','core'}, dimensions={0} | all-to-all | bytes 524288 | tf_op jit(solution)/shard_map/all_to_all | solution.py:313
  103.0 8.3 %hidden_grad.1 = bf16[2048,128]{1,0:T(8,128)(2,1)} custom-call(s32[4]{0:T(128)} %pad_add_fusion.2.place_ref, bf16[16,32,256]{2,1,0:T(8,128)(2,1)} %all_to_all.20.grad_ref, s32[8,2,3968]{2,1,0:T(2,128)} %bitcast.19, bf16[64,3968]{1,0:T(8,128)(2,1)} %own_ref.3, bf16[64,3968]{1,0:T(8,128)(2,1)} %copy-done.3), custom_call_target="tpu_custom_call" | custom-call | bytes 25900000 | tf_op jit(solution)/shard_map/hidden_grad/pallas_call | solution.py:383
  111.3 22.8 %all-to-all-start.3 = ((bf16[256,8,128]{2,1,0:T(8,128)(2,1)}), bf16[256,8,128]{2,1,0:T(8,128)(2,1)S(1)}, u32[]{:S(2)}, u32[]{:S(2)}) async-start(bf16[256,8,128]{2,1,0:T(8,128)(2,1)} %bitcast.22), calls=%async_computation.3 | async-start | bytes 1048576 | tf_op jit(solution)/shard_map/all_to_all | solution.py:313
  134.1 2.4 %collective-permute-start.6 = (bf16[16,144,128]{2,1,0:T(8,128)(2,1)S(1)}, bf16[16,144,128]{2,1,0:T(8,128)(2,1)S(1)}, u32[]{:S(2)}, u32[]{:S(2)}) collective-permute-start(bf16[16,144,128]{2,1,0:T(8,128)(2,1)S(1)} %copy-done.9), channel_id=1, source_target_pairs={{0,32},{32,0},{1,33},{33,1},{2,34},{34,2},{3,35},{35,3},{4,36},{36... | collective-permute-start | bytes 1769480 | tf_op jit(solution)/shard_map/ppermute | solution.py:317
  136.5 1.9 %collective-permute-start.5 = (s32[8,2,3968]{2,1,0:T(2,128)S(1)}, s32[8,2,3968]{2,1,0:T(2,128)S(1)}, u32[]{:S(2)}, u32[]{:S(2)}) collective-permute-start(s32[8,2,3968]{2,1,0:T(2,128)S(1)} %bitcast.21), channel_id=1, source_target_pairs={{0,32},{32,0},{1,33},{33,1},{2,34},{34,2},{3,35},{35,3},{4,36},{36... | collective-permute-start | bytes 761864 | tf_op jit(solution)/shard_map/ppermute | solution.py:317
  138.5 1.5 collective-permute-done.5.other_index
  140.9 15.6 %embedding_grad.1 = (f32[64,3968]{1,0:T(8,128)}, f32[1,3968]{1,0:T(1,128)}) custom-call(s32[4]{0:T(128)} %pad_add_fusion.2.place_ref, bf16[16,32,256]{2,1,0:T(8,128)(2,1)} %all_to_all.20.grad_ref, s32[8,2,3968]{2,1,0:T(2,128)} %bitcast.20, s32[8,2,3968]{2,1,0:T(2,128)} %copy-done.6, bf16[16,144,128]{2,1,0:T(8,128)(2,1)} %get-tuple-element.9.keep_ref, ...), custom_call_target="tpu_custom_call" | custom-call | bytes 59200000 | tf_op jit(solution)/shard_map/embedding_grad/pallas_call | solution.py:394
  156.5 1.4 reduce
  158.7 1.8 %sum_shards.1 = bf16[8,1024]{1,0:T(8,128)(2,1)} custom-call(s32[4]{0:T(128)} %pad_add_fusion.2.place_ref, bf16[256,8,128]{2,1,0:T(8,128)(2,1)} %copy-done.1), custom_call_target="tpu_custom_call" | custom-call | bytes 3700000 | tf_op jit(solution)/shard_map/sum_shards/pallas_call | solution.py:407
  (32 shorter events, 5.3 us)
Async XLA Ops:
  4.1 23.4 %copy-start.7 = (s32[2,3968]{1,0:T(2,128)S(1)}, s32[2,3968]{1,0:T(2,128)}, u32[]{:S(2)}) copy-start(s32[2,3968]{1,0:T(2,128)} %param.12) | copy-start | bytes 95236
  4.1 45.5 %copy-start.2 = (bf16[64,3968]{1,0:T(8,128)(2,1)S(1)}, bf16[64,3968]{1,0:T(8,128)(2,1)}, u32[]{:S(2)}) copy-start(bf16[64,3968]{1,0:T(8,128)(2,1)} %own_ref.3) | copy-start | bytes 1523716
  4.1 55.1 %all-to-all-start = ((bf16[256,2,1152]{2,1,0:T(2,128)(2,1)}), bf16[256,2,1152]{2,1,0:T(2,128)(2,1)S(1)}, u32[]{:S(2)}, u32[]{:S(2)}) async-start(bf16[256,2,1152]{2,1,0:T(2,128)(2,1)} %bitcast.17), calls=%async_computation | async-start | bytes 2359296 | tf_op jit(solution)/shard_map/all_to_all | solution.py:313
  27.5 14.8 %collective-permute-start = (s32[2,3968]{1,0:T(2,128)S(1)}, s32[2,3968]{1,0:T(2,128)S(1)}, u32[]{:S(2)}, u32[]{:S(2)}) collective-permute-start(s32[2,3968]{1,0:T(2,128)S(1)} %copy-done.7), channel_id=1, source_target_pairs={{0,256},{256,0},{1,257},{257,1},{2,258},{258,2},{3,259},{259,3},{4... | collective-permute-start | bytes 95240 | tf_op jit(solution)/shard_map/ppermute | solution.py:317
  42.4 14.0 %collective-permute-start.3 = (s32[2,2,3968]{2,1,0:T(2,128)S(1)}, s32[2,2,3968]{2,1,0:T(2,128)S(1)}, u32[]{:S(2)}, u32[]{:S(2)}) collective-permute-start(s32[2,2,3968]{2,1,0:T(2,128)S(1)} %get-tuple-element.14), channel_id=1, source_target_pairs={{0,192},{64,0},{128,64},{192,128},{1,193},{65,1},{129,65},{193,129... | collective-permute-start | bytes 190472 | tf_op jit(solution)/shard_map/ppermute | solution.py:344
  44.3 12.1 %collective-permute-start.2 = (s32[2,2,3968]{2,1,0:T(2,128)S(1)}, s32[2,2,3968]{2,1,0:T(2,128)S(1)}, u32[]{:S(2)}, u32[]{:S(2)}) collective-permute-start(s32[2,2,3968]{2,1,0:T(2,128)S(1)} %get-tuple-element.14), channel_id=1, source_target_pairs={{0,128},{64,192},{128,0},{192,64},{1,129},{65,193},{129,1},{193,65... | collective-permute-start | bytes 190472 | tf_op jit(solution)/shard_map/ppermute | solution.py:344
  46.7 9.7 %collective-permute-start.1 = (s32[2,2,3968]{2,1,0:T(2,128)S(1)}, s32[2,2,3968]{2,1,0:T(2,128)S(1)}, u32[]{:S(2)}, u32[]{:S(2)}) collective-permute-start(s32[2,2,3968]{2,1,0:T(2,128)S(1)} %get-tuple-element.14), channel_id=1, source_target_pairs={{0,64},{64,128},{128,192},{192,0},{1,65},{65,129},{129,193},{193,1... | collective-permute-start | bytes 190472 | tf_op jit(solution)/shard_map/ppermute | solution.py:344
  49.6 13.7 %collective-permute-start.4 = (bf16[64,3968]{1,0:T(8,128)(2,1)S(1)}, bf16[64,3968]{1,0:T(8,128)(2,1)S(1)}, u32[]{:S(2)}, u32[]{:S(2)}) collective-permute-start(bf16[64,3968]{1,0:T(8,128)(2,1)S(1)} %copy-done.2), channel_id=1, source_target_pairs={{0,32},{32,0},{1,33},{33,1},{2,34},{34,2},{3,35},{35,3},{4,36},{36... | collective-permute-start | bytes 1523720 | tf_op jit(solution)/shard_map/ppermute | solution.py:317
  63.3 0.8 copy-start.3
  64.1 15.5 %copy-start.8 = (f32[3968]{0:T(1024)S(1)}, f32[3968]{0:T(1024)}, u32[]{:S(2)}) copy-start(f32[3968]{0:T(1024)} %param.14) | copy-start | bytes 47620
  72.6 15.4 %all-to-all-start.1 = ((f32[16,24,256]{2,1,0:T(8,128)}), f32[16,24,256]{2,1,0:T(8,128)S(1)}, u32[]{:S(2)}, u32[]{:S(2)}) async-start(f32[16,24,256]{2,1,0:T(8,128)} %logits.1), calls=%async_computation.1 | async-start | bytes 786432 | tf_op jit(solution)/shard_map/all_to_all | solution.py:313
  88.0 0.8 copy-start.4
  103.0 31.1 %copy-start.9 = (bf16[16,144,128]{2,1,0:T(8,128)(2,1)S(1)}, bf16[16,144,128]{2,1,0:T(8,128)(2,1)}, u32[]{:S(2)}) copy-start(bf16[16,144,128]{2,1,0:T(8,128)(2,1)} %get-tuple-element.10) | copy-start | bytes 1769476
  103.0 33.5 %copy-start = (s32[2,4,2,3968]{3,2,1,0:T(2,128)S(1)}, s32[2,4,2,3968]{3,2,1,0:T(2,128)}, u32[]{:S(2)}) copy-start(s32[2,4,2,3968]{3,2,1,0:T(2,128)} %copy.11) | copy-start | bytes 761860
  111.3 46.5 %all-to-all-start.3 = ((bf16[256,8,128]{2,1,0:T(8,128)(2,1)}), bf16[256,8,128]{2,1,0:T(8,128)(2,1)S(1)}, u32[]{:S(2)}, u32[]{:S(2)}) async-start(bf16[256,8,128]{2,1,0:T(8,128)(2,1)} %bitcast.22), calls=%async_computation.3 | async-start | bytes 1048576 | tf_op jit(solution)/shard_map/all_to_all | solution.py:313
  134.1 5.8 %collective-permute-start.6 = (bf16[16,144,128]{2,1,0:T(8,128)(2,1)S(1)}, bf16[16,144,128]{2,1,0:T(8,128)(2,1)S(1)}, u32[]{:S(2)}, u32[]{:S(2)}) collective-permute-start(bf16[16,144,128]{2,1,0:T(8,128)(2,1)S(1)} %copy-done.9), channel_id=1, source_target_pairs={{0,32},{32,0},{1,33},{33,1},{2,34},{34,2},{3,35},{35,3},{4,36},{36... | collective-permute-start | bytes 1769480 | tf_op jit(solution)/shard_map/ppermute | solution.py:317
  136.5 3.4 %collective-permute-start.5 = (s32[8,2,3968]{2,1,0:T(2,128)S(1)}, s32[8,2,3968]{2,1,0:T(2,128)S(1)}, u32[]{:S(2)}, u32[]{:S(2)}) collective-permute-start(s32[8,2,3968]{2,1,0:T(2,128)S(1)} %bitcast.21), channel_id=1, source_target_pairs={{0,32},{32,0},{1,33},{33,1},{2,34},{34,2},{3,35},{35,3},{4,36},{36... | collective-permute-start | bytes 761864 | tf_op jit(solution)/shard_map/ppermute | solution.py:317
  140.0 0.7 copy-start.6
  140.0 0.9 copy-start.5
  157.9 0.8 copy-start.1

commit v5 on v4

--- a/solution.py
+++ b/solution.py
@@ -32,7 +32,6 @@
 CHUNK = 256
 STEP = 512
 STEPS = 8
-ROOM = 56
 CARRY = 4 * 2 * PAIR + LANES
 
 
@@ -104,11 +103,10 @@
         copy.wait()
 
 
-def turn_body(rows_ref, hidden_out, keep_out, send_out):
+def turn_body(rows_ref, keep_out, send_out):
     for p in range(OWN):
         rows = rows_ref[p * 32 : (p + 1) * 32, :].astype(F32)
         tokens = jnp.concatenate([rows[:, q * CHUNK : (q + 1) * CHUNK] for q in range(4)], axis=0)
-        hidden_out[p * SEQ : (p + 1) * SEQ, :] = tokens[:, 0:PAIR].astype(BF16)
         turned = tokens.T.astype(BF16)
         digits = rows[:, 4 * CHUNK :].T
         digits = jnp.concatenate([digits[q * 8 : q * 8 + 8] for q in range(4)], axis=1)
@@ -119,7 +117,14 @@
             out[p, PAIR:, :] = digits
 
 
-def logits_body(place_ref, hidden_ref, index_ref, own_ref, other_ref, pooled_ref, out_ref):
+def logits_body(place_ref, rows_ref, index_ref, own_ref, other_ref, pooled_ref, out_ref, hidden_ref):
+    @pl.when(pl.program_id(0) == 0)
+    def unfold():
+        for p in range(OWN):
+            for q in range(4):
+                at = p * SEQ + q * 32
+                hidden_ref[at : at + 32, :] = rows_ref[p * 32 : p * 32 + 32, q * CHUNK : q * CHUNK + PAIR]
+
     here = lax.broadcasted_iota(I32, (SEQ, 1), 0)
     inside = pl.program_id(0) * STEP + lax.broadcasted_iota(I32, (1, STEP), 1) < VOC
     embed = jnp.concatenate([own_ref[...], other_ref[...]], axis=0)
@@ -203,11 +208,8 @@
             out_ref[rows(p), :] = (total[rows(p), :] + scatter(VOC - (STEPS - 1) * STEP, p)).astype(BF16)
 
 
-def embed_body(
-    place_ref, grad_ref, own_index, other_index, keep_ref, got_ref, out_ref, bias_ref, left, right, total, grads
-):
+def token_body(place_ref, keep_ref, got_ref, out_ref, left, right, total):
     base = place_ref[0] * VOC
-    first_core = place_ref[1] == 0
     low_row = lax.broadcasted_iota(I32, (512, LANES), 0).astype(I16)
     zero = jnp.zeros((), BF16)
     one = jnp.ones((), BF16)
@@ -243,8 +245,13 @@
 
         lax.fori_loop(0, 2, one_block, 0)
     for h in range(8):
-        width = min(512, VOC - h * 512)
-        out_ref[:, h * 512 : h * 512 + width] = total[h * COLS : (h + 1) * COLS, 0:width]
+        out_ref[:, h * 512 : (h + 1) * 512] = total[h * COLS : (h + 1) * COLS, :]
+
+
+def embed_body(
+    place_ref, token_ref, grad_ref, own_index, other_index, keep_ref, got_ref, out_ref, bias_ref, grads
+):
+    first_core = place_ref[1] == 0
     for g in range(GROUPS):
         both = grad_ref[g].astype(F32)
         grads[g] = jnp.where(first_core, both, jnp.concatenate([both[OWN:], both[:OWN]], axis=0))
@@ -252,7 +259,7 @@
     def one_tile(tile, carry):
         lanes = pl.ds(pl.multiple_of(tile * LANES, LANES), LANES)
         half = pl.ds(pl.multiple_of((tile % 2) * LANES, LANES), LANES)
-        totals = [out_ref[d : d + 16, lanes] for d in range(0, COLS, 16)]
+        totals = [token_ref[d : d + 16, lanes] for d in range(0, COLS, 16)]
         for n, (table_ref, index_ref) in enumerate(((keep_ref, own_index), (got_ref, other_index))):
             for p in range(OWN):
                 index = turned_spot(index_ref[slot(place_ref, p // 2), p % 2 : p % 2 + 1, lanes])
@@ -279,14 +286,14 @@
         out_ref[:, m * PAIR : (m + 1) * PAIR] = jnp.where(swap, other, total).astype(BF16)
 
 
-def call(body, name, out, scratch=(), specs=None, us=1, grid=(), out_specs=None):
+def call(body, name, out, scratch=(), specs=None, us=1, grid=(), out_specs=None, room=56):
     extra = {key: value for key, value in (("grid", grid), ("out_specs", out_specs)) if value}
     return pl.pallas_call(
         body,
         out_shape=out,
         in_specs=specs,
         scratch_shapes=scratch,
-        compiler_params=pltpu.CompilerParams(vmem_limit_bytes=ROOM * 1024 * 1024),
+        compiler_params=pltpu.CompilerParams(vmem_limit_bytes=room * 1024 * 1024),
         cost_estimate=pl.CostEstimate(flops=0, bytes_accessed=3_700_000 * us, transcendentals=0),
         name=name,
         **extra,
@@ -339,31 +346,19 @@
     )(place, lengths, token_ids, hidden, embed_grad)
     all_rows = exchange(rows.reshape(CHIPS * SHARDS, 2, CARRY), HOME).reshape(-1, CARRY)
     other_embed = swap_over(embedding, "core")
-    index = jnp.stack([pool_index, swap_over(pool_index, "zl")])
-    shifts = [
-        lax.ppermute(index, "x", [(k, (k + s) % 4) for k in range(4)]) for s in range(1, 4)
-    ]
-    own_index = jnp.stack([index] + shifts, axis=1).reshape(CHIPS, 2, VOC)
-    other_index = swap_over(own_index, "core")
-    hidden_rows, keep, send = call(
-        turn_body,
-        "turn",
-        (
-            shape((OWN * SEQ, PAIR), BF16),
-            shape((OWN, PAIR + 16, SEQ), BF16),
-            shape((OWN, PAIR + 16, SEQ), BF16),
-        ),
-        specs=[VMEM],
-        us=2,
-    )(all_rows)
-    got = swap_over(send, "core")
+    index = [pool_index]
+    for slot_at in range(1, CHIPS):
+        pairs = [(m, ((m // 4) ^ (slot_at // 4)) * 4 + (m + slot_at) % 4) for m in range(CHIPS)]
+        index.append(lax.ppermute(pool_index, ("zl", "x"), pairs))
+    own_index = jnp.stack(index)
     partial = call(
         logits_body,
         "logits",
         shape((GROUPS, 24, CHUNK), F32),
+        [pltpu.VMEM((OWN * SEQ, PAIR), BF16)],
         specs=[
             SMEM,
-            whole(OWN * SEQ, PAIR),
+            whole(OWN * SEQ // 4, CARRY),
             lanes_of(CHIPS, 2),
             lanes_of(COLS),
             lanes_of(COLS),
@@ -371,15 +366,38 @@
         ],
         out_specs=chunks_of(24, CHUNK),
         grid=(STEPS,),
-        us=6,
-    )(place, hidden_rows, own_index, embedding, other_embed, pooled_grad)
+        us=7,
+    )(place, all_rows, own_index, embedding, other_embed, pooled_grad)
+    keep, send = call(
+        turn_body,
+        "turn",
+        (shape((OWN, PAIR + 16, SEQ), BF16), shape((OWN, PAIR + 16, SEQ), BF16)),
+        specs=[VMEM],
+        us=3,
+    )(all_rows)
+    got = swap_over(send, "core")
+    other_index = swap_over(own_index, "core")
     parts = exchange(partial, GROUP)
     bias = jnp.pad(head_bias, (0, GROUPS * CHUNK - VOC)).reshape(GROUPS, 1, CHUNK)
     bias = lax.dynamic_index_in_dim(bias, lax.axis_index(GROUP), 0, keepdims=False)
     grad_block = call(
-        slope_body, "slope", shape((GROUPS, PASSAGES, CHUNK), BF16), specs=[VMEM, VMEM]
+        slope_body, "slope", shape((GROUPS, PASSAGES, CHUNK), BF16), specs=[VMEM, VMEM], room=8
     )(parts, bias)
     all_grad = exchange(grad_block, GROUP)
+    token_grad = call(
+        token_body,
+        "token_grad",
+        shape((COLS, 4096), F32),
+        [
+            pltpu.VMEM((512, 1024), BF16),
+            pltpu.VMEM((512, 1024), BF16),
+            pltpu.VMEM((512, 512), F32),
+        ],
+        [SMEM, VMEM, VMEM],
+        us=5,
+        room=24,
+    )(place, keep, got)
+    all_grad, token_grad, other_index = lax.optimization_barrier((all_grad, token_grad, other_index))
     hidden_parts = call(
         hidden_body,
         "hidden_grad",
@@ -395,17 +413,13 @@
         embed_body,
         "embedding_grad",
         (shape((COLS, VOC), F32), shape((1, VOC), F32)),
-        [
-            pltpu.VMEM((512, 1024), BF16),
-            pltpu.VMEM((512, 1024), BF16),
-            pltpu.VMEM((512, 512), F32),
-            pltpu.VMEM((GROUPS, PASSAGES, CHUNK), F32),
-        ],
-        [SMEM] + [VMEM] * 5,
-        us=16,
-    )(place, all_grad, own_index, other_index, keep, got)
+        [pltpu.VMEM((GROUPS, PASSAGES, CHUNK), F32)],
+        [SMEM] + [VMEM] * 6,
+        us=11,
+        room=24,
+    )(place, token_grad, all_grad, own_index, other_index, keep, got)
     hidden_grad = call(
-        sum_body, "sum_shards", shape((ROWS, WIDTH), BF16), specs=[SMEM, VMEM]
+        sum_body, "sum_shards", shape((ROWS, WIDTH), BF16), specs=[SMEM, VMEM], room=8
     )(place, hidden_got)
     return hidden_grad, embedding_grad, bias_grad.reshape(VOC)
 

time: 162 us -> 157 us (0.969)
  blocking collectives: 12.4 us -> 0 us
  starting transfers between devices: 73.8 us -> 80.2 us
  local copies, waits for them, and re-layouts: 5.9 us -> 7.68 us
    ppermute x3 -> x7, starting transfers between devices: 7.2 us -> 24.4 us  [on_device(): index.append(lax.ppermute(pool_index, ('zl', 'x'), pairs))]
    ppermute x4 -> x3, waiting for transfers between devices: 13.9 us -> 0.01 us  [swap_over(): return lax.ppermute(x, axis, [(0, 1), (1, 0)])]
    all_to_all x1 -> x0, blocking collectives: 12.4 us -> none  [exchange(): return lax.all_to_all(x, axis, split_axis=0, concat_axis=0, tiled=True)]
    all_to_all x3 -> x4, waiting for transfers between devices: 9.88 us -> 22.2 us  [exchange(): return lax.all_to_all(x, axis, split_axis=0, concat_axis=0, tiled=True)]
    all_to_all x3 -> x4, starting transfers between devices: 53.1 us -> 46.7 us  [exchange(): return lax.all_to_all(x, axis, split_axis=0, concat_axis=0, tiled=True)]
    ppermute x4 -> x3, starting transfers between devices: 13.4 us -> 9.15 us  [swap_over(): return lax.ppermute(x, axis, [(0, 1), (1, 0)])]
    pallas_call x1, Pallas kernels: 15.6 us -> 11.7 us  [on_device(): call(embed_body, 'embedding_grad', (shape((COLS, VOC), F32), shape((1, VO...]
    pallas_call x3 -> x4, Pallas kernels: 13.1 us -> 16.8 us  [the longest x1 8.81 us: on_device(): call(logits_body, 'logits', shape((GROUPS, 24, CHUNK), F32), [pltpu.VMEM(...]
  transfers between devices with their start and end apart: 10 -> 14, of which waited for: 4 -> 5; matrix products, arithmetic and copies ran while one was open for 2% -> 5% of each run, Pallas kernels for 11% -> 14%
where the time goes in v5:
time: 157 us; the launch traced here: 155 us
  starting transfers between devices  80.2 us (51%)
  Pallas kernels  40.4 us (26%)
  waiting for transfers between devices  24.2 us (15%)
  local copies, waits for them, and re-layouts  7.68 us (5%)
    all_to_all x4, starting transfers between devices, exchange(): return lax.all_to_all(x, axis, split_axis=0, concat_axis=0, tiled=True)  46.7 us
    ppermute x7, starting transfers between devices, on_device(): index.append(lax.ppermute(pool_index, ('zl', 'x'), pairs))  24.4 us
    all_to_all x4, waiting for transfers between devices, exchange(): return lax.all_to_all(x, axis, split_axis=0, concat_axis=0, tiled=True)  22.2 us
    pallas_call x1, Pallas kernels, on_device(): call(embed_body, 'embedding_grad', (shape((COLS, VOC), F32), shape((1, VO...  11.7 us
    ppermute x3, starting transfers between devices, swap_over(): return lax.ppermute(x, axis, [(0, 1), (1, 0)])  9.15 us
    pallas_call x1, Pallas kernels, on_device(): call(logits_body, 'logits', shape((GROUPS, 24, CHUNK), F32), [pltpu.VMEM(...  8.81 us
    pallas_call x1, Pallas kernels, on_device(): call(hidden_body, 'hidden_grad', shape((OWN * SEQ, PAIR), BF16), [pltpu.V...  8.24 us
    unnamed x25, local copies, waits for them, and re-layouts  5.78 us
  transfers between devices with their start and end apart: 14, of which 5 were waited for; matrix products, arithmetic and copies ran while one was open for 5% of the time, Pallas kernels for 14%

profile of v5, /device:TPU:1, one launch (start us, length us, event | category | flops | bytes accessed | tf_op | source)
XLA Modules:
  0.0 154.6 jit_solution(34737002816718771)
XLA Ops:
  0.6 4.0 %collective-permute-start = (s32[2,3968]{1,0:T(2,128)}, s32[2,3968]{1,0:T(2,128)S(1)}, u32[]{:S(2)}, u32[]{:S(2)}) collective-permute-start(s32[2,3968]{1,0:T(2,128)} %param.12), channel_id=1, source_target_pairs={{0,64},{64,128},{128,192},{192,0},{256,320},{320,384},{384,448},{4... | collective-permute-start | bytes 95240 | tf_op jit(solution)/shard_map/ppermute | solution.py:352
  4.6 4.4 %collective-permute-start.1 = (s32[2,3968]{1,0:T(2,128)}, s32[2,3968]{1,0:T(2,128)S(1)}, u32[]{:S(2)}, u32[]{:S(2)}) collective-permute-start(s32[2,3968]{1,0:T(2,128)} %param.12), channel_id=1, source_target_pairs={{0,128},{64,192},{128,0},{192,64},{256,384},{320,448},{384,256},{4... | collective-permute-start | bytes 95240 | tf_op jit(solution)/shard_map/ppermute | solution.py:352
  9.0 3.1 %collective-permute-start.2 = (s32[2,3968]{1,0:T(2,128)}, s32[2,3968]{1,0:T(2,128)S(1)}, u32[]{:S(2)}, u32[]{:S(2)}) collective-permute-start(s32[2,3968]{1,0:T(2,128)} %param.12), channel_id=1, source_target_pairs={{0,192},{64,0},{128,64},{192,128},{256,448},{320,256},{384,320},{4... | collective-permute-start | bytes 95240 | tf_op jit(solution)/shard_map/ppermute | solution.py:352
  12.0 4.0 %collective-permute-start.3 = (s32[2,3968]{1,0:T(2,128)}, s32[2,3968]{1,0:T(2,128)S(1)}, u32[]{:S(2)}, u32[]{:S(2)}) collective-permute-start(s32[2,3968]{1,0:T(2,128)} %param.12), channel_id=1, source_target_pairs={{0,256},{64,320},{128,384},{192,448},{256,0},{320,64},{384,128},{4... | collective-permute-start | bytes 95240 | tf_op jit(solution)/shard_map/ppermute | solution.py:352
  16.0 2.0 %collective-permute-start.4 = (s32[2,3968]{1,0:T(2,128)}, s32[2,3968]{1,0:T(2,128)S(1)}, u32[]{:S(2)}, u32[]{:S(2)}) collective-permute-start(s32[2,3968]{1,0:T(2,128)} %param.12), channel_id=1, source_target_pairs={{0,320},{64,384},{128,448},{192,256},{256,64},{320,128},{384,192},... | collective-permute-start | bytes 95240 | tf_op jit(solution)/shard_map/ppermute | solution.py:352
  18.6 2.9 %pack.1 = bf16[8,32,2,1152]{3,2,1,0:T(2,128)(2,1)} custom-call(s32[4]{0:T(128)} %pad_add_fusion.place_ref, s32[2]{0:T(128)} %lengths.1, s32[8]{0:T(128)} %ids.1, bf16[8,1024]{1,0:T(8,128)(2,1)} %hidden.1, bf16[8,1024]{1,0:T(8,128)(2,1)} %grad.1), custom_call_target="tpu_custom_call" | custom-call | bytes 3700000 | tf_op jit(solution)/shard_map/pack/pallas_call | solution.py:331
  21.6 21.5 %all-to-all-start = ((bf16[256,2,1152]{2,1,0:T(2,128)(2,1)}), bf16[256,2,1152]{2,1,0:T(2,128)(2,1)S(1)}, u32[]{:S(2)}, u32[]{:S(2)}) async-start(bf16[256,2,1152]{2,1,0:T(2,128)(2,1)} %bitcast.25), calls=%async_computation | async-start | bytes 2359296 | tf_op jit(solution)/shard_map/all_to_all | solution.py:320
  43.7 5.2 %collective-permute-start.5 = (s32[2,3968]{1,0:T(2,128)S(1)}, s32[2,3968]{1,0:T(2,128)S(1)}, u32[]{:S(2)}, u32[]{:S(2)}) collective-permute-start(s32[2,3968]{1,0:T(2,128)S(1)} %copy-done.7), channel_id=1, source_target_pairs={{0,384},{64,448},{128,256},{192,320},{256,128},{320,192},{384,0},{... | collective-permute-start | bytes 95240 | tf_op jit(solution)/shard_map/ppermute | solution.py:352
  49.5 1.9 %collective-permute-start.6 = (s32[2,3968]{1,0:T(2,128)S(1)}, s32[2,3968]{1,0:T(2,128)S(1)}, u32[]{:S(2)}, u32[]{:S(2)}) collective-permute-start(s32[2,3968]{1,0:T(2,128)S(1)} %copy-done.7), channel_id=1, source_target_pairs={{0,448},{64,256},{128,320},{192,384},{256,192},{320,0},{384,64},{4... | collective-permute-start | bytes 95240 | tf_op jit(solution)/shard_map/ppermute | solution.py:352
  52.0 4.9 %collective-permute-start.7 = (bf16[64,3968]{1,0:T(8,128)(2,1)S(1)}, bf16[64,3968]{1,0:T(8,128)(2,1)S(1)}, u32[]{:S(2)}, u32[]{:S(2)}) collective-permute-start(bf16[64,3968]{1,0:T(8,128)(2,1)S(1)} %copy-done.5), channel_id=1, source_target_pairs={{0,32},{32,0},{1,33},{33,1},{2,34},{34,2},{3,35},{35,3},{4,36},{36... | collective-permute-start | bytes 1523720 | tf_op jit(solution)/shard_map/ppermute | solution.py:324
  59.3 2.0 %collective-permute-done.6 = s32[2,3968]{1,0:T(2,128)S(1)} collective-permute-done((s32[2,3968]{1,0:T(2,128)S(1)}, s32[2,3968]{1,0:T(2,128)S(1)}, u32[]{:S(2)}, u32[]{:S(2)}) %collective-permute-start.6) | collective-permute-done | bytes 31776 | tf_op jit(solution)/shard_map/ppermute | solution.py:352
  61.9 11.1 %all-to-all-done = bf16[256,2,1152]{2,1,0:T(2,128)(2,1)S(1)} async-done(((bf16[256,2,1152]{2,1,0:T(2,128)(2,1)}), bf16[256,2,1152]{2,1,0:T(2,128)(2,1)S(1)}, u32[]{:S(2)}, u32[]{:S(2)}) %all-to-all-start) | async-done | bytes 1179680 | tf_op jit(solution)/shard_map/all_to_all | solution.py:320
  75.1 8.8 %logits.1 = f32[16,24,256]{2,1,0:T(8,128)} custom-call(s32[4]{0:T(128)} %pad_add_fusion.place_ref, bf16[512,1152]{1,0:T(8,128)(2,1)} %reshape.22.rows_ref, s32[8,2,3968]{2,1,0:T(2,128)} %bitcast_dynamic-update-slice_fusion.index_ref.own_index, bf16[64,3968]{1,0:T(8,128)(2,1)} %own_ref.3, bf16[64,3968]{1,0:T(8,128)(2,1)} %copy-done.6, f32[2,3968]{1,0:T(2,128)} %pooled_ref.1), custom_call_target="tpu_custom_call" | custom-call | bytes 25900000 | tf_op jit(solution)/shard_map/logits/pallas_call | solution.py:354
  83.9 8.8 %all-to-all-start.1 = ((f32[16,24,256]{2,1,0:T(8,128)}), f32[16,24,256]{2,1,0:T(8,128)S(1)}, u32[]{:S(2)}, u32[]{:S(2)}) async-start(f32[16,24,256]{2,1,0:T(8,128)} %logits.1), calls=%async_computation.1 | async-start | bytes 786432 | tf_op jit(solution)/shard_map/all_to_all | solution.py:320
  92.7 2.7 %turn.1 = (bf16[16,144,128]{2,1,0:T(8,128)(2,1)}, bf16[16,144,128]{2,1,0:T(8,128)(2,1)}) custom-call(bf16[512,1152]{1,0:T(8,128)(2,1)} %reshape.22.rows_ref), custom_call_target="tpu_custom_call" | custom-call | bytes 11100000 | tf_op jit(solution)/shard_map/turn/pallas_call | solution.py:371
  95.5 2.1 %collective-permute-start.8 = (bf16[16,144,128]{2,1,0:T(8,128)(2,1)}, bf16[16,144,128]{2,1,0:T(8,128)(2,1)S(1)}, u32[]{:S(2)}, u32[]{:S(2)}) collective-permute-start(bf16[16,144,128]{2,1,0:T(8,128)(2,1)} %get-tuple-element.11), channel_id=1, source_target_pairs={{0,32},{32,0},{1,33},{33,1},{2,34},{34,2},{3,35},{35,3},{4,36},{36... | collective-permute-start | bytes 1769480 | tf_op jit(solution)/shard_map/ppermute | solution.py:324
  97.6 3.4 %all-to-all-done.1.part_ref = f32[16,24,256]{2,1,0:T(8,128)S(1)} async-done(((f32[16,24,256]{2,1,0:T(8,128)}), f32[16,24,256]{2,1,0:T(8,128)S(1)}, u32[]{:S(2)}, u32[]{:S(2)}) %all-to-all-start.1) | async-done | bytes 393248 | tf_op jit(solution)/shard_map/all_to_all | solution.py:320
  101.9 4.5 %all-to-all-start.2 = ((bf16[16,32,256]{2,1,0:T(8,128)(2,1)}), bf16[16,32,256]{2,1,0:T(8,128)(2,1)S(1)}, u32[]{:S(2)}, u32[]{:S(2)}) async-start(bf16[16,32,256]{2,1,0:T(8,128)(2,1)} %slope.1), calls=%async_computation.2 | async-start | bytes 524288 | tf_op jit(solution)/shard_map/all_to_all | solution.py:320
  106.3 2.1 %collective-permute-start.9 = (s32[8,2,3968]{2,1,0:T(2,128)}, s32[8,2,3968]{2,1,0:T(2,128)S(1)}, u32[]{:S(2)}, u32[]{:S(2)}) collective-permute-start(s32[8,2,3968]{2,1,0:T(2,128)} %bitcast_dynamic-update-slice_fusion.index_ref.own_index), channel_id=1, source_target_pairs={{0,32},{32,0},{1,33},{33,1},{2,34},{34,2},{3,35},{35,3},{4,36},{36... | collective-permute-start | bytes 761864 | tf_op jit(solution)/shard_map/ppermute | solution.py:324
  108.5 3.9 %token_grad.1.token_ref = f32[64,4096]{1,0:T(8,128)S(1)} custom-call(s32[4]{0:T(128)S(1)} %copy-done.3, bf16[16,144,128]{2,1,0:T(8,128)(2,1)S(1)} %copy-done, bf16[16,144,128]{2,1,0:T(8,128)(2,1)S(1)} %collective-permute-done.8.got_ref), custom_call_target="tpu_custom_call" | custom-call | bytes 18500000 | tf_op jit(solution)/shard_map/token_grad/pallas_call | solution.py:387
  114.3 8.2 %hidden_grad.1 = bf16[2048,128]{1,0:T(8,128)(2,1)} custom-call(s32[4]{0:T(128)} %pad_add_fusion.place_ref, bf16[16,32,256]{2,1,0:T(8,128)(2,1)} %copy-done.1, s32[8,2,3968]{2,1,0:T(2,128)} %bitcast_dynamic-update-slice_fusion.index_ref.own_index, bf16[64,3968]{1,0:T(8,128)(2,1)} %own_ref.3, bf16[64,3968]{1,0:T(8,128)(2,1)} %copy-done.6), custom_call_target="tpu_custom_call" | custom-call | bytes 25900000 | tf_op jit(solution)/shard_map/hidden_grad/pallas_call | solution.py:401
  122.5 11.9 %all-to-all-start.3 = ((bf16[256,8,128]{2,1,0:T(8,128)(2,1)}), bf16[256,8,128]{2,1,0:T(8,128)(2,1)S(1)}, u32[]{:S(2)}, u32[]{:S(2)}) async-start(bf16[256,8,128]{2,1,0:T(8,128)(2,1)} %bitcast.26), calls=%async_computation.3 | async-start | bytes 1048576 | tf_op jit(solution)/shard_map/all_to_all | solution.py:320
  134.5 11.7 %embedding_grad.1 = (f32[64,3968]{1,0:T(8,128)}, f32[1,3968]{1,0:T(1,128)S(1)}) custom-call(s32[4]{0:T(128)S(1)} %copy-done.4, f32[64,4096]{1,0:T(8,128)S(1)} %token_grad.1.token_ref, bf16[16,32,256]{2,1,0:T(8,128)(2,1)S(1)} %copy-done.2, s32[8,2,3968]{2,1,0:T(2,128)} %bitcast_dynamic-update-slice_fusion.index_ref.own_index, ...), custom_call_target="tpu_custom_call" | custom-call | bytes 40700000 | tf_op jit(solution)/shard_map/embedding_grad/pallas_call | solution.py:412
  146.8 6.5 %all-to-all-done.3.part_ref = bf16[256,8,128]{2,1,0:T(8,128)(2,1)S(1)} async-done(((bf16[256,8,128]{2,1,0:T(8,128)(2,1)}), bf16[256,8,128]{2,1,0:T(8,128)(2,1)S(1)}, u32[]{:S(2)}, u32[]{:S(2)}) %all-to-all-start.3) | async-done | bytes 524320 | tf_op jit(solution)/shard_map/all_to_all | solution.py:320
  (43 shorter events, 12.2 us)
Async XLA Ops:
  0.6 43.0 %collective-permute-start = (s32[2,3968]{1,0:T(2,128)}, s32[2,3968]{1,0:T(2,128)S(1)}, u32[]{:S(2)}, u32[]{:S(2)}) collective-permute-start(s32[2,3968]{1,0:T(2,128)} %param.12), channel_id=1, source_target_pairs={{0,64},{64,128},{128,192},{192,0},{256,320},{320,384},{384,448},{4... | collective-permute-start | bytes 95240 | tf_op jit(solution)/shard_map/ppermute | solution.py:352
  4.6 44.9 %collective-permute-start.1 = (s32[2,3968]{1,0:T(2,128)}, s32[2,3968]{1,0:T(2,128)S(1)}, u32[]{:S(2)}, u32[]{:S(2)}) collective-permute-start(s32[2,3968]{1,0:T(2,128)} %param.12), channel_id=1, source_target_pairs={{0,128},{64,192},{128,0},{192,64},{256,384},{320,448},{384,256},{4... | collective-permute-start | bytes 95240 | tf_op jit(solution)/shard_map/ppermute | solution.py:352
  9.0 43.1 %collective-permute-start.2 = (s32[2,3968]{1,0:T(2,128)}, s32[2,3968]{1,0:T(2,128)S(1)}, u32[]{:S(2)}, u32[]{:S(2)}) collective-permute-start(s32[2,3968]{1,0:T(2,128)} %param.12), channel_id=1, source_target_pairs={{0,192},{64,0},{128,64},{192,128},{256,448},{320,256},{384,320},{4... | collective-permute-start | bytes 95240 | tf_op jit(solution)/shard_map/ppermute | solution.py:352
  12.0 45.5 %collective-permute-start.3 = (s32[2,3968]{1,0:T(2,128)}, s32[2,3968]{1,0:T(2,128)S(1)}, u32[]{:S(2)}, u32[]{:S(2)}) collective-permute-start(s32[2,3968]{1,0:T(2,128)} %param.12), channel_id=1, source_target_pairs={{0,256},{64,320},{128,384},{192,448},{256,0},{320,64},{384,128},{4... | collective-permute-start | bytes 95240 | tf_op jit(solution)/shard_map/ppermute | solution.py:352
  16.0 42.1 %collective-permute-start.4 = (s32[2,3968]{1,0:T(2,128)}, s32[2,3968]{1,0:T(2,128)S(1)}, u32[]{:S(2)}, u32[]{:S(2)}) collective-permute-start(s32[2,3968]{1,0:T(2,128)} %param.12), channel_id=1, source_target_pairs={{0,320},{64,384},{128,448},{192,256},{256,64},{320,128},{384,192},... | collective-permute-start | bytes 95240 | tf_op jit(solution)/shard_map/ppermute | solution.py:352
  21.5 21.5 %copy-start.7 = (s32[2,3968]{1,0:T(2,128)S(1)}, s32[2,3968]{1,0:T(2,128)}, u32[]{:S(2)}) copy-start(s32[2,3968]{1,0:T(2,128)} %param.12) | copy-start | bytes 95236
  21.5 30.5 %copy-start.5 = (bf16[64,3968]{1,0:T(8,128)(2,1)S(1)}, bf16[64,3968]{1,0:T(8,128)(2,1)}, u32[]{:S(2)}) copy-start(bf16[64,3968]{1,0:T(8,128)(2,1)} %own_ref.3) | copy-start | bytes 1523716
  21.6 51.5 %all-to-all-start = ((bf16[256,2,1152]{2,1,0:T(2,128)(2,1)}), bf16[256,2,1152]{2,1,0:T(2,128)(2,1)S(1)}, u32[]{:S(2)}, u32[]{:S(2)}) async-start(bf16[256,2,1152]{2,1,0:T(2,128)(2,1)} %bitcast.25), calls=%async_computation | async-start | bytes 2359296 | tf_op jit(solution)/shard_map/all_to_all | solution.py:320
  43.7 15.1 %collective-permute-start.5 = (s32[2,3968]{1,0:T(2,128)S(1)}, s32[2,3968]{1,0:T(2,128)S(1)}, u32[]{:S(2)}, u32[]{:S(2)}) collective-permute-start(s32[2,3968]{1,0:T(2,128)S(1)} %copy-done.7), channel_id=1, source_target_pairs={{0,384},{64,448},{128,256},{192,320},{256,128},{320,192},{384,0},{... | collective-permute-start | bytes 95240 | tf_op jit(solution)/shard_map/ppermute | solution.py:352
  49.5 11.9 %collective-permute-start.6 = (s32[2,3968]{1,0:T(2,128)S(1)}, s32[2,3968]{1,0:T(2,128)S(1)}, u32[]{:S(2)}, u32[]{:S(2)}) collective-permute-start(s32[2,3968]{1,0:T(2,128)S(1)} %copy-done.7), channel_id=1, source_target_pairs={{0,448},{64,256},{128,320},{192,384},{256,192},{320,0},{384,64},{4... | collective-permute-start | bytes 95240 | tf_op jit(solution)/shard_map/ppermute | solution.py:352
  52.0 22.3 %collective-permute-start.7 = (bf16[64,3968]{1,0:T(8,128)(2,1)S(1)}, bf16[64,3968]{1,0:T(8,128)(2,1)S(1)}, u32[]{:S(2)}, u32[]{:S(2)}) collective-permute-start(bf16[64,3968]{1,0:T(8,128)(2,1)S(1)} %copy-done.5), channel_id=1, source_target_pairs={{0,32},{32,0},{1,33},{33,1},{2,34},{34,2},{3,35},{35,3},{4,36},{36... | collective-permute-start | bytes 1523720 | tf_op jit(solution)/shard_map/ppermute | solution.py:324
  74.3 18.4 %copy-start.8 = (f32[3968]{0:T(1024)S(1)}, f32[3968]{0:T(1024)}, u32[]{:S(2)}) copy-start(f32[3968]{0:T(1024)} %param.14) | copy-start | bytes 47620
  74.3 0.8 copy-start.6
  83.9 17.2 %all-to-all-start.1 = ((f32[16,24,256]{2,1,0:T(8,128)}), f32[16,24,256]{2,1,0:T(8,128)S(1)}, u32[]{:S(2)}, u32[]{:S(2)}) async-start(f32[16,24,256]{2,1,0:T(8,128)} %logits.1), calls=%async_computation.1 | async-start | bytes 786432 | tf_op jit(solution)/shard_map/all_to_all | solution.py:320
  92.7 15.8 %copy-start.3 = (s32[4]{0:T(128)S(1)}, s32[4]{0:T(128)}, u32[]{:S(2)}) copy-start(s32[4]{0:T(128)} %pad_add_fusion.place_ref) | copy-start | bytes 52
  95.5 13.0 %copy-start = (bf16[16,144,128]{2,1,0:T(8,128)(2,1)S(1)}, bf16[16,144,128]{2,1,0:T(8,128)(2,1)}, u32[]{:S(2)}) copy-start(bf16[16,144,128]{2,1,0:T(8,128)(2,1)} %get-tuple-element.10.keep_ref) | copy-start | bytes 1769476
  95.5 13.0 %collective-permute-start.8 = (bf16[16,144,128]{2,1,0:T(8,128)(2,1)}, bf16[16,144,128]{2,1,0:T(8,128)(2,1)S(1)}, u32[]{:S(2)}, u32[]{:S(2)}) collective-permute-start(bf16[16,144,128]{2,1,0:T(8,128)(2,1)} %get-tuple-element.11), channel_id=1, source_target_pairs={{0,32},{32,0},{1,33},{33,1},{2,34},{34,2},{3,35},{35,3},{4,36},{36... | collective-permute-start | bytes 1769480 | tf_op jit(solution)/shard_map/ppermute | solution.py:324
  101.9 11.7 %all-to-all-start.2 = ((bf16[16,32,256]{2,1,0:T(8,128)(2,1)}), bf16[16,32,256]{2,1,0:T(8,128)(2,1)S(1)}, u32[]{:S(2)}, u32[]{:S(2)}) async-start(bf16[16,32,256]{2,1,0:T(8,128)(2,1)} %slope.1), calls=%async_computation.2 | async-start | bytes 524288 | tf_op jit(solution)/shard_map/all_to_all | solution.py:320
  106.3 6.1 %collective-permute-start.9 = (s32[8,2,3968]{2,1,0:T(2,128)}, s32[8,2,3968]{2,1,0:T(2,128)S(1)}, u32[]{:S(2)}, u32[]{:S(2)}) collective-permute-start(s32[8,2,3968]{2,1,0:T(2,128)} %bitcast_dynamic-update-slice_fusion.index_ref.own_index), channel_id=1, source_target_pairs={{0,32},{32,0},{1,33},{33,1},{2,34},{34,2},{3,35},{35,3},{4,36},{36... | collective-permute-start | bytes 761864 | tf_op jit(solution)/shard_map/ppermute | solution.py:324
  112.4 22.0 %copy-start.4 = (s32[4]{0:T(128)S(1)}, s32[4]{0:T(128)}, u32[]{:S(2)}) copy-start(s32[4]{0:T(128)} %pad_add_fusion.place_ref) | copy-start | bytes 52
  113.6 0.7 copy-start.1
  122.5 11.9 %copy-start.2 = (bf16[16,32,256]{2,1,0:T(8,128)(2,1)S(1)}, bf16[16,32,256]{2,1,0:T(8,128)(2,1)}, u32[]{:S(2)}) copy-start(bf16[16,32,256]{2,1,0:T(8,128)(2,1)} %copy-done.1) | copy-start | bytes 786436
  122.5 30.8 %all-to-all-start.3 = ((bf16[256,8,128]{2,1,0:T(8,128)(2,1)}), bf16[256,8,128]{2,1,0:T(8,128)(2,1)S(1)}, u32[]{:S(2)}, u32[]{:S(2)}) async-start(bf16[256,8,128]{2,1,0:T(8,128)(2,1)} %bitcast.26), calls=%async_computation.3 | async-start | bytes 1048576 | tf_op jit(solution)/shard_map/all_to_all | solution.py:320

commit v6 on v5

--- a/solution.py
+++ b/solution.py
@@ -30,8 +30,6 @@
 TILES = 31
 VOC = TILES * LANES
 CHUNK = 256
-STEP = 512
-STEPS = 8
 CARRY = 4 * 2 * PAIR + LANES
 
 
@@ -50,10 +48,6 @@
         (1, 1),
         mode=lax.GatherScatterMode.PROMISE_IN_BOUNDS,
     )
-
-
-def slot(place_ref, m):
-    return ((m // 4) ^ place_ref[2]) * 4 + ((place_ref[3] - m % 4) & 3)
 
 
 def turned_spot(index):
@@ -117,28 +111,46 @@
             out[p, PAIR:, :] = digits
 
 
-def logits_body(place_ref, rows_ref, index_ref, own_ref, other_ref, pooled_ref, out_ref, hidden_ref):
-    @pl.when(pl.program_id(0) == 0)
-    def unfold():
+def over_terms(step, one_chunk):
+    full = VOC // step
+
+    def loop(i, carry):
+        one_chunk(pl.multiple_of(i * step, step), step)
+        return carry
+
+    lax.fori_loop(0, full, loop, 0)
+    one_chunk(full * step, VOC - full * step)
+
+
+def logits_body(rows_ref, index_ref, own_ref, other_ref, pooled_ref, out_ref, hidden_ref, embed_ref):
+    here = lax.broadcasted_iota(I32, (SEQ, 1), 0)
+    embed_ref[0:COLS, :] = own_ref[...]
+    embed_ref[COLS:, :] = other_ref[...]
+    for p in range(OWN):
+        for q in range(4):
+            at = p * SEQ + q * 32
+            hidden_ref[at : at + 32, :] = rows_ref[p * 32 : p * 32 + 32, q * CHUNK : q * CHUNK + PAIR]
+
+    def one_chunk(first, width):
+        lanes = pl.ds(first, width)
+        embed = embed_ref[:, lanes]
         for p in range(OWN):
-            for q in range(4):
-                at = p * SEQ + q * 32
-                hidden_ref[at : at + 32, :] = rows_ref[p * 32 : p * 32 + 32, q * CHUNK : q * CHUNK + PAIR]
-
-    here = lax.broadcasted_iota(I32, (SEQ, 1), 0)
-    inside = pl.program_id(0) * STEP + lax.broadcasted_iota(I32, (1, STEP), 1) < VOC
-    embed = jnp.concatenate([own_ref[...], other_ref[...]], axis=0)
-    picked = []
-    for p in range(OWN):
-        scores = jnp.dot(
-            hidden_ref[p * SEQ : (p + 1) * SEQ, :], embed, preferred_element_type=F32
-        )
-        index = turned_spot(index_ref[slot(place_ref, p // 2), p % 2 : p % 2 + 1, :])
-        picked.append(jnp.sum(jnp.where(index == here, scores, 0.0), axis=0, keepdims=True))
-    picked = jnp.concatenate(picked + [pooled_ref[...], jnp.zeros((6, STEP), F32)], axis=0)
-    picked = jnp.where(inside, picked, 0.0)
-    for n in range(2):
-        out_ref[n] = picked[:, n * CHUNK : (n + 1) * CHUNK]
+            scores = jnp.dot(
+                hidden_ref[p * SEQ : (p + 1) * SEQ, :], embed, preferred_element_type=F32
+            )
+            index = turned_spot(index_ref[p // 2, p % 2 : p % 2 + 1, lanes])
+            picked = jnp.sum(jnp.where(index == here, scores, 0.0), axis=0, keepdims=True)
+            for at in range(0, width, CHUNK):
+                some = min(CHUNK, width - at)
+                out_ref[first // CHUNK + at // CHUNK, p : p + 1, 0:some] = picked[:, at : at + some]
+        for at in range(0, width, CHUNK):
+            some = min(CHUNK, width - at)
+            upstream = pooled_ref[:, pl.ds(first + at, some)]
+            out_ref[first // CHUNK + at // CHUNK, OWN : OWN + 2, 0:some] = upstream
+
+    over_terms(1024, one_chunk)
+    out_ref[:, OWN + 2 :, :] = jnp.zeros((GROUPS, 6, CHUNK), F32)
+    out_ref[GROUPS - 1, :, LANES:] = jnp.zeros((24, CHUNK - LANES), F32)
 
 
 def slope_body(part_ref, bias_ref, out_ref):
@@ -162,50 +174,38 @@
         out_ref[g] = grad
 
 
-def hidden_body(place_ref, grad_ref, index_ref, own_ref, other_ref, out_ref, total, grads):
-    step = pl.program_id(0)
+def hidden_body(
+    place_ref, grad_ref, index_ref, own_ref, other_ref, out_ref, total, left, embed_ref, grads
+):
     here = lax.broadcasted_iota(I32, (SEQ, LANES), 0).astype(I16)
     zero = jnp.zeros((), BF16)
     first_core = place_ref[1] == 0
-    for n in range(2):
-        both = grad_ref[n].astype(F32)
-        grads[:, n * CHUNK : (n + 1) * CHUNK] = jnp.where(first_core, both[0:OWN], both[OWN:])
-
-    def scatter(width, p):
-        parts = []
-        for tile in range(width // LANES):
-            lanes = slice(tile * LANES, (tile + 1) * LANES)
-            index = index_ref[slot(place_ref, p // 2), p % 2 : p % 2 + 1, lanes]
-            index = jnp.broadcast_to(index, (16, LANES)).astype(I16)
-            value = jnp.broadcast_to(grads[p : p + 1, lanes], (16, LANES)).astype(BF16)
-            index = jnp.concatenate([index] * 8, axis=0)
-            value = jnp.concatenate([value] * 8, axis=0)
-            parts.append(jnp.where(index == here, value, zero))
-        embed = jnp.concatenate([own_ref[:, 0:width], other_ref[:, 0:width]], axis=0)
-        return lax.dot_general(
-            jnp.concatenate(parts, axis=1),
-            embed,
-            (((1,), (1,)), ((), ())),
-            preferred_element_type=F32,
-        )
-
-    def rows(p):
-        return slice(p * SEQ, (p + 1) * SEQ)
-
-    @pl.when(step == 0)
-    def first():
-        for p in range(OWN):
-            total[rows(p), :] = scatter(STEP, p)
-
-    @pl.when((step > 0) & (step < STEPS - 1))
-    def middle():
-        for p in range(OWN):
-            total[rows(p), :] += scatter(STEP, p)
-
-    @pl.when(step == STEPS - 1)
-    def last():
-        for p in range(OWN):
-            out_ref[rows(p), :] = (total[rows(p), :] + scatter(VOC - (STEPS - 1) * STEP, p)).astype(BF16)
+    embed_ref[0:COLS, :] = own_ref[...]
+    embed_ref[COLS:, :] = other_ref[...]
+    total[...] = jnp.zeros_like(total)
+
+    def one_chunk(first, width):
+        for at in range(0, width, CHUNK):
+            both = grad_ref[first // CHUNK + at // CHUNK].astype(F32)
+            grads[:, at : at + CHUNK] = jnp.where(first_core, both[0:OWN], both[OWN:])
+        embed = embed_ref[:, pl.ds(first, width)]
+        for group in range(0, OWN, 4):
+            for p in range(group, group + 4):
+                for tile in range(width // LANES):
+                    lanes = slice(tile * LANES, (tile + 1) * LANES)
+                    index = index_ref[p // 2, p % 2 : p % 2 + 1, pl.ds(first + tile * LANES, LANES)]
+                    index = jnp.broadcast_to(index, (16, LANES)).astype(I16)
+                    value = jnp.broadcast_to(grads[p : p + 1, lanes], (16, LANES)).astype(BF16)
+                    index = jnp.concatenate([index] * 8, axis=0)
+                    value = jnp.concatenate([value] * 8, axis=0)
+                    left[p * SEQ : (p + 1) * SEQ, lanes] = jnp.where(index == here, value, zero)
+            rows = slice(group * SEQ, (group + 4) * SEQ)
+            total[rows, :] += lax.dot_general(
+                left[rows, 0:width], embed, (((1,), (1,)), ((), ())), preferred_element_type=F32
+            )
+
+    over_terms(1024, one_chunk)
+    out_ref[...] = total[...].astype(BF16)
 
 
 def token_body(place_ref, keep_ref, got_ref, out_ref, left, right, total):
@@ -262,7 +262,7 @@
         totals = [token_ref[d : d + 16, lanes] for d in range(0, COLS, 16)]
         for n, (table_ref, index_ref) in enumerate(((keep_ref, own_index), (got_ref, other_index))):
             for p in range(OWN):
-                index = turned_spot(index_ref[slot(place_ref, p // 2), p % 2 : p % 2 + 1, lanes])
+                index = turned_spot(index_ref[p // 2, p % 2 : p % 2 + 1, lanes])
                 index = jnp.broadcast_to(index, (16, LANES)).astype(I16)
                 value = grads[tile // 2, n * OWN + p : n * OWN + p + 1, half]
                 for d in range(COLS // 16):
@@ -286,8 +286,8 @@
         out_ref[:, m * PAIR : (m + 1) * PAIR] = jnp.where(swap, other, total).astype(BF16)
 
 
-def call(body, name, out, scratch=(), specs=None, us=1, grid=(), out_specs=None, room=56):
-    extra = {key: value for key, value in (("grid", grid), ("out_specs", out_specs)) if value}
+def call(body, name, out, scratch=(), specs=None, us=1, out_specs=None, room=56):
+    extra = {} if out_specs is None else {"out_specs": out_specs}
     return pl.pallas_call(
         body,
         out_shape=out,
@@ -304,18 +304,6 @@
     return jax.ShapeDtypeStruct(dims, dtype)
 
 
-def lanes_of(*dims):
-    return pl.BlockSpec(dims + (STEP,), lambda i: (0,) * len(dims) + (i,))
-
-
-def chunks_of(*dims):
-    return pl.BlockSpec((2,) + dims, lambda i: (i,) + (0,) * len(dims))
-
-
-def whole(*dims):
-    return pl.BlockSpec(dims, lambda i: (0,) * len(dims))
-
-
 def exchange(x, axis):
     return lax.all_to_all(x, axis, split_axis=0, concat_axis=0, tiled=True)
 
@@ -328,6 +316,7 @@
     hidden, embed_grad, token_ids, lengths, pool_index, embedding, head_bias, pooled_grad
 ):
     place = jnp.stack([lax.axis_index(name) for name in (SHARD, "core", "zl", "x")]).astype(I32)
+    own_index = exchange(jnp.broadcast_to(pool_index, (CHIPS, 2, VOC)), ("zl", "x"))
     rows = call(
         pack_body,
         "pack",
@@ -343,31 +332,19 @@
         ],
         [SMEM] + [ANY] * 4,
         out_specs=ANY,
+        us=4,
     )(place, lengths, token_ids, hidden, embed_grad)
+    rows, own_index = lax.optimization_barrier((rows, own_index))
     all_rows = exchange(rows.reshape(CHIPS * SHARDS, 2, CARRY), HOME).reshape(-1, CARRY)
     other_embed = swap_over(embedding, "core")
-    index = [pool_index]
-    for slot_at in range(1, CHIPS):
-        pairs = [(m, ((m // 4) ^ (slot_at // 4)) * 4 + (m + slot_at) % 4) for m in range(CHIPS)]
-        index.append(lax.ppermute(pool_index, ("zl", "x"), pairs))
-    own_index = jnp.stack(index)
     partial = call(
         logits_body,
         "logits",
         shape((GROUPS, 24, CHUNK), F32),
-        [pltpu.VMEM((OWN * SEQ, PAIR), BF16)],
-        specs=[
-            SMEM,
-            whole(OWN * SEQ // 4, CARRY),
-            lanes_of(CHIPS, 2),
-            lanes_of(COLS),
-            lanes_of(COLS),
-            lanes_of(2),
-        ],
-        out_specs=chunks_of(24, CHUNK),
-        grid=(STEPS,),
-        us=7,
-    )(place, all_rows, own_index, embedding, other_embed, pooled_grad)
+        [pltpu.VMEM((OWN * SEQ, PAIR), BF16), pltpu.VMEM((PAIR, VOC), BF16)],
+        [VMEM] * 5,
+        us=6,
+    )(all_rows, own_index, embedding, other_embed, pooled_grad)
     keep, send = call(
         turn_body,
         "turn",
@@ -402,11 +379,14 @@
         hidden_body,
         "hidden_grad",
         shape((OWN * SEQ, PAIR), BF16),
-        [pltpu.VMEM((OWN * SEQ, PAIR), F32), pltpu.VMEM((OWN, STEP), F32)],
-        [SMEM, chunks_of(PASSAGES, CHUNK), lanes_of(CHIPS, 2), lanes_of(COLS), lanes_of(COLS)],
-        out_specs=whole(OWN * SEQ, PAIR),
-        grid=(STEPS,),
-        us=7,
+        [
+            pltpu.VMEM((OWN * SEQ, PAIR), F32),
+            pltpu.VMEM((OWN * SEQ, 1024), BF16),
+            pltpu.VMEM((PAIR, VOC), BF16),
+            pltpu.VMEM((OWN, 1024), F32),
+        ],
+        [SMEM] + [VMEM] * 4,
+        us=6,
     )(place, all_grad, own_index, embedding, other_embed)
     hidden_got = exchange(hidden_parts.reshape(CHIPS * SHARDS, ROWS, PAIR), HOME)
     embedding_grad, bias_grad = call(

time: 157 us -> 144 us (0.917)
  starting transfers between devices: 80.2 us -> 58.3 us
  waiting for transfers between devices: 24.2 us -> 39.8 us
  local copies, waits for them, and re-layouts: 7.68 us -> 4.35 us
  Pallas kernels: 40.4 us -> 38.6 us
    ppermute x7 -> x0, starting transfers between devices: 24.4 us -> none  [on_device(): index.append(lax.ppermute(pool_index, ('zl', 'x'), pairs))]
    all_to_all x4 -> x5, waiting for transfers between devices: 22.2 us -> 39.8 us  [exchange(): return lax.all_to_all(x, axis, split_axis=0, concat_axis=0, tiled=True)]
    unnamed x25 -> x16, local copies, waits for them, and re-layouts: 5.78 us -> 1.52 us
    all_to_all x4 -> x5, starting transfers between devices: 46.7 us -> 49.8 us  [exchange(): return lax.all_to_all(x, axis, split_axis=0, concat_axis=0, tiled=True)]
    ppermute x7 -> x0, waiting for transfers between devices: 2 us -> none  [on_device(): index.append(lax.ppermute(pool_index, ('zl', 'x'), pairs))]
  transfers between devices with their start and end apart: 14 -> 8, of which waited for: 5 -> 5; matrix products, arithmetic and copies ran while one was open for 5% -> 2% of each run, Pallas kernels for 14% -> 15%
where the time goes in v6:
time: 144 us; the launch traced here: 143 us
  starting transfers between devices  58.3 us (40%)
  waiting for transfers between devices  39.8 us (28%)
  Pallas kernels  38.6 us (27%)
  local copies, waits for them, and re-layouts  4.35 us (3%)
    all_to_all x5, starting transfers between devices, exchange(): return lax.all_to_all(x, axis, split_axis=0, concat_axis=0, tiled=True)  49.8 us
    all_to_all x5, waiting for transfers between devices, exchange(): return lax.all_to_all(x, axis, split_axis=0, concat_axis=0, tiled=True)  39.8 us
    pallas_call x1, Pallas kernels, on_device(): call(embed_body, 'embedding_grad', (shape((COLS, VOC), F32), shape((1, VO...  11.7 us
    ppermute x3, starting transfers between devices, swap_over(): return lax.ppermute(x, axis, [(0, 1), (1, 0)])  8.45 us
    pallas_call x1, Pallas kernels, on_device(): call(logits_body, 'logits', shape((GROUPS, 24, CHUNK), F32), [pltpu.VMEM(...  7.88 us
    pallas_call x1, Pallas kernels, on_device(): call(hidden_body, 'hidden_grad', shape((OWN * SEQ, PAIR), BF16), [pltpu.V...  7.37 us
    pallas_call x1, Pallas kernels, on_device(): call(token_body, 'token_grad', shape((COLS, 4096), F32), [pltpu.VMEM((512...  3.92 us
    pallas_call x1, Pallas kernels, on_device(): call(pack_body, 'pack', shape((CHIPS, SHARDS, 2, CARRY), BF16), [pltpu.SM...  2.91 us
  transfers between devices with their start and end apart: 8, of which 5 were waited for; matrix products, arithmetic and copies ran while one was open for 2% of the time, Pallas kernels for 15%

profile of v6, /device:TPU:1, one launch (start us, length us, event | category | flops | bytes accessed | tf_op | source)
XLA Modules:
  0.0 143.0 jit_solution(17384366758503941645)
XLA Ops:
  0.6 1.5 %broadcast_in_dim.3 = s32[8,2,3968]{2,1,0:T(2,128)} broadcast(s32[2,3968]{1,0:T(2,128)} %param.12), dimensions={1,2} | broadcast | bytes 285696 | tf_op jit(solution)/shard_map/broadcast_in_dim | solution.py:319
  2.1 6.7 %all-to-all-start = ((s32[8,2,3968]{2,1,0:T(2,128)}), s32[8,2,3968]{2,1,0:T(2,128)}, u32[]{:S(2)}, u32[]{:S(2)}) async-start(s32[8,2,3968]{2,1,0:T(2,128)} %broadcast_in_dim.3), calls=%async_computation | async-start | bytes 507904 | tf_op jit(solution)/shard_map/all_to_all | solution.py:308
  9.4 2.9 %pack.1 = bf16[8,32,2,1152]{3,2,1,0:T(2,128)(2,1)} custom-call(s32[4]{0:T(128)} %pad_add_fusion.place_ref, s32[2]{0:T(128)} %lengths.1, s32[8]{0:T(128)} %ids.1, bf16[8,1024]{1,0:T(8,128)(2,1)} %hidden.1, bf16[8,1024]{1,0:T(8,128)(2,1)} %grad.1), custom_call_target="tpu_custom_call" | custom-call | bytes 14800000 | tf_op jit(solution)/shard_map/pack/pallas_call | solution.py:320
  12.3 2.6 %all-to-all-done.index_ref.own_index = s32[8,2,3968]{2,1,0:T(2,128)} async-done(((s32[8,2,3968]{2,1,0:T(2,128)}), s32[8,2,3968]{2,1,0:T(2,128)}, u32[]{:S(2)}, u32[]{:S(2)}) %all-to-all-start) | async-done | bytes 253984 | tf_op jit(solution)/shard_map/all_to_all | solution.py:308
  15.0 19.8 %all-to-all-start.1 = ((bf16[256,2,1152]{2,1,0:T(2,128)(2,1)}), bf16[256,2,1152]{2,1,0:T(2,128)(2,1)S(1)}, u32[]{:S(2)}, u32[]{:S(2)}) async-start(bf16[256,2,1152]{2,1,0:T(2,128)(2,1)} %bitcast.9), calls=%async_computation.1 | async-start | bytes 2359296 | tf_op jit(solution)/shard_map/all_to_all | solution.py:308
  34.7 4.0 %collective-permute-start = (bf16[64,3968]{1,0:T(8,128)(2,1)S(1)}, bf16[64,3968]{1,0:T(8,128)(2,1)S(1)}, u32[]{:S(2)}, u32[]{:S(2)}) collective-permute-start(bf16[64,3968]{1,0:T(8,128)(2,1)S(1)} %copy-done.5), channel_id=1, source_target_pairs={{0,32},{32,0},{1,33},{33,1},{2,34},{34,2},{3,35},{35,3},{4,36},{36... | collective-permute-start | bytes 1523720 | tf_op jit(solution)/shard_map/ppermute | solution.py:312
  38.7 26.2 %all-to-all-done.1 = bf16[256,2,1152]{2,1,0:T(2,128)(2,1)S(1)} async-done(((bf16[256,2,1152]{2,1,0:T(2,128)(2,1)}), bf16[256,2,1152]{2,1,0:T(2,128)(2,1)S(1)}, u32[]{:S(2)}, u32[]{:S(2)}) %all-to-all-start.1) | async-done | bytes 1179680 | tf_op jit(solution)/shard_map/all_to_all | solution.py:308
  64.9 1.3 reshape.22.rows_ref
  66.2 0.8 copy-done.6
  67.0 7.9 %logits.1 = f32[16,24,256]{2,1,0:T(8,128)} custom-call(bf16[512,1152]{1,0:T(8,128)(2,1)} %reshape.22.rows_ref, s32[8,2,3968]{2,1,0:T(2,128)} %all-to-all-done.index_ref.own_index, bf16[64,3968]{1,0:T(8,128)(2,1)} %own_ref.3, bf16[64,3968]{1,0:T(8,128)(2,1)} %copy-done.6, f32[2,3968]{1,0:T(2,128)} %pooled_ref.1), custom_call_target="tpu_custom_call" | custom-call | bytes 22200000 | tf_op jit(solution)/shard_map/logits/pallas_call | solution.py:340
  74.9 8.6 %all-to-all-start.2 = ((f32[16,24,256]{2,1,0:T(8,128)}), f32[16,24,256]{2,1,0:T(8,128)S(1)}, u32[]{:S(2)}, u32[]{:S(2)}) async-start(f32[16,24,256]{2,1,0:T(8,128)} %logits.1), calls=%async_computation.2 | async-start | bytes 786432 | tf_op jit(solution)/shard_map/all_to_all | solution.py:308
  83.5 2.7 %turn.1 = (bf16[16,144,128]{2,1,0:T(8,128)(2,1)}, bf16[16,144,128]{2,1,0:T(8,128)(2,1)}) custom-call(bf16[512,1152]{1,0:T(8,128)(2,1)} %reshape.22.rows_ref), custom_call_target="tpu_custom_call" | custom-call | bytes 11100000 | tf_op jit(solution)/shard_map/turn/pallas_call | solution.py:348
  86.2 2.1 %collective-permute-start.1 = (bf16[16,144,128]{2,1,0:T(8,128)(2,1)}, bf16[16,144,128]{2,1,0:T(8,128)(2,1)S(1)}, u32[]{:S(2)}, u32[]{:S(2)}) collective-permute-start(bf16[16,144,128]{2,1,0:T(8,128)(2,1)} %get-tuple-element.15), channel_id=1, source_target_pairs={{0,32},{32,0},{1,33},{33,1},{2,34},{34,2},{3,35},{35,3},{4,36},{36... | collective-permute-start | bytes 1769480 | tf_op jit(solution)/shard_map/ppermute | solution.py:312
  88.4 3.4 %all-to-all-done.2.part_ref = f32[16,24,256]{2,1,0:T(8,128)S(1)} async-done(((f32[16,24,256]{2,1,0:T(8,128)}), f32[16,24,256]{2,1,0:T(8,128)S(1)}, u32[]{:S(2)}, u32[]{:S(2)}) %all-to-all-start.2) | async-done | bytes 393248 | tf_op jit(solution)/shard_map/all_to_all | solution.py:308
  91.9 0.8 slope.1
  92.6 4.5 %all-to-all-start.3 = ((bf16[16,32,256]{2,1,0:T(8,128)(2,1)}), bf16[16,32,256]{2,1,0:T(8,128)(2,1)S(1)}, u32[]{:S(2)}, u32[]{:S(2)}) async-start(bf16[16,32,256]{2,1,0:T(8,128)(2,1)} %slope.1), calls=%async_computation.3 | async-start | bytes 524288 | tf_op jit(solution)/shard_map/all_to_all | solution.py:308
  97.1 2.3 %collective-permute-start.2 = (s32[8,2,3968]{2,1,0:T(2,128)}, s32[8,2,3968]{2,1,0:T(2,128)S(1)}, u32[]{:S(2)}, u32[]{:S(2)}) collective-permute-start(s32[8,2,3968]{2,1,0:T(2,128)} %all-to-all-done.index_ref.own_index), channel_id=1, source_target_pairs={{0,32},{32,0},{1,33},{33,1},{2,34},{34,2},{3,35},{35,3},{4,36},{36... | collective-permute-start | bytes 761864 | tf_op jit(solution)/shard_map/ppermute | solution.py:312
  99.5 3.9 %token_grad.1.token_ref = f32[64,4096]{1,0:T(8,128)S(1)} custom-call(s32[4]{0:T(128)S(1)} %copy-done.3, bf16[16,144,128]{2,1,0:T(8,128)(2,1)S(1)} %copy-done, bf16[16,144,128]{2,1,0:T(8,128)(2,1)S(1)} %collective-permute-done.1.got_ref), custom_call_target="tpu_custom_call" | custom-call | bytes 18500000 | tf_op jit(solution)/shard_map/token_grad/pallas_call | solution.py:364
  103.4 0.9 all-to-all-done.3.grad_ref
  105.1 7.4 %hidden_grad.1 = bf16[2048,128]{1,0:T(8,128)(2,1)} custom-call(s32[4]{0:T(128)} %pad_add_fusion.place_ref, bf16[16,32,256]{2,1,0:T(8,128)(2,1)} %copy-done.1, s32[8,2,3968]{2,1,0:T(2,128)} %all-to-all-done.index_ref.own_index, bf16[64,3968]{1,0:T(8,128)(2,1)} %own_ref.3, bf16[64,3968]{1,0:T(8,128)(2,1)} %copy-done.6), custom_call_target="tpu_custom_call" | custom-call | bytes 22200000 | tf_op jit(solution)/shard_map/hidden_grad/pallas_call | solution.py:378
  112.4 10.4 %all-to-all-start.4 = ((bf16[256,8,128]{2,1,0:T(8,128)(2,1)}), bf16[256,8,128]{2,1,0:T(8,128)(2,1)S(1)}, u32[]{:S(2)}, u32[]{:S(2)}) async-start(bf16[256,8,128]{2,1,0:T(8,128)(2,1)} %bitcast.10), calls=%async_computation.4 | async-start | bytes 1048576 | tf_op jit(solution)/shard_map/all_to_all | solution.py:308
  122.8 11.7 %embedding_grad.1 = (f32[64,3968]{1,0:T(8,128)}, f32[1,3968]{1,0:T(1,128)S(1)}) custom-call(s32[4]{0:T(128)S(1)} %copy-done.4, f32[64,4096]{1,0:T(8,128)S(1)} %token_grad.1.token_ref, bf16[16,32,256]{2,1,0:T(8,128)(2,1)S(1)} %copy-done.2, s32[8,2,3968]{2,1,0:T(2,128)} %all-to-all-done.index_ref.own_index, ...), custom_call_target="tpu_custom_call" | custom-call | bytes 40700000 | tf_op jit(solution)/shard_map/embedding_grad/pallas_call | solution.py:392
  135.1 6.6 %all-to-all-done.4.part_ref = bf16[256,8,128]{2,1,0:T(8,128)(2,1)S(1)} async-done(((bf16[256,8,128]{2,1,0:T(8,128)(2,1)}), bf16[256,8,128]{2,1,0:T(8,128)(2,1)S(1)}, u32[]{:S(2)}, u32[]{:S(2)}) %all-to-all-start.4) | async-done | bytes 524320 | tf_op jit(solution)/shard_map/all_to_all | solution.py:308
  141.7 1.3 sum_shards.1
  (22 shorter events, 2.0 us)
Async XLA Ops:
  2.1 12.8 %all-to-all-start = ((s32[8,2,3968]{2,1,0:T(2,128)}), s32[8,2,3968]{2,1,0:T(2,128)}, u32[]{:S(2)}, u32[]{:S(2)}) async-start(s32[8,2,3968]{2,1,0:T(2,128)} %broadcast_in_dim.3), calls=%async_computation | async-start | bytes 507904 | tf_op jit(solution)/shard_map/all_to_all | solution.py:308
  15.0 19.8 %copy-start.5 = (bf16[64,3968]{1,0:T(8,128)(2,1)S(1)}, bf16[64,3968]{1,0:T(8,128)(2,1)}, u32[]{:S(2)}) copy-start(bf16[64,3968]{1,0:T(8,128)(2,1)} %own_ref.3) | copy-start | bytes 1523716
  15.0 50.0 %all-to-all-start.1 = ((bf16[256,2,1152]{2,1,0:T(2,128)(2,1)}), bf16[256,2,1152]{2,1,0:T(2,128)(2,1)S(1)}, u32[]{:S(2)}, u32[]{:S(2)}) async-start(bf16[256,2,1152]{2,1,0:T(2,128)(2,1)} %bitcast.9), calls=%async_computation.1 | async-start | bytes 2359296 | tf_op jit(solution)/shard_map/all_to_all | solution.py:308
  34.7 31.5 %collective-permute-start = (bf16[64,3968]{1,0:T(8,128)(2,1)S(1)}, bf16[64,3968]{1,0:T(8,128)(2,1)S(1)}, u32[]{:S(2)}, u32[]{:S(2)}) collective-permute-start(bf16[64,3968]{1,0:T(8,128)(2,1)S(1)} %copy-done.5), channel_id=1, source_target_pairs={{0,32},{32,0},{1,33},{33,1},{2,34},{34,2},{3,35},{35,3},{4,36},{36... | collective-permute-start | bytes 1523720 | tf_op jit(solution)/shard_map/ppermute | solution.py:312
  66.2 17.2 %copy-start.7 = (f32[3968]{0:T(1024)S(1)}, f32[3968]{0:T(1024)}, u32[]{:S(2)}) copy-start(f32[3968]{0:T(1024)} %param.14) | copy-start | bytes 47620
  66.2 0.8 copy-start.6
  74.9 17.0 %all-to-all-start.2 = ((f32[16,24,256]{2,1,0:T(8,128)}), f32[16,24,256]{2,1,0:T(8,128)S(1)}, u32[]{:S(2)}, u32[]{:S(2)}) async-start(f32[16,24,256]{2,1,0:T(8,128)} %logits.1), calls=%async_computation.2 | async-start | bytes 786432 | tf_op jit(solution)/shard_map/all_to_all | solution.py:308
  83.5 16.0 %copy-start.3 = (s32[4]{0:T(128)S(1)}, s32[4]{0:T(128)}, u32[]{:S(2)}) copy-start(s32[4]{0:T(128)} %pad_add_fusion.place_ref) | copy-start | bytes 52
  86.2 13.2 %copy-start = (bf16[16,144,128]{2,1,0:T(8,128)(2,1)S(1)}, bf16[16,144,128]{2,1,0:T(8,128)(2,1)}, u32[]{:S(2)}) copy-start(bf16[16,144,128]{2,1,0:T(8,128)(2,1)} %get-tuple-element.14.keep_ref) | copy-start | bytes 1769476
  86.2 13.2 %collective-permute-start.1 = (bf16[16,144,128]{2,1,0:T(8,128)(2,1)}, bf16[16,144,128]{2,1,0:T(8,128)(2,1)S(1)}, u32[]{:S(2)}, u32[]{:S(2)}) collective-permute-start(bf16[16,144,128]{2,1,0:T(8,128)(2,1)} %get-tuple-element.15), channel_id=1, source_target_pairs={{0,32},{32,0},{1,33},{33,1},{2,34},{34,2},{3,35},{35,3},{4,36},{36... | collective-permute-start | bytes 1769480 | tf_op jit(solution)/shard_map/ppermute | solution.py:312
  92.6 11.7 %all-to-all-start.3 = ((bf16[16,32,256]{2,1,0:T(8,128)(2,1)}), bf16[16,32,256]{2,1,0:T(8,128)(2,1)S(1)}, u32[]{:S(2)}, u32[]{:S(2)}) async-start(bf16[16,32,256]{2,1,0:T(8,128)(2,1)} %slope.1), calls=%async_computation.3 | async-start | bytes 524288 | tf_op jit(solution)/shard_map/all_to_all | solution.py:308
  97.1 6.3 %collective-permute-start.2 = (s32[8,2,3968]{2,1,0:T(2,128)}, s32[8,2,3968]{2,1,0:T(2,128)S(1)}, u32[]{:S(2)}, u32[]{:S(2)}) collective-permute-start(s32[8,2,3968]{2,1,0:T(2,128)} %all-to-all-done.index_ref.own_index), channel_id=1, source_target_pairs={{0,32},{32,0},{1,33},{33,1},{2,34},{34,2},{3,35},{35,3},{4,36},{36... | collective-permute-start | bytes 761864 | tf_op jit(solution)/shard_map/ppermute | solution.py:312
  103.4 19.4 %copy-start.4 = (s32[4]{0:T(128)S(1)}, s32[4]{0:T(128)}, u32[]{:S(2)}) copy-start(s32[4]{0:T(128)} %pad_add_fusion.place_ref) | copy-start | bytes 52
  104.4 0.7 copy-start.1
  112.4 10.4 %copy-start.2 = (bf16[16,32,256]{2,1,0:T(8,128)(2,1)S(1)}, bf16[16,32,256]{2,1,0:T(8,128)(2,1)}, u32[]{:S(2)}) copy-start(bf16[16,32,256]{2,1,0:T(8,128)(2,1)} %copy-done.1) | copy-start | bytes 786436
  112.4 29.3 %all-to-all-start.4 = ((bf16[256,8,128]{2,1,0:T(8,128)(2,1)}), bf16[256,8,128]{2,1,0:T(8,128)(2,1)S(1)}, u32[]{:S(2)}, u32[]{:S(2)}) async-start(bf16[256,8,128]{2,1,0:T(8,128)(2,1)} %bitcast.10), calls=%async_computation.4 | async-start | bytes 1048576 | tf_op jit(solution)/shard_map/all_to_all | solution.py:308

commit v7 on v6

--- a/solution.py
+++ b/solution.py
@@ -30,7 +30,7 @@
 TILES = 31
 VOC = TILES * LANES
 CHUNK = 256
-CARRY = 4 * 2 * PAIR + LANES
+IDS = 16
 
 
 def lane_gather(table, index):
@@ -50,47 +50,67 @@
     )
 
 
-def turned_spot(index):
-    return ((index & 3) << 5) | (index >> 2)
-
-
-def pack_body(place_ref, lengths, ids, hidden, grad, out_ref, *scratch):
-    held, block, sem, out_sem = scratch[:4], scratch[4], scratch[5], scratch[6]
+def load_spots(got_ref, spots):
+    for m in range(CHIPS):
+        spots[m] = got_ref[m, IDS + 16 :, :].astype(F32).astype(I32)
+
+
+def spot_row(spots, p, tile):
+    return spots[p // 2, pl.ds(2 * tile + p % 2, 1), :]
+
+
+def pack_body(place_ref, lengths, ids, hidden, grad, index, out_ref, *scratch):
+    held, spots, sem = scratch[:5], scratch[5], scratch[6]
     copies = [
         pltpu.make_async_copy(source, target, sem.at[n])
-        for n, (source, target) in enumerate(zip((lengths, ids, hidden, grad), held))
+        for n, (source, target) in enumerate(zip((lengths, ids, hidden, grad, index), held))
     ]
     for copy in copies:
         copy.start()
     for copy in copies:
         copy.wait()
-    lengths_ref, ids_ref, hidden_ref, grad_ref = held
+    lengths_ref, ids_ref, hidden_ref, grad_ref, index_ref = held
     place = place_ref[0]
     swap = place_ref[1] == 1
     limit = lengths_ref[place // (SEQ // ROWS)]
     spot = (place % (SEQ // ROWS)) * ROWS + lax.broadcasted_iota(I32, (ROWS, 1), 0)
-    rows = [hidden_ref[...].astype(F32), jnp.where(spot < limit, grad_ref[...].astype(F32), 0.0)]
-    row = lax.broadcasted_iota(I32, (2, LANES), 0)
-    lane = lax.broadcasted_iota(I32, (2, LANES), 1)
-    digits = jnp.zeros((2, LANES), I32)
+    arrays = [hidden_ref[...].astype(F32), jnp.where(spot < limit, grad_ref[...].astype(F32), 0.0)]
+    row = lax.broadcasted_iota(I32, (16, LANES), 0)
+    lane = lax.broadcasted_iota(I32, (16, LANES), 1)
+    digits = jnp.zeros((16, LANES), I32)
     for r in range(ROWS):
-        for d in range(3):
-            here = (row == r // 4) & (lane == (r % 4) * 8 + d)
-            digits = jnp.where(here, (ids_ref[r] >> (7 * d)) & 127, digits)
-    digits = digits.astype(F32)
+        digits = jnp.where(row == r, ids_ref[r], digits)
+    digits = jnp.where(lane == 0, digits & 127, jnp.where(lane == 1, (digits >> 7) & 127, digits >> 14))
+    digits = jnp.where(lane < 3, digits, 0).astype(F32).astype(BF16)
+    spots[...] = jnp.zeros_like(spots)
+    for tile in range(TILES):
+        spots[2 * tile : 2 * tile + 2, :] = index_ref[:, tile * LANES : (tile + 1) * LANES].astype(F32)
+    positions = spots[...].astype(BF16)
     for m in range(CHIPS):
         parts = []
-        for q in range(4):
-            for array in rows:
-                two = jnp.concatenate(
-                    [array[r : r + 1, m * PAIR : (m + 1) * PAIR] for r in (q, 4 + q)], axis=0
-                )
-                other = jnp.concatenate([two[:, COLS:], two[:, :COLS]], axis=1)
-                parts.append(jnp.where(swap, other, two))
-        block[m] = jnp.concatenate(parts + [digits], axis=1).astype(BF16)
-    copies = [
-        pltpu.make_async_copy(block, out_ref.at[:, s], out_sem.at[s]) for s in range(SHARDS)
-    ]
+        for array in arrays:
+            pair = array[:, m * PAIR : (m + 1) * PAIR]
+            other = jnp.concatenate([pair[:, COLS:], pair[:, :COLS]], axis=1)
+            parts.append(jnp.where(swap, other, pair))
+        out_ref[m, 0:IDS, :] = jnp.concatenate(parts, axis=0).astype(BF16)
+        out_ref[m, IDS : IDS + 16, :] = digits
+        out_ref[m, IDS + 16 :, :] = positions
+
+
+def spread_body(got_ref, out_ref, block, sem):
+    hidden = []
+    cotangents = []
+    digits = []
+    for m in range(CHIPS):
+        rows = got_ref[m, 0:IDS, :].astype(F32)
+        hidden.append(rows[0:ROWS])
+        cotangents.append(rows[ROWS:])
+        digits.append(got_ref[m, IDS : IDS + 16, :].astype(F32)[0:ROWS])
+    block[0:64, :] = jnp.concatenate(hidden, axis=0).astype(BF16)
+    block[64:128, :] = jnp.concatenate(cotangents, axis=0).astype(BF16)
+    digits = jnp.concatenate(digits + [jnp.zeros((64, LANES), F32)], axis=0).T
+    block[128:144, :] = digits[0:16].astype(BF16)
+    copies = [pltpu.make_async_copy(block, out_ref.at[s], sem.at[s]) for s in range(SHARDS)]
     for copy in copies:
         copy.start()
     for copy in copies:
@@ -98,17 +118,21 @@
 
 
 def turn_body(rows_ref, keep_out, send_out):
-    for p in range(OWN):
-        rows = rows_ref[p * 32 : (p + 1) * 32, :].astype(F32)
-        tokens = jnp.concatenate([rows[:, q * CHUNK : (q + 1) * CHUNK] for q in range(4)], axis=0)
-        turned = tokens.T.astype(BF16)
-        digits = rows[:, 4 * CHUNK :].T
-        digits = jnp.concatenate([digits[q * 8 : q * 8 + 8] for q in range(4)], axis=1)
-        digits = jnp.concatenate([digits, jnp.zeros((8, SEQ), F32)], axis=0).astype(BF16)
-        for n, out in enumerate((keep_out, send_out)):
-            out[p, 0:COLS, :] = turned[n * COLS : (n + 1) * COLS]
-            out[p, COLS:PAIR, :] = turned[PAIR + n * COLS : PAIR + (n + 1) * COLS]
-            out[p, PAIR:, :] = digits
+    for two in range(CHIPS // 2):
+        for h in range(2):
+            rows = rows_ref[h * 16 : h * 16 + 16, two * 16 : two * 16 + 16, :].astype(F32)
+            for s in range(2):
+                p = (2 * two + s) * 2 + h
+                turned = rows[:, s * ROWS : (s + 1) * ROWS, :].reshape(SEQ, PAIR).T.astype(BF16)
+                keep_out[p, 0:COLS, :] = turned[:COLS]
+                send_out[p, 0:COLS, :] = turned[COLS:]
+    for pair in range(SHARDS // 2):
+        rows = [rows_ref[2 * pair + s, 64:144, :].astype(F32) for s in range(2)]
+        turned = jnp.concatenate([r[0:64] for r in rows], axis=0).T.astype(BF16)
+        digits = jnp.concatenate([r[64:80, 0:64] for r in rows], axis=1).astype(BF16)
+        for out, part in ((keep_out, turned[:COLS]), (send_out, turned[COLS:])):
+            out[pair, COLS:PAIR, :] = part
+            out[pair, PAIR:, :] = digits
 
 
 def over_terms(step, one_chunk):
@@ -122,14 +146,20 @@
     one_chunk(full * step, VOC - full * step)
 
 
-def logits_body(rows_ref, index_ref, own_ref, other_ref, pooled_ref, out_ref, hidden_ref, embed_ref):
+def logits_body(
+    rows_ref, got_ref, own_ref, other_ref, pooled_ref, out_ref, hidden_ref, embed_ref, spots
+):
     here = lax.broadcasted_iota(I32, (SEQ, 1), 0)
     embed_ref[0:COLS, :] = own_ref[...]
     embed_ref[COLS:, :] = other_ref[...]
-    for p in range(OWN):
-        for q in range(4):
-            at = p * SEQ + q * 32
-            hidden_ref[at : at + 32, :] = rows_ref[p * 32 : p * 32 + 32, q * CHUNK : q * CHUNK + PAIR]
+    load_spots(got_ref, spots)
+    for two in range(CHIPS // 2):
+        for h in range(2):
+            rows = rows_ref[h * 16 : h * 16 + 16, two * 16 : two * 16 + 16, :].astype(F32)
+            for s in range(2):
+                p = (2 * two + s) * 2 + h
+                tokens = rows[:, s * ROWS : (s + 1) * ROWS, :].reshape(SEQ, PAIR)
+                hidden_ref[p * SEQ : (p + 1) * SEQ, :] = tokens.astype(BF16)
 
     def one_chunk(first, width):
         lanes = pl.ds(first, width)
@@ -138,7 +168,9 @@
             scores = jnp.dot(
                 hidden_ref[p * SEQ : (p + 1) * SEQ, :], embed, preferred_element_type=F32
             )
-            index = turned_spot(index_ref[p // 2, p % 2 : p % 2 + 1, lanes])
+            index = jnp.concatenate(
+                [spot_row(spots, p, first // LANES + n) for n in range(width // LANES)], axis=1
+            )
             picked = jnp.sum(jnp.where(index == here, scores, 0.0), axis=0, keepdims=True)
             for at in range(0, width, CHUNK):
                 some = min(CHUNK, width - at)
@@ -175,11 +207,12 @@
 
 
 def hidden_body(
-    place_ref, grad_ref, index_ref, own_ref, other_ref, out_ref, total, left, embed_ref, grads
+    place_ref, grad_ref, got_ref, own_ref, other_ref, out_ref, total, left, embed_ref, grads, spots
 ):
     here = lax.broadcasted_iota(I32, (SEQ, LANES), 0).astype(I16)
     zero = jnp.zeros((), BF16)
     first_core = place_ref[1] == 0
+    load_spots(got_ref, spots)
     embed_ref[0:COLS, :] = own_ref[...]
     embed_ref[COLS:, :] = other_ref[...]
     total[...] = jnp.zeros_like(total)
@@ -193,7 +226,7 @@
             for p in range(group, group + 4):
                 for tile in range(width // LANES):
                     lanes = slice(tile * LANES, (tile + 1) * LANES)
-                    index = index_ref[p // 2, p % 2 : p % 2 + 1, pl.ds(first + tile * LANES, LANES)]
+                    index = spot_row(spots, p, first // LANES + tile)
                     index = jnp.broadcast_to(index, (16, LANES)).astype(I16)
                     value = jnp.broadcast_to(grads[p : p + 1, lanes], (16, LANES)).astype(BF16)
                     index = jnp.concatenate([index] * 8, axis=0)
@@ -249,9 +282,11 @@
 
 
 def embed_body(
-    place_ref, token_ref, grad_ref, own_index, other_index, keep_ref, got_ref, out_ref, bias_ref, grads
+    place_ref, token_ref, grad_ref, own_index, other_index, keep_ref, got_ref, out_ref, bias_ref, grads, own_spots, other_spots
 ):
     first_core = place_ref[1] == 0
+    load_spots(own_index, own_spots)
+    load_spots(other_index, other_spots)
     for g in range(GROUPS):
         both = grad_ref[g].astype(F32)
         grads[g] = jnp.where(first_core, both, jnp.concatenate([both[OWN:], both[:OWN]], axis=0))
@@ -260,9 +295,9 @@
         lanes = pl.ds(pl.multiple_of(tile * LANES, LANES), LANES)
         half = pl.ds(pl.multiple_of((tile % 2) * LANES, LANES), LANES)
         totals = [token_ref[d : d + 16, lanes] for d in range(0, COLS, 16)]
-        for n, (table_ref, index_ref) in enumerate(((keep_ref, own_index), (got_ref, other_index))):
+        for n, (table_ref, spots) in enumerate(((keep_ref, own_spots), (got_ref, other_spots))):
             for p in range(OWN):
-                index = turned_spot(index_ref[p // 2, p % 2 : p % 2 + 1, lanes])
+                index = spot_row(spots, p, tile)
                 index = jnp.broadcast_to(index, (16, LANES)).astype(I16)
                 value = grads[tile // 2, n * OWN + p : n * OWN + p + 1, half]
                 for d in range(COLS // 16):
@@ -316,32 +351,42 @@
     hidden, embed_grad, token_ids, lengths, pool_index, embedding, head_bias, pooled_grad
 ):
     place = jnp.stack([lax.axis_index(name) for name in (SHARD, "core", "zl", "x")]).astype(I32)
-    own_index = exchange(jnp.broadcast_to(pool_index, (CHIPS, 2, VOC)), ("zl", "x"))
-    rows = call(
+    packed = call(
         pack_body,
         "pack",
-        shape((CHIPS, SHARDS, 2, CARRY), BF16),
+        shape((CHIPS, IDS + 80, LANES), BF16),
         [
             pltpu.SMEM((2,), I32),
             pltpu.SMEM((ROWS,), I32),
             pltpu.VMEM((ROWS, WIDTH), BF16),
             pltpu.VMEM((ROWS, WIDTH), BF16),
-            pltpu.VMEM((CHIPS, 2, CARRY), BF16),
-            pltpu.SemaphoreType.DMA((4,)),
-            pltpu.SemaphoreType.DMA((SHARDS,)),
+            pltpu.VMEM((2, VOC), I32),
+            pltpu.VMEM((64, LANES), F32),
+            pltpu.SemaphoreType.DMA((5,)),
         ],
-        [SMEM] + [ANY] * 4,
+        [SMEM] + [ANY] * 5,
+    )(place, lengths, token_ids, hidden, embed_grad, pool_index)
+    own_index = exchange(packed, ("zl", "x"))
+    rows = call(
+        spread_body,
+        "spread",
+        shape((SHARDS, 144, LANES), BF16),
+        [pltpu.VMEM((144, LANES), BF16), pltpu.SemaphoreType.DMA((SHARDS,))],
+        [VMEM],
         out_specs=ANY,
-        us=4,
-    )(place, lengths, token_ids, hidden, embed_grad)
-    rows, own_index = lax.optimization_barrier((rows, own_index))
-    all_rows = exchange(rows.reshape(CHIPS * SHARDS, 2, CARRY), HOME).reshape(-1, CARRY)
+        room=8,
+    )(own_index)
+    all_rows = exchange(rows, SHARD)
     other_embed = swap_over(embedding, "core")
     partial = call(
         logits_body,
         "logits",
         shape((GROUPS, 24, CHUNK), F32),
-        [pltpu.VMEM((OWN * SEQ, PAIR), BF16), pltpu.VMEM((PAIR, VOC), BF16)],
+        [
+            pltpu.VMEM((OWN * SEQ, PAIR), BF16),
+            pltpu.VMEM((PAIR, VOC), BF16),
+            pltpu.VMEM((CHIPS, 64, LANES), I32),
+        ],
         [VMEM] * 5,
         us=6,
     )(all_rows, own_index, embedding, other_embed, pooled_grad)
@@ -384,6 +429,7 @@
             pltpu.VMEM((OWN * SEQ, 1024), BF16),
             pltpu.VMEM((PAIR, VOC), BF16),
             pltpu.VMEM((OWN, 1024), F32),
+            pltpu.VMEM((CHIPS, 64, LANES), I32),
         ],
         [SMEM] + [VMEM] * 4,
         us=6,
@@ -393,7 +439,11 @@
         embed_body,
         "embedding_grad",
         (shape((COLS, VOC), F32), shape((1, VOC), F32)),
-        [pltpu.VMEM((GROUPS, PASSAGES, CHUNK), F32)],
+        [
+            pltpu.VMEM((GROUPS, PASSAGES, CHUNK), F32),
+            pltpu.VMEM((CHIPS, 64, LANES), I32),
+            pltpu.VMEM((CHIPS, 64, LANES), I32),
+        ],
         [SMEM] + [VMEM] * 6,
         us=11,
         room=24,

time: 144 us -> 143 us (level)
  blocking collectives: 0 us -> 12.6 us
  starting transfers between devices: 58.3 us -> 48.8 us
  waiting for transfers between devices: 39.8 us -> 36.5 us
  local copies, waits for them, and re-layouts: 4.35 us -> 1.8 us
    all_to_all x0 -> x1, blocking collectives: none -> 12.6 us  [exchange(): return lax.all_to_all(x, axis, split_axis=0, concat_axis=0, tiled=True)]
    all_to_all x5 -> x4, starting transfers between devices: 49.8 us -> 40.2 us  [exchange(): return lax.all_to_all(x, axis, split_axis=0, concat_axis=0, tiled=True)]
    all_to_all x5 -> x4, waiting for transfers between devices: 39.8 us -> 35 us  [exchange(): return lax.all_to_all(x, axis, split_axis=0, concat_axis=0, tiled=True)]
    pallas_call x1 -> x2, Pallas kernels: 2.91 us -> 4.61 us  [the longest x1 2.33 us: on_device(): call(spread_body, 'spread', shape((SHARDS, 144, LANES), BF16), [pltpu.VME...]
    broadcast_in_dim x1 -> x0, local copies, waits for them, and re-layouts: 1.52 us -> none  [on_device(): jnp.broadcast_to(pool_index, (CHIPS, 2, VOC))]
    ppermute x3, waiting for transfers between devices: 0.01 us -> 1.5 us  [swap_over(): return lax.ppermute(x, axis, [(0, 1), (1, 0)])]
  transfers between devices with their start and end apart: 8 -> 7, of which waited for: 5 -> 5; matrix products, arithmetic and copies ran while one was open for 2% -> 0% of each run, Pallas kernels for 15% -> 13%
where the time goes in v7:
time: 143 us; the launch traced here: 141 us
  starting transfers between devices  48.8 us (34%)
  Pallas kernels  39.6 us (28%)
  waiting for transfers between devices  36.5 us (26%)
  blocking collectives  12.6 us (9%)
  local copies, waits for them, and re-layouts  1.8 us (1%)
    all_to_all x4, starting transfers between devices, exchange(): return lax.all_to_all(x, axis, split_axis=0, concat_axis=0, tiled=True)  40.2 us
    all_to_all x4, waiting for transfers between devices, exchange(): return lax.all_to_all(x, axis, split_axis=0, concat_axis=0, tiled=True)  35 us
    all_to_all x1, blocking collectives, exchange(): return lax.all_to_all(x, axis, split_axis=0, concat_axis=0, tiled=True)  12.6 us
    pallas_call x1, Pallas kernels, on_device(): call(embed_body, 'embedding_grad', (shape((COLS, VOC), F32), shape((1, VO...  11.5 us
    ppermute x3, starting transfers between devices, swap_over(): return lax.ppermute(x, axis, [(0, 1), (1, 0)])  8.59 us
    pallas_call x1, Pallas kernels, on_device(): call(logits_body, 'logits', shape((GROUPS, 24, CHUNK), F32), [pltpu.VMEM(...  7.49 us
    pallas_call x1, Pallas kernels, on_device(): call(hidden_body, 'hidden_grad', shape((OWN * SEQ, PAIR), BF16), [pltpu.V...  7.36 us
    pallas_call x1, Pallas kernels, on_device(): call(token_body, 'token_grad', shape((COLS, 4096), F32), [pltpu.VMEM((512...  3.92 us
  transfers between devices with their start and end apart: 7, of which 5 were waited for; matrix products, arithmetic and copies ran while one was open for 0% of the time, Pallas kernels for 13%

profile of v7, /device:TPU:1, one launch (start us, length us, event | category | flops | bytes accessed | tf_op | source)
XLA Modules:
  0.0 141.4 jit_solution(8350853595877672414)
XLA Ops:
  1.2 2.3 %pack.1 = bf16[8,96,128]{2,1,0:T(8,128)(2,1)} custom-call(s32[4]{0:T(128)} %pad_add_fusion.place_ref, s32[2]{0:T(128)} %lengths.1, s32[8]{0:T(128)} %ids.1, bf16[8,1024]{1,0:T(8,128)(2,1)} %hidden.1, bf16[8,1024]{1,0:T(8,128)(2,1)} %grad.1, s32[2,3968]{1,0:T(2,128)} %index.1), custom_call_target="tpu_custom_call" | custom-call | bytes 3700000 | tf_op jit(solution)/shard_map/pack/pallas_call | solution.py:354
  3.5 12.6 %all_to_all.25.got_ref.own_index = bf16[8,96,128]{2,1,0:T(8,128)(2,1)} all-to-all(bf16[8,96,128]{2,1,0:T(8,128)(2,1)} %pack.1), channel_id=1, replica_groups=mesh['zl'=2,'x'=4,'core'=2,'zh'=4,'y'=8] {'zl','x'}, dimensions={0} | all-to-all | bytes 393216 | tf_op jit(solution)/shard_map/all_to_all | solution.py:343
  16.1 2.3 %spread.1 = bf16[32,144,128]{2,1,0:T(8,128)(2,1)} custom-call(bf16[8,96,128]{2,1,0:T(8,128)(2,1)} %all_to_all.25.got_ref.own_index), custom_call_target="tpu_custom_call" | custom-call | bytes 3700000 | tf_op jit(solution)/shard_map/spread/pallas_call | solution.py:370
  18.4 15.0 %all-to-all-start.1 = ((bf16[32,144,128]{2,1,0:T(8,128)(2,1)}), bf16[32,144,128]{2,1,0:T(8,128)(2,1)S(1)}, u32[]{:S(2)}, u32[]{:S(2)}) async-start(bf16[32,144,128]{2,1,0:T(8,128)(2,1)} %spread.1), calls=%async_computation.1 | async-start | bytes 2359296 | tf_op jit(solution)/shard_map/all_to_all | solution.py:343
  33.5 4.2 %collective-permute-start = (bf16[64,3968]{1,0:T(8,128)(2,1)S(1)}, bf16[64,3968]{1,0:T(8,128)(2,1)S(1)}, u32[]{:S(2)}, u32[]{:S(2)}) collective-permute-start(bf16[64,3968]{1,0:T(8,128)(2,1)S(1)} %copy-done.6), channel_id=1, source_target_pairs={{0,32},{32,0},{1,33},{33,1},{2,34},{34,2},{3,35},{35,3},{4,36},{36... | collective-permute-start | bytes 1523720 | tf_op jit(solution)/shard_map/ppermute | solution.py:347
  37.7 1.5 %collective-permute-done.other_ref = bf16[64,3968]{1,0:T(8,128)(2,1)S(1)} collective-permute-done((bf16[64,3968]{1,0:T(8,128)(2,1)S(1)}, bf16[64,3968]{1,0:T(8,128)(2,1)S(1)}, u32[]{:S(2)}, u32[]{:S(2)}) %collective-permute-start) | collective-permute-done | bytes 507936 | tf_op jit(solution)/shard_map/ppermute | solution.py:347
  39.2 23.8 %all-to-all-done.1.rows_ref = bf16[32,144,128]{2,1,0:T(8,128)(2,1)S(1)} async-done(((bf16[32,144,128]{2,1,0:T(8,128)(2,1)}), bf16[32,144,128]{2,1,0:T(8,128)(2,1)S(1)}, u32[]{:S(2)}, u32[]{:S(2)}) %all-to-all-start.1) | async-done | bytes 1179680 | tf_op jit(solution)/shard_map/all_to_all | solution.py:343
  62.9 1.1 copy-done.5
  64.0 7.5 %logits.1 = f32[16,24,256]{2,1,0:T(8,128)} custom-call(bf16[32,144,128]{2,1,0:T(8,128)(2,1)} %copy-done.5, bf16[8,96,128]{2,1,0:T(8,128)(2,1)} %all_to_all.25.got_ref.own_index, bf16[64,3968]{1,0:T(8,128)(2,1)} %own_ref.3, bf16[64,3968]{1,0:T(8,128)(2,1)} %copy-done.7, f32[2,3968]{1,0:T(2,128)} %pooled_ref.1), custom_call_target="tpu_custom_call" | custom-call | bytes 22200000 | tf_op jit(solution)/shard_map/logits/pallas_call | solution.py:381
  71.5 7.2 %all-to-all-start.2 = ((f32[16,24,256]{2,1,0:T(8,128)}), f32[16,24,256]{2,1,0:T(8,128)S(1)}, u32[]{:S(2)}, u32[]{:S(2)}) async-start(f32[16,24,256]{2,1,0:T(8,128)} %logits.1), calls=%async_computation.2 | async-start | bytes 786432 | tf_op jit(solution)/shard_map/all_to_all | solution.py:343
  78.7 2.7 %turn.1 = (bf16[16,144,128]{2,1,0:T(8,128)(2,1)}, bf16[16,144,128]{2,1,0:T(8,128)(2,1)}) custom-call(bf16[32,144,128]{2,1,0:T(8,128)(2,1)} %copy-done.5), custom_call_target="tpu_custom_call" | custom-call | bytes 11100000 | tf_op jit(solution)/shard_map/turn/pallas_call | solution.py:393
  81.4 2.3 %collective-permute-start.1 = (bf16[16,144,128]{2,1,0:T(8,128)(2,1)}, bf16[16,144,128]{2,1,0:T(8,128)(2,1)S(1)}, u32[]{:S(2)}, u32[]{:S(2)}) collective-permute-start(bf16[16,144,128]{2,1,0:T(8,128)(2,1)} %get-tuple-element.11), channel_id=1, source_target_pairs={{0,32},{32,0},{1,33},{33,1},{2,34},{34,2},{3,35},{35,3},{4,36},{36... | collective-permute-start | bytes 1769480 | tf_op jit(solution)/shard_map/ppermute | solution.py:347
  83.7 3.5 %all-to-all-done.2.part_ref = f32[16,24,256]{2,1,0:T(8,128)S(1)} async-done(((f32[16,24,256]{2,1,0:T(8,128)}), f32[16,24,256]{2,1,0:T(8,128)S(1)}, u32[]{:S(2)}, u32[]{:S(2)}) %all-to-all-start.2) | async-done | bytes 393248 | tf_op jit(solution)/shard_map/all_to_all | solution.py:343
  87.1 0.8 slope.1
  87.9 4.5 %all-to-all-start.3 = ((bf16[16,32,256]{2,1,0:T(8,128)(2,1)}), bf16[16,32,256]{2,1,0:T(8,128)(2,1)S(1)}, u32[]{:S(2)}, u32[]{:S(2)}) async-start(bf16[16,32,256]{2,1,0:T(8,128)(2,1)} %slope.1), calls=%async_computation.3 | async-start | bytes 524288 | tf_op jit(solution)/shard_map/all_to_all | solution.py:343
  92.4 2.1 %collective-permute-start.2 = (bf16[8,96,128]{2,1,0:T(8,128)(2,1)}, bf16[8,96,128]{2,1,0:T(8,128)(2,1)S(1)}, u32[]{:S(2)}, u32[]{:S(2)}) collective-permute-start(bf16[8,96,128]{2,1,0:T(8,128)(2,1)} %all_to_all.25.got_ref.own_index), channel_id=1, source_target_pairs={{0,32},{32,0},{1,33},{33,1},{2,34},{34,2},{3,35},{35,3},{4,36},{36... | collective-permute-start | bytes 589832 | tf_op jit(solution)/shard_map/ppermute | solution.py:347
  94.6 3.9 %token_grad.1.token_ref = f32[64,4096]{1,0:T(8,128)S(1)} custom-call(s32[4]{0:T(128)S(1)} %copy-done.3, bf16[16,144,128]{2,1,0:T(8,128)(2,1)S(1)} %copy-done.2, bf16[16,144,128]{2,1,0:T(8,128)(2,1)S(1)} %collective-permute-done.1.got_ref), custom_call_target="tpu_custom_call" | custom-call | bytes 18500000 | tf_op jit(solution)/shard_map/token_grad/pallas_call | solution.py:409
  98.5 1.1 all-to-all-done.3.grad_ref
  99.7 0.7 copy-done
  100.4 7.4 %hidden_grad.1 = bf16[2048,128]{1,0:T(8,128)(2,1)} custom-call(s32[4]{0:T(128)} %pad_add_fusion.place_ref, bf16[16,32,256]{2,1,0:T(8,128)(2,1)} %copy-done, bf16[8,96,128]{2,1,0:T(8,128)(2,1)} %all_to_all.25.got_ref.own_index, bf16[64,3968]{1,0:T(8,128)(2,1)} %own_ref.3, bf16[64,3968]{1,0:T(8,128)(2,1)} %copy-done.7), custom_call_target="tpu_custom_call" | custom-call | bytes 22200000 | tf_op jit(solution)/shard_map/hidden_grad/pallas_call | solution.py:423
  107.7 13.5 %all-to-all-start.4 = ((bf16[256,8,128]{2,1,0:T(8,128)(2,1)}), bf16[256,8,128]{2,1,0:T(8,128)(2,1)S(1)}, u32[]{:S(2)}, u32[]{:S(2)}) async-start(bf16[256,8,128]{2,1,0:T(8,128)(2,1)} %bitcast.8), calls=%async_computation.4 | async-start | bytes 1048576 | tf_op jit(solution)/shard_map/all_to_all | solution.py:343
  121.3 11.5 %embedding_grad.1 = (f32[64,3968]{1,0:T(8,128)}, f32[1,3968]{1,0:T(1,128)S(1)}) custom-call(s32[4]{0:T(128)S(1)} %copy-done.4, f32[64,4096]{1,0:T(8,128)S(1)} %token_grad.1.token_ref, bf16[16,32,256]{2,1,0:T(8,128)(2,1)S(1)} %copy-done.1, bf16[8,96,128]{2,1,0:T(8,128)(2,1)} %all_to_all.25.got_ref.own_index, ...), custom_call_target="tpu_custom_call" | custom-call | bytes 40700000 | tf_op jit(solution)/shard_map/embedding_grad/pallas_call | solution.py:438
  133.4 6.7 %all-to-all-done.4.part_ref = bf16[256,8,128]{2,1,0:T(8,128)(2,1)S(1)} async-done(((bf16[256,8,128]{2,1,0:T(8,128)(2,1)}), bf16[256,8,128]{2,1,0:T(8,128)(2,1)S(1)}, u32[]{:S(2)}, u32[]{:S(2)}) %all-to-all-start.4) | async-done | bytes 524320 | tf_op jit(solution)/shard_map/all_to_all | solution.py:343
  140.1 1.3 sum_shards.1
  (22 shorter events, 1.3 us)
Async XLA Ops:
  18.4 15.0 %copy-start.6 = (bf16[64,3968]{1,0:T(8,128)(2,1)S(1)}, bf16[64,3968]{1,0:T(8,128)(2,1)}, u32[]{:S(2)}) copy-start(bf16[64,3968]{1,0:T(8,128)(2,1)} %own_ref.3) | copy-start | bytes 1523716
  18.4 44.5 %all-to-all-start.1 = ((bf16[32,144,128]{2,1,0:T(8,128)(2,1)}), bf16[32,144,128]{2,1,0:T(8,128)(2,1)S(1)}, u32[]{:S(2)}, u32[]{:S(2)}) async-start(bf16[32,144,128]{2,1,0:T(8,128)(2,1)} %spread.1), calls=%async_computation.1 | async-start | bytes 2359296 | tf_op jit(solution)/shard_map/all_to_all | solution.py:343
  33.5 45.2 %copy-start.8 = (f32[3968]{0:T(1024)S(1)}, f32[3968]{0:T(1024)}, u32[]{:S(2)}) copy-start(f32[3968]{0:T(1024)} %param.14) | copy-start | bytes 47620
  33.5 5.7 %collective-permute-start = (bf16[64,3968]{1,0:T(8,128)(2,1)S(1)}, bf16[64,3968]{1,0:T(8,128)(2,1)S(1)}, u32[]{:S(2)}, u32[]{:S(2)}) collective-permute-start(bf16[64,3968]{1,0:T(8,128)(2,1)S(1)} %copy-done.6), channel_id=1, source_target_pairs={{0,32},{32,0},{1,33},{33,1},{2,34},{34,2},{3,35},{35,3},{4,36},{36... | collective-permute-start | bytes 1523720 | tf_op jit(solution)/shard_map/ppermute | solution.py:347
  39.2 23.8 %copy-start.7 = (bf16[64,3968]{1,0:T(8,128)(2,1)}, bf16[64,3968]{1,0:T(8,128)(2,1)S(1)}, u32[]{:S(2)}) copy-start(bf16[64,3968]{1,0:T(8,128)(2,1)S(1)} %collective-permute-done.other_ref) | copy-start | bytes 1523716
  62.9 1.1 copy-start.5
  71.5 15.7 %all-to-all-start.2 = ((f32[16,24,256]{2,1,0:T(8,128)}), f32[16,24,256]{2,1,0:T(8,128)S(1)}, u32[]{:S(2)}, u32[]{:S(2)}) async-start(f32[16,24,256]{2,1,0:T(8,128)} %logits.1), calls=%async_computation.2 | async-start | bytes 786432 | tf_op jit(solution)/shard_map/all_to_all | solution.py:343
  78.7 15.9 %copy-start.3 = (s32[4]{0:T(128)S(1)}, s32[4]{0:T(128)}, u32[]{:S(2)}) copy-start(s32[4]{0:T(128)} %pad_add_fusion.place_ref) | copy-start | bytes 52
  81.4 13.2 %copy-start.2 = (bf16[16,144,128]{2,1,0:T(8,128)(2,1)S(1)}, bf16[16,144,128]{2,1,0:T(8,128)(2,1)}, u32[]{:S(2)}) copy-start(bf16[16,144,128]{2,1,0:T(8,128)(2,1)} %get-tuple-element.10.keep_ref) | copy-start | bytes 1769476
  81.4 13.2 %collective-permute-start.1 = (bf16[16,144,128]{2,1,0:T(8,128)(2,1)}, bf16[16,144,128]{2,1,0:T(8,128)(2,1)S(1)}, u32[]{:S(2)}, u32[]{:S(2)}) collective-permute-start(bf16[16,144,128]{2,1,0:T(8,128)(2,1)} %get-tuple-element.11), channel_id=1, source_target_pairs={{0,32},{32,0},{1,33},{33,1},{2,34},{34,2},{3,35},{35,3},{4,36},{36... | collective-permute-start | bytes 1769480 | tf_op jit(solution)/shard_map/ppermute | solution.py:347
  87.9 11.7 %all-to-all-start.3 = ((bf16[16,32,256]{2,1,0:T(8,128)(2,1)}), bf16[16,32,256]{2,1,0:T(8,128)(2,1)S(1)}, u32[]{:S(2)}, u32[]{:S(2)}) async-start(bf16[16,32,256]{2,1,0:T(8,128)(2,1)} %slope.1), calls=%async_computation.3 | async-start | bytes 524288 | tf_op jit(solution)/shard_map/all_to_all | solution.py:343
  92.4 6.1 %collective-permute-start.2 = (bf16[8,96,128]{2,1,0:T(8,128)(2,1)}, bf16[8,96,128]{2,1,0:T(8,128)(2,1)S(1)}, u32[]{:S(2)}, u32[]{:S(2)}) collective-permute-start(bf16[8,96,128]{2,1,0:T(8,128)(2,1)} %all_to_all.25.got_ref.own_index), channel_id=1, source_target_pairs={{0,32},{32,0},{1,33},{33,1},{2,34},{34,2},{3,35},{35,3},{4,36},{36... | collective-permute-start | bytes 589832 | tf_op jit(solution)/shard_map/ppermute | solution.py:347
  98.5 22.7 %copy-start.4 = (s32[4]{0:T(128)S(1)}, s32[4]{0:T(128)}, u32[]{:S(2)}) copy-start(s32[4]{0:T(128)} %pad_add_fusion.place_ref) | copy-start | bytes 52
  99.7 0.7 copy-start
  107.7 13.5 %copy-start.1 = (bf16[16,32,256]{2,1,0:T(8,128)(2,1)S(1)}, bf16[16,32,256]{2,1,0:T(8,128)(2,1)}, u32[]{:S(2)}) copy-start(bf16[16,32,256]{2,1,0:T(8,128)(2,1)} %copy-done) | copy-start | bytes 786436
  107.7 32.4 %all-to-all-start.4 = ((bf16[256,8,128]{2,1,0:T(8,128)(2,1)}), bf16[256,8,128]{2,1,0:T(8,128)(2,1)S(1)}, u32[]{:S(2)}, u32[]{:S(2)}) async-start(bf16[256,8,128]{2,1,0:T(8,128)(2,1)} %bitcast.8), calls=%async_computation.4 | async-start | bytes 1048576 | tf_op jit(solution)/shard_map/all_to_all | solution.py:343

commit v8 on v7

v8 whole, which is shorter than its diff:
```python
import jax
import jax.numpy as jnp
from jax import lax
from jax.experimental import pallas as pl
from jax.experimental.pallas import tpu as pltpu
from jax.sharding import Mesh, PartitionSpec as P

F32 = jnp.float32
BF16 = jnp.bfloat16
I16 = jnp.int16
I32 = jnp.int32
LANES = 128
SMEM = pl.BlockSpec(memory_space=pltpu.SMEM)
VMEM = pl.BlockSpec(memory_space=pltpu.VMEM)
ANY = pl.BlockSpec(memory_space=pl.ANY)

GROUP = ("zl", "xh", "xl", "core")
FAR = ("zl", "xh")
NEAR = ("xl", "core")
SHARD = ("zh", "y")
GROUPS = 16
SHARDS = 32
QUADS = 4
SEQ = 128
PASSAGES = 32
OWN = 8
COLS = 64
PAIR = 128
QUAD = 256
WIDTH = 4 * QUAD
ROWS = 8
TILES = 31
VOC = TILES * LANES
CHUNK = 256
TOKENS = 32
SPOTS = 48
CARRY = SPOTS + 64


def lane_gather(table, index):
    numbers = lax.GatherDimensionNumbers(
        offset_dims=(),
        collapsed_slice_dims=(1,),
        start_index_map=(1,),
        operand_batching_dims=(0,),
        start_indices_batching_dims=(0,),
    )
    return lax.gather(
        table,
        index[..., None],
        numbers,
        (1, 1),
        mode=lax.GatherScatterMode.PROMISE_IN_BOUNDS,
    )


def load_spots(got_ref, spots):
    for a in range(QUADS):
        spots[a] = got_ref[a, SPOTS:, :].astype(F32).astype(I32)


def spot_row(spots, p, tile):
    return spots[p // 2, pl.ds(2 * tile + p % 2, 1), :]


def by_distance(place_ref, x, axis, unit):
    place = place_ref[1]
    blocks = [lax.slice_in_dim(x, n * unit, (n + 1) * unit, axis=axis) for n in range(4)]
    blocks = [jnp.where(place % 2 == 1, blocks[n ^ 1], blocks[n]) for n in range(4)]
    blocks = [jnp.where(place // 2 == 1, blocks[n ^ 2], blocks[n]) for n in range(4)]
    return jnp.concatenate(blocks, axis=axis)


def pack_body(place_ref, lengths, ids, hidden, grad, index, out_ref, *scratch):
    held, spots, sem = scratch[:5], scratch[5], scratch[6]
    copies = [
        pltpu.make_async_copy(source, target, sem.at[n])
        for n, (source, target) in enumerate(zip((lengths, ids, hidden, grad, index), held))
    ]
    for copy in copies:
        copy.start()
    for copy in copies:
        copy.wait()
    lengths_ref, ids_ref, hidden_ref, grad_ref, index_ref = held
    place = place_ref[0]
    limit = lengths_ref[place // (SEQ // ROWS)]
    spot = (place % (SEQ // ROWS)) * ROWS + lax.broadcasted_iota(I32, (ROWS, 1), 0)
    arrays = [hidden_ref[...].astype(F32), jnp.where(spot < limit, grad_ref[...].astype(F32), 0.0)]
    row = lax.broadcasted_iota(I32, (16, LANES), 0)
    lane = lax.broadcasted_iota(I32, (16, LANES), 1)
    digits = jnp.zeros((16, LANES), I32)
    for r in range(ROWS):
        digits = jnp.where(row == r, ids_ref[r], digits)
    digits = jnp.where(lane == 0, digits & 127, jnp.where(lane == 1, (digits >> 7) & 127, digits >> 14))
    digits = jnp.where(lane < 3, digits, 0).astype(F32).astype(BF16)
    spots[...] = jnp.zeros_like(spots)
    for tile in range(TILES):
        spots[2 * tile : 2 * tile + 2, :] = index_ref[:, tile * LANES : (tile + 1) * LANES].astype(F32)
    positions = spots[...].astype(BF16)
    for a in range(QUADS):
        parts = []
        for array in arrays:
            quad = by_distance(place_ref, array[:, a * QUAD : (a + 1) * QUAD], 1, COLS)
            parts += [quad[:, 0:PAIR], quad[:, PAIR:]]
        out_ref[a, 0:TOKENS, :] = jnp.concatenate(parts, axis=0).astype(BF16)
        out_ref[a, TOKENS:SPOTS, :] = digits
        out_ref[a, SPOTS:, :] = positions


def spread_body(got_ref, out_ref, block, sem):
    quads = [got_ref[a, 0:TOKENS, :].astype(F32) for a in range(QUADS)]
    for n in range(4):
        rows = jnp.concatenate([q[n * ROWS : (n + 1) * ROWS] for q in quads], axis=0)
        block[n * 32 : (n + 1) * 32, :] = rows.astype(BF16)
    digits = [got_ref[a, TOKENS:SPOTS, :].astype(F32)[0:ROWS] for a in range(QUADS)]
    digits = jnp.concatenate(digits + [jnp.zeros((96, LANES), F32)], axis=0).T
    block[128:144, :] = digits[0:16].astype(BF16)
    copies = [pltpu.make_async_copy(block, out_ref.at[s], sem.at[s]) for s in range(SHARDS)]
    for copy in copies:
        copy.start()
    for copy in copies:
        copy.wait()


def token_tiles(rows_ref, half):
    tiles = {}
    for two in range(QUADS // 2):
        for h in range(2):
            at = half * 32 + two * 16
            rows = rows_ref[h * 16 : h * 16 + 16, at : at + 16, :].astype(F32)
            for s in range(2):
                p = (2 * two + s) * 2 + h
                tiles[p] = rows[:, s * ROWS : (s + 1) * ROWS, :].reshape(SEQ, PAIR)
    return tiles


def turn_body(rows_ref, *outs):
    for half in range(2):
        for p, tokens in token_tiles(rows_ref, half).items():
            turned = tokens.T.astype(BF16)
            outs[2 * half][p, 0:COLS, :] = turned[:COLS]
            outs[2 * half + 1][p, 0:COLS, :] = turned[COLS:]
    for four in range(SHARDS // 4):
        rows = [rows_ref[4 * four + s, 64:144, :].astype(F32) for s in range(4)]
        digits = jnp.concatenate([r[64:80, 0:32] for r in rows], axis=1).astype(BF16)
        for half in range(2):
            turned = jnp.concatenate([r[half * 32 : half * 32 + 32] for r in rows], axis=0).T.astype(BF16)
            outs[2 * half][four, COLS:PAIR, :] = turned[:COLS]
            outs[2 * half + 1][four, COLS:PAIR, :] = turned[COLS:]
        for out in outs:
            out[four, PAIR:, :] = digits


def load_embedding(embed_ref, embed_0, embed_1, embed_23):
    embed_ref[0:COLS, :] = embed_0[...]
    embed_ref[COLS:PAIR, :] = embed_1[...]
    embed_ref[PAIR : PAIR + COLS, :] = embed_23[0]
    embed_ref[PAIR + COLS :, :] = embed_23[1]


def over_terms(step, one_chunk):
    full = VOC // step

    def loop(i, carry):
        one_chunk(pl.multiple_of(i * step, step), step)
        return carry

    lax.fori_loop(0, full, loop, 0)
    one_chunk(full * step, VOC - full * step)


def logits_body(
    rows_ref, got_ref, embed_0, embed_1, embed_23, pooled_ref, out_ref, hidden_ref, embed_ref, spots
):
    here = lax.broadcasted_iota(I32, (SEQ, 1), 0)
    load_embedding(embed_ref, embed_0, embed_1, embed_23)
    load_spots(got_ref, spots)
    for half in range(2):
        for p, tokens in token_tiles(rows_ref, half).items():
            hidden_ref[p * SEQ : (p + 1) * SEQ, half * PAIR : (half + 1) * PAIR] = tokens.astype(BF16)

    def one_chunk(first, width):
        lanes = pl.ds(first, width)
        embed = embed_ref[:, lanes]
        for p in range(OWN):
            scores = jnp.dot(
                hidden_ref[p * SEQ : (p + 1) * SEQ, :], embed, preferred_element_type=F32
            )
            index = jnp.concatenate(
                [spot_row(spots, p, first // LANES + n) for n in range(width // LANES)], axis=1
            )
            picked = jnp.sum(jnp.where(index == here, scores, 0.0), axis=0, keepdims=True)
            for at in range(0, width, CHUNK):
                some = min(CHUNK, width - at)
                out_ref[first // CHUNK + at // CHUNK, p : p + 1, 0:some] = picked[:, at : at + some]
        for at in range(0, width, CHUNK):
            some = min(CHUNK, width - at)
            upstream = pooled_ref[:, pl.ds(first + at, some)]
            out_ref[first // CHUNK + at // CHUNK, OWN : OWN + 2, 0:some] = upstream

    over_terms(1024, one_chunk)
    out_ref[:, OWN + 2 :, :] = jnp.zeros((GROUPS, 6, CHUNK), F32)
    out_ref[GROUPS - 1, :, LANES:] = jnp.zeros((16, CHUNK - LANES), F32)


def slope_body(part_ref, bias_ref, out_ref):
    logits = []
    upstream = []
    for b in range(4):
        total = part_ref[b, 0:OWN, :]
        for a in range(1, QUADS):
            total = total + part_ref[4 * a + b, 0:OWN, :]
        logits.append(total)
        upstream += [part_ref[4 * a + b, OWN : OWN + 2, :] for a in range(QUADS)]
    logits = jnp.concatenate(logits, axis=0) + bias_ref[...]
    upstream = jnp.concatenate(upstream, axis=0)
    softened = jnp.maximum(logits, 0.0) + jnp.log1p(jnp.exp(-jnp.abs(logits)))
    pooled = jnp.log1p(softened)
    sigmoid = 1.0 / (1.0 + jnp.exp(-logits))
    slope = sigmoid / (1.0 + softened)
    mean_pooled = jnp.sum(pooled, axis=0, keepdims=True) / PASSAGES
    grad = ((upstream + mean_pooled) * slope).astype(BF16)
    for g in range(GROUPS):
        out_ref[g] = grad


def hidden_body(
    place_ref, grad_ref, got_ref, embed_0, embed_1, embed_23, out_ref, total, left, embed_ref, grads, spots
):
    here = lax.broadcasted_iota(I32, (SEQ, LANES), 0).astype(I16)
    zero = jnp.zeros((), BF16)
    load_spots(got_ref, spots)
    load_embedding(embed_ref, embed_0, embed_1, embed_23)
    total[...] = jnp.zeros_like(total)

    def one_chunk(first, width):
        for at in range(0, width, CHUNK):
            every = grad_ref[first // CHUNK + at // CHUNK].astype(F32)
            grads[:, at : at + CHUNK] = by_distance(place_ref, every, 0, OWN)[0:OWN]
        embed = embed_ref[:, pl.ds(first, width)]
        for group in range(0, OWN, 4):
            for p in range(group, group + 4):
                for tile in range(width // LANES):
                    lanes = slice(tile * LANES, (tile + 1) * LANES)
                    index = spot_row(spots, p, first // LANES + tile)
                    index = jnp.broadcast_to(index, (16, LANES)).astype(I16)
                    value = jnp.broadcast_to(grads[p : p + 1, lanes], (16, LANES)).astype(BF16)
                    index = jnp.concatenate([index] * 8, axis=0)
                    value = jnp.concatenate([value] * 8, axis=0)
                    left[p * SEQ : (p + 1) * SEQ, lanes] = jnp.where(index == here, value, zero)
            rows = slice(group * SEQ, (group + 4) * SEQ)
            total[rows, :] += lax.dot_general(
                left[rows, 0:width], embed, (((1,), (1,)), ((), ())), preferred_element_type=F32
            )

    over_terms(1024, one_chunk)
    out_ref[...] = total[...].astype(BF16)


def token_body(place_ref, table_0, table_1, table_2, table_3, out_ref, left, right, total):
    base = place_ref[0] * VOC
    low_row = lax.broadcasted_iota(I32, (512, LANES), 0).astype(I16)
    zero = jnp.zeros((), BF16)
    one = jnp.ones((), BF16)
    total[...] = jnp.zeros_like(total)

    def token_block(table_ref):
        for p in range(OWN):
            digits = table_ref[p, PAIR:, :].astype(F32).astype(I32)
            local = (digits[2:3] << 14) + (digits[1:2] << 7) + digits[0:1] - base
            inside = (local >= 0) & (local < VOC)
            high = jnp.where(inside, local >> 9, 15)
            high = jnp.broadcast_to(high, (16, LANES)).astype(I16)
            low = jnp.broadcast_to(local & 511, (16, LANES)).astype(I16)
            high = jnp.concatenate([high] * 4, axis=0)
            low = jnp.concatenate([low] * 32, axis=0)
            cotangents = table_ref[p, COLS:PAIR, :]
            lanes = slice(p * LANES, (p + 1) * LANES)
            for h in range(8):
                left[h * COLS : (h + 1) * COLS, lanes] = jnp.where(
                    high == jnp.int16(h), cotangents, zero
                )
            right[:, lanes] = jnp.where(low_row == low, one, zero)
        total[...] += lax.dot_general(
            left[...], right[...], (((1,), (1,)), ((), ())), preferred_element_type=F32
        )

    for table_ref in (table_0, table_1, table_2, table_3):
        token_block(table_ref)
    for h in range(8):
        out_ref[:, h * 512 : (h + 1) * 512] = total[h * COLS : (h + 1) * COLS, :]


def embed_body(place_ref, token_ref, grad_ref, *refs):
    indices, tables = refs[0:4], refs[4:8]
    out_ref, bias_ref, grads = refs[8:11]
    spots = refs[11:15]
    for n in range(4):
        load_spots(indices[n], spots[n])
    for g in range(GROUPS):
        grads[g] = by_distance(place_ref, grad_ref[g].astype(F32), 0, OWN)

    def one_tile(tile, carry):
        lanes = pl.ds(pl.multiple_of(tile * LANES, LANES), LANES)
        half = pl.ds(pl.multiple_of((tile % 2) * LANES, LANES), LANES)
        totals = [token_ref[d : d + 16, lanes] for d in range(0, COLS, 16)]
        for n in range(4):
            for p in range(OWN):
                index = spot_row(spots[n], p, tile)
                index = jnp.broadcast_to(index, (16, LANES)).astype(I16)
                value = grads[tile // 2, n * OWN + p : n * OWN + p + 1, half]
                for d in range(COLS // 16):
                    picked = lane_gather(tables[n][p, d * 16 : d * 16 + 16, :], index).astype(F32)
                    totals[d] = totals[d] + picked * value
        for d in range(COLS // 16):
            out_ref[d * 16 : d * 16 + 16, lanes] = totals[d]
        bias_ref[:, lanes] = jnp.sum(grads[tile // 2, :, half], axis=0, keepdims=True)
        return carry

    lax.fori_loop(0, TILES, one_tile, 0)


def sum_body(place_ref, part_ref, out_ref):
    for a in range(QUADS):
        total = part_ref[a * SHARDS].astype(F32)
        for s in range(1, SHARDS):
            total = total + part_ref[a * SHARDS + s].astype(F32)
        out_ref[:, a * QUAD : (a + 1) * QUAD] = by_distance(place_ref, total, 1, COLS).astype(BF16)


def call(body, name, out, scratch=(), specs=None, us=1, out_specs=None, room=56):
    extra = {} if out_specs is None else {"out_specs": out_specs}
    return pl.pallas_call(
        body,
        out_shape=out,
        in_specs=specs,
        scratch_shapes=scratch,
        compiler_params=pltpu.CompilerParams(vmem_limit_bytes=room * 1024 * 1024),
        cost_estimate=pl.CostEstimate(flops=0, bytes_accessed=3_700_000 * us, transcendentals=0),
        name=name,
        **extra,
    )


def shape(dims, dtype):
    return jax.ShapeDtypeStruct(dims, dtype)


def exchange(x, axis):
    return lax.all_to_all(x, axis, split_axis=0, concat_axis=0, tiled=True)


def from_near(x, n):
    return lax.ppermute(x, NEAR, [(b, b ^ n) for b in range(4)])


def on_device(
    hidden, embed_grad, token_ids, lengths, pool_index, embedding, head_bias, pooled_grad
):
    place = jnp.stack([lax.axis_index(SHARD), lax.axis_index(NEAR)]).astype(I32)
    packed = call(
        pack_body,
        "pack",
        shape((QUADS, CARRY, LANES), BF16),
        [
            pltpu.SMEM((2,), I32),
            pltpu.SMEM((ROWS,), I32),
            pltpu.VMEM((ROWS, WIDTH), BF16),
            pltpu.VMEM((ROWS, WIDTH), BF16),
            pltpu.VMEM((2, VOC), I32),
            pltpu.VMEM((64, LANES), F32),
            pltpu.SemaphoreType.DMA((5,)),
        ],
        [SMEM] + [ANY] * 5,
    )(place, lengths, token_ids, hidden, embed_grad, pool_index)
    got = exchange(packed, FAR)
    rows = call(
        spread_body,
        "spread",
        shape((SHARDS, 144, LANES), BF16),
        [pltpu.VMEM((144, LANES), BF16), pltpu.SemaphoreType.DMA((SHARDS,))],
        [VMEM],
        out_specs=ANY,
        room=8,
    )(got)
    all_rows = exchange(rows, SHARD)
    embed_1 = from_near(embedding, 1)
    embed_23 = from_near(jnp.stack([embedding, embed_1]), 2)
    spots = [got] + [from_near(got, n) for n in range(1, 4)]
    all_rows, embed_1, embed_23, *spots = lax.optimization_barrier((all_rows, embed_1, embed_23, *spots))
    embed = (embedding, embed_1, embed_23)
    partial = call(
        logits_body,
        "logits",
        shape((GROUPS, 16, CHUNK), F32),
        [
            pltpu.VMEM((OWN * SEQ, QUAD), BF16),
            pltpu.VMEM((QUAD, VOC), BF16),
            pltpu.VMEM((QUADS, 64, LANES), I32),
        ],
        [VMEM] * 6,
        us=5,
    )(all_rows, spots[0], *embed, pooled_grad)
    tables = call(
        turn_body,
        "turn",
        (shape((OWN, PAIR + 16, SEQ), BF16),) * 4,
        specs=[VMEM],
        us=3,
    )(all_rows)
    tables = [tables[0]] + [from_near(tables[n], n) for n in range(1, 4)]
    parts = exchange(partial, GROUP)
    bias = jnp.pad(head_bias, (0, GROUPS * CHUNK - VOC)).reshape(GROUPS, 1, CHUNK)
    bias = lax.dynamic_index_in_dim(bias, lax.axis_index(GROUP), 0, keepdims=False)
    grad_block = call(
        slope_body, "slope", shape((GROUPS, PASSAGES, CHUNK), BF16), specs=[VMEM, VMEM], room=8
    )(parts, bias)
    all_grad = exchange(grad_block, GROUP)
    token_grad = call(
        token_body,
        "token_grad",
        shape((COLS, 4096), F32),
        [
            pltpu.VMEM((512, 1024), BF16),
            pltpu.VMEM((512, 1024), BF16),
            pltpu.VMEM((512, 512), F32),
        ],
        [SMEM] + [VMEM] * 4,
        us=5,
        room=24,
    )(place, *tables)
    all_grad, token_grad = lax.optimization_barrier((all_grad, token_grad))
    hidden_parts = call(
        hidden_body,
        "hidden_grad",
        shape((OWN * SEQ, QUAD), BF16),
        [
            pltpu.VMEM((OWN * SEQ, QUAD), F32),
            pltpu.VMEM((OWN * SEQ, 1024), BF16),
            pltpu.VMEM((QUAD, VOC), BF16),
            pltpu.VMEM((OWN, 1024), F32),
            pltpu.VMEM((QUADS, 64, LANES), I32),
        ],
        [SMEM] + [VMEM] * 5,
        us=5,
    )(place, all_grad, spots[0], *embed)
    hidden_got = exchange(hidden_parts.reshape(QUADS * SHARDS, ROWS, QUAD), FAR + SHARD)
    embedding_grad, bias_grad = call(
        embed_body,
        "embedding_grad",
        (shape((COLS, VOC), F32), shape((1, VOC), F32)),
        [pltpu.VMEM((GROUPS, PASSAGES, CHUNK), F32)] + [pltpu.VMEM((QUADS, 64, LANES), I32)] * 4,
        [SMEM] + [VMEM] * 10,
        us=11,
        room=24,
    )(place, token_grad, all_grad, *spots, *tables)
    hidden_grad = call(
        sum_body, "sum_shards", shape((ROWS, WIDTH), BF16), specs=[SMEM, VMEM], room=8
    )(place, hidden_got)
    return hidden_grad, embedding_grad, bias_grad.reshape(VOC)


def solution(mesh):
    fine = Mesh(mesh.devices.reshape(2, 2, 2, 2, 4, 8), GROUP + SHARD)
    every = P(GROUP + SHARD, None)
    split = P(GROUP, SHARD)
    return jax.shard_map(
        on_device,
        mesh=fine,
        in_specs=(every, every, P(GROUP + SHARD), P(GROUP), split, split, P(SHARD), split),
        out_specs=(every, split, P(SHARD)),
        check_vma=False,
    )
```

time: 143 us -> 165 us (1.15)
  starting transfers between devices: 48.8 us -> 62.8 us
  waiting for transfers between devices: 36.5 us -> 48.8 us
  Pallas kernels: 39.6 us -> 35.1 us
    ppermute x3 -> x8, waiting for transfers between devices: 1.5 us -> 33.3 us  [from_near(): return lax.ppermute(x, NEAR, [(b, b ^ n) for b in range(4)])]
    all_to_all x4, waiting for transfers between devices: 35 us -> 15.5 us  [exchange(): return lax.all_to_all(x, axis, split_axis=0, concat_axis=0, tiled=True)]
    ppermute x3 -> x8, starting transfers between devices: 8.59 us -> 22.4 us  [from_near(): return lax.ppermute(x, NEAR, [(b, b ^ n) for b in range(4)])]
    pallas_call x4, Pallas kernels: 19.8 us -> 16.8 us  [the longest x1 5.93 us: on_device(): call(logits_body, 'logits', shape((GROUPS, 16, CHUNK), F32), [pltpu.VMEM(...]
  transfers between devices with their start and end apart: 7 -> 12, of which waited for: 5 -> 7; matrix products, arithmetic and copies ran while one was open for 0% -> 0% of each run, Pallas kernels for 13% -> 11%
where the time goes in v8:
time: 165 us; the launch traced here: 164 us
  starting transfers between devices  62.8 us (38%)
  waiting for transfers between devices  48.8 us (30%)
  Pallas kernels  35.1 us (21%)
  blocking collectives  12 us (7%)
  local copies, waits for them, and re-layouts  2.75 us (2%)
    all_to_all x4, starting transfers between devices, exchange(): return lax.all_to_all(x, axis, split_axis=0, concat_axis=0, tiled=True)  40.4 us
    ppermute x8, waiting for transfers between devices, from_near(): return lax.ppermute(x, NEAR, [(b, b ^ n) for b in range(4)])  33.3 us
    ppermute x8, starting transfers between devices, from_near(): return lax.ppermute(x, NEAR, [(b, b ^ n) for b in range(4)])  22.4 us
    all_to_all x4, waiting for transfers between devices, exchange(): return lax.all_to_all(x, axis, split_axis=0, concat_axis=0, tiled=True)  15.5 us
    all_to_all x1, blocking collectives, exchange(): return lax.all_to_all(x, axis, split_axis=0, concat_axis=0, tiled=True)  12 us
    pallas_call x1, Pallas kernels, on_device(): call(embed_body, 'embedding_grad', (shape((COLS, VOC), F32), shape((1, VO...  11.1 us
    pallas_call x1, Pallas kernels, on_device(): call(logits_body, 'logits', shape((GROUPS, 16, CHUNK), F32), [pltpu.VMEM(...  5.93 us
    pallas_call x1, Pallas kernels, on_device(): call(hidden_body, 'hidden_grad', shape((OWN * SEQ, QUAD), BF16), [pltpu.V...  5.85 us
  transfers between devices with their start and end apart: 12, of which 7 were waited for; matrix products, arithmetic and copies ran while one was open for 0% of the time, Pallas kernels for 11%

profile of v8, /device:TPU:1, one launch (start us, length us, event | category | flops | bytes accessed | tf_op | source)
XLA Modules:
  0.0 163.7 jit_solution(10539021283055027170)
XLA Ops:
  1.3 2.3 %pack.1 = bf16[4,112,128]{2,1,0:T(8,128)(2,1)} custom-call(s32[2]{0:T(128)} %pad_add_fusion.place_ref, s32[2]{0:T(128)} %lengths.1, s32[8]{0:T(128)} %ids.1, bf16[8,1024]{1,0:T(8,128)(2,1)} %hidden.1, bf16[8,1024]{1,0:T(8,128)(2,1)} %grad.1, s32[2,3968]{1,0:T(2,128)} %index.1), custom_call_target="tpu_custom_call" | custom-call | bytes 3700000 | tf_op jit(solution)/shard_map/pack/pallas_call | solution.py:361
  3.6 12.0 %all_to_all.25.got_ref.refs_0_ = bf16[4,112,128]{2,1,0:T(8,128)(2,1)S(1)} all-to-all(bf16[4,112,128]{2,1,0:T(8,128)(2,1)} %pack.1), channel_id=1, replica_groups=mesh['zl'=2,'xh'=2,'xl'=2,'core'=2,'zh'=4,'y'=8] {'zl','xh'}, dimensions={0} | all-to-all | bytes 229376 | tf_op jit(solution)/shard_map/all_to_all | solution.py:350
  17.0 14.9 %all-to-all-start.1 = ((bf16[32,144,128]{2,1,0:T(8,128)(2,1)}), bf16[32,144,128]{2,1,0:T(8,128)(2,1)S(1)}, u32[]{:S(2)}, u32[]{:S(2)}) async-start(bf16[32,144,128]{2,1,0:T(8,128)(2,1)} %spread.1), calls=%async_computation.1 | async-start | bytes 2359296 | tf_op jit(solution)/shard_map/all_to_all | solution.py:350
  31.9 4.3 %collective-permute-start = (bf16[64,3968]{1,0:T(8,128)(2,1)S(1)}, bf16[64,3968]{1,0:T(8,128)(2,1)S(1)}, u32[]{:S(2)}, u32[]{:S(2)}) collective-permute-start(bf16[64,3968]{1,0:T(8,128)(2,1)S(1)} %copy-done.9), channel_id=1, source_target_pairs={{0,32},{32,0},{64,96},{96,64},{1,33},{33,1},{65,97},{97,65},{2,34}... | collective-permute-start | bytes 1523720 | tf_op jit(solution)/shard_map/ppermute | solution.py:354
  37.8 2.4 %collective-permute-start.1 = (bf16[2,64,3968]{2,1,0:T(8,128)(2,1)S(1)}, bf16[2,64,3968]{2,1,0:T(8,128)(2,1)}, u32[]{:S(2)}, u32[]{:S(2)}) collective-permute-start(bf16[2,64,3968]{2,1,0:T(8,128)(2,1)S(1)} %pad_maximum_fusion), channel_id=1, source_target_pairs={{0,64},{32,96},{64,0},{96,32},{1,65},{33,97},{65,1},{97,33},{2,66}... | collective-permute-start | bytes 3047432 | tf_op jit(solution)/shard_map/ppermute | solution.py:354
  40.2 3.6 %collective-permute-start.4 = (bf16[4,112,128]{2,1,0:T(8,128)(2,1)S(1)}, bf16[4,112,128]{2,1,0:T(8,128)(2,1)S(1)}, u32[]{:S(2)}, u32[]{:S(2)}) collective-permute-start(bf16[4,112,128]{2,1,0:T(8,128)(2,1)S(1)} %all_to_all.25.got_ref.refs_0_), channel_id=1, source_target_pairs={{0,96},{32,64},{64,32},{96,0},{1,97},{33,65},{65,33},{97,1},{2,98}... | collective-permute-start | bytes 344072 | tf_op jit(solution)/shard_map/ppermute | solution.py:354
  43.8 2.2 %collective-permute-start.3 = (bf16[4,112,128]{2,1,0:T(8,128)(2,1)S(1)}, bf16[4,112,128]{2,1,0:T(8,128)(2,1)S(1)}, u32[]{:S(2)}, u32[]{:S(2)}) collective-permute-start(bf16[4,112,128]{2,1,0:T(8,128)(2,1)S(1)} %all_to_all.25.got_ref.refs_0_), channel_id=1, source_target_pairs={{0,64},{32,96},{64,0},{96,32},{1,65},{33,97},{65,1},{97,33},{2,66}... | collective-permute-start | bytes 344072 | tf_op jit(solution)/shard_map/ppermute | solution.py:354
  46.1 2.0 %collective-permute-start.2 = (bf16[4,112,128]{2,1,0:T(8,128)(2,1)S(1)}, bf16[4,112,128]{2,1,0:T(8,128)(2,1)S(1)}, u32[]{:S(2)}, u32[]{:S(2)}) collective-permute-start(bf16[4,112,128]{2,1,0:T(8,128)(2,1)S(1)} %all_to_all.25.got_ref.refs_0_), channel_id=1, source_target_pairs={{0,32},{32,0},{64,96},{96,64},{1,33},{33,1},{65,97},{97,65},{2,34}... | collective-permute-start | bytes 344072 | tf_op jit(solution)/shard_map/ppermute | solution.py:354
  48.1 19.2 %collective-permute-done.4.refs_3_ = bf16[4,112,128]{2,1,0:T(8,128)(2,1)S(1)} collective-permute-done((bf16[4,112,128]{2,1,0:T(8,128)(2,1)S(1)}, bf16[4,112,128]{2,1,0:T(8,128)(2,1)S(1)}, u32[]{:S(2)}, u32[]{:S(2)}) %collective-permute-start.4) | collective-permute-done | bytes 114720 | tf_op jit(solution)/shard_map/ppermute | solution.py:354
  69.5 5.9 %logits.1 = f32[16,16,256]{2,1,0:T(8,128)} custom-call(bf16[32,144,128]{2,1,0:T(8,128)(2,1)} %copy-done.8, bf16[4,112,128]{2,1,0:T(8,128)(2,1)} %copy-done, bf16[64,3968]{1,0:T(8,128)(2,1)} %embed_0.3, bf16[64,3968]{1,0:T(8,128)(2,1)} %copy-done.10, bf16[2,64,3968]{2,1,0:T(8,128)(2,1)} %collective-permute-done.1.embed_23, f32[2,3968]{1,0:T(2,128)} %pooled_ref.1), custom_call_target="tpu_custom_call" | custom-call | bytes 18500000 | tf_op jit(solution)/shard_map/logits/pallas_call | solution.py:392
  75.5 4.5 %all-to-all-start.2 = ((f32[16,16,256]{2,1,0:T(8,128)}), f32[16,16,256]{2,1,0:T(8,128)S(1)}, u32[]{:S(2)}, u32[]{:S(2)}) async-start(f32[16,16,256]{2,1,0:T(8,128)} %logits.1), calls=%async_computation.2 | async-start | bytes 524288 | tf_op jit(solution)/shard_map/all_to_all | solution.py:350
  80.0 7.2 %all-to-all-done.2.part_ref = f32[16,16,256]{2,1,0:T(8,128)S(1)} async-done(((f32[16,16,256]{2,1,0:T(8,128)}), f32[16,16,256]{2,1,0:T(8,128)S(1)}, u32[]{:S(2)}, u32[]{:S(2)}) %all-to-all-start.2) | async-done | bytes 262176 | tf_op jit(solution)/shard_map/all_to_all | solution.py:350
  88.0 4.3 %all-to-all-start.3 = ((bf16[16,32,256]{2,1,0:T(8,128)(2,1)}), bf16[16,32,256]{2,1,0:T(8,128)(2,1)S(1)}, u32[]{:S(2)}, u32[]{:S(2)}) async-start(bf16[16,32,256]{2,1,0:T(8,128)(2,1)} %slope.1), calls=%async_computation.3 | async-start | bytes 524288 | tf_op jit(solution)/shard_map/all_to_all | solution.py:350
  92.3 2.7 %turn.1 = (bf16[8,144,128]{2,1,0:T(8,128)(2,1)}, bf16[8,144,128]{2,1,0:T(8,128)(2,1)}, bf16[8,144,128]{2,1,0:T(8,128)(2,1)}, bf16[8,144,128]{2,1,0:T(8,128)(2,1)}) custom-call(bf16[32,144,128]{2,1,0:T(8,128)(2,1)} %copy-done.8), custom_call_target="tpu_custom_call" | custom-call | bytes 11100000 | tf_op jit(solution)/shard_map/turn/pallas_call | solution.py:404
  95.0 2.1 %collective-permute-start.5 = (bf16[8,144,128]{2,1,0:T(8,128)(2,1)}, bf16[8,144,128]{2,1,0:T(8,128)(2,1)S(1)}, u32[]{:S(2)}, u32[]{:S(2)}) collective-permute-start(bf16[8,144,128]{2,1,0:T(8,128)(2,1)} %get-tuple-element.23), channel_id=1, source_target_pairs={{0,32},{32,0},{64,96},{96,64},{1,33},{33,1},{65,97},{97,65},{2,34}... | collective-permute-start | bytes 884744 | tf_op jit(solution)/shard_map/ppermute | solution.py:354
  97.1 3.4 %collective-permute-start.6 = (bf16[8,144,128]{2,1,0:T(8,128)(2,1)}, bf16[8,144,128]{2,1,0:T(8,128)(2,1)S(1)}, u32[]{:S(2)}, u32[]{:S(2)}) collective-permute-start(bf16[8,144,128]{2,1,0:T(8,128)(2,1)} %get-tuple-element.24), channel_id=1, source_target_pairs={{0,64},{32,96},{64,0},{96,32},{1,65},{33,97},{65,1},{97,33},{2,66}... | collective-permute-start | bytes 884744 | tf_op jit(solution)/shard_map/ppermute | solution.py:354
  100.6 2.3 %collective-permute-start.7 = (bf16[8,144,128]{2,1,0:T(8,128)(2,1)}, bf16[8,144,128]{2,1,0:T(8,128)(2,1)S(1)}, u32[]{:S(2)}, u32[]{:S(2)}) collective-permute-start(bf16[8,144,128]{2,1,0:T(8,128)(2,1)} %get-tuple-element.25), channel_id=1, source_target_pairs={{0,96},{32,64},{64,32},{96,0},{1,97},{33,65},{65,33},{97,1},{2,98}... | collective-permute-start | bytes 884744 | tf_op jit(solution)/shard_map/ppermute | solution.py:354
  102.9 4.8 %collective-permute-done.6.table_2.refs_6_ = bf16[8,144,128]{2,1,0:T(8,128)(2,1)S(1)} collective-permute-done((bf16[8,144,128]{2,1,0:T(8,128)(2,1)}, bf16[8,144,128]{2,1,0:T(8,128)(2,1)S(1)}, u32[]{:S(2)}, u32[]{:S(2)}) %collective-permute-start.6) | collective-permute-done | bytes 294944 | tf_op jit(solution)/shard_map/ppermute | solution.py:354
  107.7 6.7 %collective-permute-done.7.table_3.refs_7_ = bf16[8,144,128]{2,1,0:T(8,128)(2,1)S(1)} collective-permute-done((bf16[8,144,128]{2,1,0:T(8,128)(2,1)}, bf16[8,144,128]{2,1,0:T(8,128)(2,1)S(1)}, u32[]{:S(2)}, u32[]{:S(2)}) %collective-permute-start.7) | collective-permute-done | bytes 294944 | tf_op jit(solution)/shard_map/ppermute | solution.py:354
  115.3 3.6 %token_grad.1.token_ref = f32[64,4096]{1,0:T(8,128)S(1)} custom-call(s32[2]{0:T(128)S(1)} %copy-done.6, bf16[8,144,128]{2,1,0:T(8,128)(2,1)S(1)} %copy-done.4, bf16[8,144,128]{2,1,0:T(8,128)(2,1)S(1)} %collective-permute-done.5.table_1.refs_5_, bf16[8,144,128]{2,1,0:T(8,128)(2,1)S(1)} %collective-permute-done.6.table_2.refs_6_, ...), custom_call_target="tpu_custom_call" | custom-call | bytes 18500000 | tf_op jit(solution)/shard_map/token_grad/pallas_call | solution.py:419
  119.7 5.9 %hidden_grad.1 = bf16[1024,256]{1,0:T(8,128)(2,1)} custom-call(s32[2]{0:T(128)} %pad_add_fusion.place_ref, bf16[16,32,256]{2,1,0:T(8,128)(2,1)} %copy-done.2, bf16[4,112,128]{2,1,0:T(8,128)(2,1)} %copy-done, bf16[64,3968]{1,0:T(8,128)(2,1)} %embed_0.3, bf16[64,3968]{1,0:T(8,128)(2,1)} %copy-done.10, bf16[2,64,3968]{2,1,0:T(8,128)(2,1)} %collective-permute-done.1.embed_23), custom_call_target="tpu_custom_call" | custom-call | bytes 18500000 | tf_op jit(solution)/shard_map/hidden_grad/pallas_call | solution.py:433
  125.5 16.6 %all-to-all-start.4 = ((bf16[128,8,256]{2,1,0:T(8,128)(2,1)}), bf16[128,8,256]{2,1,0:T(8,128)(2,1)S(1)}, u32[]{:S(2)}, u32[]{:S(2)}) async-start(bf16[128,8,256]{2,1,0:T(8,128)(2,1)} %bitcast.10), calls=%async_computation.4 | async-start | bytes 1048576 | tf_op jit(solution)/shard_map/all_to_all | solution.py:350
  142.2 11.1 %embedding_grad.1 = (f32[64,3968]{1,0:T(8,128)}, f32[1,3968]{1,0:T(1,128)S(1)}) custom-call(s32[2]{0:T(128)S(1)} %copy-done.7, f32[64,4096]{1,0:T(8,128)S(1)} %token_grad.1.token_ref, bf16[16,32,256]{2,1,0:T(8,128)(2,1)S(1)} %copy-done.3, bf16[4,112,128]{2,1,0:T(8,128)(2,1)S(1)} %copy-done.1, bf16[4,112,128]{2,1,0:T(8,128)(2,1)S(1)} %collective-permute-done.2.refs_1_, ...), custom_call_target="tpu_custom_call" | custom-call | bytes 40700000 | tf_op jit(solution)/shard_map/embedding_grad/pallas_call | solution.py:448
  154.0 8.3 %all-to-all-done.4.part_ref = bf16[128,8,256]{2,1,0:T(8,128)(2,1)S(1)} async-done(((bf16[128,8,256]{2,1,0:T(8,128)(2,1)}), bf16[128,8,256]{2,1,0:T(8,128)(2,1)S(1)}, u32[]{:S(2)}, u32[]{:S(2)}) %all-to-all-start.4) | async-done | bytes 524320 | tf_op jit(solution)/shard_map/all_to_all | solution.py:350
  (39 shorter events, 10.3 us)
Async XLA Ops:
  15.6 30.5 %copy-start = (bf16[4,112,128]{2,1,0:T(8,128)(2,1)}, bf16[4,112,128]{2,1,0:T(8,128)(2,1)S(1)}, u32[]{:S(2)}) copy-start(bf16[4,112,128]{2,1,0:T(8,128)(2,1)S(1)} %all_to_all.25.got_ref.refs_0_) | copy-start | bytes 344068
  17.0 14.9 %copy-start.9 = (bf16[64,3968]{1,0:T(8,128)(2,1)S(1)}, bf16[64,3968]{1,0:T(8,128)(2,1)}, u32[]{:S(2)}) copy-start(bf16[64,3968]{1,0:T(8,128)(2,1)} %embed_0.3) | copy-start | bytes 1523716
  17.0 51.5 %all-to-all-start.1 = ((bf16[32,144,128]{2,1,0:T(8,128)(2,1)}), bf16[32,144,128]{2,1,0:T(8,128)(2,1)S(1)}, u32[]{:S(2)}, u32[]{:S(2)}) async-start(bf16[32,144,128]{2,1,0:T(8,128)(2,1)} %spread.1), calls=%async_computation.1 | async-start | bytes 2359296 | tf_op jit(solution)/shard_map/all_to_all | solution.py:350
  31.9 5.8 %collective-permute-start = (bf16[64,3968]{1,0:T(8,128)(2,1)S(1)}, bf16[64,3968]{1,0:T(8,128)(2,1)S(1)}, u32[]{:S(2)}, u32[]{:S(2)}) collective-permute-start(bf16[64,3968]{1,0:T(8,128)(2,1)S(1)} %copy-done.9), channel_id=1, source_target_pairs={{0,32},{32,0},{64,96},{96,64},{1,33},{33,1},{65,97},{97,65},{2,34}... | collective-permute-start | bytes 1523720 | tf_op jit(solution)/shard_map/ppermute | solution.py:354
  37.7 30.8 %copy-start.10 = (bf16[64,3968]{1,0:T(8,128)(2,1)}, bf16[64,3968]{1,0:T(8,128)(2,1)S(1)}, u32[]{:S(2)}) copy-start(bf16[64,3968]{1,0:T(8,128)(2,1)S(1)} %collective-permute-done.embed_1) | copy-start | bytes 1523716
  37.8 42.2 %copy-start.11 = (f32[3968]{0:T(1024)S(1)}, f32[3968]{0:T(1024)}, u32[]{:S(2)}) copy-start(f32[3968]{0:T(1024)} %param.14) | copy-start | bytes 47620
  37.8 30.6 %collective-permute-start.1 = (bf16[2,64,3968]{2,1,0:T(8,128)(2,1)S(1)}, bf16[2,64,3968]{2,1,0:T(8,128)(2,1)}, u32[]{:S(2)}, u32[]{:S(2)}) collective-permute-start(bf16[2,64,3968]{2,1,0:T(8,128)(2,1)S(1)} %pad_maximum_fusion), channel_id=1, source_target_pairs={{0,64},{32,96},{64,0},{96,32},{1,65},{33,97},{65,1},{97,33},{2,66}... | collective-permute-start | bytes 3047432 | tf_op jit(solution)/shard_map/ppermute | solution.py:354
  40.2 27.1 %collective-permute-start.4 = (bf16[4,112,128]{2,1,0:T(8,128)(2,1)S(1)}, bf16[4,112,128]{2,1,0:T(8,128)(2,1)S(1)}, u32[]{:S(2)}, u32[]{:S(2)}) collective-permute-start(bf16[4,112,128]{2,1,0:T(8,128)(2,1)S(1)} %all_to_all.25.got_ref.refs_0_), channel_id=1, source_target_pairs={{0,96},{32,64},{64,32},{96,0},{1,97},{33,65},{65,33},{97,1},{2,98}... | collective-permute-start | bytes 344072 | tf_op jit(solution)/shard_map/ppermute | solution.py:354
  43.8 24.6 %collective-permute-start.3 = (bf16[4,112,128]{2,1,0:T(8,128)(2,1)S(1)}, bf16[4,112,128]{2,1,0:T(8,128)(2,1)S(1)}, u32[]{:S(2)}, u32[]{:S(2)}) collective-permute-start(bf16[4,112,128]{2,1,0:T(8,128)(2,1)S(1)} %all_to_all.25.got_ref.refs_0_), channel_id=1, source_target_pairs={{0,64},{32,96},{64,0},{96,32},{1,65},{33,97},{65,1},{97,33},{2,66}... | collective-permute-start | bytes 344072 | tf_op jit(solution)/shard_map/ppermute | solution.py:354
  46.1 22.4 %collective-permute-start.2 = (bf16[4,112,128]{2,1,0:T(8,128)(2,1)S(1)}, bf16[4,112,128]{2,1,0:T(8,128)(2,1)S(1)}, u32[]{:S(2)}, u32[]{:S(2)}) collective-permute-start(bf16[4,112,128]{2,1,0:T(8,128)(2,1)S(1)} %all_to_all.25.got_ref.refs_0_), channel_id=1, source_target_pairs={{0,32},{32,0},{64,96},{96,64},{1,33},{33,1},{65,97},{97,65},{2,34}... | collective-permute-start | bytes 344072 | tf_op jit(solution)/shard_map/ppermute | solution.py:354
  68.5 1.0 copy-start.8
  75.5 11.8 %all-to-all-start.2 = ((f32[16,16,256]{2,1,0:T(8,128)}), f32[16,16,256]{2,1,0:T(8,128)S(1)}, u32[]{:S(2)}, u32[]{:S(2)}) async-start(f32[16,16,256]{2,1,0:T(8,128)} %logits.1), calls=%async_computation.2 | async-start | bytes 524288 | tf_op jit(solution)/shard_map/all_to_all | solution.py:350
  80.0 34.4 %copy-start.6 = (s32[2]{0:T(128)S(1)}, s32[2]{0:T(128)}, u32[]{:S(2)}) copy-start(s32[2]{0:T(128)} %pad_add_fusion.place_ref) | copy-start | bytes 28
  88.0 31.0 %all-to-all-start.3 = ((bf16[16,32,256]{2,1,0:T(8,128)(2,1)}), bf16[16,32,256]{2,1,0:T(8,128)(2,1)S(1)}, u32[]{:S(2)}, u32[]{:S(2)}) async-start(bf16[16,32,256]{2,1,0:T(8,128)(2,1)} %slope.1), calls=%async_computation.3 | async-start | bytes 524288 | tf_op jit(solution)/shard_map/all_to_all | solution.py:350
  95.0 7.9 %collective-permute-start.5 = (bf16[8,144,128]{2,1,0:T(8,128)(2,1)}, bf16[8,144,128]{2,1,0:T(8,128)(2,1)S(1)}, u32[]{:S(2)}, u32[]{:S(2)}) collective-permute-start(bf16[8,144,128]{2,1,0:T(8,128)(2,1)} %get-tuple-element.23), channel_id=1, source_target_pairs={{0,32},{32,0},{64,96},{96,64},{1,33},{33,1},{65,97},{97,65},{2,34}... | collective-permute-start | bytes 884744 | tf_op jit(solution)/shard_map/ppermute | solution.py:354
  97.1 10.6 %collective-permute-start.6 = (bf16[8,144,128]{2,1,0:T(8,128)(2,1)}, bf16[8,144,128]{2,1,0:T(8,128)(2,1)S(1)}, u32[]{:S(2)}, u32[]{:S(2)}) collective-permute-start(bf16[8,144,128]{2,1,0:T(8,128)(2,1)} %get-tuple-element.24), channel_id=1, source_target_pairs={{0,64},{32,96},{64,0},{96,32},{1,65},{33,97},{65,1},{97,33},{2,66}... | collective-permute-start | bytes 884744 | tf_op jit(solution)/shard_map/ppermute | solution.py:354
  100.6 13.8 %collective-permute-start.7 = (bf16[8,144,128]{2,1,0:T(8,128)(2,1)}, bf16[8,144,128]{2,1,0:T(8,128)(2,1)S(1)}, u32[]{:S(2)}, u32[]{:S(2)}) collective-permute-start(bf16[8,144,128]{2,1,0:T(8,128)(2,1)} %get-tuple-element.25), channel_id=1, source_target_pairs={{0,96},{32,64},{64,32},{96,0},{1,97},{33,65},{65,33},{97,1},{2,98}... | collective-permute-start | bytes 884744 | tf_op jit(solution)/shard_map/ppermute | solution.py:354
  114.4 1.0 copy-start.4
  119.0 23.2 %copy-start.1 = (bf16[4,112,128]{2,1,0:T(8,128)(2,1)S(1)}, bf16[4,112,128]{2,1,0:T(8,128)(2,1)}, u32[]{:S(2)}) copy-start(bf16[4,112,128]{2,1,0:T(8,128)(2,1)} %copy-done) | copy-start | bytes 344068
  119.0 23.2 %copy-start.7 = (s32[2]{0:T(128)S(1)}, s32[2]{0:T(128)}, u32[]{:S(2)}) copy-start(s32[2]{0:T(128)} %pad_add_fusion.place_ref) | copy-start | bytes 28
  119.0 0.7 copy-start.2
  125.5 16.7 %copy-start.3 = (bf16[16,32,256]{2,1,0:T(8,128)(2,1)S(1)}, bf16[16,32,256]{2,1,0:T(8,128)(2,1)}, u32[]{:S(2)}) copy-start(bf16[16,32,256]{2,1,0:T(8,128)(2,1)} %copy-done.2) | copy-start | bytes 786436
  125.5 16.7 %copy-start.5 = (bf16[8,144,128]{2,1,0:T(8,128)(2,1)S(1)}, bf16[8,144,128]{2,1,0:T(8,128)(2,1)}, u32[]{:S(2)}) copy-start(bf16[8,144,128]{2,1,0:T(8,128)(2,1)} %get-tuple-element.22.table_0.refs_4_) | copy-start | bytes 884740
  125.5 36.8 %all-to-all-start.4 = ((bf16[128,8,256]{2,1,0:T(8,128)(2,1)}), bf16[128,8,256]{2,1,0:T(8,128)(2,1)S(1)}, u32[]{:S(2)}, u32[]{:S(2)}) async-start(bf16[128,8,256]{2,1,0:T(8,128)(2,1)} %bitcast.10), calls=%async_computation.4 | async-start | bytes 1048576 | tf_op jit(solution)/shard_map/all_to_all | solution.py:350

commit v9 on v7

--- a/solution.py
+++ b/solution.py
@@ -59,7 +59,7 @@
     return spots[p // 2, pl.ds(2 * tile + p % 2, 1), :]
 
 
-def pack_body(place_ref, lengths, ids, hidden, grad, index, out_ref, *scratch):
+def pack_body(lengths, ids, hidden, grad, index, out_ref, *scratch):
     held, spots, sem = scratch[:5], scratch[5], scratch[6]
     copies = [
         pltpu.make_async_copy(source, target, sem.at[n])
@@ -70,8 +70,8 @@
     for copy in copies:
         copy.wait()
     lengths_ref, ids_ref, hidden_ref, grad_ref, index_ref = held
-    place = place_ref[0]
-    swap = place_ref[1] == 1
+    place = lax.axis_index(SHARD)
+    swap = lax.axis_index("core") == 1
     limit = lengths_ref[place // (SEQ // ROWS)]
     spot = (place % (SEQ // ROWS)) * ROWS + lax.broadcasted_iota(I32, (ROWS, 1), 0)
     arrays = [hidden_ref[...].astype(F32), jnp.where(spot < limit, grad_ref[...].astype(F32), 0.0)]
@@ -321,7 +321,7 @@
         out_ref[:, m * PAIR : (m + 1) * PAIR] = jnp.where(swap, other, total).astype(BF16)
 
 
-def call(body, name, out, scratch=(), specs=None, us=1, out_specs=None, room=56):
+def call(body, name, out, scratch=(), specs=None, us=1, out_specs=None, room=24):
     extra = {} if out_specs is None else {"out_specs": out_specs}
     return pl.pallas_call(
         body,
@@ -364,8 +364,9 @@
             pltpu.VMEM((64, LANES), F32),
             pltpu.SemaphoreType.DMA((5,)),
         ],
-        [SMEM] + [ANY] * 5,
-    )(place, lengths, token_ids, hidden, embed_grad, pool_index)
+        [ANY] * 5,
+        room=56,
+    )(lengths, token_ids, hidden, embed_grad, pool_index)
     own_index = exchange(packed, ("zl", "x"))
     rows = call(
         spread_body,

time: 143 us -> 138 us (0.965)
  Pallas kernels: 39.6 us -> 34.7 us
  waiting for transfers between devices: 36.5 us -> 38.6 us
    all_to_all x4, waiting for transfers between devices: 35 us -> 37.1 us  [exchange(): return lax.all_to_all(x, axis, split_axis=0, concat_axis=0, tiled=True)]
    pallas_call x1, Pallas kernels: 7.49 us -> 5.84 us  [on_device(): call(logits_body, 'logits', shape((GROUPS, 24, CHUNK), F32), [pltpu.VMEM(...]
    pallas_call x1, Pallas kernels: 2.68 us -> 1.19 us  [on_device(): call(turn_body, 'turn', (shape((OWN, PAIR + 16, SEQ), BF16), shape((OWN,...]
  transfers between devices with their start and end apart: 7 -> 7, of which waited for: 5 -> 5; matrix products, arithmetic and copies ran while one was open for 0% -> 1% of each run, Pallas kernels for 13% -> 13%
where the time goes in v9:
time: 138 us; the launch traced here: 137 us
  starting transfers between devices  49 us (36%)
  waiting for transfers between devices  38.6 us (28%)
  Pallas kernels  34.7 us (25%)
  blocking collectives  12.4 us (9%)
    all_to_all x4, starting transfers between devices, exchange(): return lax.all_to_all(x, axis, split_axis=0, concat_axis=0, tiled=True)  40.5 us
    all_to_all x4, waiting for transfers between devices, exchange(): return lax.all_to_all(x, axis, split_axis=0, concat_axis=0, tiled=True)  37.1 us
    all_to_all x1, blocking collectives, exchange(): return lax.all_to_all(x, axis, split_axis=0, concat_axis=0, tiled=True)  12.4 us
    pallas_call x1, Pallas kernels, on_device(): call(embed_body, 'embedding_grad', (shape((COLS, VOC), F32), shape((1, VO...  11.1 us
    ppermute x3, starting transfers between devices, swap_over(): return lax.ppermute(x, axis, [(0, 1), (1, 0)])  8.51 us
    pallas_call x1, Pallas kernels, on_device(): call(hidden_body, 'hidden_grad', shape((OWN * SEQ, PAIR), BF16), [pltpu.V...  6.52 us
    pallas_call x1, Pallas kernels, on_device(): call(logits_body, 'logits', shape((GROUPS, 24, CHUNK), F32), [pltpu.VMEM(...  5.84 us
    pallas_call x1, Pallas kernels, on_device(): call(token_body, 'token_grad', shape((COLS, 4096), F32), [pltpu.VMEM((512...  3.92 us
  transfers between devices with their start and end apart: 7, of which 5 were waited for; matrix products, arithmetic and copies ran while one was open for 1% of the time, Pallas kernels for 13%

profile of v9, /device:TPU:1, one launch (start us, length us, event | category | flops | bytes accessed | tf_op | source)
XLA Modules:
  0.0 137.3 jit_solution(12599369987297165259)
XLA Ops:
  0.6 1.6 %pack.1 = bf16[8,96,128]{2,1,0:T(8,128)(2,1)} custom-call(s32[2]{0:T(128)} %lengths.1, s32[8]{0:T(128)} %ids.1, bf16[8,1024]{1,0:T(8,128)(2,1)} %hidden.1, bf16[8,1024]{1,0:T(8,128)(2,1)} %grad.1, s32[2,3968]{1,0:T(2,128)} %index.1), custom_call_target="tpu_custom_call" | custom-call | bytes 3700000 | tf_op jit(solution)/shard_map/pack/pallas_call | solution.py:354
  2.3 12.4 %all_to_all.25.got_ref.own_index = bf16[8,96,128]{2,1,0:T(8,128)(2,1)S(1)} all-to-all(bf16[8,96,128]{2,1,0:T(8,128)(2,1)} %pack.1), channel_id=1, replica_groups=mesh['zl'=2,'x'=4,'core'=2,'zh'=4,'y'=8] {'zl','x'}, dimensions={0} | all-to-all | bytes 393216 | tf_op jit(solution)/shard_map/all_to_all | solution.py:343
  14.7 1.4 %spread.1 = bf16[32,144,128]{2,1,0:T(8,128)(2,1)} custom-call(bf16[8,96,128]{2,1,0:T(8,128)(2,1)S(1)} %all_to_all.25.got_ref.own_index), custom_call_target="tpu_custom_call" | custom-call | bytes 3700000 | tf_op jit(solution)/shard_map/spread/pallas_call | solution.py:371
  16.1 15.0 %all-to-all-start.1 = ((bf16[32,144,128]{2,1,0:T(8,128)(2,1)}), bf16[32,144,128]{2,1,0:T(8,128)(2,1)S(1)}, u32[]{:S(2)}, u32[]{:S(2)}) async-start(bf16[32,144,128]{2,1,0:T(8,128)(2,1)} %spread.1), calls=%async_computation.1 | async-start | bytes 2359296 | tf_op jit(solution)/shard_map/all_to_all | solution.py:343
  31.2 4.2 %collective-permute-start = (bf16[64,3968]{1,0:T(8,128)(2,1)S(1)}, bf16[64,3968]{1,0:T(8,128)(2,1)S(1)}, u32[]{:S(2)}, u32[]{:S(2)}) collective-permute-start(bf16[64,3968]{1,0:T(8,128)(2,1)S(1)} %copy-done), channel_id=1, source_target_pairs={{0,32},{32,0},{1,33},{33,1},{2,34},{34,2},{3,35},{35,3},{4,36},{36... | collective-permute-start | bytes 1523720 | tf_op jit(solution)/shard_map/ppermute | solution.py:347
  35.4 1.5 %collective-permute-done.other_ref = bf16[64,3968]{1,0:T(8,128)(2,1)S(1)} collective-permute-done((bf16[64,3968]{1,0:T(8,128)(2,1)S(1)}, bf16[64,3968]{1,0:T(8,128)(2,1)S(1)}, u32[]{:S(2)}, u32[]{:S(2)}) %collective-permute-start) | collective-permute-done | bytes 507936 | tf_op jit(solution)/shard_map/ppermute | solution.py:347
  36.9 23.8 %all-to-all-done.1.rows_ref = bf16[32,144,128]{2,1,0:T(8,128)(2,1)S(1)} async-done(((bf16[32,144,128]{2,1,0:T(8,128)(2,1)}), bf16[32,144,128]{2,1,0:T(8,128)(2,1)S(1)}, u32[]{:S(2)}, u32[]{:S(2)}) %all-to-all-start.1) | async-done | bytes 1179680 | tf_op jit(solution)/shard_map/all_to_all | solution.py:343
  60.6 5.8 %logits.1 = f32[16,24,256]{2,1,0:T(8,128)} custom-call(bf16[32,144,128]{2,1,0:T(8,128)(2,1)S(1)} %all-to-all-done.1.rows_ref, bf16[8,96,128]{2,1,0:T(8,128)(2,1)S(1)} %all_to_all.25.got_ref.own_index, bf16[64,3968]{1,0:T(8,128)(2,1)S(1)} %copy-done, bf16[64,3968]{1,0:T(8,128)(2,1)S(1)} %collective-permute-done.other_ref, f32[2,3968]{1,0:T(2,128)S(1)} %copy-done.3), custom_call_target="tpu_custom_call" | custom-call | bytes 22200000 | tf_op jit(solution)/shard_map/logits/pallas_call | solution.py:382
  66.5 7.8 %all-to-all-start.2 = ((f32[16,24,256]{2,1,0:T(8,128)}), f32[16,24,256]{2,1,0:T(8,128)}, u32[]{:S(2)}, u32[]{:S(2)}) async-start(f32[16,24,256]{2,1,0:T(8,128)} %logits.1), calls=%async_computation.2 | async-start | bytes 786432 | tf_op jit(solution)/shard_map/all_to_all | solution.py:343
  74.3 1.2 turn.1
  75.5 2.2 %collective-permute-start.1 = (bf16[16,144,128]{2,1,0:T(8,128)(2,1)}, bf16[16,144,128]{2,1,0:T(8,128)(2,1)S(1)}, u32[]{:S(2)}, u32[]{:S(2)}) collective-permute-start(bf16[16,144,128]{2,1,0:T(8,128)(2,1)} %get-tuple-element.11), channel_id=1, source_target_pairs={{0,32},{32,0},{1,33},{33,1},{2,34},{34,2},{3,35},{35,3},{4,36},{36... | collective-permute-start | bytes 1769480 | tf_op jit(solution)/shard_map/ppermute | solution.py:347
  77.7 5.1 %all-to-all-done.2.part_ref = f32[16,24,256]{2,1,0:T(8,128)} async-done(((f32[16,24,256]{2,1,0:T(8,128)}), f32[16,24,256]{2,1,0:T(8,128)}, u32[]{:S(2)}, u32[]{:S(2)}) %all-to-all-start.2) | async-done | bytes 393248 | tf_op jit(solution)/shard_map/all_to_all | solution.py:343
  82.9 1.8 %slope.1 = bf16[16,32,256]{2,1,0:T(8,128)(2,1)} custom-call(f32[16,24,256]{2,1,0:T(8,128)} %all-to-all-done.2.part_ref, f32[1,256]{1,0:T(1,128)S(1)} %dynamic-slice_bitcast_fusion.bias_ref), custom_call_target="tpu_custom_call" | custom-call | bytes 3700000 | tf_op jit(solution)/shard_map/slope/pallas_call | solution.py:406
  84.7 4.5 %all-to-all-start.3 = ((bf16[16,32,256]{2,1,0:T(8,128)(2,1)}), bf16[16,32,256]{2,1,0:T(8,128)(2,1)S(1)}, u32[]{:S(2)}, u32[]{:S(2)}) async-start(bf16[16,32,256]{2,1,0:T(8,128)(2,1)} %slope.1), calls=%async_computation.3 | async-start | bytes 524288 | tf_op jit(solution)/shard_map/all_to_all | solution.py:343
  89.1 2.1 %collective-permute-start.2 = (bf16[8,96,128]{2,1,0:T(8,128)(2,1)S(1)}, bf16[8,96,128]{2,1,0:T(8,128)(2,1)S(1)}, u32[]{:S(2)}, u32[]{:S(2)}) collective-permute-start(bf16[8,96,128]{2,1,0:T(8,128)(2,1)S(1)} %all_to_all.25.got_ref.own_index), channel_id=1, source_target_pairs={{0,32},{32,0},{1,33},{33,1},{2,34},{34,2},{3,35},{35,3},{4,36},{36... | collective-permute-start | bytes 589832 | tf_op jit(solution)/shard_map/ppermute | solution.py:347
  91.4 3.9 %token_grad.1.token_ref = f32[64,4096]{1,0:T(8,128)S(1)} custom-call(s32[4]{0:T(128)S(1)} %pad_add_fusion.place_ref, bf16[16,144,128]{2,1,0:T(8,128)(2,1)S(1)} %get-tuple-element.10.keep_ref, bf16[16,144,128]{2,1,0:T(8,128)(2,1)S(1)} %collective-permute-done.1.got_ref), custom_call_target="tpu_custom_call" | custom-call | bytes 18500000 | tf_op jit(solution)/shard_map/token_grad/pallas_call | solution.py:410
  95.3 1.1 all-to-all-done.3.grad_ref
  96.4 1.0 copy-done.2
  97.4 6.5 %hidden_grad.1 = bf16[2048,128]{1,0:T(8,128)(2,1)} custom-call(s32[4]{0:T(128)S(1)} %pad_add_fusion.place_ref, bf16[16,32,256]{2,1,0:T(8,128)(2,1)S(1)} %all-to-all-done.3.grad_ref, bf16[8,96,128]{2,1,0:T(8,128)(2,1)S(1)} %all_to_all.25.got_ref.own_index, bf16[64,3968]{1,0:T(8,128)(2,1)S(1)} %copy-done, bf16[64,3968]{1,0:T(8,128)(2,1)S(1)} %copy-done.2), custom_call_target="tpu_custom_call" | custom-call | bytes 22200000 | tf_op jit(solution)/shard_map/hidden_grad/pallas_call | solution.py:424
  103.9 13.2 %all-to-all-start.4 = ((bf16[256,8,128]{2,1,0:T(8,128)(2,1)}), bf16[256,8,128]{2,1,0:T(8,128)(2,1)S(1)}, u32[]{:S(2)}, u32[]{:S(2)}) async-start(bf16[256,8,128]{2,1,0:T(8,128)(2,1)} %bitcast.6), calls=%async_computation.4 | async-start | bytes 1048576 | tf_op jit(solution)/shard_map/all_to_all | solution.py:343
  117.1 11.1 %embedding_grad.1 = (f32[64,3968]{1,0:T(8,128)}, f32[1,3968]{1,0:T(1,128)S(1)}) custom-call(s32[4]{0:T(128)S(1)} %pad_add_fusion.place_ref, f32[64,4096]{1,0:T(8,128)S(1)} %token_grad.1.token_ref, bf16[16,32,256]{2,1,0:T(8,128)(2,1)S(1)} %all-to-all-done.3.grad_ref, bf16[8,96,128]{2,1,0:T(8,128)(2,1)S(1)} %all_to_all.25.got_ref.own_index, ...), custom_call_target="tpu_custom_call" | custom-call | bytes 40700000 | tf_op jit(solution)/shard_map/embedding_grad/pallas_call | solution.py:439
  128.3 0.6 reduce
  128.9 7.1 %all-to-all-done.4.part_ref = bf16[256,8,128]{2,1,0:T(8,128)(2,1)S(1)} async-done(((bf16[256,8,128]{2,1,0:T(8,128)(2,1)}), bf16[256,8,128]{2,1,0:T(8,128)(2,1)S(1)}, u32[]{:S(2)}, u32[]{:S(2)}) %all-to-all-start.4) | async-done | bytes 524320 | tf_op jit(solution)/shard_map/all_to_all | solution.py:343
  136.0 1.3 sum_shards.1
  (14 shorter events, 0.1 us)
Async XLA Ops:
  16.1 15.1 %copy-start = (bf16[64,3968]{1,0:T(8,128)(2,1)S(1)}, bf16[64,3968]{1,0:T(8,128)(2,1)}, u32[]{:S(2)}) copy-start(bf16[64,3968]{1,0:T(8,128)(2,1)} %own_ref.3) | copy-start | bytes 1523716
  16.1 44.5 %copy-start.3 = (f32[2,3968]{1,0:T(2,128)S(1)}, f32[2,3968]{1,0:T(2,128)}, u32[]{:S(2)}) copy-start(f32[2,3968]{1,0:T(2,128)} %pooled_ref.1) | copy-start | bytes 95236
  16.1 44.5 %all-to-all-start.1 = ((bf16[32,144,128]{2,1,0:T(8,128)(2,1)}), bf16[32,144,128]{2,1,0:T(8,128)(2,1)S(1)}, u32[]{:S(2)}, u32[]{:S(2)}) async-start(bf16[32,144,128]{2,1,0:T(8,128)(2,1)} %spread.1), calls=%async_computation.1 | async-start | bytes 2359296 | tf_op jit(solution)/shard_map/all_to_all | solution.py:343
  31.2 43.1 %copy-start.4 = (f32[3968]{0:T(1024)S(1)}, f32[3968]{0:T(1024)}, u32[]{:S(2)}) copy-start(f32[3968]{0:T(1024)} %param.14) | copy-start | bytes 47620
  31.2 5.7 %collective-permute-start = (bf16[64,3968]{1,0:T(8,128)(2,1)S(1)}, bf16[64,3968]{1,0:T(8,128)(2,1)S(1)}, u32[]{:S(2)}, u32[]{:S(2)}) collective-permute-start(bf16[64,3968]{1,0:T(8,128)(2,1)S(1)} %copy-done), channel_id=1, source_target_pairs={{0,32},{32,0},{1,33},{33,1},{2,34},{34,2},{3,35},{35,3},{4,36},{36... | collective-permute-start | bytes 1523720 | tf_op jit(solution)/shard_map/ppermute | solution.py:347
  36.9 29.6 %copy-start.1 = (bf16[64,3968]{1,0:T(8,128)(2,1)}, bf16[64,3968]{1,0:T(8,128)(2,1)S(1)}, u32[]{:S(2)}) copy-start(bf16[64,3968]{1,0:T(8,128)(2,1)S(1)} %collective-permute-done.other_ref) | copy-start | bytes 1523716
  66.5 16.4 %all-to-all-start.2 = ((f32[16,24,256]{2,1,0:T(8,128)}), f32[16,24,256]{2,1,0:T(8,128)}, u32[]{:S(2)}, u32[]{:S(2)}) async-start(f32[16,24,256]{2,1,0:T(8,128)} %logits.1), calls=%async_computation.2 | async-start | bytes 786432 | tf_op jit(solution)/shard_map/all_to_all | solution.py:343
  75.5 15.8 %collective-permute-start.1 = (bf16[16,144,128]{2,1,0:T(8,128)(2,1)}, bf16[16,144,128]{2,1,0:T(8,128)(2,1)S(1)}, u32[]{:S(2)}, u32[]{:S(2)}) collective-permute-start(bf16[16,144,128]{2,1,0:T(8,128)(2,1)} %get-tuple-element.11), channel_id=1, source_target_pairs={{0,32},{32,0},{1,33},{33,1},{2,34},{34,2},{3,35},{35,3},{4,36},{36... | collective-permute-start | bytes 1769480 | tf_op jit(solution)/shard_map/ppermute | solution.py:347
  84.7 11.7 %all-to-all-start.3 = ((bf16[16,32,256]{2,1,0:T(8,128)(2,1)}), bf16[16,32,256]{2,1,0:T(8,128)(2,1)S(1)}, u32[]{:S(2)}, u32[]{:S(2)}) async-start(bf16[16,32,256]{2,1,0:T(8,128)(2,1)} %slope.1), calls=%async_computation.3 | async-start | bytes 524288 | tf_op jit(solution)/shard_map/all_to_all | solution.py:343
  89.1 6.2 %collective-permute-start.2 = (bf16[8,96,128]{2,1,0:T(8,128)(2,1)S(1)}, bf16[8,96,128]{2,1,0:T(8,128)(2,1)S(1)}, u32[]{:S(2)}, u32[]{:S(2)}) collective-permute-start(bf16[8,96,128]{2,1,0:T(8,128)(2,1)S(1)} %all_to_all.25.got_ref.own_index), channel_id=1, source_target_pairs={{0,32},{32,0},{1,33},{33,1},{2,34},{34,2},{3,35},{35,3},{4,36},{36... | collective-permute-start | bytes 589832 | tf_op jit(solution)/shard_map/ppermute | solution.py:347
  96.4 1.0 copy-start.2
  103.9 32.1 %all-to-all-start.4 = ((bf16[256,8,128]{2,1,0:T(8,128)(2,1)}), bf16[256,8,128]{2,1,0:T(8,128)(2,1)S(1)}, u32[]{:S(2)}, u32[]{:S(2)}) async-start(bf16[256,8,128]{2,1,0:T(8,128)(2,1)} %bitcast.6), calls=%async_computation.4 | async-start | bytes 1048576 | tf_op jit(solution)/shard_map/all_to_all | solution.py:343

commit v10 on v9

--- a/solution.py
+++ b/solution.py
@@ -31,6 +31,7 @@
 VOC = TILES * LANES
 CHUNK = 256
 IDS = 16
+SLOTS = 24
 
 
 def lane_gather(table, index):
@@ -97,7 +98,8 @@
         out_ref[m, IDS + 16 :, :] = positions
 
 
-def spread_body(got_ref, out_ref, block, sem):
+def spread_body(got_ref, out_ref, rest_ref):
+    tokens = 64
     hidden = []
     cotangents = []
     digits = []
@@ -106,15 +108,41 @@
         hidden.append(rows[0:ROWS])
         cotangents.append(rows[ROWS:])
         digits.append(got_ref[m, IDS : IDS + 16, :].astype(F32)[0:ROWS])
-    block[0:64, :] = jnp.concatenate(hidden, axis=0).astype(BF16)
-    block[64:128, :] = jnp.concatenate(cotangents, axis=0).astype(BF16)
-    digits = jnp.concatenate(digits + [jnp.zeros((64, LANES), F32)], axis=0).T
-    block[128:144, :] = digits[0:16].astype(BF16)
-    copies = [pltpu.make_async_copy(block, out_ref.at[s], sem.at[s]) for s in range(SHARDS)]
-    for copy in copies:
-        copy.start()
-    for copy in copies:
-        copy.wait()
+    hidden = jnp.concatenate(hidden, axis=0).astype(BF16)
+    blank = jnp.zeros((LANES - tokens, LANES), F32)
+    cotangents = jnp.concatenate(cotangents + [blank], axis=0)
+    digits = jnp.concatenate(digits + [blank], axis=0)
+    across = digits.T[0:16]
+
+    def owner(ids):
+        return ((ids + 0.5) * (1.0 / VOC)).astype(I32)
+
+    lane = lax.broadcasted_iota(I32, (LANES, LANES), 1)
+    row = lax.broadcasted_iota(I32, (LANES, LANES), 0)
+    across_owner = owner(across[0:1] + 128.0 * across[1:2] + 16384.0 * across[2:3])
+    across_owner = jnp.where(lane[0:1] < tokens, across_owner, SHARDS)
+    down_owner = owner(digits[:, 0:1] + 128.0 * digits[:, 1:2] + 16384.0 * digits[:, 2:3])
+    down_owner = jnp.where(row < tokens, down_owner, SHARDS + 1)
+    same = down_owner == across_owner
+    across_rank = jnp.sum(jnp.where(same & (row < lane), 1.0, 0.0), axis=0, keepdims=True).astype(I32)
+    down_rank = jnp.sum(jnp.where(same & (lane < row), 1.0, 0.0), axis=1, keepdims=True).astype(I32)
+    more = jnp.max(jnp.where(lane[0:1] < tokens, across_rank, 0), axis=1, keepdims=True) >= SLOTS
+    rest = jnp.where(down_rank >= SLOTS, cotangents, 0.0)[0:tokens]
+    rest_ref[...] = jnp.concatenate([rest, across], axis=0).astype(BF16)
+    flag = jnp.where(more, 1.0, 0.0) + jnp.zeros((1, LANES), F32)
+    packed = cotangents.astype(BF16)
+    across = across.astype(BF16)
+    slot = lax.broadcasted_iota(I32, (32, 1), 0)
+    slot = jnp.where(slot < SLOTS, slot, -1)
+    for s in range(SHARDS):
+        place = jnp.where((across_owner == s) & (across_rank == slot), 1.0, 0.0).astype(BF16)
+        rows = jnp.dot(place, packed, preferred_element_type=F32)
+        codes = lax.dot_general(
+            across, place, (((1,), (1,)), ((), ())), preferred_element_type=F32
+        )
+        codes = jnp.concatenate([codes[0:7], jnp.zeros((7, LANES - 32), F32)], axis=1)
+        out_ref[s, 0:64, :] = hidden
+        out_ref[s, 64:96, :] = jnp.concatenate([rows[0:SLOTS], codes, flag], axis=0).astype(BF16)
 
 
 def turn_body(rows_ref, keep_out, send_out):
@@ -126,13 +154,17 @@
                 turned = rows[:, s * ROWS : (s + 1) * ROWS, :].reshape(SEQ, PAIR).T.astype(BF16)
                 keep_out[p, 0:COLS, :] = turned[:COLS]
                 send_out[p, 0:COLS, :] = turned[COLS:]
-    for pair in range(SHARDS // 2):
-        rows = [rows_ref[2 * pair + s, 64:144, :].astype(F32) for s in range(2)]
-        turned = jnp.concatenate([r[0:64] for r in rows], axis=0).T.astype(BF16)
-        digits = jnp.concatenate([r[64:80, 0:64] for r in rows], axis=1).astype(BF16)
-        for out, part in ((keep_out, turned[:COLS]), (send_out, turned[COLS:])):
-            out[pair, COLS:PAIR, :] = part
-            out[pair, PAIR:, :] = digits
+    keep = lax.broadcasted_iota(I32, (32, 1), 0) < SLOTS
+    for four in range(SHARDS // 4):
+        rows = [rows_ref[4 * four + s, 64:96, :].astype(F32) for s in range(4)]
+        turned = jnp.concatenate([jnp.where(keep, r, 0.0) for r in rows], axis=0).T.astype(BF16)
+        digits = jnp.concatenate([r[24:32, 0:32] for r in rows], axis=1)
+        digits = jnp.concatenate([digits, jnp.zeros((8, LANES), F32)], axis=0).astype(BF16)
+        for n, out in enumerate((keep_out, send_out)):
+            for part in range(2):
+                at = n * COLS + part * 32
+                out[2 * four + part, COLS : COLS + 32, :] = turned[at : at + 32]
+                out[2 * four + part, COLS + 32 :, :] = digits
 
 
 def over_terms(step, one_chunk):
@@ -181,11 +213,17 @@
             out_ref[first // CHUNK + at // CHUNK, OWN : OWN + 2, 0:some] = upstream
 
     over_terms(1024, one_chunk)
-    out_ref[:, OWN + 2 :, :] = jnp.zeros((GROUPS, 6, CHUNK), F32)
-    out_ref[GROUPS - 1, :, LANES:] = jnp.zeros((24, CHUNK - LANES), F32)
-
-
-def slope_body(part_ref, bias_ref, out_ref):
+    more = rows_ref[0, 80:96, :].astype(F32)
+    for s in range(1, SHARDS):
+        more = jnp.maximum(more, rows_ref[s, 80:96, :].astype(F32))
+    more = jnp.concatenate([more[15:16], more[15:16]], axis=1)
+    tail = jnp.concatenate([more, jnp.zeros((5, CHUNK), F32)], axis=0)
+    for g in range(GROUPS):
+        out_ref[g, OWN + 2 :, :] = tail
+    out_ref[GROUPS - 1, 0 : OWN + 2, LANES:] = jnp.zeros((OWN + 2, CHUNK - LANES), F32)
+
+
+def slope_body(part_ref, bias_ref, out_ref, more_ref):
     logits = []
     upstream = []
     for c in range(2):
@@ -202,6 +240,10 @@
     slope = sigmoid / (1.0 + softened)
     mean_pooled = jnp.sum(pooled, axis=0, keepdims=True) / PASSAGES
     grad = ((upstream + mean_pooled) * slope).astype(BF16)
+    more = part_ref[0, OWN : OWN + 8, 0:LANES]
+    for g in range(1, GROUPS):
+        more = jnp.maximum(more, part_ref[g, OWN : OWN + 8, 0:LANES])
+    more_ref[...] = more[2:3]
     for g in range(GROUPS):
         out_ref[g] = grad
 
@@ -241,6 +283,35 @@
     out_ref[...] = total[...].astype(BF16)
 
 
+def rest_body(place_ref, every_ref, swapped_ref, total_ref, out_ref, total):
+    base = place_ref[0] * VOC
+    low_row = lax.broadcasted_iota(I32, (512, LANES), 0)
+    total[...] = jnp.zeros_like(total)
+    for n, ref in enumerate((every_ref, swapped_ref)):
+
+        def pair(k, carry, n=n, ref=ref):
+            rows = [ref[2 * k + part].astype(F32) for part in range(2)]
+            digits = jnp.concatenate([r[64:72, 0:64] for r in rows], axis=1).astype(I32)
+            local = (digits[2:3] << 14) + (digits[1:2] << 7) + digits[0:1] - base
+            inside = (local >= 0) & (local < VOC)
+            high = jnp.where(inside, local >> 9, 15)
+            turned = jnp.concatenate([r[0:64] for r in rows], axis=0).T[n * COLS : (n + 1) * COLS]
+            left = [jnp.where(high == h, turned, 0.0) for h in range(8)]
+            right = jnp.where(low_row == (local & 511), 1.0, 0.0)
+            total[...] += lax.dot_general(
+                jnp.concatenate(left, axis=0).astype(BF16),
+                right.astype(BF16),
+                (((1,), (1,)), ((), ())),
+                preferred_element_type=F32,
+            )
+            return carry
+
+        lax.fori_loop(0, SHARDS // 2, pair, 0)
+    for h in range(8):
+        lanes = slice(h * 512, (h + 1) * 512)
+        out_ref[:, lanes] = total_ref[:, lanes] + total[h * COLS : (h + 1) * COLS, :]
+
+
 def token_body(place_ref, keep_ref, got_ref, out_ref, left, right, total):
     base = place_ref[0] * VOC
     low_row = lax.broadcasted_iota(I32, (512, LANES), 0).astype(I16)
@@ -248,10 +319,9 @@
     one = jnp.ones((), BF16)
     total[...] = jnp.zeros_like(total)
 
-    def token_block(table_ref, block):
-        for s in range(8):
-            p = block * 8 + s
-            digits = table_ref[p, PAIR:, :].astype(F32).astype(I32)
+    def token_block(table_ref):
+        for group in range(8):
+            digits = table_ref[2 * group, COLS + 32 :, :].astype(F32).astype(I32)
             local = (digits[2:3] << 14) + (digits[1:2] << 7) + digits[0:1] - base
             inside = (local >= 0) & (local < VOC)
             high = jnp.where(inside, local >> 9, 15)
@@ -259,8 +329,10 @@
             low = jnp.broadcast_to(local & 511, (16, LANES)).astype(I16)
             high = jnp.concatenate([high] * 4, axis=0)
             low = jnp.concatenate([low] * 32, axis=0)
-            cotangents = table_ref[p, COLS:PAIR, :]
-            lanes = slice(s * LANES, (s + 1) * LANES)
+            cotangents = jnp.concatenate(
+                [table_ref[2 * group + part, COLS : COLS + 32, :] for part in range(2)], axis=0
+            )
+            lanes = slice(group * LANES, (group + 1) * LANES)
             for h in range(8):
                 left[h * COLS : (h + 1) * COLS, lanes] = jnp.where(
                     high == jnp.int16(h), cotangents, zero
@@ -271,12 +343,7 @@
         )
 
     for table_ref in (keep_ref, got_ref):
-
-        def one_block(block, carry, table_ref=table_ref):
-            token_block(table_ref, block)
-            return carry
-
-        lax.fori_loop(0, 2, one_block, 0)
+        token_block(table_ref)
     for h in range(8):
         out_ref[:, h * 512 : (h + 1) * 512] = total[h * COLS : (h + 1) * COLS, :]
 
@@ -345,6 +412,26 @@
 
 def swap_over(x, axis):
     return lax.ppermute(x, axis, [(0, 1), (1, 0)])
+
+
+def add_rest(total, rest):
+    ring = [(k, (k + 1) % SHARDS) for k in range(SHARDS)]
+
+    def step(k, carry):
+        held, every = carry
+        held = lax.ppermute(held, SHARD, ring)
+        return held, lax.dynamic_update_index_in_dim(every, held, k, 0)
+
+    every = jnp.zeros((SHARDS,) + rest.shape, BF16).at[0].set(rest)
+    every = lax.fori_loop(1, SHARDS, step, (rest, every))[1]
+    place = jnp.stack([lax.axis_index(SHARD)]).astype(I32)
+    return call(
+        rest_body,
+        "rest",
+        shape(total.shape, F32),
+        [pltpu.VMEM((512, 512), F32)],
+        [SMEM, VMEM, VMEM, VMEM],
+    )(place, every, swap_over(every, "core"), total)
 
 
 def on_device(
@@ -368,13 +455,11 @@
         room=56,
     )(lengths, token_ids, hidden, embed_grad, pool_index)
     own_index = exchange(packed, ("zl", "x"))
-    rows = call(
+    rows, rest = call(
         spread_body,
         "spread",
-        shape((SHARDS, 144, LANES), BF16),
-        [pltpu.VMEM((144, LANES), BF16), pltpu.SemaphoreType.DMA((SHARDS,))],
-        [VMEM],
-        out_specs=ANY,
+        (shape((SHARDS, 96, LANES), BF16), shape((80, LANES), BF16)),
+        specs=[VMEM],
         room=8,
     )(own_index)
     all_rows = exchange(rows, SHARD)
@@ -394,7 +479,7 @@
     keep, send = call(
         turn_body,
         "turn",
-        (shape((OWN, PAIR + 16, SEQ), BF16), shape((OWN, PAIR + 16, SEQ), BF16)),
+        (shape((OWN, COLS + 48, SEQ), BF16),) * 2,
         specs=[VMEM],
         us=3,
     )(all_rows)
@@ -403,8 +488,12 @@
     parts = exchange(partial, GROUP)
     bias = jnp.pad(head_bias, (0, GROUPS * CHUNK - VOC)).reshape(GROUPS, 1, CHUNK)
     bias = lax.dynamic_index_in_dim(bias, lax.axis_index(GROUP), 0, keepdims=False)
-    grad_block = call(
-        slope_body, "slope", shape((GROUPS, PASSAGES, CHUNK), BF16), specs=[VMEM, VMEM], room=8
+    grad_block, more = call(
+        slope_body,
+        "slope",
+        (shape((GROUPS, PASSAGES, CHUNK), BF16), shape((1, LANES), F32)),
+        specs=[VMEM, VMEM],
+        room=8,
     )(parts, bias)
     all_grad = exchange(grad_block, GROUP)
     token_grad = call(
@@ -435,6 +524,7 @@
         [SMEM] + [VMEM] * 4,
         us=6,
     )(place, all_grad, own_index, embedding, other_embed)
+    token_grad = lax.cond(more[0, 0] > 0.0, add_rest, lambda total, rest: total, token_grad, rest)
     hidden_got = exchange(hidden_parts.reshape(CHIPS * SHARDS, ROWS, PAIR), HOME)
     embedding_grad, bias_grad = call(
         embed_body,

time: 138 us -> 130 us (0.942)
  waiting for transfers between devices: 38.6 us -> 29.2 us
  starting transfers between devices: 49 us -> 50.6 us
    all_to_all x4, waiting for transfers between devices: 37.1 us -> 27.7 us  [exchange(): return lax.all_to_all(x, axis, split_axis=0, concat_axis=0, tiled=True)]
    all_to_all x4, starting transfers between devices: 40.5 us -> 42.1 us  [exchange(): return lax.all_to_all(x, axis, split_axis=0, concat_axis=0, tiled=True)]
  transfers between devices with their start and end apart: 7 -> 7, of which waited for: 5 -> 4; matrix products, arithmetic and copies ran while one was open for 1% -> 1% of each run, Pallas kernels for 13% -> 13%
where the time goes in v10:
time: 130 us; the launch traced here: 128 us
  starting transfers between devices  50.6 us (39%)
  Pallas kernels  33.7 us (26%)
  waiting for transfers between devices  29.2 us (22%)
  blocking collectives  12.4 us (10%)
    all_to_all x4, starting transfers between devices, exchange(): return lax.all_to_all(x, axis, split_axis=0, concat_axis=0, tiled=True)  42.1 us
    all_to_all x4, waiting for transfers between devices, exchange(): return lax.all_to_all(x, axis, split_axis=0, concat_axis=0, tiled=True)  27.7 us
    all_to_all x1, blocking collectives, exchange(): return lax.all_to_all(x, axis, split_axis=0, concat_axis=0, tiled=True)  12.4 us
    pallas_call x1, Pallas kernels, on_device(): call(embed_body, 'embedding_grad', (shape((COLS, VOC), F32), shape((1, VO...  11.8 us
    ppermute x3, starting transfers between devices, swap_over(): return lax.ppermute(x, axis, [(0, 1), (1, 0)])  8.51 us
    pallas_call x1, Pallas kernels, on_device(): call(hidden_body, 'hidden_grad', shape((OWN * SEQ, PAIR), BF16), [pltpu.V...  6.56 us
    pallas_call x1, Pallas kernels, on_device(): call(logits_body, 'logits', shape((GROUPS, 24, CHUNK), F32), [pltpu.VMEM(...  5.86 us
    pallas_call x1, Pallas kernels, on_device(): call(token_body, 'token_grad', shape((COLS, 4096), F32), [pltpu.VMEM((512...  3.2 us
  transfers between devices with their start and end apart: 7, of which 4 were waited for; matrix products, arithmetic and copies ran while one was open for 1% of the time, Pallas kernels for 13%

profile of v10, /device:TPU:1, one launch (start us, length us, event | category | flops | bytes accessed | tf_op | source)
XLA Modules:
  0.0 128.1 jit_solution(13806274816170696798)
XLA Ops:
  0.6 1.6 %pack.1 = bf16[8,96,128]{2,1,0:T(8,128)(2,1)} custom-call(s32[2]{0:T(128)} %lengths.1, s32[8]{0:T(128)} %ids.1, bf16[8,1024]{1,0:T(8,128)(2,1)} %hidden.1, bf16[8,1024]{1,0:T(8,128)(2,1)} %grad.1, s32[2,3968]{1,0:T(2,128)} %index.1), custom_call_target="tpu_custom_call" | custom-call | bytes 3700000 | tf_op jit(solution)/shard_map/pack/pallas_call | solution.py:441
  2.3 12.4 %all_to_all.25.got_ref.own_index = bf16[8,96,128]{2,1,0:T(8,128)(2,1)S(1)} all-to-all(bf16[8,96,128]{2,1,0:T(8,128)(2,1)} %pack.1), channel_id=1, replica_groups=mesh['zl'=2,'x'=4,'core'=2,'zh'=4,'y'=8] {'zl','x'}, dimensions={0} | all-to-all | bytes 393216 | tf_op jit(solution)/shard_map/all_to_all | solution.py:410
  14.7 1.5 %spread.1 = (bf16[32,96,128]{2,1,0:T(8,128)(2,1)}, bf16[80,128]{1,0:T(8,128)(2,1)S(1)}) custom-call(bf16[8,96,128]{2,1,0:T(8,128)(2,1)S(1)} %all_to_all.25.got_ref.own_index), custom_call_target="tpu_custom_call" | custom-call | bytes 3700000 | tf_op jit(solution)/shard_map/spread/pallas_call | solution.py:458
  16.2 15.0 %all-to-all-start.1 = ((bf16[32,96,128]{2,1,0:T(8,128)(2,1)}), bf16[32,96,128]{2,1,0:T(8,128)(2,1)S(1)}, u32[]{:S(2)}, u32[]{:S(2)}) async-start(bf16[32,96,128]{2,1,0:T(8,128)(2,1)} %get-tuple-element.100), calls=%async_computation.1 | async-start | bytes 1572864 | tf_op jit(solution)/shard_map/all_to_all | solution.py:410
  31.2 4.2 %collective-permute-start.2 = (bf16[64,3968]{1,0:T(8,128)(2,1)S(1)}, bf16[64,3968]{1,0:T(8,128)(2,1)S(1)}, u32[]{:S(2)}, u32[]{:S(2)}) collective-permute-start(bf16[64,3968]{1,0:T(8,128)(2,1)S(1)} %copy-done), channel_id=1, source_target_pairs={{0,32},{32,0},{1,33},{33,1},{2,34},{34,2},{3,35},{35,3},{4,36},{36... | collective-permute-start | bytes 1523720 | tf_op jit(solution)/shard_map/ppermute | solution.py:414
  35.4 1.5 %collective-permute-done.2.other_ref = bf16[64,3968]{1,0:T(8,128)(2,1)S(1)} collective-permute-done((bf16[64,3968]{1,0:T(8,128)(2,1)S(1)}, bf16[64,3968]{1,0:T(8,128)(2,1)S(1)}, u32[]{:S(2)}, u32[]{:S(2)}) %collective-permute-start.2) | collective-permute-done | bytes 507936 | tf_op jit(solution)/shard_map/ppermute | solution.py:414
  36.9 13.9 %all-to-all-done.1.rows_ref = bf16[32,96,128]{2,1,0:T(8,128)(2,1)S(1)} async-done(((bf16[32,96,128]{2,1,0:T(8,128)(2,1)}), bf16[32,96,128]{2,1,0:T(8,128)(2,1)S(1)}, u32[]{:S(2)}, u32[]{:S(2)}) %all-to-all-start.1) | async-done | bytes 786464 | tf_op jit(solution)/shard_map/all_to_all | solution.py:410
  50.8 5.9 %logits.1 = f32[16,24,256]{2,1,0:T(8,128)} custom-call(bf16[32,96,128]{2,1,0:T(8,128)(2,1)S(1)} %all-to-all-done.1.rows_ref, bf16[8,96,128]{2,1,0:T(8,128)(2,1)S(1)} %all_to_all.25.got_ref.own_index, bf16[64,3968]{1,0:T(8,128)(2,1)S(1)} %copy-done, bf16[64,3968]{1,0:T(8,128)(2,1)S(1)} %collective-permute-done.2.other_ref, f32[2,3968]{1,0:T(2,128)S(1)} %copy-done.1), custom_call_target="tpu_custom_call" | custom-call | bytes 22200000 | tf_op jit(solution)/shard_map/logits/pallas_call | solution.py:467
  56.6 8.6 %all-to-all-start.2 = ((f32[16,24,256]{2,1,0:T(8,128)}), f32[16,24,256]{2,1,0:T(8,128)S(1)}, u32[]{:S(2)}, u32[]{:S(2)}) async-start(f32[16,24,256]{2,1,0:T(8,128)} %logits.1), calls=%async_computation.2 | async-start | bytes 786432 | tf_op jit(solution)/shard_map/all_to_all | solution.py:410
  65.2 0.7 copy-done.2
  65.9 7.7 %all-to-all-done.2.part_ref = f32[16,24,256]{2,1,0:T(8,128)S(1)} async-done(((f32[16,24,256]{2,1,0:T(8,128)}), f32[16,24,256]{2,1,0:T(8,128)S(1)}, u32[]{:S(2)}, u32[]{:S(2)}) %all-to-all-start.2) | async-done | bytes 393248 | tf_op jit(solution)/shard_map/all_to_all | solution.py:410
  73.7 0.8 slope.1
  74.5 4.5 %all-to-all-start.3 = ((bf16[16,32,256]{2,1,0:T(8,128)(2,1)}), bf16[16,32,256]{2,1,0:T(8,128)(2,1)S(1)}, u32[]{:S(2)}, u32[]{:S(2)}) async-start(bf16[16,32,256]{2,1,0:T(8,128)(2,1)} %get-tuple-element.101), calls=%async_computation.3 | async-start | bytes 524288 | tf_op jit(solution)/shard_map/all_to_all | solution.py:410
  79.0 1.1 turn.1
  80.0 2.1 %collective-permute-start.3 = (bf16[16,112,128]{2,1,0:T(8,128)(2,1)}, bf16[16,112,128]{2,1,0:T(8,128)(2,1)S(1)}, u32[]{:S(2)}, u32[]{:S(2)}) collective-permute-start(bf16[16,112,128]{2,1,0:T(8,128)(2,1)} %get-tuple-element.103), channel_id=1, source_target_pairs={{0,32},{32,0},{1,33},{33,1},{2,34},{34,2},{3,35},{35,3},{4,36},{36... | collective-permute-start | bytes 1376264 | tf_op jit(solution)/shard_map/ppermute | solution.py:414
  82.2 2.2 %collective-permute-start.4 = (bf16[8,96,128]{2,1,0:T(8,128)(2,1)S(1)}, bf16[8,96,128]{2,1,0:T(8,128)(2,1)S(1)}, u32[]{:S(2)}, u32[]{:S(2)}) collective-permute-start(bf16[8,96,128]{2,1,0:T(8,128)(2,1)S(1)} %all_to_all.25.got_ref.own_index), channel_id=1, source_target_pairs={{0,32},{32,0},{1,33},{33,1},{2,34},{34,2},{3,35},{35,3},{4,36},{36... | collective-permute-start | bytes 589832 | tf_op jit(solution)/shard_map/ppermute | solution.py:414
  84.4 0.1 pad_add_fusion.place_ref
  84.4 3.2 %token_grad.1 = f32[64,4096]{1,0:T(8,128)} custom-call(s32[4]{0:T(128)S(1)} %pad_add_fusion.place_ref, bf16[16,112,128]{2,1,0:T(8,128)(2,1)S(1)} %get-tuple-element.102.keep_ref, bf16[16,112,128]{2,1,0:T(8,128)(2,1)S(1)} %collective-permute-done.3.got_ref), custom_call_target="tpu_custom_call" | custom-call | bytes 18500000 | tf_op jit(solution)/shard_map/token_grad/pallas_call | solution.py:499
  87.7 6.6 %hidden_grad.1 = bf16[2048,128]{1,0:T(8,128)(2,1)} custom-call(s32[4]{0:T(128)S(1)} %pad_add_fusion.place_ref, bf16[16,32,256]{2,1,0:T(8,128)(2,1)S(1)} %all-to-all-done.3.grad_ref, bf16[8,96,128]{2,1,0:T(8,128)(2,1)S(1)} %all_to_all.25.got_ref.own_index, bf16[64,3968]{1,0:T(8,128)(2,1)S(1)} %copy-done, bf16[64,3968]{1,0:T(8,128)(2,1)S(1)} %collective-permute-done.2.other_ref), custom_call_target="tpu_custom_call" | custom-call | bytes 22200000 | tf_op jit(solution)/shard_map/hidden_grad/pallas_call | solution.py:513
  94.2 14.0 %all-to-all-start.4 = ((bf16[256,8,128]{2,1,0:T(8,128)(2,1)}), bf16[256,8,128]{2,1,0:T(8,128)(2,1)S(1)}, u32[]{:S(2)}, u32[]{:S(2)}) async-start(bf16[256,8,128]{2,1,0:T(8,128)(2,1)} %bitcast.9), calls=%async_computation.4 | async-start | bytes 1048576 | tf_op jit(solution)/shard_map/all_to_all | solution.py:410
  108.3 11.8 %embedding_grad.1 = (f32[64,3968]{1,0:T(8,128)}, f32[1,3968]{1,0:T(1,128)S(1)}) custom-call(s32[4]{0:T(128)S(1)} %pad_add_fusion.place_ref, f32[64,4096]{1,0:T(8,128)} %get-tuple-element.154.token_ref, bf16[16,32,256]{2,1,0:T(8,128)(2,1)S(1)} %all-to-all-done.3.grad_ref, bf16[8,96,128]{2,1,0:T(8,128)(2,1)S(1)} %all_to_all.25.got_ref.own_index, ...), custom_call_target="tpu_custom_call" | custom-call | bytes 40700000 | tf_op jit(solution)/shard_map/embedding_grad/pallas_call | solution.py:529
  120.1 0.6 reduce.2
  120.7 6.1 %all-to-all-done.4.part_ref = bf16[256,8,128]{2,1,0:T(8,128)(2,1)S(1)} async-done(((bf16[256,8,128]{2,1,0:T(8,128)(2,1)}), bf16[256,8,128]{2,1,0:T(8,128)(2,1)S(1)}, u32[]{:S(2)}, u32[]{:S(2)}) %all-to-all-start.4) | async-done | bytes 524320 | tf_op jit(solution)/shard_map/all_to_all | solution.py:410
  126.8 1.3 %sum_shards.1 = bf16[8,1024]{1,0:T(8,128)(2,1)} custom-call(s32[4]{0:T(128)S(1)} %pad_add_fusion.place_ref, bf16[256,8,128]{2,1,0:T(8,128)(2,1)S(1)} %all-to-all-done.4.part_ref), custom_call_target="tpu_custom_call" | custom-call | bytes 3700000 | tf_op jit(solution)/shard_map/sum_shards/pallas_call | solution.py:542
  (11 shorter events, 0.0 us)
Async XLA Ops:
  16.2 15.0 %copy-start = (bf16[64,3968]{1,0:T(8,128)(2,1)S(1)}, bf16[64,3968]{1,0:T(8,128)(2,1)}, u32[]{:S(2)}) copy-start(bf16[64,3968]{1,0:T(8,128)(2,1)} %own_ref.3) | copy-start | bytes 1523716
  16.2 34.6 %copy-start.1 = (f32[2,3968]{1,0:T(2,128)S(1)}, f32[2,3968]{1,0:T(2,128)}, u32[]{:S(2)}) copy-start(f32[2,3968]{1,0:T(2,128)} %pooled_ref.1) | copy-start | bytes 95236
  16.2 34.6 %all-to-all-start.1 = ((bf16[32,96,128]{2,1,0:T(8,128)(2,1)}), bf16[32,96,128]{2,1,0:T(8,128)(2,1)S(1)}, u32[]{:S(2)}, u32[]{:S(2)}) async-start(bf16[32,96,128]{2,1,0:T(8,128)(2,1)} %get-tuple-element.100), calls=%async_computation.1 | async-start | bytes 1572864 | tf_op jit(solution)/shard_map/all_to_all | solution.py:410
  31.2 5.7 %collective-permute-start.2 = (bf16[64,3968]{1,0:T(8,128)(2,1)S(1)}, bf16[64,3968]{1,0:T(8,128)(2,1)S(1)}, u32[]{:S(2)}, u32[]{:S(2)}) collective-permute-start(bf16[64,3968]{1,0:T(8,128)(2,1)S(1)} %copy-done), channel_id=1, source_target_pairs={{0,32},{32,0},{1,33},{33,1},{2,34},{34,2},{3,35},{35,3},{4,36},{36... | collective-permute-start | bytes 1523720 | tf_op jit(solution)/shard_map/ppermute | solution.py:414
  56.6 17.0 %all-to-all-start.2 = ((f32[16,24,256]{2,1,0:T(8,128)}), f32[16,24,256]{2,1,0:T(8,128)S(1)}, u32[]{:S(2)}, u32[]{:S(2)}) async-start(f32[16,24,256]{2,1,0:T(8,128)} %logits.1), calls=%async_computation.2 | async-start | bytes 786432 | tf_op jit(solution)/shard_map/all_to_all | solution.py:410
  65.2 0.7 copy-start.2
  74.5 13.2 %all-to-all-start.3 = ((bf16[16,32,256]{2,1,0:T(8,128)(2,1)}), bf16[16,32,256]{2,1,0:T(8,128)(2,1)S(1)}, u32[]{:S(2)}, u32[]{:S(2)}) async-start(bf16[16,32,256]{2,1,0:T(8,128)(2,1)} %get-tuple-element.101), calls=%async_computation.3 | async-start | bytes 524288 | tf_op jit(solution)/shard_map/all_to_all | solution.py:410
  80.0 4.4 %collective-permute-start.3 = (bf16[16,112,128]{2,1,0:T(8,128)(2,1)}, bf16[16,112,128]{2,1,0:T(8,128)(2,1)S(1)}, u32[]{:S(2)}, u32[]{:S(2)}) collective-permute-start(bf16[16,112,128]{2,1,0:T(8,128)(2,1)} %get-tuple-element.103), channel_id=1, source_target_pairs={{0,32},{32,0},{1,33},{33,1},{2,34},{34,2},{3,35},{35,3},{4,36},{36... | collective-permute-start | bytes 1376264 | tf_op jit(solution)/shard_map/ppermute | solution.py:414
  82.2 5.5 %collective-permute-start.4 = (bf16[8,96,128]{2,1,0:T(8,128)(2,1)S(1)}, bf16[8,96,128]{2,1,0:T(8,128)(2,1)S(1)}, u32[]{:S(2)}, u32[]{:S(2)}) collective-permute-start(bf16[8,96,128]{2,1,0:T(8,128)(2,1)S(1)} %all_to_all.25.got_ref.own_index), channel_id=1, source_target_pairs={{0,32},{32,0},{1,33},{33,1},{2,34},{34,2},{3,35},{35,3},{4,36},{36... | collective-permute-start | bytes 589832 | tf_op jit(solution)/shard_map/ppermute | solution.py:414
  94.2 32.6 %all-to-all-start.4 = ((bf16[256,8,128]{2,1,0:T(8,128)(2,1)}), bf16[256,8,128]{2,1,0:T(8,128)(2,1)S(1)}, u32[]{:S(2)}, u32[]{:S(2)}) async-start(bf16[256,8,128]{2,1,0:T(8,128)(2,1)} %bitcast.9), calls=%async_computation.4 | async-start | bytes 1048576 | tf_op jit(solution)/shard_map/all_to_all | solution.py:410

commit v11 on v10

--- a/solution.py
+++ b/solution.py
@@ -181,7 +181,7 @@
 def logits_body(
     rows_ref, got_ref, own_ref, other_ref, pooled_ref, out_ref, hidden_ref, embed_ref, spots
 ):
-    here = lax.broadcasted_iota(I32, (SEQ, 1), 0)
+    here = lax.broadcasted_iota(I32, (8, 1), 0)
     embed_ref[0:COLS, :] = own_ref[...]
     embed_ref[COLS:, :] = other_ref[...]
     load_spots(got_ref, spots)
@@ -203,7 +203,11 @@
             index = jnp.concatenate(
                 [spot_row(spots, p, first // LANES + n) for n in range(width // LANES)], axis=1
             )
-            picked = jnp.sum(jnp.where(index == here, scores, 0.0), axis=0, keepdims=True)
+            high = jnp.broadcast_to(index >> 3, (8, width))
+            rows = scores[0:8]
+            for n in range(1, SEQ // 8):
+                rows = jnp.where(high == n, scores[8 * n : 8 * n + 8], rows)
+            picked = jnp.sum(jnp.where((index & 7) == here, rows, 0.0), axis=0, keepdims=True)
             for at in range(0, width, CHUNK):
                 some = min(CHUNK, width - at)
                 out_ref[first // CHUNK + at // CHUNK, p : p + 1, 0:some] = picked[:, at : at + some]
@@ -212,7 +216,7 @@
             upstream = pooled_ref[:, pl.ds(first + at, some)]
             out_ref[first // CHUNK + at // CHUNK, OWN : OWN + 2, 0:some] = upstream
 
-    over_terms(1024, one_chunk)
+    over_terms(2048, one_chunk)
     more = rows_ref[0, 80:96, :].astype(F32)
     for s in range(1, SHARDS):
         more = jnp.maximum(more, rows_ref[s, 80:96, :].astype(F32))
@@ -245,15 +249,14 @@
         more = jnp.maximum(more, part_ref[g, OWN : OWN + 8, 0:LANES])
     more_ref[...] = more[2:3]
     for g in range(GROUPS):
-        out_ref[g] = grad
+        out_ref[g] = grad[g % 2 * OWN : g % 2 * OWN + OWN]
 
 
 def hidden_body(
-    place_ref, grad_ref, got_ref, own_ref, other_ref, out_ref, total, left, embed_ref, grads, spots
+    grad_ref, got_ref, own_ref, other_ref, out_ref, total, left, embed_ref, grads, spots
 ):
     here = lax.broadcasted_iota(I32, (SEQ, LANES), 0).astype(I16)
     zero = jnp.zeros((), BF16)
-    first_core = place_ref[1] == 0
     load_spots(got_ref, spots)
     embed_ref[0:COLS, :] = own_ref[...]
     embed_ref[COLS:, :] = other_ref[...]
@@ -261,8 +264,7 @@
 
     def one_chunk(first, width):
         for at in range(0, width, CHUNK):
-            both = grad_ref[first // CHUNK + at // CHUNK].astype(F32)
-            grads[:, at : at + CHUNK] = jnp.where(first_core, both[0:OWN], both[OWN:])
+            grads[:, at : at + CHUNK] = grad_ref[first // CHUNK + at // CHUNK].astype(F32)
         embed = embed_ref[:, pl.ds(first, width)]
         for group in range(0, OWN, 4):
             for p in range(group, group + 4):
@@ -349,14 +351,13 @@
 
 
 def embed_body(
-    place_ref, token_ref, grad_ref, own_index, other_index, keep_ref, got_ref, out_ref, bias_ref, grads, own_spots, other_spots
+    token_ref, own_grad, other_grad, own_index, other_index, keep_ref, got_ref, out_ref, bias_ref, grads, own_spots, other_spots
 ):
-    first_core = place_ref[1] == 0
     load_spots(own_index, own_spots)
     load_spots(other_index, other_spots)
     for g in range(GROUPS):
-        both = grad_ref[g].astype(F32)
-        grads[g] = jnp.where(first_core, both, jnp.concatenate([both[OWN:], both[:OWN]], axis=0))
+        grads[g, 0:OWN, :] = own_grad[g].astype(F32)
+        grads[g, OWN:, :] = other_grad[g].astype(F32)
 
     def one_tile(tile, carry):
         lanes = pl.ds(pl.multiple_of(tile * LANES, LANES), LANES)
@@ -486,12 +487,13 @@
     got = swap_over(send, "core")
     other_index = swap_over(own_index, "core")
     parts = exchange(partial, GROUP)
+    parts, keep = lax.optimization_barrier((parts, keep))
     bias = jnp.pad(head_bias, (0, GROUPS * CHUNK - VOC)).reshape(GROUPS, 1, CHUNK)
     bias = lax.dynamic_index_in_dim(bias, lax.axis_index(GROUP), 0, keepdims=False)
     grad_block, more = call(
         slope_body,
         "slope",
-        (shape((GROUPS, PASSAGES, CHUNK), BF16), shape((1, LANES), F32)),
+        (shape((GROUPS, OWN, CHUNK), BF16), shape((1, LANES), F32)),
         specs=[VMEM, VMEM],
         room=8,
     )(parts, bias)
@@ -521,11 +523,12 @@
             pltpu.VMEM((OWN, 1024), F32),
             pltpu.VMEM((CHIPS, 64, LANES), I32),
         ],
-        [SMEM] + [VMEM] * 4,
+        [VMEM] * 4,
         us=6,
-    )(place, all_grad, own_index, embedding, other_embed)
+    )(all_grad, own_index, embedding, other_embed)
     token_grad = lax.cond(more[0, 0] > 0.0, add_rest, lambda total, rest: total, token_grad, rest)
     hidden_got = exchange(hidden_parts.reshape(CHIPS * SHARDS, ROWS, PAIR), HOME)
+    other_grad = swap_over(all_grad, "core")
     embedding_grad, bias_grad = call(
         embed_body,
         "embedding_grad",
@@ -535,10 +538,10 @@
             pltpu.VMEM((CHIPS, 64, LANES), I32),
             pltpu.VMEM((CHIPS, 64, LANES), I32),
         ],
-        [SMEM] + [VMEM] * 6,
+        [VMEM] * 7,
         us=11,
         room=24,
-    )(place, token_grad, all_grad, own_index, other_index, keep, got)
+    )(token_grad, all_grad, other_grad, own_index, other_index, keep, got)
     hidden_grad = call(
         sum_body, "sum_shards", shape((ROWS, WIDTH), BF16), specs=[SMEM, VMEM], room=8
     )(place, hidden_got)

time: 130 us -> 125 us (0.962)
  waiting for transfers between devices: 29.2 us -> 25.2 us
  starting transfers between devices: 50.6 us -> 52.5 us
  Pallas kernels: 33.7 us -> 32.3 us
    all_to_all x4, waiting for transfers between devices: 27.7 us -> 22.8 us  [exchange(): return lax.all_to_all(x, axis, split_axis=0, concat_axis=0, tiled=True)]
    ppermute x3 -> x4, starting transfers between devices: 8.51 us -> 10.9 us  [swap_over(): return lax.ppermute(x, axis, [(0, 1), (1, 0)])]
  transfers between devices with their start and end apart: 7 -> 8, of which waited for: 4 -> 6; matrix products, arithmetic and copies ran while one was open for 1% -> 1% of each run, Pallas kernels for 13% -> 14%
where the time goes in v11:
time: 125 us; the launch traced here: 124 us
  starting transfers between devices  52.5 us (42%)
  Pallas kernels  32.3 us (26%)
  waiting for transfers between devices  25.2 us (20%)
  blocking collectives  12.4 us (10%)
    all_to_all x4, starting transfers between devices, exchange(): return lax.all_to_all(x, axis, split_axis=0, concat_axis=0, tiled=True)  41.5 us
    all_to_all x4, waiting for transfers between devices, exchange(): return lax.all_to_all(x, axis, split_axis=0, concat_axis=0, tiled=True)  22.8 us
    all_to_all x1, blocking collectives, exchange(): return lax.all_to_all(x, axis, split_axis=0, concat_axis=0, tiled=True)  12.4 us
    pallas_call x1, Pallas kernels, on_device(): call(embed_body, 'embedding_grad', (shape((COLS, VOC), F32), shape((1, VO...  11.8 us
    ppermute x4, starting transfers between devices, swap_over(): return lax.ppermute(x, axis, [(0, 1), (1, 0)])  10.9 us
    pallas_call x1, Pallas kernels, on_device(): call(hidden_body, 'hidden_grad', shape((OWN * SEQ, PAIR), BF16), [pltpu.V...  5.98 us
    pallas_call x1, Pallas kernels, on_device(): call(logits_body, 'logits', shape((GROUPS, 24, CHUNK), F32), [pltpu.VMEM(...  5.16 us
    pallas_call x1, Pallas kernels, on_device(): call(token_body, 'token_grad', shape((COLS, 4096), F32), [pltpu.VMEM((512...  3.2 us
  transfers between devices with their start and end apart: 8, of which 6 were waited for; matrix products, arithmetic and copies ran while one was open for 1% of the time, Pallas kernels for 14%

profile of v11, /device:TPU:1, one launch (start us, length us, event | category | flops | bytes accessed | tf_op | source)
XLA Modules:
  0.0 124.0 jit_solution(13986216272147295128)
XLA Ops:
  0.6 1.6 %pack.1 = bf16[8,96,128]{2,1,0:T(8,128)(2,1)} custom-call(s32[2]{0:T(128)} %lengths.1, s32[8]{0:T(128)} %ids.1, bf16[8,1024]{1,0:T(8,128)(2,1)} %hidden.1, bf16[8,1024]{1,0:T(8,128)(2,1)} %grad.1, s32[2,3968]{1,0:T(2,128)} %index.1), custom_call_target="tpu_custom_call" | custom-call | bytes 3700000 | tf_op jit(solution)/shard_map/pack/pallas_call | solution.py:442
  2.3 12.4 %all_to_all.25.got_ref.own_index = bf16[8,96,128]{2,1,0:T(8,128)(2,1)S(1)} all-to-all(bf16[8,96,128]{2,1,0:T(8,128)(2,1)} %pack.1), channel_id=1, replica_groups=mesh['zl'=2,'x'=4,'core'=2,'zh'=4,'y'=8] {'zl','x'}, dimensions={0} | all-to-all | bytes 393216 | tf_op jit(solution)/shard_map/all_to_all | solution.py:411
  14.7 1.5 %spread.1 = (bf16[32,96,128]{2,1,0:T(8,128)(2,1)}, bf16[80,128]{1,0:T(8,128)(2,1)S(1)}) custom-call(bf16[8,96,128]{2,1,0:T(8,128)(2,1)S(1)} %all_to_all.25.got_ref.own_index), custom_call_target="tpu_custom_call" | custom-call | bytes 3700000 | tf_op jit(solution)/shard_map/spread/pallas_call | solution.py:459
  16.2 15.0 %all-to-all-start.1 = ((bf16[32,96,128]{2,1,0:T(8,128)(2,1)}), bf16[32,96,128]{2,1,0:T(8,128)(2,1)S(1)}, u32[]{:S(2)}, u32[]{:S(2)}) async-start(bf16[32,96,128]{2,1,0:T(8,128)(2,1)} %get-tuple-element.102), calls=%async_computation.1 | async-start | bytes 1572864 | tf_op jit(solution)/shard_map/all_to_all | solution.py:411
  31.2 4.2 %collective-permute-start.2 = (bf16[64,3968]{1,0:T(8,128)(2,1)S(1)}, bf16[64,3968]{1,0:T(8,128)(2,1)S(1)}, u32[]{:S(2)}, u32[]{:S(2)}) collective-permute-start(bf16[64,3968]{1,0:T(8,128)(2,1)S(1)} %copy-done), channel_id=1, source_target_pairs={{0,32},{32,0},{1,33},{33,1},{2,34},{34,2},{3,35},{35,3},{4,36},{36... | collective-permute-start | bytes 1523720 | tf_op jit(solution)/shard_map/ppermute | solution.py:415
  35.4 1.5 %collective-permute-done.2.other_ref = bf16[64,3968]{1,0:T(8,128)(2,1)S(1)} collective-permute-done((bf16[64,3968]{1,0:T(8,128)(2,1)S(1)}, bf16[64,3968]{1,0:T(8,128)(2,1)S(1)}, u32[]{:S(2)}, u32[]{:S(2)}) %collective-permute-start.2) | collective-permute-done | bytes 507936 | tf_op jit(solution)/shard_map/ppermute | solution.py:415
  36.9 13.9 %all-to-all-done.1.rows_ref = bf16[32,96,128]{2,1,0:T(8,128)(2,1)S(1)} async-done(((bf16[32,96,128]{2,1,0:T(8,128)(2,1)}), bf16[32,96,128]{2,1,0:T(8,128)(2,1)S(1)}, u32[]{:S(2)}, u32[]{:S(2)}) %all-to-all-start.1) | async-done | bytes 786464 | tf_op jit(solution)/shard_map/all_to_all | solution.py:411
  50.8 5.2 %logits.1 = f32[16,24,256]{2,1,0:T(8,128)} custom-call(bf16[32,96,128]{2,1,0:T(8,128)(2,1)S(1)} %all-to-all-done.1.rows_ref, bf16[8,96,128]{2,1,0:T(8,128)(2,1)S(1)} %all_to_all.25.got_ref.own_index, bf16[64,3968]{1,0:T(8,128)(2,1)S(1)} %copy-done, bf16[64,3968]{1,0:T(8,128)(2,1)S(1)} %collective-permute-done.2.other_ref, f32[2,3968]{1,0:T(2,128)S(1)} %copy-done.1), custom_call_target="tpu_custom_call" | custom-call | bytes 22200000 | tf_op jit(solution)/shard_map/logits/pallas_call | solution.py:468
  55.9 8.6 %all-to-all-start.2 = ((f32[16,24,256]{2,1,0:T(8,128)}), f32[16,24,256]{2,1,0:T(8,128)S(1)}, u32[]{:S(2)}, u32[]{:S(2)}) async-start(f32[16,24,256]{2,1,0:T(8,128)} %logits.1), calls=%async_computation.2 | async-start | bytes 786432 | tf_op jit(solution)/shard_map/all_to_all | solution.py:411
  64.5 1.1 turn.1
  65.6 2.2 %collective-permute-start.3 = (bf16[16,112,128]{2,1,0:T(8,128)(2,1)}, bf16[16,112,128]{2,1,0:T(8,128)(2,1)S(1)}, u32[]{:S(2)}, u32[]{:S(2)}) collective-permute-start(bf16[16,112,128]{2,1,0:T(8,128)(2,1)} %get-tuple-element.107), channel_id=1, source_target_pairs={{0,32},{32,0},{1,33},{33,1},{2,34},{34,2},{3,35},{35,3},{4,36},{36... | collective-permute-start | bytes 1376264 | tf_op jit(solution)/shard_map/ppermute | solution.py:415
  67.9 5.1 %all-to-all-done.2.part_ref = f32[16,24,256]{2,1,0:T(8,128)S(1)} async-done(((f32[16,24,256]{2,1,0:T(8,128)}), f32[16,24,256]{2,1,0:T(8,128)S(1)}, u32[]{:S(2)}, u32[]{:S(2)}) %all-to-all-start.2) | async-done | bytes 393248 | tf_op jit(solution)/shard_map/all_to_all | solution.py:411
  73.0 0.7 slope.1
  73.7 4.5 %all-to-all-start.3 = ((bf16[16,16,256]{2,1,0:T(8,128)(2,1)}), bf16[16,16,256]{2,1,0:T(8,128)(2,1)S(1)}, u32[]{:S(2)}, u32[]{:S(2)}) async-start(bf16[16,16,256]{2,1,0:T(8,128)(2,1)} %get-tuple-element.105), calls=%async_computation.3 | async-start | bytes 262144 | tf_op jit(solution)/shard_map/all_to_all | solution.py:411
  78.2 2.1 %collective-permute-start.4 = (bf16[8,96,128]{2,1,0:T(8,128)(2,1)S(1)}, bf16[8,96,128]{2,1,0:T(8,128)(2,1)S(1)}, u32[]{:S(2)}, u32[]{:S(2)}) collective-permute-start(bf16[8,96,128]{2,1,0:T(8,128)(2,1)S(1)} %all_to_all.25.got_ref.own_index), channel_id=1, source_target_pairs={{0,32},{32,0},{1,33},{33,1},{2,34},{34,2},{3,35},{35,3},{4,36},{36... | collective-permute-start | bytes 589832 | tf_op jit(solution)/shard_map/ppermute | solution.py:415
  80.4 3.2 %token_grad.1 = f32[64,4096]{1,0:T(8,128)} custom-call(s32[4]{0:T(128)S(1)} %pad_add_fusion.place_ref, bf16[16,112,128]{2,1,0:T(8,128)(2,1)S(1)} %get-tuple-element.106.keep_ref, bf16[16,112,128]{2,1,0:T(8,128)(2,1)S(1)} %collective-permute-done.3.got_ref), custom_call_target="tpu_custom_call" | custom-call | bytes 18500000 | tf_op jit(solution)/shard_map/token_grad/pallas_call | solution.py:501
  83.6 0.8 all-to-all-done.3.grad_ref.own_grad
  84.4 6.0 %hidden_grad.1 = bf16[2048,128]{1,0:T(8,128)(2,1)} custom-call(bf16[16,16,256]{2,1,0:T(8,128)(2,1)S(1)} %all-to-all-done.3.grad_ref.own_grad, bf16[8,96,128]{2,1,0:T(8,128)(2,1)S(1)} %all_to_all.25.got_ref.own_index, bf16[64,3968]{1,0:T(8,128)(2,1)S(1)} %copy-done, bf16[64,3968]{1,0:T(8,128)(2,1)S(1)} %collective-permute-done.2.other_ref), custom_call_target="tpu_custom_call" | custom-call | bytes 22200000 | tf_op jit(solution)/shard_map/hidden_grad/pallas_call | solution.py:515
  90.4 13.5 %all-to-all-start.4 = ((bf16[256,8,128]{2,1,0:T(8,128)(2,1)}), bf16[256,8,128]{2,1,0:T(8,128)(2,1)S(1)}, u32[]{:S(2)}, u32[]{:S(2)}) async-start(bf16[256,8,128]{2,1,0:T(8,128)(2,1)} %bitcast.9), calls=%async_computation.4 | async-start | bytes 1048576 | tf_op jit(solution)/shard_map/all_to_all | solution.py:411
  103.9 2.4 %collective-permute-start.5 = (bf16[16,16,256]{2,1,0:T(8,128)(2,1)S(1)}, bf16[16,16,256]{2,1,0:T(8,128)(2,1)S(1)}, u32[]{:S(2)}, u32[]{:S(2)}) collective-permute-start(bf16[16,16,256]{2,1,0:T(8,128)(2,1)S(1)} %all-to-all-done.3.grad_ref.own_grad), channel_id=1, source_target_pairs={{0,32},{32,0},{1,33},{33,1},{2,34},{34,2},{3,35},{35,3},{4,36},{36... | collective-permute-start | bytes 393224 | tf_op jit(solution)/shard_map/ppermute | solution.py:415
  106.3 0.9 collective-permute-done.5.other_grad
  107.2 11.8 %embedding_grad.1 = (f32[64,3968]{1,0:T(8,128)}, f32[1,3968]{1,0:T(1,128)S(1)}) custom-call(f32[64,4096]{1,0:T(8,128)} %get-tuple-element.158.token_ref, bf16[16,16,256]{2,1,0:T(8,128)(2,1)S(1)} %all-to-all-done.3.grad_ref.own_grad, bf16[16,16,256]{2,1,0:T(8,128)(2,1)S(1)} %collective-permute-done.5.other_grad, ...), custom_call_target="tpu_custom_call" | custom-call | bytes 40700000 | tf_op jit(solution)/shard_map/embedding_grad/pallas_call | solution.py:532
  119.7 3.1 %all-to-all-done.4.part_ref = bf16[256,8,128]{2,1,0:T(8,128)(2,1)S(1)} async-done(((bf16[256,8,128]{2,1,0:T(8,128)(2,1)}), bf16[256,8,128]{2,1,0:T(8,128)(2,1)S(1)}, u32[]{:S(2)}, u32[]{:S(2)}) %all-to-all-start.4) | async-done | bytes 524320 | tf_op jit(solution)/shard_map/all_to_all | solution.py:411
  122.7 1.3 %sum_shards.1 = bf16[8,1024]{1,0:T(8,128)(2,1)} custom-call(s32[4]{0:T(128)S(1)} %pad_add_fusion.place_ref, bf16[256,8,128]{2,1,0:T(8,128)(2,1)S(1)} %all-to-all-done.4.part_ref), custom_call_target="tpu_custom_call" | custom-call | bytes 3700000 | tf_op jit(solution)/shard_map/sum_shards/pallas_call | solution.py:545
  (13 shorter events, 0.8 us)
Async XLA Ops:
  16.2 15.0 %copy-start = (bf16[64,3968]{1,0:T(8,128)(2,1)S(1)}, bf16[64,3968]{1,0:T(8,128)(2,1)}, u32[]{:S(2)}) copy-start(bf16[64,3968]{1,0:T(8,128)(2,1)} %own_ref.3) | copy-start | bytes 1523716
  16.2 34.6 %copy-start.1 = (f32[2,3968]{1,0:T(2,128)S(1)}, f32[2,3968]{1,0:T(2,128)}, u32[]{:S(2)}) copy-start(f32[2,3968]{1,0:T(2,128)} %pooled_ref.1) | copy-start | bytes 95236
  16.2 34.6 %all-to-all-start.1 = ((bf16[32,96,128]{2,1,0:T(8,128)(2,1)}), bf16[32,96,128]{2,1,0:T(8,128)(2,1)S(1)}, u32[]{:S(2)}, u32[]{:S(2)}) async-start(bf16[32,96,128]{2,1,0:T(8,128)(2,1)} %get-tuple-element.102), calls=%async_computation.1 | async-start | bytes 1572864 | tf_op jit(solution)/shard_map/all_to_all | solution.py:411
  31.2 5.7 %collective-permute-start.2 = (bf16[64,3968]{1,0:T(8,128)(2,1)S(1)}, bf16[64,3968]{1,0:T(8,128)(2,1)S(1)}, u32[]{:S(2)}, u32[]{:S(2)}) collective-permute-start(bf16[64,3968]{1,0:T(8,128)(2,1)S(1)} %copy-done), channel_id=1, source_target_pairs={{0,32},{32,0},{1,33},{33,1},{2,34},{34,2},{3,35},{35,3},{4,36},{36... | collective-permute-start | bytes 1523720 | tf_op jit(solution)/shard_map/ppermute | solution.py:415
  55.9 17.0 %all-to-all-start.2 = ((f32[16,24,256]{2,1,0:T(8,128)}), f32[16,24,256]{2,1,0:T(8,128)S(1)}, u32[]{:S(2)}, u32[]{:S(2)}) async-start(f32[16,24,256]{2,1,0:T(8,128)} %logits.1), calls=%async_computation.2 | async-start | bytes 786432 | tf_op jit(solution)/shard_map/all_to_all | solution.py:411
  65.6 2.3 %copy-start.2 = (f32[3968]{0:T(1024)S(1)}, f32[3968]{0:T(1024)}, u32[]{:S(2)}) copy-start(f32[3968]{0:T(1024)} %param.20) | copy-start | bytes 47620
  65.6 14.8 %collective-permute-start.3 = (bf16[16,112,128]{2,1,0:T(8,128)(2,1)}, bf16[16,112,128]{2,1,0:T(8,128)(2,1)S(1)}, u32[]{:S(2)}, u32[]{:S(2)}) collective-permute-start(bf16[16,112,128]{2,1,0:T(8,128)(2,1)} %get-tuple-element.107), channel_id=1, source_target_pairs={{0,32},{32,0},{1,33},{33,1},{2,34},{34,2},{3,35},{35,3},{4,36},{36... | collective-permute-start | bytes 1376264 | tf_op jit(solution)/shard_map/ppermute | solution.py:415
  73.7 10.7 %all-to-all-start.3 = ((bf16[16,16,256]{2,1,0:T(8,128)(2,1)}), bf16[16,16,256]{2,1,0:T(8,128)(2,1)S(1)}, u32[]{:S(2)}, u32[]{:S(2)}) async-start(bf16[16,16,256]{2,1,0:T(8,128)(2,1)} %get-tuple-element.105), calls=%async_computation.3 | async-start | bytes 262144 | tf_op jit(solution)/shard_map/all_to_all | solution.py:411
  78.2 5.4 %collective-permute-start.4 = (bf16[8,96,128]{2,1,0:T(8,128)(2,1)S(1)}, bf16[8,96,128]{2,1,0:T(8,128)(2,1)S(1)}, u32[]{:S(2)}, u32[]{:S(2)}) collective-permute-start(bf16[8,96,128]{2,1,0:T(8,128)(2,1)S(1)} %all_to_all.25.got_ref.own_index), channel_id=1, source_target_pairs={{0,32},{32,0},{1,33},{33,1},{2,34},{34,2},{3,35},{35,3},{4,36},{36... | collective-permute-start | bytes 589832 | tf_op jit(solution)/shard_map/ppermute | solution.py:415
  90.4 32.4 %all-to-all-start.4 = ((bf16[256,8,128]{2,1,0:T(8,128)(2,1)}), bf16[256,8,128]{2,1,0:T(8,128)(2,1)S(1)}, u32[]{:S(2)}, u32[]{:S(2)}) async-start(bf16[256,8,128]{2,1,0:T(8,128)(2,1)} %bitcast.9), calls=%async_computation.4 | async-start | bytes 1048576 | tf_op jit(solution)/shard_map/all_to_all | solution.py:411
  103.9 3.3 %collective-permute-start.5 = (bf16[16,16,256]{2,1,0:T(8,128)(2,1)S(1)}, bf16[16,16,256]{2,1,0:T(8,128)(2,1)S(1)}, u32[]{:S(2)}, u32[]{:S(2)}) collective-permute-start(bf16[16,16,256]{2,1,0:T(8,128)(2,1)S(1)} %all-to-all-done.3.grad_ref.own_grad), channel_id=1, source_target_pairs={{0,32},{32,0},{1,33},{33,1},{2,34},{34,2},{3,35},{35,3},{4,36},{36... | collective-permute-start | bytes 393224 | tf_op jit(solution)/shard_map/ppermute | solution.py:415

commit v12 on v11

--- a/solution.py
+++ b/solution.py
@@ -16,7 +16,7 @@
 
 GROUP = ("zl", "x", "core")
 SHARD = ("zh", "y")
-HOME = ("zl", "x", "zh", "y")
+PLANES = ("x", "zh", "y")
 GROUPS = 16
 SHARDS = 32
 CHIPS = 8
@@ -210,32 +210,39 @@
             picked = jnp.sum(jnp.where((index & 7) == here, rows, 0.0), axis=0, keepdims=True)
             for at in range(0, width, CHUNK):
                 some = min(CHUNK, width - at)
-                out_ref[first // CHUNK + at // CHUNK, p : p + 1, 0:some] = picked[:, at : at + some]
+                left = p // 8 * CHUNK
+                out_ref[first // CHUNK + at // CHUNK, p % 8 : p % 8 + 1, left : left + some] = picked[
+                    :, at : at + some
+                ]
         for at in range(0, width, CHUNK):
             some = min(CHUNK, width - at)
-            upstream = pooled_ref[:, pl.ds(first + at, some)]
-            out_ref[first // CHUNK + at // CHUNK, OWN : OWN + 2, 0:some] = upstream
+            for half in range(some // LANES):
+                upstream = pooled_ref[:, pl.ds(first + at + half * LANES, LANES)]
+                out_ref[first // CHUNK + at // CHUNK, 2 * half : 2 * half + 2, 2 * CHUNK :] = upstream
 
     over_terms(2048, one_chunk)
     more = rows_ref[0, 80:96, :].astype(F32)
     for s in range(1, SHARDS):
         more = jnp.maximum(more, rows_ref[s, 80:96, :].astype(F32))
-    more = jnp.concatenate([more[15:16], more[15:16]], axis=1)
-    tail = jnp.concatenate([more, jnp.zeros((5, CHUNK), F32)], axis=0)
+    tail = jnp.concatenate([more[15:16], jnp.zeros((3, LANES), F32)], axis=0)
     for g in range(GROUPS):
-        out_ref[g, OWN + 2 :, :] = tail
-    out_ref[GROUPS - 1, 0 : OWN + 2, LANES:] = jnp.zeros((OWN + 2, CHUNK - LANES), F32)
+        out_ref[g, 4:8, 2 * CHUNK :] = tail
+    for left in range(LANES, 2 * CHUNK, CHUNK):
+        out_ref[GROUPS - 1, :, left : left + LANES] = jnp.zeros((8, LANES), F32)
+    out_ref[GROUPS - 1, 2:4, 2 * CHUNK :] = jnp.zeros((2, LANES), F32)
 
 
 def slope_body(part_ref, bias_ref, out_ref, more_ref):
     logits = []
     upstream = []
     for c in range(2):
-        total = part_ref[c, 0:OWN, :]
+        total = part_ref[c, :, 0 : 2 * CHUNK]
         for m in range(1, CHIPS):
-            total = total + part_ref[2 * m + c, 0:OWN, :]
-        logits.append(total)
-        upstream += [part_ref[2 * m + c, OWN : OWN + 2, :] for m in range(CHIPS)]
+            total = total + part_ref[2 * m + c, :, 0 : 2 * CHUNK]
+        logits += [total[:, :CHUNK], total[:, CHUNK:]]
+        for m in range(CHIPS):
+            halves = part_ref[2 * m + c, :, 2 * CHUNK :]
+            upstream.append(jnp.concatenate([halves[0:2], halves[2:4]], axis=1))
     logits = jnp.concatenate(logits, axis=0) + bias_ref[...]
     upstream = jnp.concatenate(upstream, axis=0)
     softened = jnp.maximum(logits, 0.0) + jnp.log1p(jnp.exp(-jnp.abs(logits)))
@@ -244,10 +251,10 @@
     slope = sigmoid / (1.0 + softened)
     mean_pooled = jnp.sum(pooled, axis=0, keepdims=True) / PASSAGES
     grad = ((upstream + mean_pooled) * slope).astype(BF16)
-    more = part_ref[0, OWN : OWN + 8, 0:LANES]
+    more = part_ref[0, :, 2 * CHUNK :]
     for g in range(1, GROUPS):
-        more = jnp.maximum(more, part_ref[g, OWN : OWN + 8, 0:LANES])
-    more_ref[...] = more[2:3]
+        more = jnp.maximum(more, part_ref[g, :, 2 * CHUNK :])
+    more_ref[...] = more[4:5]
     for g in range(GROUPS):
         out_ref[g] = grad[g % 2 * OWN : g % 2 * OWN + OWN]
 
@@ -282,7 +289,14 @@
             )
 
     over_terms(1024, one_chunk)
-    out_ref[...] = total[...].astype(BF16)
+    for x in range(4):
+        for h in range(2):
+            halves = []
+            for z in range(2):
+                p = 2 * (4 * z + x) + h
+                halves.append(total[p * SEQ : (p + 1) * SEQ, :].reshape(16, ROWS, PAIR))
+            at = x * SHARDS + h * 16
+            out_ref[at : at + 16] = jnp.concatenate(halves, axis=1).astype(BF16)
 
 
 def rest_body(place_ref, every_ref, swapped_ref, total_ref, out_ref, total):
@@ -379,14 +393,24 @@
     lax.fori_loop(0, TILES, one_tile, 0)
 
 
-def sum_body(place_ref, part_ref, out_ref):
+def sum_body(place_ref, part_ref, keep_out, send_out):
+    upper = place_ref[2] == 1
+    for x in range(4):
+        total = part_ref[x * SHARDS].astype(F32)
+        for s in range(1, SHARDS):
+            total = total + part_ref[x * SHARDS + s].astype(F32)
+        keep_out[x] = jnp.where(upper, total[ROWS:], total[:ROWS])
+        send_out[x] = jnp.where(upper, total[:ROWS], total[ROWS:])
+
+
+def join_body(place_ref, keep_ref, got_ref, out_ref):
     swap = place_ref[1] == 1
+    upper = place_ref[2] == 1
     for m in range(CHIPS):
-        total = part_ref[m * SHARDS].astype(F32)
-        for s in range(1, SHARDS):
-            total = total + part_ref[m * SHARDS + s].astype(F32)
-        other = jnp.concatenate([total[:, COLS:], total[:, :COLS]], axis=1)
-        out_ref[:, m * PAIR : (m + 1) * PAIR] = jnp.where(swap, other, total).astype(BF16)
+        x = m % 4
+        pair = jnp.where(upper == (m >= 4), keep_ref[x], got_ref[x])
+        other = jnp.concatenate([pair[:, COLS:], pair[:, :COLS]], axis=1)
+        out_ref[:, m * PAIR : (m + 1) * PAIR] = jnp.where(swap, other, pair).astype(BF16)
 
 
 def call(body, name, out, scratch=(), specs=None, us=1, out_specs=None, room=24):
@@ -468,7 +492,7 @@
     partial = call(
         logits_body,
         "logits",
-        shape((GROUPS, 24, CHUNK), F32),
+        shape((GROUPS, 8, 2 * CHUNK + LANES), F32),
         [
             pltpu.VMEM((OWN * SEQ, PAIR), BF16),
             pltpu.VMEM((PAIR, VOC), BF16),
@@ -515,7 +539,7 @@
     hidden_parts = call(
         hidden_body,
         "hidden_grad",
-        shape((OWN * SEQ, PAIR), BF16),
+        shape((4 * SHARDS, 2 * ROWS, PAIR), BF16),
         [
             pltpu.VMEM((OWN * SEQ, PAIR), F32),
             pltpu.VMEM((OWN * SEQ, 1024), BF16),
@@ -527,7 +551,7 @@
         us=6,
     )(all_grad, own_index, embedding, other_embed)
     token_grad = lax.cond(more[0, 0] > 0.0, add_rest, lambda total, rest: total, token_grad, rest)
-    hidden_got = exchange(hidden_parts.reshape(CHIPS * SHARDS, ROWS, PAIR), HOME)
+    hidden_got = exchange(hidden_parts, PLANES)
     other_grad = swap_over(all_grad, "core")
     embedding_grad, bias_grad = call(
         embed_body,
@@ -542,9 +566,16 @@
         us=11,
         room=24,
     )(token_grad, all_grad, other_grad, own_index, other_index, keep, got)
+    summed, send = call(
+        sum_body,
+        "sum_shards",
+        (shape((4, ROWS, PAIR), F32),) * 2,
+        specs=[SMEM, VMEM],
+        room=8,
+    )(place, hidden_got)
     hidden_grad = call(
-        sum_body, "sum_shards", shape((ROWS, WIDTH), BF16), specs=[SMEM, VMEM], room=8
-    )(place, hidden_got)
+        join_body, "join", shape((ROWS, WIDTH), BF16), specs=[SMEM, VMEM, VMEM], room=8
+    )(place, summed, swap_over(send, "zl"))
     return hidden_grad, embedding_grad, bias_grad.reshape(VOC)
 
 

time: 125 us -> 139 us (1.11)
  waiting for transfers between devices: 25.2 us -> 38.6 us
    all_to_all x4, waiting for transfers between devices: 22.8 us -> 37.1 us  [exchange(): return lax.all_to_all(x, axis, split_axis=0, concat_axis=0, tiled=True)]
    ppermute x4 -> x5, starting transfers between devices: 10.9 us -> 14.1 us  [swap_over(): return lax.ppermute(x, axis, [(0, 1), (1, 0)])]
    all_to_all x4, starting transfers between devices: 41.5 us -> 38.5 us  [exchange(): return lax.all_to_all(x, axis, split_axis=0, concat_axis=0, tiled=True)]
    pallas_call x3 -> x4, Pallas kernels: 12.4 us -> 13 us  [the longest x1 5.97 us: on_device(): call(hidden_body, 'hidden_grad', shape((4 * SHARDS, 2 * ROWS, PAIR), BF16...]
  transfers between devices with their start and end apart: 8 -> 9, of which waited for: 6 -> 5; matrix products, arithmetic and copies ran while one was open for 1% -> 1% of each run, Pallas kernels for 14% -> 13%
where the time goes in v12:
time: 139 us; the launch traced here: 138 us
  starting transfers between devices  52.5 us (38%)
  waiting for transfers between devices  38.6 us (28%)
  Pallas kernels  32.9 us (24%)
  blocking collectives  12.4 us (9%)
    all_to_all x4, starting transfers between devices, exchange(): return lax.all_to_all(x, axis, split_axis=0, concat_axis=0, tiled=True)  38.5 us
    all_to_all x4, waiting for transfers between devices, exchange(): return lax.all_to_all(x, axis, split_axis=0, concat_axis=0, tiled=True)  37.1 us
    ppermute x5, starting transfers between devices, swap_over(): return lax.ppermute(x, axis, [(0, 1), (1, 0)])  14.1 us
    all_to_all x1, blocking collectives, exchange(): return lax.all_to_all(x, axis, split_axis=0, concat_axis=0, tiled=True)  12.4 us
    pallas_call x1, Pallas kernels, on_device(): call(embed_body, 'embedding_grad', (shape((COLS, VOC), F32), shape((1, VO...  11.8 us
    pallas_call x1, Pallas kernels, on_device(): call(hidden_body, 'hidden_grad', shape((4 * SHARDS, 2 * ROWS, PAIR), BF16...  5.97 us
    pallas_call x1, Pallas kernels, on_device(): call(logits_body, 'logits', shape((GROUPS, 8, 2 * CHUNK + LANES), F32), [...  5.15 us
    pallas_call x1, Pallas kernels, on_device(): call(token_body, 'token_grad', shape((COLS, 4096), F32), [pltpu.VMEM((512...  3.21 us
  transfers between devices with their start and end apart: 9, of which 5 were waited for; matrix products, arithmetic and copies ran while one was open for 1% of the time, Pallas kernels for 13%

profile of v12, /device:TPU:1, one launch (start us, length us, event | category | flops | bytes accessed | tf_op | source)
XLA Modules:
  0.0 138.0 jit_solution(92879271511017368)
XLA Ops:
  0.6 1.6 %pack.1 = bf16[8,96,128]{2,1,0:T(8,128)(2,1)} custom-call(s32[2]{0:T(128)} %lengths.1, s32[8]{0:T(128)} %ids.1, bf16[8,1024]{1,0:T(8,128)(2,1)} %hidden.1, bf16[8,1024]{1,0:T(8,128)(2,1)} %grad.1, s32[2,3968]{1,0:T(2,128)} %index.1), custom_call_target="tpu_custom_call" | custom-call | bytes 3700000 | tf_op jit(solution)/shard_map/pack/pallas_call | solution.py:466
  2.3 12.4 %all_to_all.25.got_ref.own_index = bf16[8,96,128]{2,1,0:T(8,128)(2,1)S(1)} all-to-all(bf16[8,96,128]{2,1,0:T(8,128)(2,1)} %pack.1), channel_id=1, replica_groups=mesh['zl'=2,'x'=4,'core'=2,'zh'=4,'y'=8] {'zl','x'}, dimensions={0} | all-to-all | bytes 393216 | tf_op jit(solution)/shard_map/all_to_all | solution.py:435
  14.7 1.5 %spread.1 = (bf16[32,96,128]{2,1,0:T(8,128)(2,1)}, bf16[80,128]{1,0:T(8,128)(2,1)S(1)}) custom-call(bf16[8,96,128]{2,1,0:T(8,128)(2,1)S(1)} %all_to_all.25.got_ref.own_index), custom_call_target="tpu_custom_call" | custom-call | bytes 3700000 | tf_op jit(solution)/shard_map/spread/pallas_call | solution.py:483
  16.2 15.0 %all-to-all-start.1 = ((bf16[32,96,128]{2,1,0:T(8,128)(2,1)}), bf16[32,96,128]{2,1,0:T(8,128)(2,1)S(1)}, u32[]{:S(2)}, u32[]{:S(2)}) async-start(bf16[32,96,128]{2,1,0:T(8,128)(2,1)} %get-tuple-element.104), calls=%async_computation.1 | async-start | bytes 1572864 | tf_op jit(solution)/shard_map/all_to_all | solution.py:435
  31.2 4.2 %collective-permute-start.2 = (bf16[64,3968]{1,0:T(8,128)(2,1)S(1)}, bf16[64,3968]{1,0:T(8,128)(2,1)S(1)}, u32[]{:S(2)}, u32[]{:S(2)}) collective-permute-start(bf16[64,3968]{1,0:T(8,128)(2,1)S(1)} %copy-done), channel_id=1, source_target_pairs={{0,32},{32,0},{1,33},{33,1},{2,34},{34,2},{3,35},{35,3},{4,36},{36... | collective-permute-start | bytes 1523720 | tf_op jit(solution)/shard_map/ppermute | solution.py:439
  35.4 1.5 %collective-permute-done.2.other_ref = bf16[64,3968]{1,0:T(8,128)(2,1)S(1)} collective-permute-done((bf16[64,3968]{1,0:T(8,128)(2,1)S(1)}, bf16[64,3968]{1,0:T(8,128)(2,1)S(1)}, u32[]{:S(2)}, u32[]{:S(2)}) %collective-permute-start.2) | collective-permute-done | bytes 507936 | tf_op jit(solution)/shard_map/ppermute | solution.py:439
  36.9 13.9 %all-to-all-done.1.rows_ref = bf16[32,96,128]{2,1,0:T(8,128)(2,1)S(1)} async-done(((bf16[32,96,128]{2,1,0:T(8,128)(2,1)}), bf16[32,96,128]{2,1,0:T(8,128)(2,1)S(1)}, u32[]{:S(2)}, u32[]{:S(2)}) %all-to-all-start.1) | async-done | bytes 786464 | tf_op jit(solution)/shard_map/all_to_all | solution.py:435
  50.8 5.1 %logits.1 = f32[16,8,640]{2,1,0:T(8,128)} custom-call(bf16[32,96,128]{2,1,0:T(8,128)(2,1)S(1)} %all-to-all-done.1.rows_ref, bf16[8,96,128]{2,1,0:T(8,128)(2,1)S(1)} %all_to_all.25.got_ref.own_index, bf16[64,3968]{1,0:T(8,128)(2,1)S(1)} %copy-done, bf16[64,3968]{1,0:T(8,128)(2,1)S(1)} %collective-permute-done.2.other_ref, f32[2,3968]{1,0:T(2,128)S(1)} %copy-done.1), custom_call_target="tpu_custom_call" | custom-call | bytes 22200000 | tf_op jit(solution)/shard_map/logits/pallas_call | solution.py:492
  55.9 8.6 %all-to-all-start.2 = ((f32[16,8,640]{2,1,0:T(8,128)}), f32[16,8,640]{2,1,0:T(8,128)S(1)}, u32[]{:S(2)}, u32[]{:S(2)}) async-start(f32[16,8,640]{2,1,0:T(8,128)} %logits.1), calls=%async_computation.2 | async-start | bytes 655360 | tf_op jit(solution)/shard_map/all_to_all | solution.py:435
  64.5 1.1 turn.1
  65.6 2.2 %collective-permute-start.3 = (bf16[16,112,128]{2,1,0:T(8,128)(2,1)}, bf16[16,112,128]{2,1,0:T(8,128)(2,1)S(1)}, u32[]{:S(2)}, u32[]{:S(2)}) collective-permute-start(bf16[16,112,128]{2,1,0:T(8,128)(2,1)} %get-tuple-element.109), channel_id=1, source_target_pairs={{0,32},{32,0},{1,33},{33,1},{2,34},{34,2},{3,35},{35,3},{4,36},{36... | collective-permute-start | bytes 1376264 | tf_op jit(solution)/shard_map/ppermute | solution.py:439
  67.9 4.4 %all-to-all-done.2.part_ref = f32[16,8,640]{2,1,0:T(8,128)S(1)} async-done(((f32[16,8,640]{2,1,0:T(8,128)}), f32[16,8,640]{2,1,0:T(8,128)S(1)}, u32[]{:S(2)}, u32[]{:S(2)}) %all-to-all-start.2) | async-done | bytes 327712 | tf_op jit(solution)/shard_map/all_to_all | solution.py:435
  72.2 0.7 slope.1
  73.0 4.5 %all-to-all-start.3 = ((bf16[16,16,256]{2,1,0:T(8,128)(2,1)}), bf16[16,16,256]{2,1,0:T(8,128)(2,1)S(1)}, u32[]{:S(2)}, u32[]{:S(2)}) async-start(bf16[16,16,256]{2,1,0:T(8,128)(2,1)} %get-tuple-element.107), calls=%async_computation.3 | async-start | bytes 262144 | tf_op jit(solution)/shard_map/all_to_all | solution.py:435
  77.4 2.1 %collective-permute-start.4 = (bf16[8,96,128]{2,1,0:T(8,128)(2,1)S(1)}, bf16[8,96,128]{2,1,0:T(8,128)(2,1)S(1)}, u32[]{:S(2)}, u32[]{:S(2)}) collective-permute-start(bf16[8,96,128]{2,1,0:T(8,128)(2,1)S(1)} %all_to_all.25.got_ref.own_index), channel_id=1, source_target_pairs={{0,32},{32,0},{1,33},{33,1},{2,34},{34,2},{3,35},{35,3},{4,36},{36... | collective-permute-start | bytes 589832 | tf_op jit(solution)/shard_map/ppermute | solution.py:439
  79.7 3.2 %token_grad.1 = f32[64,4096]{1,0:T(8,128)} custom-call(s32[4]{0:T(128)S(1)} %pad_add_fusion.place_ref, bf16[16,112,128]{2,1,0:T(8,128)(2,1)S(1)} %get-tuple-element.108.keep_ref, bf16[16,112,128]{2,1,0:T(8,128)(2,1)S(1)} %collective-permute-done.3.got_ref), custom_call_target="tpu_custom_call" | custom-call | bytes 18500000 | tf_op jit(solution)/shard_map/token_grad/pallas_call | solution.py:525
  82.9 0.8 all-to-all-done.3.grad_ref.own_grad
  83.7 6.0 %hidden_grad.1 = bf16[128,16,128]{2,1,0:T(8,128)(2,1)} custom-call(bf16[16,16,256]{2,1,0:T(8,128)(2,1)S(1)} %all-to-all-done.3.grad_ref.own_grad, bf16[8,96,128]{2,1,0:T(8,128)(2,1)S(1)} %all_to_all.25.got_ref.own_index, bf16[64,3968]{1,0:T(8,128)(2,1)S(1)} %copy-done, bf16[64,3968]{1,0:T(8,128)(2,1)S(1)} %collective-permute-done.2.other_ref), custom_call_target="tpu_custom_call" | custom-call | bytes 22200000 | tf_op jit(solution)/shard_map/hidden_grad/pallas_call | solution.py:539
  89.6 10.4 %all-to-all-start.4 = ((bf16[128,16,128]{2,1,0:T(8,128)(2,1)}), bf16[128,16,128]{2,1,0:T(8,128)(2,1)S(1)}, u32[]{:S(2)}, u32[]{:S(2)}) async-start(bf16[128,16,128]{2,1,0:T(8,128)(2,1)} %hidden_grad.1), calls=%async_computation.4 | async-start | bytes 1048576 | tf_op jit(solution)/shard_map/all_to_all | solution.py:435
  100.0 2.3 %collective-permute-start.6 = (bf16[16,16,256]{2,1,0:T(8,128)(2,1)S(1)}, bf16[16,16,256]{2,1,0:T(8,128)(2,1)S(1)}, u32[]{:S(2)}, u32[]{:S(2)}) collective-permute-start(bf16[16,16,256]{2,1,0:T(8,128)(2,1)S(1)} %all-to-all-done.3.grad_ref.own_grad), channel_id=1, source_target_pairs={{0,32},{32,0},{1,33},{33,1},{2,34},{34,2},{3,35},{35,3},{4,36},{36... | collective-permute-start | bytes 393224 | tf_op jit(solution)/shard_map/ppermute | solution.py:439
  102.4 18.1 %all-to-all-done.4.part_ref = bf16[128,16,128]{2,1,0:T(8,128)(2,1)S(1)} async-done(((bf16[128,16,128]{2,1,0:T(8,128)(2,1)}), bf16[128,16,128]{2,1,0:T(8,128)(2,1)S(1)}, u32[]{:S(2)}, u32[]{:S(2)}) %all-to-all-start.4) | async-done | bytes 524320 | tf_op jit(solution)/shard_map/all_to_all | solution.py:435
  121.1 3.1 %collective-permute-start.5 = (f32[4,8,128]{2,1,0:T(8,128)S(1)}, f32[4,8,128]{2,1,0:T(8,128)S(1)}, u32[]{:S(2)}, u32[]{:S(2)}) collective-permute-start(f32[4,8,128]{2,1,0:T(8,128)S(1)} %get-tuple-element.112), channel_id=1, source_target_pairs={{0,256},{256,0},{1,257},{257,1},{2,258},{258,2},{3,259},{259,3},{4... | collective-permute-start | bytes 49160 | tf_op jit(solution)/shard_map/ppermute | solution.py:439
  124.3 11.8 %embedding_grad.1 = (f32[64,3968]{1,0:T(8,128)}, f32[1,3968]{1,0:T(1,128)S(1)}) custom-call(f32[64,4096]{1,0:T(8,128)} %get-tuple-element.162.token_ref, bf16[16,16,256]{2,1,0:T(8,128)(2,1)S(1)} %all-to-all-done.3.grad_ref.own_grad, bf16[16,16,256]{2,1,0:T(8,128)(2,1)S(1)} %collective-permute-done.6.other_grad, ...), custom_call_target="tpu_custom_call" | custom-call | bytes 40700000 | tf_op jit(solution)/shard_map/embedding_grad/pallas_call | solution.py:556
  136.8 1.2 join.1
  (16 shorter events, 1.4 us)
Async XLA Ops:
  16.2 15.0 %copy-start = (bf16[64,3968]{1,0:T(8,128)(2,1)S(1)}, bf16[64,3968]{1,0:T(8,128)(2,1)}, u32[]{:S(2)}) copy-start(bf16[64,3968]{1,0:T(8,128)(2,1)} %own_ref.3) | copy-start | bytes 1523716
  16.2 34.6 %copy-start.1 = (f32[2,3968]{1,0:T(2,128)S(1)}, f32[2,3968]{1,0:T(2,128)}, u32[]{:S(2)}) copy-start(f32[2,3968]{1,0:T(2,128)} %pooled_ref.1) | copy-start | bytes 95236
  16.2 34.6 %all-to-all-start.1 = ((bf16[32,96,128]{2,1,0:T(8,128)(2,1)}), bf16[32,96,128]{2,1,0:T(8,128)(2,1)S(1)}, u32[]{:S(2)}, u32[]{:S(2)}) async-start(bf16[32,96,128]{2,1,0:T(8,128)(2,1)} %get-tuple-element.104), calls=%async_computation.1 | async-start | bytes 1572864 | tf_op jit(solution)/shard_map/all_to_all | solution.py:435
  31.2 5.7 %collective-permute-start.2 = (bf16[64,3968]{1,0:T(8,128)(2,1)S(1)}, bf16[64,3968]{1,0:T(8,128)(2,1)S(1)}, u32[]{:S(2)}, u32[]{:S(2)}) collective-permute-start(bf16[64,3968]{1,0:T(8,128)(2,1)S(1)} %copy-done), channel_id=1, source_target_pairs={{0,32},{32,0},{1,33},{33,1},{2,34},{34,2},{3,35},{35,3},{4,36},{36... | collective-permute-start | bytes 1523720 | tf_op jit(solution)/shard_map/ppermute | solution.py:439
  55.9 16.3 %all-to-all-start.2 = ((f32[16,8,640]{2,1,0:T(8,128)}), f32[16,8,640]{2,1,0:T(8,128)S(1)}, u32[]{:S(2)}, u32[]{:S(2)}) async-start(f32[16,8,640]{2,1,0:T(8,128)} %logits.1), calls=%async_computation.2 | async-start | bytes 655360 | tf_op jit(solution)/shard_map/all_to_all | solution.py:435
  65.6 2.3 %copy-start.2 = (f32[3968]{0:T(1024)S(1)}, f32[3968]{0:T(1024)}, u32[]{:S(2)}) copy-start(f32[3968]{0:T(1024)} %param.20) | copy-start | bytes 47620
  65.6 14.1 %collective-permute-start.3 = (bf16[16,112,128]{2,1,0:T(8,128)(2,1)}, bf16[16,112,128]{2,1,0:T(8,128)(2,1)S(1)}, u32[]{:S(2)}, u32[]{:S(2)}) collective-permute-start(bf16[16,112,128]{2,1,0:T(8,128)(2,1)} %get-tuple-element.109), channel_id=1, source_target_pairs={{0,32},{32,0},{1,33},{33,1},{2,34},{34,2},{3,35},{35,3},{4,36},{36... | collective-permute-start | bytes 1376264 | tf_op jit(solution)/shard_map/ppermute | solution.py:439
  73.0 10.7 %all-to-all-start.3 = ((bf16[16,16,256]{2,1,0:T(8,128)(2,1)}), bf16[16,16,256]{2,1,0:T(8,128)(2,1)S(1)}, u32[]{:S(2)}, u32[]{:S(2)}) async-start(bf16[16,16,256]{2,1,0:T(8,128)(2,1)} %get-tuple-element.107), calls=%async_computation.3 | async-start | bytes 262144 | tf_op jit(solution)/shard_map/all_to_all | solution.py:435
  77.4 5.4 %collective-permute-start.4 = (bf16[8,96,128]{2,1,0:T(8,128)(2,1)S(1)}, bf16[8,96,128]{2,1,0:T(8,128)(2,1)S(1)}, u32[]{:S(2)}, u32[]{:S(2)}) collective-permute-start(bf16[8,96,128]{2,1,0:T(8,128)(2,1)S(1)} %all_to_all.25.got_ref.own_index), channel_id=1, source_target_pairs={{0,32},{32,0},{1,33},{33,1},{2,34},{34,2},{3,35},{35,3},{4,36},{36... | collective-permute-start | bytes 589832 | tf_op jit(solution)/shard_map/ppermute | solution.py:439
  89.6 30.9 %all-to-all-start.4 = ((bf16[128,16,128]{2,1,0:T(8,128)(2,1)}), bf16[128,16,128]{2,1,0:T(8,128)(2,1)S(1)}, u32[]{:S(2)}, u32[]{:S(2)}) async-start(bf16[128,16,128]{2,1,0:T(8,128)(2,1)} %hidden_grad.1), calls=%async_computation.4 | async-start | bytes 1048576 | tf_op jit(solution)/shard_map/all_to_all | solution.py:435
  100.0 24.3 %collective-permute-start.6 = (bf16[16,16,256]{2,1,0:T(8,128)(2,1)S(1)}, bf16[16,16,256]{2,1,0:T(8,128)(2,1)S(1)}, u32[]{:S(2)}, u32[]{:S(2)}) collective-permute-start(bf16[16,16,256]{2,1,0:T(8,128)(2,1)S(1)} %all-to-all-done.3.grad_ref.own_grad), channel_id=1, source_target_pairs={{0,32},{32,0},{1,33},{33,1},{2,34},{34,2},{3,35},{35,3},{4,36},{36... | collective-permute-start | bytes 393224 | tf_op jit(solution)/shard_map/ppermute | solution.py:439
  121.1 15.7 %collective-permute-start.5 = (f32[4,8,128]{2,1,0:T(8,128)S(1)}, f32[4,8,128]{2,1,0:T(8,128)S(1)}, u32[]{:S(2)}, u32[]{:S(2)}) collective-permute-start(f32[4,8,128]{2,1,0:T(8,128)S(1)} %get-tuple-element.112), channel_id=1, source_target_pairs={{0,256},{256,0},{1,257},{257,1},{2,258},{258,2},{3,259},{259,3},{4... | collective-permute-start | bytes 49160 | tf_op jit(solution)/shard_map/ppermute | solution.py:439

commit v13 on v11

--- a/solution.py
+++ b/solution.py
@@ -210,32 +210,39 @@
             picked = jnp.sum(jnp.where((index & 7) == here, rows, 0.0), axis=0, keepdims=True)
             for at in range(0, width, CHUNK):
                 some = min(CHUNK, width - at)
-                out_ref[first // CHUNK + at // CHUNK, p : p + 1, 0:some] = picked[:, at : at + some]
+                left = p // 8 * CHUNK
+                out_ref[first // CHUNK + at // CHUNK, p % 8 : p % 8 + 1, left : left + some] = picked[
+                    :, at : at + some
+                ]
         for at in range(0, width, CHUNK):
             some = min(CHUNK, width - at)
-            upstream = pooled_ref[:, pl.ds(first + at, some)]
-            out_ref[first // CHUNK + at // CHUNK, OWN : OWN + 2, 0:some] = upstream
+            for half in range(some // LANES):
+                upstream = pooled_ref[:, pl.ds(first + at + half * LANES, LANES)]
+                out_ref[first // CHUNK + at // CHUNK, 2 * half : 2 * half + 2, 2 * CHUNK :] = upstream
 
     over_terms(2048, one_chunk)
     more = rows_ref[0, 80:96, :].astype(F32)
     for s in range(1, SHARDS):
         more = jnp.maximum(more, rows_ref[s, 80:96, :].astype(F32))
-    more = jnp.concatenate([more[15:16], more[15:16]], axis=1)
-    tail = jnp.concatenate([more, jnp.zeros((5, CHUNK), F32)], axis=0)
+    tail = jnp.concatenate([more[15:16], jnp.zeros((3, LANES), F32)], axis=0)
     for g in range(GROUPS):
-        out_ref[g, OWN + 2 :, :] = tail
-    out_ref[GROUPS - 1, 0 : OWN + 2, LANES:] = jnp.zeros((OWN + 2, CHUNK - LANES), F32)
+        out_ref[g, 4:8, 2 * CHUNK :] = tail
+    for left in range(LANES, 2 * CHUNK, CHUNK):
+        out_ref[GROUPS - 1, :, left : left + LANES] = jnp.zeros((8, LANES), F32)
+    out_ref[GROUPS - 1, 2:4, 2 * CHUNK :] = jnp.zeros((2, LANES), F32)
 
 
 def slope_body(part_ref, bias_ref, out_ref, more_ref):
     logits = []
     upstream = []
     for c in range(2):
-        total = part_ref[c, 0:OWN, :]
+        total = part_ref[c, :, 0 : 2 * CHUNK]
         for m in range(1, CHIPS):
-            total = total + part_ref[2 * m + c, 0:OWN, :]
-        logits.append(total)
-        upstream += [part_ref[2 * m + c, OWN : OWN + 2, :] for m in range(CHIPS)]
+            total = total + part_ref[2 * m + c, :, 0 : 2 * CHUNK]
+        logits += [total[:, :CHUNK], total[:, CHUNK:]]
+        for m in range(CHIPS):
+            halves = part_ref[2 * m + c, :, 2 * CHUNK :]
+            upstream.append(jnp.concatenate([halves[0:2], halves[2:4]], axis=1))
     logits = jnp.concatenate(logits, axis=0) + bias_ref[...]
     upstream = jnp.concatenate(upstream, axis=0)
     softened = jnp.maximum(logits, 0.0) + jnp.log1p(jnp.exp(-jnp.abs(logits)))
@@ -244,10 +251,10 @@
     slope = sigmoid / (1.0 + softened)
     mean_pooled = jnp.sum(pooled, axis=0, keepdims=True) / PASSAGES
     grad = ((upstream + mean_pooled) * slope).astype(BF16)
-    more = part_ref[0, OWN : OWN + 8, 0:LANES]
+    more = part_ref[0, :, 2 * CHUNK :]
     for g in range(1, GROUPS):
-        more = jnp.maximum(more, part_ref[g, OWN : OWN + 8, 0:LANES])
-    more_ref[...] = more[2:3]
+        more = jnp.maximum(more, part_ref[g, :, 2 * CHUNK :])
+    more_ref[...] = more[4:5]
     for g in range(GROUPS):
         out_ref[g] = grad[g % 2 * OWN : g % 2 * OWN + OWN]
 
@@ -382,9 +389,10 @@
 def sum_body(place_ref, part_ref, out_ref):
     swap = place_ref[1] == 1
     for m in range(CHIPS):
-        total = part_ref[m * SHARDS].astype(F32)
-        for s in range(1, SHARDS):
-            total = total + part_ref[m * SHARDS + s].astype(F32)
+        total = part_ref[m * SHARDS // 2].astype(F32)
+        for s in range(1, SHARDS // 2):
+            total = total + part_ref[m * SHARDS // 2 + s].astype(F32)
+        total = total[:ROWS] + total[ROWS:]
         other = jnp.concatenate([total[:, COLS:], total[:, :COLS]], axis=1)
         out_ref[:, m * PAIR : (m + 1) * PAIR] = jnp.where(swap, other, total).astype(BF16)
 
@@ -468,7 +476,7 @@
     partial = call(
         logits_body,
         "logits",
-        shape((GROUPS, 24, CHUNK), F32),
+        shape((GROUPS, 8, 2 * CHUNK + LANES), F32),
         [
             pltpu.VMEM((OWN * SEQ, PAIR), BF16),
             pltpu.VMEM((PAIR, VOC), BF16),
@@ -544,7 +552,7 @@
     )(token_grad, all_grad, other_grad, own_index, other_index, keep, got)
     hidden_grad = call(
         sum_body, "sum_shards", shape((ROWS, WIDTH), BF16), specs=[SMEM, VMEM], room=8
-    )(place, hidden_got)
+    )(place, hidden_got.reshape(CHIPS * SHARDS // 2, 2 * ROWS, PAIR))
     return hidden_grad, embedding_grad, bias_grad.reshape(VOC)
 
 

time: 125 us -> 124 us (level)
  no operation moved by 1% of the time
where the time goes in v13:
time: 124 us; the launch traced here: 123 us
  starting transfers between devices  52.5 us (42%)
  Pallas kernels  32.3 us (26%)
  waiting for transfers between devices  24.5 us (20%)
  blocking collectives  12.4 us (10%)
    all_to_all x4, starting transfers between devices, exchange(): return lax.all_to_all(x, axis, split_axis=0, concat_axis=0, tiled=True)  41.5 us
    all_to_all x4, waiting for transfers between devices, exchange(): return lax.all_to_all(x, axis, split_axis=0, concat_axis=0, tiled=True)  22.1 us
    all_to_all x1, blocking collectives, exchange(): return lax.all_to_all(x, axis, split_axis=0, concat_axis=0, tiled=True)  12.4 us
    pallas_call x1, Pallas kernels, on_device(): call(embed_body, 'embedding_grad', (shape((COLS, VOC), F32), shape((1, VO...  11.8 us
    ppermute x4, starting transfers between devices, swap_over(): return lax.ppermute(x, axis, [(0, 1), (1, 0)])  10.9 us
    pallas_call x1, Pallas kernels, on_device(): call(hidden_body, 'hidden_grad', shape((OWN * SEQ, PAIR), BF16), [pltpu.V...  5.98 us
    pallas_call x1, Pallas kernels, on_device(): call(logits_body, 'logits', shape((GROUPS, 8, 2 * CHUNK + LANES), F32), [...  5.16 us
    pallas_call x1, Pallas kernels, on_device(): call(token_body, 'token_grad', shape((COLS, 4096), F32), [pltpu.VMEM((512...  3.2 us
  transfers between devices with their start and end apart: 8, of which 6 were waited for; matrix products, arithmetic and copies ran while one was open for 1% of the time, Pallas kernels for 14%

profile of v13, /device:TPU:1, one launch (start us, length us, event | category | flops | bytes accessed | tf_op | source)
XLA Modules:
  0.0 123.3 jit_solution(15165759526062018311)
XLA Ops:
  0.6 1.6 %pack.1 = bf16[8,96,128]{2,1,0:T(8,128)(2,1)} custom-call(s32[2]{0:T(128)} %lengths.1, s32[8]{0:T(128)} %ids.1, bf16[8,1024]{1,0:T(8,128)(2,1)} %hidden.1, bf16[8,1024]{1,0:T(8,128)(2,1)} %grad.1, s32[2,3968]{1,0:T(2,128)} %index.1), custom_call_target="tpu_custom_call" | custom-call | bytes 3700000 | tf_op jit(solution)/shard_map/pack/pallas_call | solution.py:450
  2.3 12.4 %all_to_all.25.got_ref.own_index = bf16[8,96,128]{2,1,0:T(8,128)(2,1)S(1)} all-to-all(bf16[8,96,128]{2,1,0:T(8,128)(2,1)} %pack.1), channel_id=1, replica_groups=mesh['zl'=2,'x'=4,'core'=2,'zh'=4,'y'=8] {'zl','x'}, dimensions={0} | all-to-all | bytes 393216 | tf_op jit(solution)/shard_map/all_to_all | solution.py:419
  14.7 1.5 %spread.1 = (bf16[32,96,128]{2,1,0:T(8,128)(2,1)}, bf16[80,128]{1,0:T(8,128)(2,1)S(1)}) custom-call(bf16[8,96,128]{2,1,0:T(8,128)(2,1)S(1)} %all_to_all.25.got_ref.own_index), custom_call_target="tpu_custom_call" | custom-call | bytes 3700000 | tf_op jit(solution)/shard_map/spread/pallas_call | solution.py:467
  16.2 15.0 %all-to-all-start.1 = ((bf16[32,96,128]{2,1,0:T(8,128)(2,1)}), bf16[32,96,128]{2,1,0:T(8,128)(2,1)S(1)}, u32[]{:S(2)}, u32[]{:S(2)}) async-start(bf16[32,96,128]{2,1,0:T(8,128)(2,1)} %get-tuple-element.102), calls=%async_computation.1 | async-start | bytes 1572864 | tf_op jit(solution)/shard_map/all_to_all | solution.py:419
  31.2 4.2 %collective-permute-start.2 = (bf16[64,3968]{1,0:T(8,128)(2,1)S(1)}, bf16[64,3968]{1,0:T(8,128)(2,1)S(1)}, u32[]{:S(2)}, u32[]{:S(2)}) collective-permute-start(bf16[64,3968]{1,0:T(8,128)(2,1)S(1)} %copy-done), channel_id=1, source_target_pairs={{0,32},{32,0},{1,33},{33,1},{2,34},{34,2},{3,35},{35,3},{4,36},{36... | collective-permute-start | bytes 1523720 | tf_op jit(solution)/shard_map/ppermute | solution.py:423
  35.4 1.5 %collective-permute-done.2.other_ref = bf16[64,3968]{1,0:T(8,128)(2,1)S(1)} collective-permute-done((bf16[64,3968]{1,0:T(8,128)(2,1)S(1)}, bf16[64,3968]{1,0:T(8,128)(2,1)S(1)}, u32[]{:S(2)}, u32[]{:S(2)}) %collective-permute-start.2) | collective-permute-done | bytes 507936 | tf_op jit(solution)/shard_map/ppermute | solution.py:423
  36.9 13.9 %all-to-all-done.1.rows_ref = bf16[32,96,128]{2,1,0:T(8,128)(2,1)S(1)} async-done(((bf16[32,96,128]{2,1,0:T(8,128)(2,1)}), bf16[32,96,128]{2,1,0:T(8,128)(2,1)S(1)}, u32[]{:S(2)}, u32[]{:S(2)}) %all-to-all-start.1) | async-done | bytes 786464 | tf_op jit(solution)/shard_map/all_to_all | solution.py:419
  50.8 5.2 %logits.1 = f32[16,8,640]{2,1,0:T(8,128)} custom-call(bf16[32,96,128]{2,1,0:T(8,128)(2,1)S(1)} %all-to-all-done.1.rows_ref, bf16[8,96,128]{2,1,0:T(8,128)(2,1)S(1)} %all_to_all.25.got_ref.own_index, bf16[64,3968]{1,0:T(8,128)(2,1)S(1)} %copy-done, bf16[64,3968]{1,0:T(8,128)(2,1)S(1)} %collective-permute-done.2.other_ref, f32[2,3968]{1,0:T(2,128)S(1)} %copy-done.1), custom_call_target="tpu_custom_call" | custom-call | bytes 22200000 | tf_op jit(solution)/shard_map/logits/pallas_call | solution.py:476
  55.9 8.6 %all-to-all-start.2 = ((f32[16,8,640]{2,1,0:T(8,128)}), f32[16,8,640]{2,1,0:T(8,128)S(1)}, u32[]{:S(2)}, u32[]{:S(2)}) async-start(f32[16,8,640]{2,1,0:T(8,128)} %logits.1), calls=%async_computation.2 | async-start | bytes 655360 | tf_op jit(solution)/shard_map/all_to_all | solution.py:419
  64.5 1.1 turn.1
  65.6 2.2 %collective-permute-start.3 = (bf16[16,112,128]{2,1,0:T(8,128)(2,1)}, bf16[16,112,128]{2,1,0:T(8,128)(2,1)S(1)}, u32[]{:S(2)}, u32[]{:S(2)}) collective-permute-start(bf16[16,112,128]{2,1,0:T(8,128)(2,1)} %get-tuple-element.107), channel_id=1, source_target_pairs={{0,32},{32,0},{1,33},{33,1},{2,34},{34,2},{3,35},{35,3},{4,36},{36... | collective-permute-start | bytes 1376264 | tf_op jit(solution)/shard_map/ppermute | solution.py:423
  67.9 4.4 %all-to-all-done.2.part_ref = f32[16,8,640]{2,1,0:T(8,128)S(1)} async-done(((f32[16,8,640]{2,1,0:T(8,128)}), f32[16,8,640]{2,1,0:T(8,128)S(1)}, u32[]{:S(2)}, u32[]{:S(2)}) %all-to-all-start.2) | async-done | bytes 327712 | tf_op jit(solution)/shard_map/all_to_all | solution.py:419
  72.3 0.7 slope.1
  73.0 4.5 %all-to-all-start.3 = ((bf16[16,16,256]{2,1,0:T(8,128)(2,1)}), bf16[16,16,256]{2,1,0:T(8,128)(2,1)S(1)}, u32[]{:S(2)}, u32[]{:S(2)}) async-start(bf16[16,16,256]{2,1,0:T(8,128)(2,1)} %get-tuple-element.105), calls=%async_computation.3 | async-start | bytes 262144 | tf_op jit(solution)/shard_map/all_to_all | solution.py:419
  77.4 2.1 %collective-permute-start.4 = (bf16[8,96,128]{2,1,0:T(8,128)(2,1)S(1)}, bf16[8,96,128]{2,1,0:T(8,128)(2,1)S(1)}, u32[]{:S(2)}, u32[]{:S(2)}) collective-permute-start(bf16[8,96,128]{2,1,0:T(8,128)(2,1)S(1)} %all_to_all.25.got_ref.own_index), channel_id=1, source_target_pairs={{0,32},{32,0},{1,33},{33,1},{2,34},{34,2},{3,35},{35,3},{4,36},{36... | collective-permute-start | bytes 589832 | tf_op jit(solution)/shard_map/ppermute | solution.py:423
  79.7 3.2 %token_grad.1 = f32[64,4096]{1,0:T(8,128)} custom-call(s32[4]{0:T(128)S(1)} %pad_add_fusion.place_ref, bf16[16,112,128]{2,1,0:T(8,128)(2,1)S(1)} %get-tuple-element.106.keep_ref, bf16[16,112,128]{2,1,0:T(8,128)(2,1)S(1)} %collective-permute-done.3.got_ref), custom_call_target="tpu_custom_call" | custom-call | bytes 18500000 | tf_op jit(solution)/shard_map/token_grad/pallas_call | solution.py:509
  82.9 0.8 all-to-all-done.3.grad_ref.own_grad
  83.7 6.0 %hidden_grad.1 = bf16[2048,128]{1,0:T(8,128)(2,1)} custom-call(bf16[16,16,256]{2,1,0:T(8,128)(2,1)S(1)} %all-to-all-done.3.grad_ref.own_grad, bf16[8,96,128]{2,1,0:T(8,128)(2,1)S(1)} %all_to_all.25.got_ref.own_index, bf16[64,3968]{1,0:T(8,128)(2,1)S(1)} %copy-done, bf16[64,3968]{1,0:T(8,128)(2,1)S(1)} %collective-permute-done.2.other_ref), custom_call_target="tpu_custom_call" | custom-call | bytes 22200000 | tf_op jit(solution)/shard_map/hidden_grad/pallas_call | solution.py:523
  89.7 13.5 %all-to-all-start.4 = ((bf16[256,8,128]{2,1,0:T(8,128)(2,1)}), bf16[256,8,128]{2,1,0:T(8,128)(2,1)S(1)}, u32[]{:S(2)}, u32[]{:S(2)}) async-start(bf16[256,8,128]{2,1,0:T(8,128)(2,1)} %bitcast.9), calls=%async_computation.4 | async-start | bytes 1048576 | tf_op jit(solution)/shard_map/all_to_all | solution.py:419
  103.2 2.4 %collective-permute-start.5 = (bf16[16,16,256]{2,1,0:T(8,128)(2,1)S(1)}, bf16[16,16,256]{2,1,0:T(8,128)(2,1)S(1)}, u32[]{:S(2)}, u32[]{:S(2)}) collective-permute-start(bf16[16,16,256]{2,1,0:T(8,128)(2,1)S(1)} %all-to-all-done.3.grad_ref.own_grad), channel_id=1, source_target_pairs={{0,32},{32,0},{1,33},{33,1},{2,34},{34,2},{3,35},{35,3},{4,36},{36... | collective-permute-start | bytes 393224 | tf_op jit(solution)/shard_map/ppermute | solution.py:423
  105.6 0.9 collective-permute-done.5.other_grad
  106.5 11.8 %embedding_grad.1 = (f32[64,3968]{1,0:T(8,128)}, f32[1,3968]{1,0:T(1,128)S(1)}) custom-call(f32[64,4096]{1,0:T(8,128)} %get-tuple-element.158.token_ref, bf16[16,16,256]{2,1,0:T(8,128)(2,1)S(1)} %all-to-all-done.3.grad_ref.own_grad, bf16[16,16,256]{2,1,0:T(8,128)(2,1)S(1)} %collective-permute-done.5.other_grad, ...), custom_call_target="tpu_custom_call" | custom-call | bytes 40700000 | tf_op jit(solution)/shard_map/embedding_grad/pallas_call | solution.py:540
  118.9 3.1 %all-to-all-done.4 = bf16[256,8,128]{2,1,0:T(8,128)(2,1)S(1)} async-done(((bf16[256,8,128]{2,1,0:T(8,128)(2,1)}), bf16[256,8,128]{2,1,0:T(8,128)(2,1)S(1)}, u32[]{:S(2)}, u32[]{:S(2)}) %all-to-all-start.4) | async-done | bytes 524320 | tf_op jit(solution)/shard_map/all_to_all | solution.py:419
  122.0 1.3 %sum_shards.1 = bf16[8,1024]{1,0:T(8,128)(2,1)} custom-call(s32[4]{0:T(128)S(1)} %pad_add_fusion.place_ref, bf16[128,16,128]{2,1,0:T(8,128)(2,1)S(1)} %bitcast.17), custom_call_target="tpu_custom_call" | custom-call | bytes 3700000 | tf_op jit(solution)/shard_map/sum_shards/pallas_call | solution.py:553
  (13 shorter events, 0.8 us)
Async XLA Ops:
  16.2 15.0 %copy-start = (bf16[64,3968]{1,0:T(8,128)(2,1)S(1)}, bf16[64,3968]{1,0:T(8,128)(2,1)}, u32[]{:S(2)}) copy-start(bf16[64,3968]{1,0:T(8,128)(2,1)} %own_ref.3) | copy-start | bytes 1523716
  16.2 34.6 %copy-start.1 = (f32[2,3968]{1,0:T(2,128)S(1)}, f32[2,3968]{1,0:T(2,128)}, u32[]{:S(2)}) copy-start(f32[2,3968]{1,0:T(2,128)} %pooled_ref.1) | copy-start | bytes 95236
  16.2 34.6 %all-to-all-start.1 = ((bf16[32,96,128]{2,1,0:T(8,128)(2,1)}), bf16[32,96,128]{2,1,0:T(8,128)(2,1)S(1)}, u32[]{:S(2)}, u32[]{:S(2)}) async-start(bf16[32,96,128]{2,1,0:T(8,128)(2,1)} %get-tuple-element.102), calls=%async_computation.1 | async-start | bytes 1572864 | tf_op jit(solution)/shard_map/all_to_all | solution.py:419
  31.2 5.7 %collective-permute-start.2 = (bf16[64,3968]{1,0:T(8,128)(2,1)S(1)}, bf16[64,3968]{1,0:T(8,128)(2,1)S(1)}, u32[]{:S(2)}, u32[]{:S(2)}) collective-permute-start(bf16[64,3968]{1,0:T(8,128)(2,1)S(1)} %copy-done), channel_id=1, source_target_pairs={{0,32},{32,0},{1,33},{33,1},{2,34},{34,2},{3,35},{35,3},{4,36},{36... | collective-permute-start | bytes 1523720 | tf_op jit(solution)/shard_map/ppermute | solution.py:423
  55.9 16.3 %all-to-all-start.2 = ((f32[16,8,640]{2,1,0:T(8,128)}), f32[16,8,640]{2,1,0:T(8,128)S(1)}, u32[]{:S(2)}, u32[]{:S(2)}) async-start(f32[16,8,640]{2,1,0:T(8,128)} %logits.1), calls=%async_computation.2 | async-start | bytes 655360 | tf_op jit(solution)/shard_map/all_to_all | solution.py:419
  65.6 2.3 %copy-start.2 = (f32[3968]{0:T(1024)S(1)}, f32[3968]{0:T(1024)}, u32[]{:S(2)}) copy-start(f32[3968]{0:T(1024)} %param.20) | copy-start | bytes 47620
  65.6 14.1 %collective-permute-start.3 = (bf16[16,112,128]{2,1,0:T(8,128)(2,1)}, bf16[16,112,128]{2,1,0:T(8,128)(2,1)S(1)}, u32[]{:S(2)}, u32[]{:S(2)}) collective-permute-start(bf16[16,112,128]{2,1,0:T(8,128)(2,1)} %get-tuple-element.107), channel_id=1, source_target_pairs={{0,32},{32,0},{1,33},{33,1},{2,34},{34,2},{3,35},{35,3},{4,36},{36... | collective-permute-start | bytes 1376264 | tf_op jit(solution)/shard_map/ppermute | solution.py:423
  73.0 10.7 %all-to-all-start.3 = ((bf16[16,16,256]{2,1,0:T(8,128)(2,1)}), bf16[16,16,256]{2,1,0:T(8,128)(2,1)S(1)}, u32[]{:S(2)}, u32[]{:S(2)}) async-start(bf16[16,16,256]{2,1,0:T(8,128)(2,1)} %get-tuple-element.105), calls=%async_computation.3 | async-start | bytes 262144 | tf_op jit(solution)/shard_map/all_to_all | solution.py:419
  77.4 5.4 %collective-permute-start.4 = (bf16[8,96,128]{2,1,0:T(8,128)(2,1)S(1)}, bf16[8,96,128]{2,1,0:T(8,128)(2,1)S(1)}, u32[]{:S(2)}, u32[]{:S(2)}) collective-permute-start(bf16[8,96,128]{2,1,0:T(8,128)(2,1)S(1)} %all_to_all.25.got_ref.own_index), channel_id=1, source_target_pairs={{0,32},{32,0},{1,33},{33,1},{2,34},{34,2},{3,35},{35,3},{4,36},{36... | collective-permute-start | bytes 589832 | tf_op jit(solution)/shard_map/ppermute | solution.py:423
  89.7 32.4 %all-to-all-start.4 = ((bf16[256,8,128]{2,1,0:T(8,128)(2,1)}), bf16[256,8,128]{2,1,0:T(8,128)(2,1)S(1)}, u32[]{:S(2)}, u32[]{:S(2)}) async-start(bf16[256,8,128]{2,1,0:T(8,128)(2,1)} %bitcast.9), calls=%async_computation.4 | async-start | bytes 1048576 | tf_op jit(solution)/shard_map/all_to_all | solution.py:419
  103.2 3.3 %collective-permute-start.5 = (bf16[16,16,256]{2,1,0:T(8,128)(2,1)S(1)}, bf16[16,16,256]{2,1,0:T(8,128)(2,1)S(1)}, u32[]{:S(2)}, u32[]{:S(2)}) collective-permute-start(bf16[16,16,256]{2,1,0:T(8,128)(2,1)S(1)} %all-to-all-done.3.grad_ref.own_grad), channel_id=1, source_target_pairs={{0,32},{32,0},{1,33},{33,1},{2,34},{34,2},{3,35},{35,3},{4,36},{36... | collective-permute-start | bytes 393224 | tf_op jit(solution)/shard_map/ppermute | solution.py:423

commit v14 on v13

--- a/solution.py
+++ b/solution.py
@@ -167,6 +167,12 @@
                 out[2 * four + part, COLS + 32 :, :] = digits
 
 
+def ready_body(got_ref, own_ref, other_ref, spots_ref, embed_ref):
+    load_spots(got_ref, spots_ref)
+    embed_ref[0:COLS, :] = own_ref[...]
+    embed_ref[COLS:, :] = other_ref[...]
+
+
 def over_terms(step, one_chunk):
     full = VOC // step
 
@@ -179,12 +185,9 @@
 
 
 def logits_body(
-    rows_ref, got_ref, own_ref, other_ref, pooled_ref, out_ref, hidden_ref, embed_ref, spots
+    rows_ref, spots, embed_ref, pooled_ref, out_ref, hidden_ref
 ):
     here = lax.broadcasted_iota(I32, (8, 1), 0)
-    embed_ref[0:COLS, :] = own_ref[...]
-    embed_ref[COLS:, :] = other_ref[...]
-    load_spots(got_ref, spots)
     for two in range(CHIPS // 2):
         for h in range(2):
             rows = rows_ref[h * 16 : h * 16 + 16, two * 16 : two * 16 + 16, :].astype(F32)
@@ -260,13 +263,10 @@
 
 
 def hidden_body(
-    grad_ref, got_ref, own_ref, other_ref, out_ref, total, left, embed_ref, grads, spots
+    grad_ref, spots, embed_ref, out_ref, total, left, grads
 ):
     here = lax.broadcasted_iota(I32, (SEQ, LANES), 0).astype(I16)
     zero = jnp.zeros((), BF16)
-    load_spots(got_ref, spots)
-    embed_ref[0:COLS, :] = own_ref[...]
-    embed_ref[COLS:, :] = other_ref[...]
     total[...] = jnp.zeros_like(total)
 
     def one_chunk(first, width):
@@ -358,9 +358,8 @@
 
 
 def embed_body(
-    token_ref, own_grad, other_grad, own_index, other_index, keep_ref, got_ref, out_ref, bias_ref, grads, own_spots, other_spots
+    token_ref, own_grad, other_grad, own_spots, other_index, keep_ref, got_ref, out_ref, bias_ref, grads, other_spots
 ):
-    load_spots(own_index, own_spots)
     load_spots(other_index, other_spots)
     for g in range(GROUPS):
         grads[g, 0:OWN, :] = own_grad[g].astype(F32)
@@ -473,18 +472,22 @@
     )(own_index)
     all_rows = exchange(rows, SHARD)
     other_embed = swap_over(embedding, "core")
+    spots, embed = call(
+        ready_body,
+        "ready",
+        (shape((CHIPS, 64, LANES), I32), shape((PAIR, VOC), BF16)),
+        specs=[VMEM] * 3,
+        us=2,
+        room=8,
+    )(own_index, embedding, other_embed)
     partial = call(
         logits_body,
         "logits",
         shape((GROUPS, 8, 2 * CHUNK + LANES), F32),
-        [
-            pltpu.VMEM((OWN * SEQ, PAIR), BF16),
-            pltpu.VMEM((PAIR, VOC), BF16),
-            pltpu.VMEM((CHIPS, 64, LANES), I32),
-        ],
-        [VMEM] * 5,
+        [pltpu.VMEM((OWN * SEQ, PAIR), BF16)],
+        [VMEM] * 4,
         us=6,
-    )(all_rows, own_index, embedding, other_embed, pooled_grad)
+    )(all_rows, spots, embed, pooled_grad)
     keep, send = call(
         turn_body,
         "turn",
@@ -527,13 +530,11 @@
         [
             pltpu.VMEM((OWN * SEQ, PAIR), F32),
             pltpu.VMEM((OWN * SEQ, 1024), BF16),
-            pltpu.VMEM((PAIR, VOC), BF16),
             pltpu.VMEM((OWN, 1024), F32),
-            pltpu.VMEM((CHIPS, 64, LANES), I32),
         ],
-        [VMEM] * 4,
+        [VMEM] * 3,
         us=6,
-    )(all_grad, own_index, embedding, other_embed)
+    )(all_grad, spots, embed)
     token_grad = lax.cond(more[0, 0] > 0.0, add_rest, lambda total, rest: total, token_grad, rest)
     hidden_got = exchange(hidden_parts.reshape(CHIPS * SHARDS, ROWS, PAIR), HOME)
     other_grad = swap_over(all_grad, "core")
@@ -544,12 +545,11 @@
         [
             pltpu.VMEM((GROUPS, PASSAGES, CHUNK), F32),
             pltpu.VMEM((CHIPS, 64, LANES), I32),
-            pltpu.VMEM((CHIPS, 64, LANES), I32),
         ],
         [VMEM] * 7,
         us=11,
         room=24,
-    )(token_grad, all_grad, other_grad, own_index, other_index, keep, got)
+    )(token_grad, all_grad, other_grad, spots, other_index, keep, got)
     hidden_grad = call(
         sum_body, "sum_shards", shape((ROWS, WIDTH), BF16), specs=[SMEM, VMEM], room=8
     )(place, hidden_got.reshape(CHIPS * SHARDS // 2, 2 * ROWS, PAIR))

time: 124 us -> 124 us (level)
  no operation moved by 1% of the time
where the time goes in v14:
time: 124 us; the launch traced here: 123 us
  starting transfers between devices  52.5 us (42%)
  Pallas kernels  32.3 us (26%)
  waiting for transfers between devices  24.5 us (20%)
  blocking collectives  12.4 us (10%)
    all_to_all x4, starting transfers between devices, exchange(): return lax.all_to_all(x, axis, split_axis=0, concat_axis=0, tiled=True)  41.6 us
    all_to_all x4, waiting for transfers between devices, exchange(): return lax.all_to_all(x, axis, split_axis=0, concat_axis=0, tiled=True)  22 us
    all_to_all x1, blocking collectives, exchange(): return lax.all_to_all(x, axis, split_axis=0, concat_axis=0, tiled=True)  12.4 us
    pallas_call x1, Pallas kernels, on_device(): call(embed_body, 'embedding_grad', (shape((COLS, VOC), F32), shape((1, VO...  11.8 us
    ppermute x4, starting transfers between devices, swap_over(): return lax.ppermute(x, axis, [(0, 1), (1, 0)])  10.9 us
    pallas_call x1, Pallas kernels, on_device(): call(hidden_body, 'hidden_grad', shape((OWN * SEQ, PAIR), BF16), [pltpu.V...  5.92 us
    pallas_call x1, Pallas kernels, on_device(): call(logits_body, 'logits', shape((GROUPS, 8, 2 * CHUNK + LANES), F32), [...  5.14 us
    pallas_call x1, Pallas kernels, on_device(): call(token_body, 'token_grad', shape((COLS, 4096), F32), [pltpu.VMEM((512...  3.21 us
  transfers between devices with their start and end apart: 8, of which 6 were waited for; matrix products, arithmetic and copies ran while one was open for 1% of the time, Pallas kernels for 14%

profile of v14, /device:TPU:1, one launch (start us, length us, event | category | flops | bytes accessed | tf_op | source)
XLA Modules:
  0.0 123.3 jit_solution(10205904446340757410)
XLA Ops:
  0.6 1.6 %pack.1 = bf16[8,96,128]{2,1,0:T(8,128)(2,1)} custom-call(s32[2]{0:T(128)} %lengths.1, s32[8]{0:T(128)} %ids.1, bf16[8,1024]{1,0:T(8,128)(2,1)} %hidden.1, bf16[8,1024]{1,0:T(8,128)(2,1)} %grad.1, s32[2,3968]{1,0:T(2,128)} %index.1), custom_call_target="tpu_custom_call" | custom-call | bytes 3700000 | tf_op jit(solution)/shard_map/pack/pallas_call | solution.py:449
  2.3 12.4 %all_to_all.25.got_ref = bf16[8,96,128]{2,1,0:T(8,128)(2,1)S(1)} all-to-all(bf16[8,96,128]{2,1,0:T(8,128)(2,1)} %pack.1), channel_id=1, replica_groups=mesh['zl'=2,'x'=4,'core'=2,'zh'=4,'y'=8] {'zl','x'}, dimensions={0} | all-to-all | bytes 393216 | tf_op jit(solution)/shard_map/all_to_all | solution.py:418
  14.7 1.5 %spread.1 = (bf16[32,96,128]{2,1,0:T(8,128)(2,1)}, bf16[80,128]{1,0:T(8,128)(2,1)S(1)}) custom-call(bf16[8,96,128]{2,1,0:T(8,128)(2,1)S(1)} %all_to_all.25.got_ref), custom_call_target="tpu_custom_call" | custom-call | bytes 3700000 | tf_op jit(solution)/shard_map/spread/pallas_call | solution.py:466
  16.2 15.0 %all-to-all-start.1 = ((bf16[32,96,128]{2,1,0:T(8,128)(2,1)}), bf16[32,96,128]{2,1,0:T(8,128)(2,1)S(1)}, u32[]{:S(2)}, u32[]{:S(2)}) async-start(bf16[32,96,128]{2,1,0:T(8,128)(2,1)} %get-tuple-element.104), calls=%async_computation.1 | async-start | bytes 1572864 | tf_op jit(solution)/shard_map/all_to_all | solution.py:418
  31.2 4.2 %collective-permute-start.2 = (bf16[64,3968]{1,0:T(8,128)(2,1)S(1)}, bf16[64,3968]{1,0:T(8,128)(2,1)S(1)}, u32[]{:S(2)}, u32[]{:S(2)}) collective-permute-start(bf16[64,3968]{1,0:T(8,128)(2,1)S(1)} %copy-done), channel_id=1, source_target_pairs={{0,32},{32,0},{1,33},{33,1},{2,34},{34,2},{3,35},{35,3},{4,36},{36... | collective-permute-start | bytes 1523720 | tf_op jit(solution)/shard_map/ppermute | solution.py:422
  35.4 1.5 %collective-permute-done.2.other_ref = bf16[64,3968]{1,0:T(8,128)(2,1)S(1)} collective-permute-done((bf16[64,3968]{1,0:T(8,128)(2,1)S(1)}, bf16[64,3968]{1,0:T(8,128)(2,1)S(1)}, u32[]{:S(2)}, u32[]{:S(2)}) %collective-permute-start.2) | collective-permute-done | bytes 507936 | tf_op jit(solution)/shard_map/ppermute | solution.py:422
  37.0 13.7 %all-to-all-done.1.rows_ref = bf16[32,96,128]{2,1,0:T(8,128)(2,1)S(1)} async-done(((bf16[32,96,128]{2,1,0:T(8,128)(2,1)}), bf16[32,96,128]{2,1,0:T(8,128)(2,1)S(1)}, u32[]{:S(2)}, u32[]{:S(2)}) %all-to-all-start.1) | async-done | bytes 786464 | tf_op jit(solution)/shard_map/all_to_all | solution.py:418
  50.8 5.1 %logits.1 = f32[16,8,640]{2,1,0:T(8,128)} custom-call(bf16[32,96,128]{2,1,0:T(8,128)(2,1)S(1)} %all-to-all-done.1.rows_ref, s32[8,64,128]{2,1,0:T(8,128)S(1)} %get-tuple-element.105.spots.own_spots, bf16[128,3968]{1,0:T(8,128)(2,1)S(1)} %get-tuple-element.106.embed_ref, f32[2,3968]{1,0:T(2,128)S(1)} %copy-done.1), custom_call_target="tpu_custom_call" | custom-call | bytes 22200000 | tf_op jit(solution)/shard_map/logits/pallas_call | solution.py:483
  55.9 8.6 %all-to-all-start.2 = ((f32[16,8,640]{2,1,0:T(8,128)}), f32[16,8,640]{2,1,0:T(8,128)S(1)}, u32[]{:S(2)}, u32[]{:S(2)}) async-start(f32[16,8,640]{2,1,0:T(8,128)} %logits.1), calls=%async_computation.2 | async-start | bytes 655360 | tf_op jit(solution)/shard_map/all_to_all | solution.py:418
  64.5 1.1 turn.1
  65.5 2.2 %collective-permute-start.3 = (bf16[16,112,128]{2,1,0:T(8,128)(2,1)}, bf16[16,112,128]{2,1,0:T(8,128)(2,1)S(1)}, u32[]{:S(2)}, u32[]{:S(2)}) collective-permute-start(bf16[16,112,128]{2,1,0:T(8,128)(2,1)} %get-tuple-element.111), channel_id=1, source_target_pairs={{0,32},{32,0},{1,33},{33,1},{2,34},{34,2},{3,35},{35,3},{4,36},{36... | collective-permute-start | bytes 1376264 | tf_op jit(solution)/shard_map/ppermute | solution.py:422
  67.9 4.4 %all-to-all-done.2.part_ref = f32[16,8,640]{2,1,0:T(8,128)S(1)} async-done(((f32[16,8,640]{2,1,0:T(8,128)}), f32[16,8,640]{2,1,0:T(8,128)S(1)}, u32[]{:S(2)}, u32[]{:S(2)}) %all-to-all-start.2) | async-done | bytes 327712 | tf_op jit(solution)/shard_map/all_to_all | solution.py:418
  72.2 0.7 slope.1
  73.0 4.5 %all-to-all-start.3 = ((bf16[16,16,256]{2,1,0:T(8,128)(2,1)}), bf16[16,16,256]{2,1,0:T(8,128)(2,1)S(1)}, u32[]{:S(2)}, u32[]{:S(2)}) async-start(bf16[16,16,256]{2,1,0:T(8,128)(2,1)} %get-tuple-element.109), calls=%async_computation.3 | async-start | bytes 262144 | tf_op jit(solution)/shard_map/all_to_all | solution.py:418
  77.4 2.1 %collective-permute-start.4 = (bf16[8,96,128]{2,1,0:T(8,128)(2,1)S(1)}, bf16[8,96,128]{2,1,0:T(8,128)(2,1)S(1)}, u32[]{:S(2)}, u32[]{:S(2)}) collective-permute-start(bf16[8,96,128]{2,1,0:T(8,128)(2,1)S(1)} %all_to_all.25.got_ref), channel_id=1, source_target_pairs={{0,32},{32,0},{1,33},{33,1},{2,34},{34,2},{3,35},{35,3},{4,36},{36... | collective-permute-start | bytes 589832 | tf_op jit(solution)/shard_map/ppermute | solution.py:422
  79.7 3.2 %token_grad.1 = f32[64,4096]{1,0:T(8,128)} custom-call(s32[4]{0:T(128)S(1)} %pad_add_fusion.place_ref, bf16[16,112,128]{2,1,0:T(8,128)(2,1)S(1)} %get-tuple-element.110.keep_ref, bf16[16,112,128]{2,1,0:T(8,128)(2,1)S(1)} %collective-permute-done.3.got_ref), custom_call_target="tpu_custom_call" | custom-call | bytes 18500000 | tf_op jit(solution)/shard_map/token_grad/pallas_call | solution.py:512
  82.9 0.8 all-to-all-done.3.grad_ref.own_grad
  83.7 5.9 %hidden_grad.1 = bf16[2048,128]{1,0:T(8,128)(2,1)} custom-call(bf16[16,16,256]{2,1,0:T(8,128)(2,1)S(1)} %all-to-all-done.3.grad_ref.own_grad, s32[8,64,128]{2,1,0:T(8,128)S(1)} %get-tuple-element.105.spots.own_spots, bf16[128,3968]{1,0:T(8,128)(2,1)S(1)} %get-tuple-element.106.embed_ref), custom_call_target="tpu_custom_call" | custom-call | bytes 22200000 | tf_op jit(solution)/shard_map/hidden_grad/pallas_call | solution.py:526
  89.6 13.5 %all-to-all-start.4 = ((bf16[256,8,128]{2,1,0:T(8,128)(2,1)}), bf16[256,8,128]{2,1,0:T(8,128)(2,1)S(1)}, u32[]{:S(2)}, u32[]{:S(2)}) async-start(bf16[256,8,128]{2,1,0:T(8,128)(2,1)} %bitcast.9), calls=%async_computation.4 | async-start | bytes 1048576 | tf_op jit(solution)/shard_map/all_to_all | solution.py:418
  103.1 2.3 %collective-permute-start.5 = (bf16[16,16,256]{2,1,0:T(8,128)(2,1)S(1)}, bf16[16,16,256]{2,1,0:T(8,128)(2,1)S(1)}, u32[]{:S(2)}, u32[]{:S(2)}) collective-permute-start(bf16[16,16,256]{2,1,0:T(8,128)(2,1)S(1)} %all-to-all-done.3.grad_ref.own_grad), channel_id=1, source_target_pairs={{0,32},{32,0},{1,33},{33,1},{2,34},{34,2},{3,35},{35,3},{4,36},{36... | collective-permute-start | bytes 393224 | tf_op jit(solution)/shard_map/ppermute | solution.py:422
  105.5 0.9 collective-permute-done.5.other_grad
  106.4 11.8 %embedding_grad.1 = (f32[64,3968]{1,0:T(8,128)}, f32[1,3968]{1,0:T(1,128)S(1)}) custom-call(f32[64,4096]{1,0:T(8,128)} %get-tuple-element.162.token_ref, bf16[16,16,256]{2,1,0:T(8,128)(2,1)S(1)} %all-to-all-done.3.grad_ref.own_grad, bf16[16,16,256]{2,1,0:T(8,128)(2,1)S(1)} %collective-permute-done.5.other_grad, ...), custom_call_target="tpu_custom_call" | custom-call | bytes 40700000 | tf_op jit(solution)/shard_map/embedding_grad/pallas_call | solution.py:541
  118.8 3.1 %all-to-all-done.4 = bf16[256,8,128]{2,1,0:T(8,128)(2,1)S(1)} async-done(((bf16[256,8,128]{2,1,0:T(8,128)(2,1)}), bf16[256,8,128]{2,1,0:T(8,128)(2,1)S(1)}, u32[]{:S(2)}, u32[]{:S(2)}) %all-to-all-start.4) | async-done | bytes 524320 | tf_op jit(solution)/shard_map/all_to_all | solution.py:418
  122.0 1.3 %sum_shards.1 = bf16[8,1024]{1,0:T(8,128)(2,1)} custom-call(s32[4]{0:T(128)S(1)} %pad_add_fusion.place_ref, bf16[128,16,128]{2,1,0:T(8,128)(2,1)S(1)} %bitcast.17), custom_call_target="tpu_custom_call" | custom-call | bytes 3700000 | tf_op jit(solution)/shard_map/sum_shards/pallas_call | solution.py:553
  (14 shorter events, 0.9 us)
Async XLA Ops:
  16.2 15.0 %copy-start = (bf16[64,3968]{1,0:T(8,128)(2,1)S(1)}, bf16[64,3968]{1,0:T(8,128)(2,1)}, u32[]{:S(2)}) copy-start(bf16[64,3968]{1,0:T(8,128)(2,1)} %own_ref.1) | copy-start | bytes 1523716
  16.2 34.6 %all-to-all-start.1 = ((bf16[32,96,128]{2,1,0:T(8,128)(2,1)}), bf16[32,96,128]{2,1,0:T(8,128)(2,1)S(1)}, u32[]{:S(2)}, u32[]{:S(2)}) async-start(bf16[32,96,128]{2,1,0:T(8,128)(2,1)} %get-tuple-element.104), calls=%async_computation.1 | async-start | bytes 1572864 | tf_op jit(solution)/shard_map/all_to_all | solution.py:418
  31.2 19.6 %copy-start.1 = (f32[2,3968]{1,0:T(2,128)S(1)}, f32[2,3968]{1,0:T(2,128)}, u32[]{:S(2)}) copy-start(f32[2,3968]{1,0:T(2,128)} %pooled_ref.1) | copy-start | bytes 95236
  31.2 5.7 %collective-permute-start.2 = (bf16[64,3968]{1,0:T(8,128)(2,1)S(1)}, bf16[64,3968]{1,0:T(8,128)(2,1)S(1)}, u32[]{:S(2)}, u32[]{:S(2)}) collective-permute-start(bf16[64,3968]{1,0:T(8,128)(2,1)S(1)} %copy-done), channel_id=1, source_target_pairs={{0,32},{32,0},{1,33},{33,1},{2,34},{34,2},{3,35},{35,3},{4,36},{36... | collective-permute-start | bytes 1523720 | tf_op jit(solution)/shard_map/ppermute | solution.py:422
  55.9 16.3 %all-to-all-start.2 = ((f32[16,8,640]{2,1,0:T(8,128)}), f32[16,8,640]{2,1,0:T(8,128)S(1)}, u32[]{:S(2)}, u32[]{:S(2)}) async-start(f32[16,8,640]{2,1,0:T(8,128)} %logits.1), calls=%async_computation.2 | async-start | bytes 655360 | tf_op jit(solution)/shard_map/all_to_all | solution.py:418
  65.5 2.3 %copy-start.2 = (f32[3968]{0:T(1024)S(1)}, f32[3968]{0:T(1024)}, u32[]{:S(2)}) copy-start(f32[3968]{0:T(1024)} %param.20) | copy-start | bytes 47620
  65.5 14.1 %collective-permute-start.3 = (bf16[16,112,128]{2,1,0:T(8,128)(2,1)}, bf16[16,112,128]{2,1,0:T(8,128)(2,1)S(1)}, u32[]{:S(2)}, u32[]{:S(2)}) collective-permute-start(bf16[16,112,128]{2,1,0:T(8,128)(2,1)} %get-tuple-element.111), channel_id=1, source_target_pairs={{0,32},{32,0},{1,33},{33,1},{2,34},{34,2},{3,35},{35,3},{4,36},{36... | collective-permute-start | bytes 1376264 | tf_op jit(solution)/shard_map/ppermute | solution.py:422
  73.0 10.7 %all-to-all-start.3 = ((bf16[16,16,256]{2,1,0:T(8,128)(2,1)}), bf16[16,16,256]{2,1,0:T(8,128)(2,1)S(1)}, u32[]{:S(2)}, u32[]{:S(2)}) async-start(bf16[16,16,256]{2,1,0:T(8,128)(2,1)} %get-tuple-element.109), calls=%async_computation.3 | async-start | bytes 262144 | tf_op jit(solution)/shard_map/all_to_all | solution.py:418
  77.4 5.4 %collective-permute-start.4 = (bf16[8,96,128]{2,1,0:T(8,128)(2,1)S(1)}, bf16[8,96,128]{2,1,0:T(8,128)(2,1)S(1)}, u32[]{:S(2)}, u32[]{:S(2)}) collective-permute-start(bf16[8,96,128]{2,1,0:T(8,128)(2,1)S(1)} %all_to_all.25.got_ref), channel_id=1, source_target_pairs={{0,32},{32,0},{1,33},{33,1},{2,34},{34,2},{3,35},{35,3},{4,36},{36... | collective-permute-start | bytes 589832 | tf_op jit(solution)/shard_map/ppermute | solution.py:422
  89.6 32.4 %all-to-all-start.4 = ((bf16[256,8,128]{2,1,0:T(8,128)(2,1)}), bf16[256,8,128]{2,1,0:T(8,128)(2,1)S(1)}, u32[]{:S(2)}, u32[]{:S(2)}) async-start(bf16[256,8,128]{2,1,0:T(8,128)(2,1)} %bitcast.9), calls=%async_computation.4 | async-start | bytes 1048576 | tf_op jit(solution)/shard_map/all_to_all | solution.py:418
  103.1 3.3 %collective-permute-start.5 = (bf16[16,16,256]{2,1,0:T(8,128)(2,1)S(1)}, bf16[16,16,256]{2,1,0:T(8,128)(2,1)S(1)}, u32[]{:S(2)}, u32[]{:S(2)}) collective-permute-start(bf16[16,16,256]{2,1,0:T(8,128)(2,1)S(1)} %all-to-all-done.3.grad_ref.own_grad), channel_id=1, source_target_pairs={{0,32},{32,0},{1,33},{33,1},{2,34},{34,2},{3,35},{35,3},{4,36},{36... | collective-permute-start | bytes 393224 | tf_op jit(solution)/shard_map/ppermute | solution.py:422

commit v15 on v13

--- a/solution.py
+++ b/solution.py
@@ -16,7 +16,7 @@
 
 GROUP = ("zl", "x", "core")
 SHARD = ("zh", "y")
-HOME = ("zl", "x", "zh", "y")
+HOME = ("zh", "y", "zl", "x")
 GROUPS = 16
 SHARDS = 32
 CHIPS = 8
@@ -289,7 +289,14 @@
             )
 
     over_terms(1024, one_chunk)
-    out_ref[...] = total[...].astype(BF16)
+    for two in range(CHIPS // 2):
+        for h in range(2):
+            halves = []
+            for s in range(2):
+                p = (2 * two + s) * 2 + h
+                halves.append(total[p * SEQ : (p + 1) * SEQ, :].reshape(16, ROWS, PAIR))
+            rows = jnp.concatenate(halves, axis=1).astype(BF16)
+            out_ref[h * 16 : h * 16 + 16, two * 16 : two * 16 + 16, :] = rows
 
 
 def rest_body(place_ref, every_ref, swapped_ref, total_ref, out_ref, total):
@@ -388,13 +395,13 @@
 
 def sum_body(place_ref, part_ref, out_ref):
     swap = place_ref[1] == 1
+    total = part_ref[0].astype(F32)
+    for s in range(1, SHARDS):
+        total = total + part_ref[s].astype(F32)
     for m in range(CHIPS):
-        total = part_ref[m * SHARDS // 2].astype(F32)
-        for s in range(1, SHARDS // 2):
-            total = total + part_ref[m * SHARDS // 2 + s].astype(F32)
-        total = total[:ROWS] + total[ROWS:]
-        other = jnp.concatenate([total[:, COLS:], total[:, :COLS]], axis=1)
-        out_ref[:, m * PAIR : (m + 1) * PAIR] = jnp.where(swap, other, total).astype(BF16)
+        pair = total[m * ROWS : (m + 1) * ROWS]
+        other = jnp.concatenate([pair[:, COLS:], pair[:, :COLS]], axis=1)
+        out_ref[:, m * PAIR : (m + 1) * PAIR] = jnp.where(swap, other, pair).astype(BF16)
 
 
 def call(body, name, out, scratch=(), specs=None, us=1, out_specs=None, room=24):
@@ -523,7 +530,7 @@
     hidden_parts = call(
         hidden_body,
         "hidden_grad",
-        shape((OWN * SEQ, PAIR), BF16),
+        shape((SHARDS, CHIPS * ROWS, PAIR), BF16),
         [
             pltpu.VMEM((OWN * SEQ, PAIR), F32),
             pltpu.VMEM((OWN * SEQ, 1024), BF16),
@@ -552,7 +559,7 @@
     )(token_grad, all_grad, other_grad, own_index, other_index, keep, got)
     hidden_grad = call(
         sum_body, "sum_shards", shape((ROWS, WIDTH), BF16), specs=[SMEM, VMEM], room=8
-    )(place, hidden_got.reshape(CHIPS * SHARDS // 2, 2 * ROWS, PAIR))
+    )(place, hidden_got.reshape(SHARDS, CHIPS * ROWS, PAIR))
     return hidden_grad, embedding_grad, bias_grad.reshape(VOC)
 
 

time: 124 us -> 125 us (level)
  no operation moved by 1% of the time
where the time goes in v15:
time: 125 us; the launch traced here: 124 us
  starting transfers between devices  52.5 us (42%)
  Pallas kernels  32.3 us (26%)
  waiting for transfers between devices  25.4 us (20%)
  blocking collectives  12.4 us (10%)
    all_to_all x4, starting transfers between devices, exchange(): return lax.all_to_all(x, axis, split_axis=0, concat_axis=0, tiled=True)  41.5 us
    all_to_all x4, waiting for transfers between devices, exchange(): return lax.all_to_all(x, axis, split_axis=0, concat_axis=0, tiled=True)  23 us
    all_to_all x1, blocking collectives, exchange(): return lax.all_to_all(x, axis, split_axis=0, concat_axis=0, tiled=True)  12.4 us
    pallas_call x1, Pallas kernels, on_device(): call(embed_body, 'embedding_grad', (shape((COLS, VOC), F32), shape((1, VO...  11.8 us
    ppermute x4, starting transfers between devices, swap_over(): return lax.ppermute(x, axis, [(0, 1), (1, 0)])  10.9 us
    pallas_call x1, Pallas kernels, on_device(): call(hidden_body, 'hidden_grad', shape((SHARDS, CHIPS * ROWS, PAIR), BF16...  5.98 us
    pallas_call x1, Pallas kernels, on_device(): call(logits_body, 'logits', shape((GROUPS, 8, 2 * CHUNK + LANES), F32), [...  5.16 us
    pallas_call x1, Pallas kernels, on_device(): call(token_body, 'token_grad', shape((COLS, 4096), F32), [pltpu.VMEM((512...  3.2 us
  transfers between devices with their start and end apart: 8, of which 6 were waited for; matrix products, arithmetic and copies ran while one was open for 1% of the time, Pallas kernels for 14%

profile of v15, /device:TPU:1, one launch (start us, length us, event | category | flops | bytes accessed | tf_op | source)
XLA Modules:
  0.0 124.2 jit_solution(17517494300992166222)
XLA Ops:
  0.6 1.6 %pack.1 = bf16[8,96,128]{2,1,0:T(8,128)(2,1)} custom-call(s32[2]{0:T(128)} %lengths.1, s32[8]{0:T(128)} %ids.1, bf16[8,1024]{1,0:T(8,128)(2,1)} %hidden.1, bf16[8,1024]{1,0:T(8,128)(2,1)} %grad.1, s32[2,3968]{1,0:T(2,128)} %index.1), custom_call_target="tpu_custom_call" | custom-call | bytes 3700000 | tf_op jit(solution)/shard_map/pack/pallas_call | solution.py:457
  2.3 12.4 %all_to_all.25.got_ref.own_index = bf16[8,96,128]{2,1,0:T(8,128)(2,1)S(1)} all-to-all(bf16[8,96,128]{2,1,0:T(8,128)(2,1)} %pack.1), channel_id=1, replica_groups=mesh['zl'=2,'x'=4,'core'=2,'zh'=4,'y'=8] {'zl','x'}, dimensions={0} | all-to-all | bytes 393216 | tf_op jit(solution)/shard_map/all_to_all | solution.py:426
  14.7 1.5 %spread.1 = (bf16[32,96,128]{2,1,0:T(8,128)(2,1)}, bf16[80,128]{1,0:T(8,128)(2,1)S(1)}) custom-call(bf16[8,96,128]{2,1,0:T(8,128)(2,1)S(1)} %all_to_all.25.got_ref.own_index), custom_call_target="tpu_custom_call" | custom-call | bytes 3700000 | tf_op jit(solution)/shard_map/spread/pallas_call | solution.py:474
  16.2 15.0 %all-to-all-start.1 = ((bf16[32,96,128]{2,1,0:T(8,128)(2,1)}), bf16[32,96,128]{2,1,0:T(8,128)(2,1)S(1)}, u32[]{:S(2)}, u32[]{:S(2)}) async-start(bf16[32,96,128]{2,1,0:T(8,128)(2,1)} %get-tuple-element.102), calls=%async_computation.1 | async-start | bytes 1572864 | tf_op jit(solution)/shard_map/all_to_all | solution.py:426
  31.2 4.2 %collective-permute-start.2 = (bf16[64,3968]{1,0:T(8,128)(2,1)S(1)}, bf16[64,3968]{1,0:T(8,128)(2,1)S(1)}, u32[]{:S(2)}, u32[]{:S(2)}) collective-permute-start(bf16[64,3968]{1,0:T(8,128)(2,1)S(1)} %copy-done), channel_id=1, source_target_pairs={{0,32},{32,0},{1,33},{33,1},{2,34},{34,2},{3,35},{35,3},{4,36},{36... | collective-permute-start | bytes 1523720 | tf_op jit(solution)/shard_map/ppermute | solution.py:430
  35.4 1.5 %collective-permute-done.2.other_ref = bf16[64,3968]{1,0:T(8,128)(2,1)S(1)} collective-permute-done((bf16[64,3968]{1,0:T(8,128)(2,1)S(1)}, bf16[64,3968]{1,0:T(8,128)(2,1)S(1)}, u32[]{:S(2)}, u32[]{:S(2)}) %collective-permute-start.2) | collective-permute-done | bytes 507936 | tf_op jit(solution)/shard_map/ppermute | solution.py:430
  36.9 13.9 %all-to-all-done.1.rows_ref = bf16[32,96,128]{2,1,0:T(8,128)(2,1)S(1)} async-done(((bf16[32,96,128]{2,1,0:T(8,128)(2,1)}), bf16[32,96,128]{2,1,0:T(8,128)(2,1)S(1)}, u32[]{:S(2)}, u32[]{:S(2)}) %all-to-all-start.1) | async-done | bytes 786464 | tf_op jit(solution)/shard_map/all_to_all | solution.py:426
  50.8 5.2 %logits.1 = f32[16,8,640]{2,1,0:T(8,128)} custom-call(bf16[32,96,128]{2,1,0:T(8,128)(2,1)S(1)} %all-to-all-done.1.rows_ref, bf16[8,96,128]{2,1,0:T(8,128)(2,1)S(1)} %all_to_all.25.got_ref.own_index, bf16[64,3968]{1,0:T(8,128)(2,1)S(1)} %copy-done, bf16[64,3968]{1,0:T(8,128)(2,1)S(1)} %collective-permute-done.2.other_ref, f32[2,3968]{1,0:T(2,128)S(1)} %copy-done.1), custom_call_target="tpu_custom_call" | custom-call | bytes 22200000 | tf_op jit(solution)/shard_map/logits/pallas_call | solution.py:483
  55.9 8.6 %all-to-all-start.2 = ((f32[16,8,640]{2,1,0:T(8,128)}), f32[16,8,640]{2,1,0:T(8,128)S(1)}, u32[]{:S(2)}, u32[]{:S(2)}) async-start(f32[16,8,640]{2,1,0:T(8,128)} %logits.1), calls=%async_computation.2 | async-start | bytes 655360 | tf_op jit(solution)/shard_map/all_to_all | solution.py:426
  64.5 1.1 turn.1
  65.6 2.2 %collective-permute-start.3 = (bf16[16,112,128]{2,1,0:T(8,128)(2,1)}, bf16[16,112,128]{2,1,0:T(8,128)(2,1)S(1)}, u32[]{:S(2)}, u32[]{:S(2)}) collective-permute-start(bf16[16,112,128]{2,1,0:T(8,128)(2,1)} %get-tuple-element.107), channel_id=1, source_target_pairs={{0,32},{32,0},{1,33},{33,1},{2,34},{34,2},{3,35},{35,3},{4,36},{36... | collective-permute-start | bytes 1376264 | tf_op jit(solution)/shard_map/ppermute | solution.py:430
  67.9 4.4 %all-to-all-done.2.part_ref = f32[16,8,640]{2,1,0:T(8,128)S(1)} async-done(((f32[16,8,640]{2,1,0:T(8,128)}), f32[16,8,640]{2,1,0:T(8,128)S(1)}, u32[]{:S(2)}, u32[]{:S(2)}) %all-to-all-start.2) | async-done | bytes 327712 | tf_op jit(solution)/shard_map/all_to_all | solution.py:426
  72.3 0.7 slope.1
  73.0 4.5 %all-to-all-start.3 = ((bf16[16,16,256]{2,1,0:T(8,128)(2,1)}), bf16[16,16,256]{2,1,0:T(8,128)(2,1)S(1)}, u32[]{:S(2)}, u32[]{:S(2)}) async-start(bf16[16,16,256]{2,1,0:T(8,128)(2,1)} %get-tuple-element.105), calls=%async_computation.3 | async-start | bytes 262144 | tf_op jit(solution)/shard_map/all_to_all | solution.py:426
  77.4 2.1 %collective-permute-start.4 = (bf16[8,96,128]{2,1,0:T(8,128)(2,1)S(1)}, bf16[8,96,128]{2,1,0:T(8,128)(2,1)S(1)}, u32[]{:S(2)}, u32[]{:S(2)}) collective-permute-start(bf16[8,96,128]{2,1,0:T(8,128)(2,1)S(1)} %all_to_all.25.got_ref.own_index), channel_id=1, source_target_pairs={{0,32},{32,0},{1,33},{33,1},{2,34},{34,2},{3,35},{35,3},{4,36},{36... | collective-permute-start | bytes 589832 | tf_op jit(solution)/shard_map/ppermute | solution.py:430
  79.7 3.2 %token_grad.1 = f32[64,4096]{1,0:T(8,128)} custom-call(s32[4]{0:T(128)S(1)} %pad_add_fusion.place_ref, bf16[16,112,128]{2,1,0:T(8,128)(2,1)S(1)} %get-tuple-element.106.keep_ref, bf16[16,112,128]{2,1,0:T(8,128)(2,1)S(1)} %collective-permute-done.3.got_ref), custom_call_target="tpu_custom_call" | custom-call | bytes 18500000 | tf_op jit(solution)/shard_map/token_grad/pallas_call | solution.py:516
  82.9 0.8 all-to-all-done.3.grad_ref.own_grad
  83.7 6.0 %hidden_grad.1 = bf16[32,64,128]{2,1,0:T(8,128)(2,1)} custom-call(bf16[16,16,256]{2,1,0:T(8,128)(2,1)S(1)} %all-to-all-done.3.grad_ref.own_grad, bf16[8,96,128]{2,1,0:T(8,128)(2,1)S(1)} %all_to_all.25.got_ref.own_index, bf16[64,3968]{1,0:T(8,128)(2,1)S(1)} %copy-done, bf16[64,3968]{1,0:T(8,128)(2,1)S(1)} %collective-permute-done.2.other_ref), custom_call_target="tpu_custom_call" | custom-call | bytes 22200000 | tf_op jit(solution)/shard_map/hidden_grad/pallas_call | solution.py:530
  89.7 13.5 %all-to-all-start.4 = ((bf16[256,8,128]{2,1,0:T(8,128)(2,1)}), bf16[256,8,128]{2,1,0:T(8,128)(2,1)S(1)}, u32[]{:S(2)}, u32[]{:S(2)}) async-start(bf16[256,8,128]{2,1,0:T(8,128)(2,1)} %bitcast.9), calls=%async_computation.4 | async-start | bytes 1048576 | tf_op jit(solution)/shard_map/all_to_all | solution.py:426
  103.2 2.4 %collective-permute-start.5 = (bf16[16,16,256]{2,1,0:T(8,128)(2,1)S(1)}, bf16[16,16,256]{2,1,0:T(8,128)(2,1)S(1)}, u32[]{:S(2)}, u32[]{:S(2)}) collective-permute-start(bf16[16,16,256]{2,1,0:T(8,128)(2,1)S(1)} %all-to-all-done.3.grad_ref.own_grad), channel_id=1, source_target_pairs={{0,32},{32,0},{1,33},{33,1},{2,34},{34,2},{3,35},{35,3},{4,36},{36... | collective-permute-start | bytes 393224 | tf_op jit(solution)/shard_map/ppermute | solution.py:430
  105.6 0.9 collective-permute-done.5.other_grad
  106.5 11.8 %embedding_grad.1 = (f32[64,3968]{1,0:T(8,128)}, f32[1,3968]{1,0:T(1,128)S(1)}) custom-call(f32[64,4096]{1,0:T(8,128)} %get-tuple-element.158.token_ref, bf16[16,16,256]{2,1,0:T(8,128)(2,1)S(1)} %all-to-all-done.3.grad_ref.own_grad, bf16[16,16,256]{2,1,0:T(8,128)(2,1)S(1)} %collective-permute-done.5.other_grad, ...), custom_call_target="tpu_custom_call" | custom-call | bytes 40700000 | tf_op jit(solution)/shard_map/embedding_grad/pallas_call | solution.py:547
  118.9 3.9 %all-to-all-done.4 = bf16[256,8,128]{2,1,0:T(8,128)(2,1)S(1)} async-done(((bf16[256,8,128]{2,1,0:T(8,128)(2,1)}), bf16[256,8,128]{2,1,0:T(8,128)(2,1)S(1)}, u32[]{:S(2)}, u32[]{:S(2)}) %all-to-all-start.4) | async-done | bytes 524320 | tf_op jit(solution)/shard_map/all_to_all | solution.py:426
  122.9 1.3 %sum_shards.1 = bf16[8,1024]{1,0:T(8,128)(2,1)} custom-call(s32[4]{0:T(128)S(1)} %pad_add_fusion.place_ref, bf16[32,64,128]{2,1,0:T(8,128)(2,1)S(1)} %bitcast.17), custom_call_target="tpu_custom_call" | custom-call | bytes 3700000 | tf_op jit(solution)/shard_map/sum_shards/pallas_call | solution.py:560
  (13 shorter events, 0.8 us)
Async XLA Ops:
  16.2 15.0 %copy-start = (bf16[64,3968]{1,0:T(8,128)(2,1)S(1)}, bf16[64,3968]{1,0:T(8,128)(2,1)}, u32[]{:S(2)}) copy-start(bf16[64,3968]{1,0:T(8,128)(2,1)} %own_ref.3) | copy-start | bytes 1523716
  16.2 34.6 %copy-start.1 = (f32[2,3968]{1,0:T(2,128)S(1)}, f32[2,3968]{1,0:T(2,128)}, u32[]{:S(2)}) copy-start(f32[2,3968]{1,0:T(2,128)} %pooled_ref.1) | copy-start | bytes 95236
  16.2 34.6 %all-to-all-start.1 = ((bf16[32,96,128]{2,1,0:T(8,128)(2,1)}), bf16[32,96,128]{2,1,0:T(8,128)(2,1)S(1)}, u32[]{:S(2)}, u32[]{:S(2)}) async-start(bf16[32,96,128]{2,1,0:T(8,128)(2,1)} %get-tuple-element.102), calls=%async_computation.1 | async-start | bytes 1572864 | tf_op jit(solution)/shard_map/all_to_all | solution.py:426
  31.2 5.7 %collective-permute-start.2 = (bf16[64,3968]{1,0:T(8,128)(2,1)S(1)}, bf16[64,3968]{1,0:T(8,128)(2,1)S(1)}, u32[]{:S(2)}, u32[]{:S(2)}) collective-permute-start(bf16[64,3968]{1,0:T(8,128)(2,1)S(1)} %copy-done), channel_id=1, source_target_pairs={{0,32},{32,0},{1,33},{33,1},{2,34},{34,2},{3,35},{35,3},{4,36},{36... | collective-permute-start | bytes 1523720 | tf_op jit(solution)/shard_map/ppermute | solution.py:430
  55.9 16.3 %all-to-all-start.2 = ((f32[16,8,640]{2,1,0:T(8,128)}), f32[16,8,640]{2,1,0:T(8,128)S(1)}, u32[]{:S(2)}, u32[]{:S(2)}) async-start(f32[16,8,640]{2,1,0:T(8,128)} %logits.1), calls=%async_computation.2 | async-start | bytes 655360 | tf_op jit(solution)/shard_map/all_to_all | solution.py:426
  65.6 2.3 %copy-start.2 = (f32[3968]{0:T(1024)S(1)}, f32[3968]{0:T(1024)}, u32[]{:S(2)}) copy-start(f32[3968]{0:T(1024)} %param.20) | copy-start | bytes 47620
  65.6 14.1 %collective-permute-start.3 = (bf16[16,112,128]{2,1,0:T(8,128)(2,1)}, bf16[16,112,128]{2,1,0:T(8,128)(2,1)S(1)}, u32[]{:S(2)}, u32[]{:S(2)}) collective-permute-start(bf16[16,112,128]{2,1,0:T(8,128)(2,1)} %get-tuple-element.107), channel_id=1, source_target_pairs={{0,32},{32,0},{1,33},{33,1},{2,34},{34,2},{3,35},{35,3},{4,36},{36... | collective-permute-start | bytes 1376264 | tf_op jit(solution)/shard_map/ppermute | solution.py:430
  73.0 10.7 %all-to-all-start.3 = ((bf16[16,16,256]{2,1,0:T(8,128)(2,1)}), bf16[16,16,256]{2,1,0:T(8,128)(2,1)S(1)}, u32[]{:S(2)}, u32[]{:S(2)}) async-start(bf16[16,16,256]{2,1,0:T(8,128)(2,1)} %get-tuple-element.105), calls=%async_computation.3 | async-start | bytes 262144 | tf_op jit(solution)/shard_map/all_to_all | solution.py:426
  77.4 5.4 %collective-permute-start.4 = (bf16[8,96,128]{2,1,0:T(8,128)(2,1)S(1)}, bf16[8,96,128]{2,1,0:T(8,128)(2,1)S(1)}, u32[]{:S(2)}, u32[]{:S(2)}) collective-permute-start(bf16[8,96,128]{2,1,0:T(8,128)(2,1)S(1)} %all_to_all.25.got_ref.own_index), channel_id=1, source_target_pairs={{0,32},{32,0},{1,33},{33,1},{2,34},{34,2},{3,35},{35,3},{4,36},{36... | collective-permute-start | bytes 589832 | tf_op jit(solution)/shard_map/ppermute | solution.py:430
  89.7 33.2 %all-to-all-start.4 = ((bf16[256,8,128]{2,1,0:T(8,128)(2,1)}), bf16[256,8,128]{2,1,0:T(8,128)(2,1)S(1)}, u32[]{:S(2)}, u32[]{:S(2)}) async-start(bf16[256,8,128]{2,1,0:T(8,128)(2,1)} %bitcast.9), calls=%async_computation.4 | async-start | bytes 1048576 | tf_op jit(solution)/shard_map/all_to_all | solution.py:426
  103.2 3.3 %collective-permute-start.5 = (bf16[16,16,256]{2,1,0:T(8,128)(2,1)S(1)}, bf16[16,16,256]{2,1,0:T(8,128)(2,1)S(1)}, u32[]{:S(2)}, u32[]{:S(2)}) collective-permute-start(bf16[16,16,256]{2,1,0:T(8,128)(2,1)S(1)} %all-to-all-done.3.grad_ref.own_grad), channel_id=1, source_target_pairs={{0,32},{32,0},{1,33},{33,1},{2,34},{34,2},{3,35},{35,3},{4,36},{36... | collective-permute-start | bytes 393224 | tf_op jit(solution)/shard_map/ppermute | solution.py:430
